TPU v7x, 32 devices: a whole 2x2x4 slice. The times are simulated.
32 devices in a mesh: dp: 8 (over z, y), seq: 4 (over x, core).
Axes of the slice: x: 2, y: 2, z: 4, core: 2. Of those that a mesh axis runs over, the one named last changes fastest.
Arguments:
- queries: bfloat16 [8, 512, 2048], P('dp', 'seq'), may hold values from -6 to 6
- grad_out: bfloat16 [8, 512, 2048], P('dp', 'seq'), may hold values from -6 to 6
- encoded: bfloat16 [8, 8, 64, 896], P('dp', 'seq'), may hold values from -6 to 6
- kv_weight: bfloat16 [896, 4096], P(None, 'dp'), may hold values from -0.1875 to 0.1875
- neighbour_ids: int32 [8, 8, 2], P('dp', 'seq'), may hold values from 0 to 7, all different within a row
- slot_map: int32 [8, 8], P('dp'), may hold values from 0 to 7, each once within a row
Outputs:
- attended: bfloat16 [8, 512, 2048], P('dp', 'seq')
- grad_queries: bfloat16 [8, 512, 2048], P('dp', 'seq')
- grad_encoded: float32 [8, 8, 64, 896], P('dp', 'seq')
Inputs may be any that keep to these rules, and one draw needn't show every extreme that they name: `neighbour_ids`: each span names 2 different neighbour ids of its own sequence. `slot_map`: for each sequence a permutation; storage position p lies on the seq index p // 2.
All inputs are finite; a program needn't handle non-finite values.
Results may differ from a plain program's by a relative error of at most 0.018.
Values may be sent and summed in bfloat16 or wider, within the bound.
No kernel may reach another device: no remote copies, remote signals or barrier semaphores. Data moves between devices by JAX's collectives and lax.ppermute only.
A program may use at most 64 MiB of HBM per device.

v0:
```python
import jax
import jax.numpy as jnp
from jax import lax
from jax.sharding import PartitionSpec as P

HEAD_SIZE = 128
HEADS = 16
SPAN = 64
NLEN = 64
READS = 2


def lookup_positions(neighbour_ids, slot_map):
    pool_size = slot_map.shape[1]
    matches = neighbour_ids[0][:, :, None] == jnp.arange(pool_size, dtype=jnp.int32)[None, None, :]
    positions = jnp.sum(jnp.where(matches, slot_map[0][None, None, :], 0), axis=2)
    return positions.reshape(-1)


def per_device(queries, grad_out, encoded, kv_weight, neighbour_ids, slot_map):
    hidden = HEADS * HEAD_SIZE
    scale_factor = HEAD_SIZE ** (-0.5)
    spans = queries.shape[1] // SPAN
    pool_size = slot_map.shape[1]
    width_enc = encoded.shape[3]
    flat_pos = lookup_positions(neighbour_ids, slot_map)
    read_count = flat_pos.shape[0]
    read_rows = read_count * NLEN
    pool_rows = lax.all_gather(encoded, "seq", axis=1, tiled=True)[0]
    picked = jnp.take(pool_rows, flat_pos, axis=0).reshape(read_rows, width_enc)
    whole_weight = lax.all_gather(kv_weight, "dp", axis=1, tiled=True)
    kv_flat = jnp.dot(picked, whole_weight, preferred_element_type=jnp.float32).astype(jnp.bfloat16)
    kv_spans = kv_flat.reshape(spans, READS * NLEN, 2 * hidden)
    keys = kv_spans[:, :, :hidden].reshape(spans, READS * NLEN, HEADS, HEAD_SIZE)
    values = kv_spans[:, :, hidden:].reshape(spans, READS * NLEN, HEADS, HEAD_SIZE)
    query_tiles = queries[0].reshape(spans, SPAN, HEADS, HEAD_SIZE)
    grad_tiles = grad_out[0].reshape(spans, SPAN, HEADS, HEAD_SIZE)
    scores = (
        jnp.einsum("cqhd,ckhd->chqk", query_tiles, keys, preferred_element_type=jnp.float32)
        * scale_factor
    )
    expos = jnp.exp(scores)
    probs = expos / jnp.sum(expos, axis=-1, keepdims=True)
    probs_low = probs.astype(jnp.bfloat16)
    attended = jnp.einsum("chqk,ckhd->cqhd", probs_low, values, preferred_element_type=jnp.float32)
    attended = attended.astype(jnp.bfloat16).reshape(1, spans * SPAN, hidden)
    d_probs = jnp.einsum("cqhd,ckhd->chqk", grad_tiles, values, preferred_element_type=jnp.float32)
    delta = jnp.sum(probs * d_probs, axis=-1, keepdims=True)
    d_scores = (probs * (d_probs - delta) * scale_factor).astype(jnp.bfloat16)
    grad_queries = jnp.einsum("chqk,ckhd->cqhd", d_scores, keys, preferred_element_type=jnp.float32)
    grad_queries = grad_queries.astype(jnp.bfloat16).reshape(1, spans * SPAN, hidden)
    d_keys = jnp.einsum(
        "chqk,cqhd->ckhd", d_scores, query_tiles, preferred_element_type=jnp.float32
    )
    d_values = jnp.einsum(
        "chqk,cqhd->ckhd", probs_low, grad_tiles, preferred_element_type=jnp.float32
    )
    grad_reads = jnp.concatenate(
        [d_keys.reshape(read_rows, hidden), d_values.reshape(read_rows, hidden)], axis=-1
    ).astype(jnp.bfloat16)
    enc_reads = lax.dot_general(
        grad_reads, whole_weight, (((1,), (1,)), ((), ())), preferred_element_type=jnp.float32
    )
    enc_reads = enc_reads.reshape(read_count, NLEN, width_enc)
    onehot = (flat_pos[:, None] == jnp.arange(pool_size, dtype=jnp.int32)[None, :]).astype(
        jnp.float32
    )
    partial_value = jnp.einsum("rn,rlk->nlk", onehot, enc_reads, precision=lax.Precision.HIGHEST)
    rounded = lax.optimization_barrier(partial_value.astype(jnp.bfloat16))
    grad_encoded = lax.psum_scatter(
        rounded.astype(jnp.float32)[None].astype(jnp.bfloat16),
        "seq",
        scatter_dimension=1,
        tiled=True,
    ).astype(jnp.float32)
    return (attended, grad_queries, grad_encoded)


def solution(mesh):
    in_specs = (
        P("dp", "seq", None),
        P("dp", "seq", None),
        P("dp", "seq", None, None),
        P(None, "dp"),
        P("dp", "seq", None),
        P("dp", None),
    )
    out_specs = (P("dp", "seq", None), P("dp", "seq", None), P("dp", "seq", None, None))
    return jax.shard_map(
        per_device, mesh=mesh, in_specs=in_specs, out_specs=out_specs, check_vma=False
    )
```

profile of v0, /device:TPU:0, one launch (start us, length us, event | category | flops | bytes accessed | tf_op | source)
XLA Modules:
  0.0 190.3 jit_solution(6413959391140076882)
XLA Ops:
  7.2 0.7 all-gather.2.cloned.1.call-update
  7.9 0.9 fusion.30
  9.2 1.2 copy.73
  10.4 1.1 copy.74
  11.5 11.0 %all_gather.6 = bf16[1,8,64,896]{3,2,0,1:T(8,128)(2,1)S(1)} all-gather(bf16[1,2,64,896]{3,2,0,1:T(8,128)(2,1)} %bitcast.77), channel_id=1, replica_groups=mesh['dp'=8,'seq'=4] {'seq'}, dimensions={1}, use_global_device_ids=true | all-gather | bytes 1146880 | tf_op jit(solution)/shard_map/all_gather | solution.py:29
  22.5 0.6 gather_fusion
  23.1 0.1 bitcast_select_fusion
  23.3 102.1 %all-gather.2.cloned.1.call-done = bf16[896,4096]{1,0:T(8,128)(2,1)} async-done(((bf16[896,512]{1,0:T(8,128)(2,1)}), bf16[896,4096]{1,0:T(8,128)(2,1)}) %all-gather.2.cloned.1.call-update) | async-done | bytes 7340048 | tf_op jit(solution)/shard_map/all_gather | solution.py:31
  125.4 5.4 %convolution_convert_fusion = bf16[256,4096]{1,0:T(8,128)(2,1)S(1)} fusion(bf16[256,896]{1,0:T(8,128)(2,1)S(1)} %bitcast_select_fusion, bf16[896,4096]{1,0:T(8,128)(2,1)} %all-gather.2.cloned.1.call-done), kind=kOutput, calls=%fused_computation.2 | convolution fusion | flops 1880096768 | bytes 9895936 | tf_op jit(solution)/shard_map/dot_general | solution.py:32
  130.8 1.3 fusion.42
  132.1 0.7 copy.71
  132.8 2.0 %copy.72 = bf16[2,128,2048]{1,2,0:T(8,128)(2,1)S(1)} copy(bf16[2,128,2048]{2,1,0:T(8,128)(2,1)} %get-tuple-element.15) | data formatting | bytes 2097152
  134.8 0.4 fusion.11
  135.2 1.1 copy-done.2
  136.3 1.3 fusion.23
  137.6 3.5 %fusion.6 = bf16[2,128,16,128]{3,1,2,0:T(8,128)(2,1)} fusion(bf16[2,64,16,128]{3,2,1,0:T(8,128)(2,1)S(1)} %bitcast.70, f32[2,16,64,128]{3,2,1,0:T(8,128)} %copy-done.2), kind=kOutput, calls=%fused_computation.11 | convolution fusion | flops 68159616 | bytes 2621440 | tf_op jit(solution)/shard_map/chqk,cqhd->ckhd/dot_general | solution.py:55
  141.1 1.4 convolution_bitcast_fusion
  142.4 3.0 %copy.63 = bf16[2,128,16,128]{3,2,1,0:T(8,128)(2,1)} copy(bf16[2,128,16,128]{3,1,2,0:T(8,128)(2,1)} %fusion.6) | data formatting | bytes 2097152 | tf_op jit(solution)/shard_map/chqk,cqhd->ckhd/transpose | solution.py:55
  145.4 2.9 %fusion.5 = bf16[2,128,16,128]{3,1,2,0:T(8,128)(2,1)S(1)} fusion(f32[2,16,64,128]{3,2,1,0:T(8,128)} %fusion.23, f32[2,16,64,128]{3,2,1,0:T(8,128)} %convolution_bitcast_fusion, bf16[2,64,16,128]{3,2,1,0:T(8,128)(2,1)S(1)} %bitcast.62), kind=kOutput, calls=%fused_computation.10 | convolution fusion | flops 68946048 | bytes 3670016 | tf_op jit(solution)/shard_map/chqk,cqhd->ckhd/dot_general | solution.py:52
  148.4 0.7 copy.61
  149.0 1.7 copy_bitcast_fusion
  150.8 5.7 %fusion.1 = f32[256,896]{1,0:T(8,128)S(1)} fusion(bf16[896,4096]{1,0:T(8,128)(2,1)} %all-gather.2.cloned.1.call-done, bf16[256,2048]{1,0:T(8,128)(2,1)S(1)} %get-tuple-element.17, bf16[256,2048]{1,0:T(8,128)(2,1)S(1)} %get-tuple-element.18), kind=kOutput, calls=%fused_computation.3 | convolution fusion | flops 1883242496 | bytes 10354688 | tf_op jit(solution)/shard_map/dot_general | solution.py:61
  156.5 1.7 convolution_convert_fusion.3
  158.2 1.1 copy.65
  159.3 2.6 %fusion.13 = bf16[2,64,16,128]{3,1,2,0:T(8,128)(2,1)S(1)} fusion(bf16[2,128,16,128]{1,3,2,0:T(8,128)(2,1)S(1)} %bitcast.66, f32[2,16,64,128]{3,2,1,0:T(8,128)} %copy-done.2), kind=kOutput, calls=%fused_computation.22 | convolution fusion | flops 67897472 | bytes 2621440 | tf_op jit(solution)/shard_map/chqk,ckhd->cqhd/dot_general | solution.py:45
  161.9 0.3 copy.55
  162.2 1.0 reshape.85
  163.3 3.2 %fusion.14 = bf16[2,64,16,128]{3,1,2,0:T(8,128)(2,1)S(1)} fusion(bf16[2,128,16,128]{1,3,2,0:T(8,128)(2,1)S(1)} %bitcast.64, f32[2,16,64,128]{3,2,1,0:T(8,128)} %fusion.23, f32[2,16,64,128]{3,2,1,0:T(8,128)} %convolution_bitcast_fusion), kind=kOutput, calls=%fused_computation.23 | convolution fusion | flops 68683904 | bytes 3670016 | tf_op jit(solution)/shard_map/chqk,ckhd->cqhd/dot_general | solution.py:50
  166.5 0.3 copy.59
  166.8 1.0 reshape.86
  167.9 13.9 %reduce-scatter.2.cloned.1.call-done = bf16[1,2,64,896]{3,2,0,1:T(8,128)(2,1)} async-done(((bf16[1,8,64,896]{3,2,0,1:T(8,128)(2,1)}), bf16[1,2,64,896]{3,2,0,1:T(8,128)(2,1)}) %reduce-scatter.2.cloned.1.call-update) | async-done | bytes 229392 | tf_op jit(solution)/shard_map/reduce_scatter | solution.py:70
  181.7 1.7 bitcast_convert_fusion
  (15 shorter events, 0.5 us)
Async XLA Ops:
  7.2 118.2 %all-gather.2.cloned.1.call-start = ((), (), s32[]{:S(2)}) async-start(), calls=%async_computation.1 | async-start | bytes 8257536 | tf_op jit(solution)/shard_map/all_gather | solution.py:31
  7.9 173.8 %reduce-scatter.2.cloned.1.call-start = ((), (), s32[]{:S(2)}) async-start(), calls=%async_computation.2 | async-start | bytes 1146880 | tf_op jit(solution)/shard_map/reduce_scatter | solution.py:70
  132.8 8.3 %copy-start = (bf16[2,128,2048]{1,2,0:T(8,128)(2,1)}, bf16[2,128,2048]{1,2,0:T(8,128)(2,1)S(1)}, u32[]{:S(2)}) copy-start(bf16[2,128,2048]{1,2,0:T(8,128)(2,1)S(1)} %copy.71) | copy-start | bytes 3145732
  135.2 1.1 copy-start.2
  156.5 2.8 %copy-start.1 = (bf16[2,128,2048]{1,2,0:T(8,128)(2,1)S(1)}, bf16[2,128,2048]{1,2,0:T(8,128)(2,1)}, u32[]{:S(2)}) copy-start(bf16[2,128,2048]{1,2,0:T(8,128)(2,1)} %copy-done) | copy-start | bytes 3145732
Sparse Core Ops, SparseCore 0:
  10.0 115.3 all-gather.1
  159.4 22.2 reduce-scatter.1
where the time goes:
time: 191 us; the launch traced here: 190 us
  waiting for transfers between devices  117 us (61%)
  matrix products  26.8 us (14%)
  local copies, waits for them, and re-layouts  17.4 us (9%)
  between operations  14.2 us (7%)
  blocking collectives  11 us (6%)
  other arithmetic  4.12 us (2%)
    all_gather x1, waiting for transfers between devices, per_device(): whole_weight = lax.all_gather(kv_weight, 'dp', axis=1, tiled=True)  102 us
    reduce_scatter x1, waiting for transfers between devices, per_device(): lax.psum_scatter(rounded.astype(jnp.float32)[None].astype(jnp.bfloat16),...  13.9 us
    all_gather x1, blocking collectives, per_device(): pool_rows = lax.all_gather(encoded, 'seq', axis=1, tiled=True)[0]  11 us
    unnamed x10, local copies, waits for them, and re-layouts  6.01 us
    dot_general x1, matrix products, per_device(): lax.dot_general(grad_reads, whole_weight, (((1,), (1,)), ((), ())), prefe...  5.69 us
    dot_general x1, matrix products, per_device(): jnp.dot(picked, whole_weight, preferred_element_type=jnp.float32)  5.42 us
  transfers between devices with their start and end apart: 2, of which 2 were waited for; matrix products, arithmetic and copies ran while one was open for 7% of the time, Pallas kernels for 0%

commit v1 on v0

v1 whole, which is shorter than its diff:
```python
import functools

import jax
import jax.numpy as jnp
from jax import lax
from jax.experimental import pallas as pl
from jax.experimental.pallas import tpu as pltpu
from jax.sharding import PartitionSpec as P

HEAD_SIZE = 128
HEADS = 16
SPAN = 64
NLEN = 64
READS = 2
VMEM_BYTES = 48 * 1024 * 1024

NT = (((1,), (1,)), ((), ()))
TN = (((0,), (0,)), ((), ()))


def xor_send(value, axis, size, bit):
    return lax.ppermute(value, axis, [(i, i ^ bit) for i in range(size)])


def bit_reverse(index, bits):
    result = index * 0
    for i in range(bits):
        result = result + (((index >> i) & 1) << (bits - 1 - i))
    return result


def pack_body(seq_size, meta, queries, grad_out, *pieces):
    own, first = meta[0], meta[1]
    for k in range(seq_size):
        for r in range(HEADS // seq_size):
            column = pl.multiple_of(((first ^ r) * seq_size + (own ^ k)) * HEAD_SIZE, HEAD_SIZE)
            place = slice(r * HEAD_SIZE, (r + 1) * HEAD_SIZE)
            pieces[k][0, :, place] = queries[0, :, pl.ds(column, HEAD_SIZE)]
            pieces[k][1, :, place] = grad_out[0, :, pl.ds(column, HEAD_SIZE)]


def pack(meta, queries, grad_out, seq_size):
    tokens = queries.shape[1]
    shape = jax.ShapeDtypeStruct((2, tokens, HEADS // seq_size * HEAD_SIZE), jnp.bfloat16)
    return pl.pallas_call(
        functools.partial(pack_body, seq_size),
        out_shape=[shape] * seq_size,
        in_specs=[pl.BlockSpec(memory_space=pltpu.SMEM)] + [pl.BlockSpec(memory_space=pltpu.VMEM)] * 2,
        out_specs=[pl.BlockSpec(memory_space=pltpu.VMEM)] * seq_size,
        compiler_params=pltpu.CompilerParams(vmem_limit_bytes=VMEM_BYTES),
        name="pack",
    )(meta, queries, grad_out)


def attention_body(seq_size, spans, heads, has_prior, *refs):
    meta = refs[0]
    count = len(heads)
    enc_low, enc_high = refs[1], refs[2]
    weights = refs[3 : 3 + 2 * count]
    at = 3 + 2 * count
    pieces = refs[at : at + seq_size]
    at += seq_size
    prior = refs[at] if has_prior else None
    at += has_prior
    outs = refs[at : at + seq_size]
    grad_rows = refs[at + seq_size]
    pair, kv, d_kv = refs[at + seq_size + 1 :]
    half = enc_low.shape[0]
    bits = seq_size.bit_length() - 1
    scale = HEAD_SIZE ** (-0.5)
    keys_first = meta[2] == 1
    for i, head in enumerate(heads):
        first, second = weights[2 * i][...], weights[2 * i + 1][...]
        pair[:, :HEAD_SIZE] = jnp.where(keys_first, first, second)
        pair[:, HEAD_SIZE:] = jnp.where(keys_first, second, first)
        kv[:half] = jnp.dot(enc_low[...], pair[...], preferred_element_type=jnp.float32).astype(jnp.bfloat16)
        kv[half:] = jnp.dot(enc_high[...], pair[...], preferred_element_type=jnp.float32).astype(jnp.bfloat16)
        d_kv[...] = jnp.zeros_like(d_kv)
        columns = slice(head * HEAD_SIZE, (head + 1) * HEAD_SIZE)
        out_columns = slice(i * HEAD_SIZE, (i + 1) * HEAD_SIZE)
        for k in range(seq_size):
            order = bit_reverse(k, bits)
            for c in range(spans):
                rows = slice(c * SPAN, (c + 1) * SPAN)
                starts = [
                    pl.multiple_of(meta[4 + (order * spans + c) * READS + r] * NLEN, NLEN)
                    for r in range(READS)
                ]
                read = jnp.concatenate([kv[pl.ds(start, NLEN), :] for start in starts], axis=0)
                keys, values = read[:, :HEAD_SIZE], read[:, HEAD_SIZE:]
                query = pieces[k][0, rows, columns]
                grad = pieces[k][1, rows, columns]
                scores = lax.dot_general(query, keys, NT, preferred_element_type=jnp.float32) * scale
                d_probs = lax.dot_general(grad, values, NT, preferred_element_type=jnp.float32)
                expos = jnp.exp(scores)
                probs = expos / jnp.sum(expos, axis=-1, keepdims=True)
                probs_low = probs.astype(jnp.bfloat16)
                delta = jnp.sum(probs * d_probs, axis=-1, keepdims=True)
                d_scores = (probs * (d_probs - delta) * scale).astype(jnp.bfloat16)
                outs[k][0, rows, out_columns] = jnp.dot(
                    probs_low, values, preferred_element_type=jnp.float32
                ).astype(jnp.bfloat16)
                outs[k][1, rows, out_columns] = jnp.dot(
                    d_scores, keys, preferred_element_type=jnp.float32
                ).astype(jnp.bfloat16)
                d_keys = lax.dot_general(d_scores, query, TN, preferred_element_type=jnp.float32)
                d_values = lax.dot_general(probs_low, grad, TN, preferred_element_type=jnp.float32)
                for r, start in enumerate(starts):
                    part = slice(r * NLEN, (r + 1) * NLEN)
                    d_kv[pl.ds(start, NLEN), :HEAD_SIZE] += d_keys[part]
                    d_kv[pl.ds(start, NLEN), HEAD_SIZE:] += d_values[part]
        term = lax.dot_general(
            d_kv[...].astype(jnp.bfloat16), pair[...], NT, preferred_element_type=jnp.float32
        )
        if i == 0:
            grad_rows[...] = term + prior[...] if has_prior else term
        else:
            grad_rows[...] += term


def attention(meta, enc_low, enc_high, weights, pieces, heads, spans, prior):
    seq_size = len(pieces)
    tokens = pieces[0].shape[1]
    rows = 2 * enc_low.shape[0]
    width = enc_low.shape[1]
    count = len(heads)
    prior = [] if prior is None else [prior]
    vmem = pl.BlockSpec(memory_space=pltpu.VMEM)
    operands = [enc_low, enc_high, *weights, *pieces, *prior]
    out_shape = [jax.ShapeDtypeStruct((2, tokens, count * HEAD_SIZE), jnp.bfloat16)] * seq_size
    out_shape.append(jax.ShapeDtypeStruct((rows, width), jnp.float32))
    outs = pl.pallas_call(
        functools.partial(attention_body, seq_size, spans, heads, len(prior)),
        out_shape=out_shape,
        in_specs=[pl.BlockSpec(memory_space=pltpu.SMEM)] + [vmem] * len(operands),
        out_specs=[vmem] * len(out_shape),
        scratch_shapes=[
            pltpu.VMEM((width, 2 * HEAD_SIZE), jnp.bfloat16),
            pltpu.VMEM((rows, 2 * HEAD_SIZE), jnp.bfloat16),
            pltpu.VMEM((rows, 2 * HEAD_SIZE), jnp.float32),
        ],
        compiler_params=pltpu.CompilerParams(vmem_limit_bytes=VMEM_BYTES),
        cost_estimate=pl.CostEstimate(
            flops=count * (8 * rows * width * HEAD_SIZE), bytes_accessed=2 * rows * width, transcendentals=0
        ),
        name="attention",
    )(meta, *operands)
    return outs[:-1], outs[-1]


def unpack_body(seq_size, groups, meta, *refs):
    count = len(groups) * seq_size
    attended, grad_queries, sems = refs[count:]
    own, first = meta[0], meta[1]
    copies = []
    for g, heads in enumerate(groups):
        for k in range(seq_size):
            for i, r in enumerate(heads):
                column = pl.multiple_of(((first ^ r) * seq_size + (own ^ k)) * HEAD_SIZE, HEAD_SIZE)
                for which, target in enumerate((attended, grad_queries)):
                    copy = pltpu.make_async_copy(
                        refs[g * seq_size + k].at[which, :, pl.ds(i * HEAD_SIZE, HEAD_SIZE)],
                        target.at[0, :, pl.ds(column, HEAD_SIZE)],
                        sems.at[len(copies)],
                    )
                    copy.start()
                    copies.append(copy)
    for copy in copies:
        copy.wait()


def unpack(meta, parts, groups, seq_size):
    tokens = parts[0].shape[1]
    shape = jax.ShapeDtypeStruct((1, tokens, HEADS * HEAD_SIZE), jnp.bfloat16)
    anywhere = pl.BlockSpec(memory_space=pl.ANY)
    return pl.pallas_call(
        functools.partial(unpack_body, seq_size, groups),
        out_shape=[shape, shape],
        in_specs=[pl.BlockSpec(memory_space=pltpu.SMEM)] + [anywhere] * len(parts),
        out_specs=[anywhere, anywhere],
        scratch_shapes=[pltpu.SemaphoreType.DMA((2 * HEADS,))],
        name="unpack",
    )(meta, *parts)


def gather_weights(kv_weight, own, dp_size, seq_size):
    blocks = 2 * HEADS // dp_size
    if dp_size == 8 and blocks == seq_size:
        mine = lax.dynamic_slice_in_dim(kv_weight, own * HEAD_SIZE, HEAD_SIZE, axis=1)
        send = functools.partial(xor_send, axis="dp", size=dp_size)
        far = send(mine, bit=4)
        near = send(mine, bit=2)
        side = send(mine, bit=1)
        side_far = send(far, bit=1)
        near_far = send(far, bit=2)
        side_near = send(side, bit=2)
        side_near_far = send(near_far, bit=1)
        return [(mine, far), (side, side_far), (near, near_far), (side_near, side_near_far)]
    whole = lax.all_gather(kv_weight, "dp", axis=1, tiled=True)
    pairs = []
    for r in range(HEADS // seq_size):
        column = (r * seq_size + own) * HEAD_SIZE
        pairs.append(
            tuple(
                lax.dynamic_slice_in_dim(whole, column + part * HEADS * HEAD_SIZE, HEAD_SIZE, axis=1)
                for part in range(2)
            )
        )
    return pairs


def per_device(dp_size, seq_size, queries, grad_out, encoded, kv_weight, neighbour_ids, slot_map):
    own = lax.axis_index("seq")
    place = lax.axis_index("dp")
    bits = seq_size.bit_length() - 1
    stored = encoded.shape[1]
    spans = neighbour_ids.shape[1]
    width = encoded.shape[3]
    split = dp_size == 8 and 2 * HEADS == dp_size * seq_size
    first = place % (HEADS // seq_size) if split else place * 0
    keys_first = (place < dp_size // 2).astype(jnp.int32) if split else place * 0 + 1
    send = functools.partial(xor_send, axis="seq", size=seq_size)

    pool_size = slot_map.shape[1]
    matches = neighbour_ids[0][:, :, None] == jnp.arange(pool_size, dtype=jnp.int32)[None, None, :]
    positions = jnp.sum(jnp.where(matches, slot_map[0][None, None, :], 0), axis=2).reshape(-1)
    rows = encoded[0].reshape(stored * NLEN, width)
    head_meta = jnp.stack([own, first, keys_first, place])
    pieces = pack(head_meta, queries, grad_out, seq_size)
    pieces = [pieces[0]] + [send(pieces[k], bit=k) for k in range(1, seq_size)]
    for level in range(bits - 1, 0, -1):
        rows = jnp.concatenate([rows, send(rows, bit=1 << level)], axis=0)
    enc_low, enc_high = rows, send(rows, bit=1)
    for level in range(bits - 1, -1, -1):
        positions = jnp.concatenate([positions, send(positions, bit=1 << level)])
    relative = bit_reverse((positions // stored) ^ own, bits) * stored + positions % stored
    meta = jnp.concatenate([head_meta, relative])

    pairs = gather_weights(kv_weight, own, dp_size, seq_size)
    groups = [(0, 1), (2, 3)] if len(pairs) == 4 else [tuple(range(len(pairs)))]
    parts = []
    grads = None
    for heads in groups:
        weights = [block for head in heads for block in pairs[head]]
        outs, grads = attention(meta, enc_low, enc_high, weights, pieces, heads, spans, grads)
        parts.append([outs[0]] + [send(outs[k], bit=k) for k in range(1, seq_size)])
    for level in range(bits):
        half = grads.shape[0] // 2
        arrived = send(grads[half:].astype(jnp.bfloat16), bit=1 << level)
        grads = grads[:half] + arrived.astype(jnp.float32)
    flat = [part for group in parts for part in group]
    attended, grad_queries = unpack(head_meta, flat, groups, seq_size)
    return attended, grad_queries, grads.reshape(1, stored, NLEN, width)


def solution(mesh):
    in_specs = (
        P("dp", "seq", None),
        P("dp", "seq", None),
        P("dp", "seq", None, None),
        P(None, "dp"),
        P("dp", "seq", None),
        P("dp", None),
    )
    out_specs = (P("dp", "seq", None), P("dp", "seq", None), P("dp", "seq", None, None))
    return jax.shard_map(
        functools.partial(per_device, mesh.shape["dp"], mesh.shape["seq"]),
        mesh=mesh,
        in_specs=in_specs,
        out_specs=out_specs,
        check_vma=False,
    )
```

time: 191 us -> 108 us (0.57)
  waiting for transfers between devices: 117 us -> 23 us
  Pallas kernels: 0 us -> 53.5 us
  matrix products: 26.8 us -> 0 us
  starting transfers between devices: 0.08 us -> 21 us
  between operations: 14.2 us -> 0.83 us
  local copies, waits for them, and re-layouts: 17.4 us -> 5.89 us
  blocking collectives: 11 us -> 0 us
    all_gather x1 -> x0, waiting for transfers between devices: 102 us -> none  [per_device(): whole_weight = lax.all_gather(kv_weight, 'dp', axis=1, tiled=True)]
    pallas_call x0 -> x4, Pallas kernels: none -> 53.5 us  [the longest x1 33.8 us: unpack(): pl.pallas_call(functools.partial(unpack_body, seq_size, groups), out_shap...]
    dot_general x9 -> x0, matrix products: 26.8 us -> none  [the longest x1 5.69 us: per_device(): lax.dot_general(grad_reads, whole_weight, (((1,), (1,)), ((), ())), prefe...]
    ppermute x0 -> x22, waiting for transfers between devices: none -> 23 us  [xor_send(): return lax.ppermute(value, axis, [(i, i ^ bit) for i in range(size)])]
    ppermute x0 -> x22, starting transfers between devices: none -> 21 us  [xor_send(): return lax.ppermute(value, axis, [(i, i ^ bit) for i in range(size)])]
    reduce_scatter x1 -> x0, waiting for transfers between devices: 13.9 us -> none  [per_device(): lax.psum_scatter(rounded.astype(jnp.float32)[None].astype(jnp.bfloat16),...]
    all_gather x1 -> x0, blocking collectives: 11 us -> none  [per_device(): pool_rows = lax.all_gather(encoded, 'seq', axis=1, tiled=True)[0]]
    reshape x5 -> x1, local copies, waits for them, and re-layouts: 3.93 us -> 0.08 us  [per_device(): jnp.sum(jnp.where(matches, slot_map[0][None, None, :], 0), axis=2)]
  transfers between devices with their start and end apart: 2 -> 22, of which waited for: 2 -> 8; matrix products, arithmetic and copies ran while one was open for 7% -> 2% of each run, Pallas kernels for 0% -> 41%
where the time goes in v1:
time: 108 us; the launch traced here: 107 us
  Pallas kernels  53.5 us (50%)
  waiting for transfers between devices  23 us (21%)
  starting transfers between devices  21 us (19%)
  local copies, waits for them, and re-layouts  5.89 us (5%)
  other arithmetic  3.01 us (3%)
    pallas_call x1, Pallas kernels, unpack(): pl.pallas_call(functools.partial(unpack_body, seq_size, groups), out_shap...  33.8 us
    ppermute x22, waiting for transfers between devices, xor_send(): return lax.ppermute(value, axis, [(i, i ^ bit) for i in range(size)])  23 us
    ppermute x22, starting transfers between devices, xor_send(): return lax.ppermute(value, axis, [(i, i ^ bit) for i in range(size)])  21 us
    pallas_call x2, Pallas kernels, attention(): pl.pallas_call(functools.partial(attention_body, seq_size, spans, heads,...  18.8 us
    unnamed x30, local copies, waits for them, and re-layouts  5.61 us
  transfers between devices with their start and end apart: 22, of which 8 were waited for; matrix products, arithmetic and copies ran while one was open for 2% of the time, Pallas kernels for 41%

profile of v1, /device:TPU:0, one launch (start us, length us, event | category | flops | bytes accessed | tf_op | source)
XLA Modules:
  0.0 107.2 jit_solution(13744094875977828356)
XLA Ops:
  0.6 3.0 %collective-permute-start.2 = (bf16[128,896]{1,0:T(8,128)(2,1)}, bf16[128,896]{1,0:T(8,128)(2,1)S(1)}, u32[]{:S(2)}, u32[]{:S(2)}) collective-permute-start(bf16[128,896]{1,0:T(8,128)(2,1)} %bitcast.9), channel_id=1, source_target_pairs={{0,2},{1,3},{2,0},{3,1},{4,6},{5,7},{6,4},{7,5},{8,10},{9,11},{10,... | collective-permute-start | bytes 688136 | tf_op jit(solution)/shard_map/ppermute | solution.py:22
  3.7 2.7 %collective-permute-start.4 = (bf16[896,128]{1,0:T(8,128)(2,1)S(1)}, bf16[896,128]{1,0:T(8,128)(2,1)S(1)}, u32[]{:S(2)}, u32[]{:S(2)}) collective-permute-start(bf16[896,128]{1,0:T(8,128)(2,1)S(1)} %constant_dynamic-slice_fusion.refs_3_), channel_id=1, source_target_pairs={{0,16},{4,20},{8,24},{12,28},{16,0},{20,4},{24,8},{28,12},{1,17},{... | collective-permute-start | bytes 688136 | tf_op jit(solution)/shard_map/ppermute | solution.py:22
  6.3 1.5 %collective-permute-start.5 = (bf16[896,128]{1,0:T(8,128)(2,1)S(1)}, bf16[896,128]{1,0:T(8,128)(2,1)}, u32[]{:S(2)}, u32[]{:S(2)}) collective-permute-start(bf16[896,128]{1,0:T(8,128)(2,1)S(1)} %constant_dynamic-slice_fusion.refs_3_), channel_id=1, source_target_pairs={{0,4},{4,0},{8,12},{12,8},{16,20},{20,16},{24,28},{28,24},{1,5},{5... | collective-permute-start | bytes 688136 | tf_op jit(solution)/shard_map/ppermute | solution.py:22
  7.9 0.9 fusion
  8.8 1.1 %collective-permute-start = (s32[4]{0:T(128)S(1)}, s32[4]{0:T(128)S(1)}, u32[]{:S(2)}, u32[]{:S(2)}) collective-permute-start(s32[4]{0:T(128)S(1)} %reshape.14), channel_id=1, source_target_pairs={{0,2},{1,3},{2,0},{3,1},{4,6},{5,7},{6,4},{7,5},{8,10},{9,11},{10,... | collective-permute-start | bytes 56 | tf_op jit(solution)/shard_map/ppermute | solution.py:22
  10.0 1.0 copy-done.2
  11.1 1.0 copy-done.3
  12.1 0.8 pack.1
  13.0 1.0 pad_maximum_fusion.refs_1_
  14.7 1.3 %collective-permute-done.1 = s32[8]{0:T(128)S(1)} collective-permute-done((s32[8]{0:T(128)S(1)}, s32[8]{0:T(128)S(1)}, u32[]{:S(2)}, u32[]{:S(2)}) %collective-permute-start.1) | collective-permute-done | bytes 64 | tf_op jit(solution)/shard_map/ppermute | solution.py:22
  16.0 0.9 collective-permute-start.8
  17.0 0.7 copy-done.7
  17.6 0.8 collective-permute-start.9
  18.4 1.6 %collective-permute-start.14 = (bf16[896,128]{1,0:T(8,128)(2,1)}, bf16[896,128]{1,0:T(8,128)(2,1)S(1)}, u32[]{:S(2)}, u32[]{:S(2)}) collective-permute-start(bf16[896,128]{1,0:T(8,128)(2,1)} %copy-done.7), channel_id=1, source_target_pairs={{0,8},{4,12},{8,0},{12,4},{16,24},{20,28},{24,16},{28,20},{1,9},{5... | collective-permute-start | bytes 688136 | tf_op jit(solution)/shard_map/ppermute | solution.py:22
  20.5 4.6 %collective-permute-done.8.refs_9_ = bf16[2,128,512]{2,1,0:T(8,128)(2,1)S(1)} collective-permute-done((bf16[2,128,512]{2,1,0:T(8,128)(2,1)S(1)}, bf16[2,128,512]{2,1,0:T(8,128)(2,1)S(1)}, u32[]{:S(2)}, u32[]{:S(2)}) %collective-permute-start.8) | collective-permute-done | bytes 262176 | tf_op jit(solution)/shard_map/ppermute | solution.py:22
  25.2 1.6 %collective-permute-start.13 = (bf16[896,128]{1,0:T(8,128)(2,1)S(1)}, bf16[896,128]{1,0:T(8,128)(2,1)}, u32[]{:S(2)}, u32[]{:S(2)}) collective-permute-start(bf16[896,128]{1,0:T(8,128)(2,1)S(1)} %constant_dynamic-slice_fusion.refs_3_), channel_id=1, source_target_pairs={{0,8},{4,12},{8,0},{12,4},{16,24},{20,28},{24,16},{28,20},{1,9},{5... | collective-permute-start | bytes 688136 | tf_op jit(solution)/shard_map/ppermute | solution.py:22
  26.7 2.9 %collective-permute-done.9.refs_10_ = bf16[2,128,512]{2,1,0:T(8,128)(2,1)S(1)} collective-permute-done((bf16[2,128,512]{2,1,0:T(8,128)(2,1)S(1)}, bf16[2,128,512]{2,1,0:T(8,128)(2,1)S(1)}, u32[]{:S(2)}, u32[]{:S(2)}) %collective-permute-start.9) | collective-permute-done | bytes 262176 | tf_op jit(solution)/shard_map/ppermute | solution.py:22
  29.7 1.6 %collective-permute-start.15 = (bf16[896,128]{1,0:T(8,128)(2,1)}, bf16[896,128]{1,0:T(8,128)(2,1)}, u32[]{:S(2)}, u32[]{:S(2)}) collective-permute-start(bf16[896,128]{1,0:T(8,128)(2,1)} %collective-permute-done.5.refs_5_), channel_id=1, source_target_pairs={{0,8},{4,12},{8,0},{12,4},{16,24},{20,28},{24,16},{28,20},{1,9},{5... | collective-permute-start | bytes 688136 | tf_op jit(solution)/shard_map/ppermute | solution.py:22
  31.9 0.9 copy-done.8
  32.9 9.0 %attention.2 = (bf16[2,128,256]{2,1,0:T(8,128)(2,1)S(1)}, bf16[2,128,256]{2,1,0:T(8,128)(2,1)S(1)}, bf16[2,128,256]{2,1,0:T(8,128)(2,1)S(1)}, bf16[2,128,256]{2,1,0:T(8,128)(2,1)S(1)}, f32[512,896]{1,0:T(8,128)S(1)}) custom-call(s32[20]{0:T(128)S(1)} %concatenate.16.refs_0_, bf16[256,896]{1,0:T(8,128)(2,1)S(1)} %pad_maximum_fusion.refs_1_, ...), custom_call_target="tpu_custom_call" | custom-call | flops 939524096 | bytes 917504 | tf_op jit(solution)/shard_map/attention/pallas_call | solution.py:132
  41.9 1.2 %copy-done.1 = f32[512,896]{1,0:T(8,128)} copy-done((f32[512,896]{1,0:T(8,128)}, f32[512,896]{1,0:T(8,128)S(1)}, u32[]{:S(2)}) %copy-start.1) | copy-done | bytes 1835032
  43.1 9.9 %attention.3 = (bf16[2,128,256]{2,1,0:T(8,128)(2,1)S(1)}, bf16[2,128,256]{2,1,0:T(8,128)(2,1)S(1)}, bf16[2,128,256]{2,1,0:T(8,128)(2,1)S(1)}, bf16[2,128,256]{2,1,0:T(8,128)(2,1)S(1)}, f32[512,896]{1,0:T(8,128)S(1)}) custom-call(s32[20]{0:T(128)S(1)} %concatenate.16.refs_0_, bf16[256,896]{1,0:T(8,128)(2,1)S(1)} %pad_maximum_fusion.refs_1_, ...), custom_call_target="tpu_custom_call" | custom-call | flops 939524096 | bytes 917504 | tf_op jit(solution)/shard_map/attention/pallas_call | solution.py:132
  53.6 0.9 collective-permute-start.11
  55.1 1.0 collective-permute-start.21
  56.1 0.6 collective-permute-start.12
  57.3 0.9 collective-permute-start.18
  58.2 1.8 %collective-permute-done.11.refs_2_ = bf16[2,128,256]{2,1,0:T(8,128)(2,1)S(1)} collective-permute-done((bf16[2,128,256]{2,1,0:T(8,128)(2,1)S(1)}, bf16[2,128,256]{2,1,0:T(8,128)(2,1)S(1)}, u32[]{:S(2)}, u32[]{:S(2)}) %collective-permute-start.11) | collective-permute-done | bytes 131104 | tf_op jit(solution)/shard_map/ppermute | solution.py:22
  60.0 6.3 %collective-permute-done.12.refs_3_ = bf16[2,128,256]{2,1,0:T(8,128)(2,1)S(1)} collective-permute-done((bf16[2,128,256]{2,1,0:T(8,128)(2,1)S(1)}, bf16[2,128,256]{2,1,0:T(8,128)(2,1)S(1)}, u32[]{:S(2)}, u32[]{:S(2)}) %collective-permute-start.12) | collective-permute-done | bytes 131104 | tf_op jit(solution)/shard_map/ppermute | solution.py:22
  66.3 4.3 %collective-permute-done.18.refs_6_ = bf16[2,128,256]{2,1,0:T(8,128)(2,1)S(1)} collective-permute-done((bf16[2,128,256]{2,1,0:T(8,128)(2,1)S(1)}, bf16[2,128,256]{2,1,0:T(8,128)(2,1)S(1)}, u32[]{:S(2)}, u32[]{:S(2)}) %collective-permute-start.18) | collective-permute-done | bytes 131104 | tf_op jit(solution)/shard_map/ppermute | solution.py:22
  70.5 1.3 %collective-permute-done.19.refs_7_ = bf16[2,128,256]{2,1,0:T(8,128)(2,1)S(1)} collective-permute-done((bf16[2,128,256]{2,1,0:T(8,128)(2,1)S(1)}, bf16[2,128,256]{2,1,0:T(8,128)(2,1)S(1)}, u32[]{:S(2)}, u32[]{:S(2)}) %collective-permute-start.19) | collective-permute-done | bytes 131104 | tf_op jit(solution)/shard_map/ppermute | solution.py:22
  72.5 33.8 %unpack.1 = (bf16[1,128,2048]{2,1,0:T(8,128)(2,1)}, bf16[1,128,2048]{2,1,0:T(8,128)(2,1)}) custom-call(s32[4]{0:T(128)} %copy-done.6, bf16[2,128,256]{2,1,0:T(8,128)(2,1)} %copy-done.4, bf16[2,128,256]{2,1,0:T(8,128)(2,1)} %copy-done.9, bf16[2,128,256]{2,1,0:T(8,128)(2,1)} %copy-done.10, bf16[2,128,256]{2,1,0:T(8,128)(2,1)} %copy-done.11, ...), custom_call_target="tpu_custom_call" | custom-call | tf_op jit(solution)/shard_map/unpack/pallas_call | solution.py:176
  106.4 0.8 slice_add_fusion
  (58 shorter events, 4.5 us)
Async XLA Ops:
  0.6 3.0 %copy-start = (bf16[896,512]{1,0:T(8,128)(2,1)S(1)}, bf16[896,512]{1,0:T(8,128)(2,1)}, u32[]{:S(2)}) copy-start(bf16[896,512]{1,0:T(8,128)(2,1)} %param.9) | copy-start | bytes 2752516
  0.6 12.4 %collective-permute-start.2 = (bf16[128,896]{1,0:T(8,128)(2,1)}, bf16[128,896]{1,0:T(8,128)(2,1)S(1)}, u32[]{:S(2)}, u32[]{:S(2)}) collective-permute-start(bf16[128,896]{1,0:T(8,128)(2,1)} %bitcast.9), channel_id=1, source_target_pairs={{0,2},{1,3},{2,0},{3,1},{4,6},{5,7},{6,4},{7,5},{8,10},{9,11},{10,... | collective-permute-start | bytes 688136 | tf_op jit(solution)/shard_map/ppermute | solution.py:22
  3.7 13.3 %collective-permute-start.4 = (bf16[896,128]{1,0:T(8,128)(2,1)S(1)}, bf16[896,128]{1,0:T(8,128)(2,1)S(1)}, u32[]{:S(2)}, u32[]{:S(2)}) collective-permute-start(bf16[896,128]{1,0:T(8,128)(2,1)S(1)} %constant_dynamic-slice_fusion.refs_3_), channel_id=1, source_target_pairs={{0,16},{4,20},{8,24},{12,28},{16,0},{20,4},{24,8},{28,12},{1,17},{... | collective-permute-start | bytes 688136 | tf_op jit(solution)/shard_map/ppermute | solution.py:22
  6.3 12.1 %collective-permute-start.5 = (bf16[896,128]{1,0:T(8,128)(2,1)S(1)}, bf16[896,128]{1,0:T(8,128)(2,1)}, u32[]{:S(2)}, u32[]{:S(2)}) collective-permute-start(bf16[896,128]{1,0:T(8,128)(2,1)S(1)} %constant_dynamic-slice_fusion.refs_3_), channel_id=1, source_target_pairs={{0,4},{4,0},{8,12},{12,8},{16,20},{20,16},{24,28},{28,24},{1,5},{5... | collective-permute-start | bytes 688136 | tf_op jit(solution)/shard_map/ppermute | solution.py:22
  8.8 5.7 %collective-permute-start = (s32[4]{0:T(128)S(1)}, s32[4]{0:T(128)S(1)}, u32[]{:S(2)}, u32[]{:S(2)}) collective-permute-start(s32[4]{0:T(128)S(1)} %reshape.14), channel_id=1, source_target_pairs={{0,2},{1,3},{2,0},{3,1},{4,6},{5,7},{6,4},{7,5},{8,10},{9,11},{10,... | collective-permute-start | bytes 56 | tf_op jit(solution)/shard_map/ppermute | solution.py:22
  12.1 29.7 %copy-start.6 = (s32[4]{0:T(128)}, s32[4]{0:T(128)S(1)}, u32[]{:S(2)}) copy-start(s32[4]{0:T(128)S(1)} %pad_add_fusion.meta) | copy-start | bytes 52
  12.9 7.1 %collective-permute-start.7 = (bf16[2,128,512]{2,1,0:T(8,128)(2,1)S(1)}, bf16[2,128,512]{2,1,0:T(8,128)(2,1)S(1)}, u32[]{:S(2)}, u32[]{:S(2)}) collective-permute-start(bf16[2,128,512]{2,1,0:T(8,128)(2,1)S(1)} %get-tuple-element.20), channel_id=1, source_target_pairs={{0,1},{1,0},{2,3},{3,2},{4,5},{5,4},{6,7},{7,6},{8,9},{9,8},{10,11... | collective-permute-start | bytes 786440 | tf_op jit(solution)/shard_map/ppermute | solution.py:22
  14.0 17.9 %collective-permute-start.3 = (bf16[256,896]{1,0:T(8,128)(2,1)S(1)}, bf16[256,896]{1,0:T(8,128)(2,1)S(1)}, u32[]{:S(2)}, u32[]{:S(2)}) collective-permute-start(bf16[256,896]{1,0:T(8,128)(2,1)S(1)} %pad_maximum_fusion.refs_1_), channel_id=1, source_target_pairs={{0,1},{1,0},{2,3},{3,2},{4,5},{5,4},{6,7},{7,6},{8,9},{9,8},{10,11... | collective-permute-start | bytes 1376264 | tf_op jit(solution)/shard_map/ppermute | solution.py:22
  14.7 1.4 %collective-permute-start.1 = (s32[8]{0:T(128)S(1)}, s32[8]{0:T(128)S(1)}, u32[]{:S(2)}, u32[]{:S(2)}) collective-permute-start(s32[8]{0:T(128)S(1)} %pad_add_fusion.1), channel_id=1, source_target_pairs={{0,1},{1,0},{2,3},{3,2},{4,5},{5,4},{6,7},{7,6},{8,9},{9,8},{10,11... | collective-permute-start | bytes 104 | tf_op jit(solution)/shard_map/ppermute | solution.py:22
  16.0 9.1 %collective-permute-start.8 = (bf16[2,128,512]{2,1,0:T(8,128)(2,1)S(1)}, bf16[2,128,512]{2,1,0:T(8,128)(2,1)S(1)}, u32[]{:S(2)}, u32[]{:S(2)}) collective-permute-start(bf16[2,128,512]{2,1,0:T(8,128)(2,1)S(1)} %get-tuple-element.21), channel_id=1, source_target_pairs={{0,2},{1,3},{2,0},{3,1},{4,6},{5,7},{6,4},{7,5},{8,10},{9,11},{10,... | collective-permute-start | bytes 786440 | tf_op jit(solution)/shard_map/ppermute | solution.py:22
  17.6 12.0 %collective-permute-start.9 = (bf16[2,128,512]{2,1,0:T(8,128)(2,1)S(1)}, bf16[2,128,512]{2,1,0:T(8,128)(2,1)S(1)}, u32[]{:S(2)}, u32[]{:S(2)}) collective-permute-start(bf16[2,128,512]{2,1,0:T(8,128)(2,1)S(1)} %get-tuple-element.22), channel_id=1, source_target_pairs={{0,3},{1,2},{2,1},{3,0},{4,7},{5,6},{6,5},{7,4},{8,11},{9,10},{10,... | collective-permute-start | bytes 786440 | tf_op jit(solution)/shard_map/ppermute | solution.py:22
  18.4 12.8 %collective-permute-start.14 = (bf16[896,128]{1,0:T(8,128)(2,1)}, bf16[896,128]{1,0:T(8,128)(2,1)S(1)}, u32[]{:S(2)}, u32[]{:S(2)}) collective-permute-start(bf16[896,128]{1,0:T(8,128)(2,1)} %copy-done.7), channel_id=1, source_target_pairs={{0,8},{4,12},{8,0},{12,4},{16,24},{20,28},{24,16},{28,20},{1,9},{5... | collective-permute-start | bytes 688136 | tf_op jit(solution)/shard_map/ppermute | solution.py:22
  20.0 11.9 %collective-permute-start.6 = (bf16[896,128]{1,0:T(8,128)(2,1)}, bf16[896,128]{1,0:T(8,128)(2,1)}, u32[]{:S(2)}, u32[]{:S(2)}) collective-permute-start(bf16[896,128]{1,0:T(8,128)(2,1)} %copy-done.7), channel_id=1, source_target_pairs={{0,4},{4,0},{8,12},{12,8},{16,20},{20,16},{24,28},{28,24},{1,5},{5... | collective-permute-start | bytes 688136 | tf_op jit(solution)/shard_map/ppermute | solution.py:22
  25.2 18.0 %collective-permute-start.13 = (bf16[896,128]{1,0:T(8,128)(2,1)S(1)}, bf16[896,128]{1,0:T(8,128)(2,1)}, u32[]{:S(2)}, u32[]{:S(2)}) collective-permute-start(bf16[896,128]{1,0:T(8,128)(2,1)S(1)} %constant_dynamic-slice_fusion.refs_3_), channel_id=1, source_target_pairs={{0,8},{4,12},{8,0},{12,4},{16,24},{20,28},{24,16},{28,20},{1,9},{5... | collective-permute-start | bytes 688136 | tf_op jit(solution)/shard_map/ppermute | solution.py:22
  29.7 13.5 %collective-permute-start.15 = (bf16[896,128]{1,0:T(8,128)(2,1)}, bf16[896,128]{1,0:T(8,128)(2,1)}, u32[]{:S(2)}, u32[]{:S(2)}) collective-permute-start(bf16[896,128]{1,0:T(8,128)(2,1)} %collective-permute-done.5.refs_5_), channel_id=1, source_target_pairs={{0,8},{4,12},{8,0},{12,4},{16,24},{20,28},{24,16},{28,20},{1,9},{5... | collective-permute-start | bytes 688136 | tf_op jit(solution)/shard_map/ppermute | solution.py:22
  31.2 11.9 %collective-permute-start.16 = (bf16[896,128]{1,0:T(8,128)(2,1)S(1)}, bf16[896,128]{1,0:T(8,128)(2,1)}, u32[]{:S(2)}, u32[]{:S(2)}) collective-permute-start(bf16[896,128]{1,0:T(8,128)(2,1)S(1)} %collective-permute-done.14.refs_4_), channel_id=1, source_target_pairs={{0,4},{4,0},{8,12},{12,8},{16,20},{20,16},{24,28},{28,24},{1,5},{5... | collective-permute-start | bytes 688136 | tf_op jit(solution)/shard_map/ppermute | solution.py:22
  41.9 1.2 %copy-start.1 = (f32[512,896]{1,0:T(8,128)}, f32[512,896]{1,0:T(8,128)S(1)}, u32[]{:S(2)}) copy-start(f32[512,896]{1,0:T(8,128)S(1)} %get-tuple-element.27.refs_11_) | copy-start | bytes 5505028
  43.1 9.9 %copy-start.4 = (bf16[2,128,256]{2,1,0:T(8,128)(2,1)}, bf16[2,128,256]{2,1,0:T(8,128)(2,1)S(1)}, u32[]{:S(2)}) copy-start(bf16[2,128,256]{2,1,0:T(8,128)(2,1)S(1)} %get-tuple-element.23.refs_0_) | copy-start | bytes 393220
  53.0 2.1 %copy-start.5 = (bf16[2,128,256]{2,1,0:T(8,128)(2,1)}, bf16[2,128,256]{2,1,0:T(8,128)(2,1)S(1)}, u32[]{:S(2)}) copy-start(bf16[2,128,256]{2,1,0:T(8,128)(2,1)S(1)} %get-tuple-element.28.refs_4_) | copy-start | bytes 393220
  53.1 1.9 %collective-permute-start.20 = (bf16[256,896]{1,0:T(8,128)(2,1)S(1)}, bf16[256,896]{1,0:T(8,128)(2,1)S(1)}, u32[]{:S(2)}, u32[]{:S(2)}) collective-permute-start(bf16[256,896]{1,0:T(8,128)(2,1)S(1)} %slice.25), channel_id=1, source_target_pairs={{0,1},{1,0},{2,3},{3,2},{4,5},{5,4},{6,7},{7,6},{8,9},{9,8},{10,11... | collective-permute-start | bytes 1376264 | tf_op jit(solution)/shard_map/ppermute | solution.py:22
  53.3 3.9 %collective-permute-start.10 = (bf16[2,128,256]{2,1,0:T(8,128)(2,1)S(1)}, bf16[2,128,256]{2,1,0:T(8,128)(2,1)S(1)}, u32[]{:S(2)}, u32[]{:S(2)}) collective-permute-start(bf16[2,128,256]{2,1,0:T(8,128)(2,1)S(1)} %get-tuple-element.24), channel_id=1, source_target_pairs={{0,1},{1,0},{2,3},{3,2},{4,5},{5,4},{6,7},{7,6},{8,9},{9,8},{10,11... | collective-permute-start | bytes 393224 | tf_op jit(solution)/shard_map/ppermute | solution.py:22
  53.6 6.3 %collective-permute-start.11 = (bf16[2,128,256]{2,1,0:T(8,128)(2,1)S(1)}, bf16[2,128,256]{2,1,0:T(8,128)(2,1)S(1)}, u32[]{:S(2)}, u32[]{:S(2)}) collective-permute-start(bf16[2,128,256]{2,1,0:T(8,128)(2,1)S(1)} %get-tuple-element.25), channel_id=1, source_target_pairs={{0,2},{1,3},{2,0},{3,1},{4,6},{5,7},{6,4},{7,5},{8,10},{9,11},{10,... | collective-permute-start | bytes 393224 | tf_op jit(solution)/shard_map/ppermute | solution.py:22
  55.1 51.3 %collective-permute-start.21 = (bf16[128,896]{1,0:T(8,128)(2,1)S(1)}, bf16[128,896]{1,0:T(8,128)(2,1)S(1)}, u32[]{:S(2)}, u32[]{:S(2)}) collective-permute-start(bf16[128,896]{1,0:T(8,128)(2,1)S(1)} %slice.26), channel_id=1, source_target_pairs={{0,2},{1,3},{2,0},{3,1},{4,6},{5,7},{6,4},{7,5},{8,10},{9,11},{10,... | collective-permute-start | bytes 688136 | tf_op jit(solution)/shard_map/ppermute | solution.py:22
  56.1 10.2 %collective-permute-start.12 = (bf16[2,128,256]{2,1,0:T(8,128)(2,1)S(1)}, bf16[2,128,256]{2,1,0:T(8,128)(2,1)S(1)}, u32[]{:S(2)}, u32[]{:S(2)}) collective-permute-start(bf16[2,128,256]{2,1,0:T(8,128)(2,1)S(1)} %get-tuple-element.26), channel_id=1, source_target_pairs={{0,3},{1,2},{2,1},{3,0},{4,7},{5,6},{6,5},{7,4},{8,11},{9,10},{10,... | collective-permute-start | bytes 393224 | tf_op jit(solution)/shard_map/ppermute | solution.py:22
  56.7 9.5 %collective-permute-start.17 = (bf16[2,128,256]{2,1,0:T(8,128)(2,1)S(1)}, bf16[2,128,256]{2,1,0:T(8,128)(2,1)S(1)}, u32[]{:S(2)}, u32[]{:S(2)}) collective-permute-start(bf16[2,128,256]{2,1,0:T(8,128)(2,1)S(1)} %get-tuple-element.29), channel_id=1, source_target_pairs={{0,1},{1,0},{2,3},{3,2},{4,5},{5,4},{6,7},{7,6},{8,9},{9,8},{10,11... | collective-permute-start | bytes 393224 | tf_op jit(solution)/shard_map/ppermute | solution.py:22
  57.3 14.6 %copy-start.9 = (bf16[2,128,256]{2,1,0:T(8,128)(2,1)}, bf16[2,128,256]{2,1,0:T(8,128)(2,1)S(1)}, u32[]{:S(2)}) copy-start(bf16[2,128,256]{2,1,0:T(8,128)(2,1)S(1)} %collective-permute-done.10.refs_1_) | copy-start | bytes 393220
  57.3 13.2 %collective-permute-start.18 = (bf16[2,128,256]{2,1,0:T(8,128)(2,1)S(1)}, bf16[2,128,256]{2,1,0:T(8,128)(2,1)S(1)}, u32[]{:S(2)}, u32[]{:S(2)}) collective-permute-start(bf16[2,128,256]{2,1,0:T(8,128)(2,1)S(1)} %get-tuple-element.30), channel_id=1, source_target_pairs={{0,2},{1,3},{2,0},{3,1},{4,6},{5,7},{6,4},{7,5},{8,10},{9,11},{10,... | collective-permute-start | bytes 393224 | tf_op jit(solution)/shard_map/ppermute | solution.py:22
  60.0 11.9 %copy-start.10 = (bf16[2,128,256]{2,1,0:T(8,128)(2,1)}, bf16[2,128,256]{2,1,0:T(8,128)(2,1)S(1)}, u32[]{:S(2)}) copy-start(bf16[2,128,256]{2,1,0:T(8,128)(2,1)S(1)} %collective-permute-done.11.refs_2_) | copy-start | bytes 393220
  60.0 11.9 %collective-permute-start.19 = (bf16[2,128,256]{2,1,0:T(8,128)(2,1)S(1)}, bf16[2,128,256]{2,1,0:T(8,128)(2,1)S(1)}, u32[]{:S(2)}, u32[]{:S(2)}) collective-permute-start(bf16[2,128,256]{2,1,0:T(8,128)(2,1)S(1)} %get-tuple-element.31), channel_id=1, source_target_pairs={{0,3},{1,2},{2,1},{3,0},{4,7},{5,6},{6,5},{7,4},{8,11},{9,10},{10,... | collective-permute-start | bytes 393224 | tf_op jit(solution)/shard_map/ppermute | solution.py:22
  66.2 5.6 %copy-start.11 = (bf16[2,128,256]{2,1,0:T(8,128)(2,1)}, bf16[2,128,256]{2,1,0:T(8,128)(2,1)S(1)}, u32[]{:S(2)}) copy-start(bf16[2,128,256]{2,1,0:T(8,128)(2,1)S(1)} %collective-permute-done.12.refs_3_) | copy-start | bytes 393220
  66.3 5.6 %copy-start.12 = (bf16[2,128,256]{2,1,0:T(8,128)(2,1)}, bf16[2,128,256]{2,1,0:T(8,128)(2,1)S(1)}, u32[]{:S(2)}) copy-start(bf16[2,128,256]{2,1,0:T(8,128)(2,1)S(1)} %collective-permute-done.17.refs_5_) | copy-start | bytes 393220
  70.5 1.4 %copy-start.13 = (bf16[2,128,256]{2,1,0:T(8,128)(2,1)}, bf16[2,128,256]{2,1,0:T(8,128)(2,1)S(1)}, u32[]{:S(2)}) copy-start(bf16[2,128,256]{2,1,0:T(8,128)(2,1)S(1)} %collective-permute-done.18.refs_6_) | copy-start | bytes 393220
  (5 other events, 4.4 us)

commit v2 on v1

v2 whole, which is shorter than its diff:
```python
import functools

import jax
import jax.numpy as jnp
from jax import lax
from jax.experimental import pallas as pl
from jax.experimental.pallas import tpu as pltpu
from jax.sharding import PartitionSpec as P

HEAD_SIZE = 128
HEADS = 16
SPAN = 64
NLEN = 64
READS = 2

NT = (((1,), (1,)), ((), ()))
TN = (((0,), (0,)), ((), ()))
EXTRA = 16


def vmem_bytes(rows):
    return (8 << 20) + rows * (16 << 10)


def xor_send(value, axis, size, bit):
    return lax.ppermute(value, axis, [(i, i ^ bit) for i in range(size)])


def bit_reverse(index, bits):
    result = index * 0
    for i in range(bits):
        result = result + (((index >> i) & 1) << (bits - 1 - i))
    return result


def pack_body(seq_size, reads, meta, queries, grad_out, *pieces):
    own, first = meta[0], meta[1]
    tokens = queries.shape[1]
    lanes = lax.broadcasted_iota(jnp.int32, (EXTRA, pieces[0].shape[1]), 1)
    positions = jnp.zeros(lanes.shape, jnp.int32)
    for i in range(reads):
        positions = jnp.where(lanes == i, meta[4 + i], positions)
    positions = positions.astype(jnp.float32).astype(jnp.bfloat16)
    for k in range(seq_size):
        for r in range(HEADS // seq_size):
            column = pl.multiple_of(((first ^ r) * seq_size + (own ^ k)) * HEAD_SIZE, HEAD_SIZE)
            place = slice(r * HEAD_SIZE, (r + 1) * HEAD_SIZE)
            pieces[k][:tokens, place] = queries[0, :, pl.ds(column, HEAD_SIZE)]
            pieces[k][tokens : 2 * tokens, place] = grad_out[0, :, pl.ds(column, HEAD_SIZE)]
        pieces[k][2 * tokens :, :] = positions


def pack(meta, queries, grad_out, seq_size):
    tokens = queries.shape[1]
    shape = jax.ShapeDtypeStruct((2 * tokens + EXTRA, HEADS // seq_size * HEAD_SIZE), jnp.bfloat16)
    return pl.pallas_call(
        functools.partial(pack_body, seq_size, meta.shape[0] - 4),
        out_shape=[shape] * seq_size,
        in_specs=[pl.BlockSpec(memory_space=pltpu.SMEM)] + [pl.BlockSpec(memory_space=pltpu.VMEM)] * 2,
        out_specs=[pl.BlockSpec(memory_space=pltpu.VMEM)] * seq_size,
        compiler_params=pltpu.CompilerParams(vmem_limit_bytes=vmem_bytes(0)),
        name="pack",
    )(meta, queries, grad_out)


def attention_body(seq_size, spans, heads, has_prior, last, *refs):
    count = len(heads)
    meta, refs = refs[0], refs[1:]
    stored, refs = refs[:seq_size], refs[seq_size:]
    weights, refs = refs[: 2 * count], refs[2 * count :]
    pieces, refs = refs[:seq_size], refs[seq_size:]
    prior, refs = (refs[0], refs[1:]) if has_prior else (None, refs)
    outs, refs = refs[:seq_size], refs[seq_size:]
    grads, refs = (refs[:2], refs[2:]) if last else (refs[:1], refs[1:])
    enc, pair, kv, d_kv = refs
    block = stored[0].shape[0]
    rows = enc.shape[0]
    tokens = spans * SPAN
    scale = HEAD_SIZE ** (-0.5)
    keys_first = meta[2] == 1
    for i in range(seq_size):
        enc[i * block : (i + 1) * block] = stored[i][...]
    spots = []
    for k in range(seq_size):
        for c in range(spans):
            at = 4 + (k * spans + c) * READS
            spots.append((k, c, [pl.multiple_of(meta[at + r] * NLEN, NLEN) for r in range(READS)]))
    for i, head in enumerate(heads):
        first, second = weights[2 * i][...], weights[2 * i + 1][...]
        wide = slice(2 * i * HEAD_SIZE, 2 * (i + 1) * HEAD_SIZE)
        pair[:, 2 * i * HEAD_SIZE : (2 * i + 1) * HEAD_SIZE] = jnp.where(keys_first, first, second)
        pair[:, (2 * i + 1) * HEAD_SIZE : (2 * i + 2) * HEAD_SIZE] = jnp.where(keys_first, second, first)
        kv[...] = jnp.dot(enc[...], pair[:, wide], preferred_element_type=jnp.float32).astype(jnp.bfloat16)
        d_kv[:, wide] = jnp.zeros((rows, 2 * HEAD_SIZE), jnp.float32)
        columns = slice(head * HEAD_SIZE, (head + 1) * HEAD_SIZE)
        out_columns = slice(i * HEAD_SIZE, (i + 1) * HEAD_SIZE)
        reads, queries, grad_rows, scores, d_probs = [], [], [], [], []
        for k, c, starts in spots:
            read = jnp.concatenate([kv[pl.ds(start, NLEN), :] for start in starts], axis=0)
            query = pieces[k][c * SPAN : (c + 1) * SPAN, columns]
            grad = pieces[k][tokens + c * SPAN : tokens + (c + 1) * SPAN, columns]
            reads.append((read[:, :HEAD_SIZE], read[:, HEAD_SIZE:]))
            queries.append(query)
            grad_rows.append(grad)
            scores.append(lax.dot_general(query, reads[-1][0], NT, preferred_element_type=jnp.float32))
            d_probs.append(lax.dot_general(grad, reads[-1][1], NT, preferred_element_type=jnp.float32))
        probs_low, d_scores = [], []
        for score, d_prob in zip(scores, d_probs):
            expos = jnp.exp(score * scale)
            probs = expos / jnp.sum(expos, axis=-1, keepdims=True)
            delta = jnp.sum(probs * d_prob, axis=-1, keepdims=True)
            probs_low.append(probs.astype(jnp.bfloat16))
            d_scores.append((probs * (d_prob - delta) * scale).astype(jnp.bfloat16))
        for n, (k, c, starts) in enumerate(spots):
            keys, values = reads[n]
            span = slice(c * SPAN, (c + 1) * SPAN)
            outs[k][0, span, out_columns] = jnp.dot(
                probs_low[n], values, preferred_element_type=jnp.float32
            ).astype(jnp.bfloat16)
            outs[k][1, span, out_columns] = jnp.dot(
                d_scores[n], keys, preferred_element_type=jnp.float32
            ).astype(jnp.bfloat16)
            d_keys = lax.dot_general(d_scores[n], queries[n], TN, preferred_element_type=jnp.float32)
            d_values = lax.dot_general(probs_low[n], grad_rows[n], TN, preferred_element_type=jnp.float32)
            both = jnp.concatenate([d_keys, d_values], axis=1)
            for r, start in enumerate(starts):
                d_kv[pl.ds(start, NLEN), wide] += both[r * NLEN : (r + 1) * NLEN]
    half = rows // 2
    for part in range(2):
        place = slice(part * half, (part + 1) * half)
        term = lax.dot_general(
            d_kv[place, :].astype(jnp.bfloat16), pair[...], NT, preferred_element_type=jnp.float32
        )
        if has_prior:
            term = term + prior[place, :].astype(jnp.float32)
        if last:
            grads[part][...] = term.astype(grads[part].dtype)
        else:
            grads[0][place, :] = term.astype(grads[0].dtype)


def attention(meta, stored, weights, pieces, heads, spans, prior, last):
    seq_size = len(pieces)
    block, width = stored[0].shape
    rows = seq_size * block
    count = len(heads)
    prior = [] if prior is None else [prior]
    vmem = pl.BlockSpec(memory_space=pltpu.VMEM)
    operands = [*stored, *weights, *pieces, *prior]
    out_shape = [jax.ShapeDtypeStruct((2, spans * SPAN, count * HEAD_SIZE), jnp.bfloat16)] * seq_size
    if last:
        out_shape.append(jax.ShapeDtypeStruct((rows // 2, width), jnp.float32))
        out_shape.append(jax.ShapeDtypeStruct((rows // 2, width), jnp.bfloat16))
    else:
        out_shape.append(jax.ShapeDtypeStruct((rows, width), jnp.bfloat16))
    outs = pl.pallas_call(
        functools.partial(attention_body, seq_size, spans, heads, len(prior), last),
        out_shape=out_shape,
        in_specs=[pl.BlockSpec(memory_space=pltpu.SMEM)] + [vmem] * len(operands),
        out_specs=[vmem] * len(out_shape),
        scratch_shapes=[
            pltpu.VMEM((rows, width), jnp.bfloat16),
            pltpu.VMEM((width, 2 * count * HEAD_SIZE), jnp.bfloat16),
            pltpu.VMEM((rows, 2 * HEAD_SIZE), jnp.bfloat16),
            pltpu.VMEM((rows, 2 * count * HEAD_SIZE), jnp.float32),
        ],
        compiler_params=pltpu.CompilerParams(vmem_limit_bytes=vmem_bytes(rows)),
        cost_estimate=pl.CostEstimate(
            flops=count * 32 * rows * width * HEAD_SIZE, bytes_accessed=4 * rows * width, transcendentals=0
        ),
        name="attention",
    )(meta, *operands)
    return outs[:seq_size], outs[seq_size:]


def unpack_body(seq_size, groups, meta, *refs):
    count = len(groups) * seq_size
    attended, grad_queries = refs[count:]
    own, first = meta[0], meta[1]
    for g, heads in enumerate(groups):
        for k in range(seq_size):
            for i, r in enumerate(heads):
                column = pl.multiple_of(((first ^ r) * seq_size + (own ^ k)) * HEAD_SIZE, HEAD_SIZE)
                place = slice(i * HEAD_SIZE, (i + 1) * HEAD_SIZE)
                attended[0, :, pl.ds(column, HEAD_SIZE)] = refs[g * seq_size + k][0, :, place]
                grad_queries[0, :, pl.ds(column, HEAD_SIZE)] = refs[g * seq_size + k][1, :, place]


def unpack(meta, parts, groups, seq_size):
    tokens = parts[0].shape[1]
    shape = jax.ShapeDtypeStruct((1, tokens, HEADS * HEAD_SIZE), jnp.bfloat16)
    vmem = pl.BlockSpec(memory_space=pltpu.VMEM)
    return pl.pallas_call(
        functools.partial(unpack_body, seq_size, groups),
        out_shape=[shape, shape],
        in_specs=[pl.BlockSpec(memory_space=pltpu.SMEM)] + [vmem] * len(parts),
        out_specs=[vmem, vmem],
        compiler_params=pltpu.CompilerParams(vmem_limit_bytes=vmem_bytes(0)),
        name="unpack",
    )(meta, *parts)


def weight_slice(kv_weight, column):
    return lax.dynamic_slice_in_dim(kv_weight, column, HEAD_SIZE, axis=1)


def gather_split(mine, dp_size):
    send = functools.partial(xor_send, axis="dp", size=dp_size)
    far = send(mine, bit=4)
    near = send(mine, bit=2)
    side = send(mine, bit=1)
    near_far = send(far, bit=2)
    side_far = send(far, bit=1)
    side_near = send(side, bit=2)
    side_near_far = send(near_far, bit=1)
    return [(mine, far), (side, side_far), (near, near_far), (side_near, side_near_far)]


def gather_whole(kv_weight, own, seq_size):
    whole = lax.all_gather(kv_weight, "dp", axis=1, tiled=True)
    pairs = []
    for r in range(HEADS // seq_size):
        column = (r * seq_size + own) * HEAD_SIZE
        pairs.append((weight_slice(whole, column), weight_slice(whole, column + HEADS * HEAD_SIZE)))
    return pairs


def per_device(dp_size, seq_size, queries, grad_out, encoded, kv_weight, neighbour_ids, slot_map):
    own = lax.axis_index("seq")
    place = lax.axis_index("dp")
    bits = seq_size.bit_length() - 1
    per_owner = encoded.shape[1]
    spans = neighbour_ids.shape[1]
    tokens = queries.shape[1]
    width = encoded.shape[3]
    pool_size = slot_map.shape[1]
    assert pool_size <= 256 and 1 << bits == seq_size
    split = dp_size == 8 and 2 * HEADS == dp_size * seq_size
    send = functools.partial(xor_send, axis="seq", size=seq_size)

    if split:
        mine = weight_slice(kv_weight, own * HEAD_SIZE)
        mine, queries, grad_out, encoded, neighbour_ids = lax.optimization_barrier(
            (mine, queries, grad_out, encoded, neighbour_ids)
        )
        pairs = gather_split(mine, dp_size)
        first = place % (HEADS // seq_size)
        keys_first = (place < dp_size // 2).astype(jnp.int32)
        groups = [(0,), (1, 2), (3,)]
    else:
        pairs = gather_whole(kv_weight, own, seq_size)
        first, keys_first = place * 0, place * 0 + 1
        groups = [tuple(range(HEADS // seq_size))]

    matches = neighbour_ids[0][:, :, None] == jnp.arange(pool_size, dtype=jnp.int32)[None, None, :]
    positions = jnp.sum(jnp.where(matches, slot_map[0][None, None, :], 0), axis=2).reshape(-1)
    head_meta = jnp.stack([own, first, keys_first, place])
    pieces = pack(jnp.concatenate([head_meta, positions]), queries, grad_out, seq_size)
    pieces = [pieces[0]] + [send(pieces[k], bit=k) for k in range(1, seq_size)]
    stored = [encoded[0].reshape(per_owner * NLEN, width)]
    for level in range(bits - 1, -1, -1):
        stored = stored + [send(rows, bit=1 << level) for rows in stored]
    positions = jnp.concatenate(
        [positions]
        + [piece[2 * tokens, : spans * READS].astype(jnp.int32) for piece in pieces[1:]]
    )
    relative = bit_reverse((positions // per_owner) ^ own, bits) * per_owner + positions % per_owner
    meta = jnp.concatenate([head_meta, relative])

    parts, grads = [], [None]
    for heads in groups:
        weights = [block for head in heads for block in pairs[head]]
        outs, grads = attention(
            meta, stored, weights, pieces, heads, spans, grads[0], heads == groups[-1]
        )
        parts = parts + [outs[0]] + [send(outs[k], bit=k) for k in range(1, seq_size)]
    total, leaving = grads
    for level in range(bits):
        total = total + send(leaving, bit=1 << level).astype(jnp.float32)
        half = total.shape[0] // 2
        if level < bits - 1:
            total, leaving = total[:half], total[half:].astype(jnp.bfloat16)
    attended, grad_queries = unpack(head_meta, parts, groups, seq_size)
    return attended, grad_queries, total.reshape(1, per_owner, NLEN, width)


def solution(mesh):
    in_specs = (
        P("dp", "seq", None),
        P("dp", "seq", None),
        P("dp", "seq", None, None),
        P(None, "dp"),
        P("dp", "seq", None),
        P("dp", None),
    )
    out_specs = (P("dp", "seq", None), P("dp", "seq", None), P("dp", "seq", None, None))
    return jax.shard_map(
        functools.partial(per_device, mesh.shape["dp"], mesh.shape["seq"]),
        mesh=mesh,
        in_specs=in_specs,
        out_specs=out_specs,
        check_vma=False,
    )
```

time: 108 us -> 78.2 us (0.72)
  Pallas kernels: 53.5 us -> 13.8 us
  waiting for transfers between devices: 23 us -> 32.3 us
  starting transfers between devices: 21 us -> 25.5 us
  other arithmetic: 3.01 us -> 1.29 us
  local copies, waits for them, and re-layouts: 5.89 us -> 4.24 us
    pallas_call x1, Pallas kernels: 33.8 us -> 1.8 us  [unpack(): pl.pallas_call(functools.partial(unpack_body, seq_size, groups), out_shap...]
    ppermute x22 -> x24, waiting for transfers between devices: 23 us -> 32.3 us  [xor_send(): return lax.ppermute(value, axis, [(i, i ^ bit) for i in range(size)])]
    pallas_call x2 -> x3, Pallas kernels: 18.8 us -> 11.2 us  [attention(): pl.pallas_call(functools.partial(attention_body, seq_size, spans, heads,...]
    ppermute x22 -> x24, starting transfers between devices: 21 us -> 25.5 us  [xor_send(): return lax.ppermute(value, axis, [(i, i ^ bit) for i in range(size)])]
    unnamed x30 -> x12, local copies, waits for them, and re-layouts: 5.61 us -> 3.93 us
  transfers between devices with their start and end apart: 22 -> 24, of which waited for: 8 -> 10; matrix products, arithmetic and copies ran while one was open for 2% -> 1% of each run, Pallas kernels for 41% -> 13%
where the time goes in v2:
time: 78.2 us; the launch traced here: 77.8 us
  waiting for transfers between devices  32.3 us (41%)
  starting transfers between devices  25.5 us (33%)
  Pallas kernels  13.8 us (18%)
  local copies, waits for them, and re-layouts  4.24 us (5%)
  other arithmetic  1.29 us (2%)
    ppermute x24, waiting for transfers between devices, xor_send(): return lax.ppermute(value, axis, [(i, i ^ bit) for i in range(size)])  32.3 us
    ppermute x24, starting transfers between devices, xor_send(): return lax.ppermute(value, axis, [(i, i ^ bit) for i in range(size)])  25.5 us
    pallas_call x3, Pallas kernels, attention(): pl.pallas_call(functools.partial(attention_body, seq_size, spans, heads,...  11.2 us
    unnamed x12, local copies, waits for them, and re-layouts  3.93 us
    pallas_call x1, Pallas kernels, unpack(): pl.pallas_call(functools.partial(unpack_body, seq_size, groups), out_shap...  1.8 us
  transfers between devices with their start and end apart: 24, of which 10 were waited for; matrix products, arithmetic and copies ran while one was open for 1% of the time, Pallas kernels for 13%

profile of v2, /device:TPU:0, one launch (start us, length us, event | category | flops | bytes accessed | tf_op | source)
XLA Modules:
  0.0 77.8 jit_solution(963465320585528088)
XLA Ops:
  0.7 1.2 %copy-done = bf16[896,512]{1,0:T(8,128)(2,1)S(1)} copy-done((bf16[896,512]{1,0:T(8,128)(2,1)S(1)}, bf16[896,512]{1,0:T(8,128)(2,1)}, u32[]{:S(2)}) %copy-start) | copy-done | bytes 917528
  1.9 0.7 copy-done.4
  2.9 1.1 %copy-done.1 = bf16[1,128,2048]{2,1,0:T(8,128)(2,1)S(1)} copy-done((bf16[1,128,2048]{2,1,0:T(8,128)(2,1)S(1)}, bf16[1,128,2048]{2,1,0:T(8,128)(2,1)}, u32[]{:S(2)}) %copy-start.1) | copy-done | bytes 524312
  4.0 1.0 %copy-done.2 = bf16[1,128,2048]{2,1,0:T(8,128)(2,1)S(1)} copy-done((bf16[1,128,2048]{2,1,0:T(8,128)(2,1)S(1)}, bf16[1,128,2048]{2,1,0:T(8,128)(2,1)}, u32[]{:S(2)}) %copy-start.2) | copy-done | bytes 524312
  5.0 0.8 %pack.1 = (bf16[272,512]{1,0:T(8,128)(2,1)S(1)}, bf16[272,512]{1,0:T(8,128)(2,1)S(1)}, bf16[272,512]{1,0:T(8,128)(2,1)S(1)}, bf16[272,512]{1,0:T(8,128)(2,1)S(1)}) custom-call(s32[8]{0:T(128)S(1)} %concatenate.11.meta, bf16[1,128,2048]{2,1,0:T(8,128)(2,1)S(1)} %copy-done.1, bf16[1,128,2048]{2,1,0:T(8,128)(2,1)S(1)} %copy-done.2), custom_call_target="tpu_custom_call" | custom-call | tf_op jit(solution)/shard_map/pack/pallas_call | solution.py:56
  5.8 2.4 %collective-permute-start.2 = (bf16[272,512]{1,0:T(8,128)(2,1)S(1)}, bf16[272,512]{1,0:T(8,128)(2,1)S(1)}, u32[]{:S(2)}, u32[]{:S(2)}) collective-permute-start(bf16[272,512]{1,0:T(8,128)(2,1)S(1)} %get-tuple-element.35), channel_id=1, source_target_pairs={{0,3},{1,2},{2,1},{3,0},{4,7},{5,6},{6,5},{7,4},{8,11},{9,10},{10,... | collective-permute-start | bytes 835592 | tf_op jit(solution)/shard_map/ppermute | solution.py:26
  8.9 1.4 %collective-permute-start.3 = (bf16[128,896]{1,0:T(8,128)(2,1)S(1)}, bf16[128,896]{1,0:T(8,128)(2,1)S(1)}, u32[]{:S(2)}, u32[]{:S(2)}) collective-permute-start(bf16[128,896]{1,0:T(8,128)(2,1)S(1)} %bitcast.23), channel_id=1, source_target_pairs={{0,2},{1,3},{2,0},{3,1},{4,6},{5,7},{6,4},{7,5},{8,10},{9,11},{10,... | collective-permute-start | bytes 688136 | tf_op jit(solution)/shard_map/ppermute | solution.py:26
  10.8 4.5 %collective-permute-done.2.refs_10_.refs_12_ = bf16[272,512]{1,0:T(8,128)(2,1)S(1)} collective-permute-done((bf16[272,512]{1,0:T(8,128)(2,1)S(1)}, bf16[272,512]{1,0:T(8,128)(2,1)S(1)}, u32[]{:S(2)}, u32[]{:S(2)}) %collective-permute-start.2) | collective-permute-done | bytes 278560 | tf_op jit(solution)/shard_map/ppermute | solution.py:26
  15.3 3.5 %collective-permute-start.6 = (bf16[896,128]{1,0:T(8,128)(2,1)S(1)}, bf16[896,128]{1,0:T(8,128)(2,1)}, u32[]{:S(2)}, u32[]{:S(2)}) collective-permute-start(bf16[896,128]{1,0:T(8,128)(2,1)S(1)} %constant_dynamic-slice_fusion.refs_5_), channel_id=1, source_target_pairs={{0,16},{4,20},{8,24},{12,28},{16,0},{20,4},{24,8},{28,12},{1,17},{... | collective-permute-start | bytes 688136 | tf_op jit(solution)/shard_map/ppermute | solution.py:26
  18.9 3.4 %collective-permute-done.1.refs_9_.refs_11_ = bf16[272,512]{1,0:T(8,128)(2,1)S(1)} collective-permute-done((bf16[272,512]{1,0:T(8,128)(2,1)S(1)}, bf16[272,512]{1,0:T(8,128)(2,1)S(1)}, u32[]{:S(2)}, u32[]{:S(2)}) %collective-permute-start.1) | collective-permute-done | bytes 278560 | tf_op jit(solution)/shard_map/ppermute | solution.py:26
  22.3 1.5 %collective-permute-start.10 = (bf16[896,128]{1,0:T(8,128)(2,1)S(1)}, bf16[896,128]{1,0:T(8,128)(2,1)S(1)}, u32[]{:S(2)}, u32[]{:S(2)}) collective-permute-start(bf16[896,128]{1,0:T(8,128)(2,1)S(1)} %constant_dynamic-slice_fusion.refs_5_), channel_id=1, source_target_pairs={{0,4},{4,0},{8,12},{12,8},{16,20},{20,16},{24,28},{28,24},{1,5},{5... | collective-permute-start | bytes 688136 | tf_op jit(solution)/shard_map/ppermute | solution.py:26
  23.8 2.5 %collective-permute-done.3.refs_2_ = bf16[128,896]{1,0:T(8,128)(2,1)S(1)} collective-permute-done((bf16[128,896]{1,0:T(8,128)(2,1)S(1)}, bf16[128,896]{1,0:T(8,128)(2,1)S(1)}, u32[]{:S(2)}, u32[]{:S(2)}) %collective-permute-start.3) | collective-permute-done | bytes 229408 | tf_op jit(solution)/shard_map/ppermute | solution.py:26
  26.4 2.4 %collective-permute-start.12 = (bf16[896,128]{1,0:T(8,128)(2,1)S(1)}, bf16[896,128]{1,0:T(8,128)(2,1)}, u32[]{:S(2)}, u32[]{:S(2)}) collective-permute-start(bf16[896,128]{1,0:T(8,128)(2,1)S(1)} %constant_dynamic-slice_fusion.refs_5_), channel_id=1, source_target_pairs={{0,8},{4,12},{8,0},{12,4},{16,24},{20,28},{24,16},{28,20},{1,9},{5... | collective-permute-start | bytes 688136 | tf_op jit(solution)/shard_map/ppermute | solution.py:26
  28.8 1.0 %collective-permute-done.6.refs_6_ = bf16[896,128]{1,0:T(8,128)(2,1)} collective-permute-done((bf16[896,128]{1,0:T(8,128)(2,1)S(1)}, bf16[896,128]{1,0:T(8,128)(2,1)}, u32[]{:S(2)}, u32[]{:S(2)}) %collective-permute-start.6) | collective-permute-done | bytes 229408 | tf_op jit(solution)/shard_map/ppermute | solution.py:26
  30.4 1.5 %collective-permute-start.11 = (bf16[896,128]{1,0:T(8,128)(2,1)}, bf16[896,128]{1,0:T(8,128)(2,1)}, u32[]{:S(2)}, u32[]{:S(2)}) collective-permute-start(bf16[896,128]{1,0:T(8,128)(2,1)} %collective-permute-done.6.refs_6_), channel_id=1, source_target_pairs={{0,4},{4,0},{8,12},{12,8},{16,20},{20,16},{24,28},{28,24},{1,5},{5... | collective-permute-start | bytes 688136 | tf_op jit(solution)/shard_map/ppermute | solution.py:26
  32.1 1.4 %collective-permute-start.17 = (bf16[896,128]{1,0:T(8,128)(2,1)S(1)}, bf16[896,128]{1,0:T(8,128)(2,1)S(1)}, u32[]{:S(2)}, u32[]{:S(2)}) collective-permute-start(bf16[896,128]{1,0:T(8,128)(2,1)S(1)} %collective-permute-done.10.refs_5_), channel_id=1, source_target_pairs={{0,8},{4,12},{8,0},{12,4},{16,24},{20,28},{24,16},{28,20},{1,9},{5... | collective-permute-start | bytes 688136 | tf_op jit(solution)/shard_map/ppermute | solution.py:26
  33.6 6.6 %collective-permute-done.13.refs_8_ = bf16[896,128]{1,0:T(8,128)(2,1)} collective-permute-done((bf16[896,128]{1,0:T(8,128)(2,1)}, bf16[896,128]{1,0:T(8,128)(2,1)}, u32[]{:S(2)}, u32[]{:S(2)}) %collective-permute-start.13) | collective-permute-done | bytes 229408 | tf_op jit(solution)/shard_map/ppermute | solution.py:26
  40.2 2.0 %collective-permute-start.18 = (bf16[896,128]{1,0:T(8,128)(2,1)}, bf16[896,128]{1,0:T(8,128)(2,1)S(1)}, u32[]{:S(2)}, u32[]{:S(2)}) collective-permute-start(bf16[896,128]{1,0:T(8,128)(2,1)} %collective-permute-done.13.refs_8_), channel_id=1, source_target_pairs={{0,4},{4,0},{8,12},{12,8},{16,20},{20,16},{24,28},{28,24},{1,5},{5... | collective-permute-start | bytes 688136 | tf_op jit(solution)/shard_map/ppermute | solution.py:26
  42.2 3.1 %attention.3 = (bf16[2,128,128]{2,1,0:T(8,128)(2,1)S(1)}, bf16[2,128,128]{2,1,0:T(8,128)(2,1)S(1)}, bf16[2,128,128]{2,1,0:T(8,128)(2,1)S(1)}, bf16[2,128,128]{2,1,0:T(8,128)(2,1)S(1)}, bf16[512,896]{1,0:T(8,128)(2,1)S(1)}) custom-call(s32[20]{0:T(128)S(1)} %concatenate.13.refs_0_, bf16[128,896]{1,0:T(8,128)(2,1)S(1)} %bitcast.25, ...), custom_call_target="tpu_custom_call" | custom-call | flops 1879048192 | bytes 1835008 | tf_op jit(solution)/shard_map/attention/pallas_call | solution.py:156
  45.3 5.3 %attention.4 = (bf16[2,128,256]{2,1,0:T(8,128)(2,1)S(1)}, bf16[2,128,256]{2,1,0:T(8,128)(2,1)S(1)}, bf16[2,128,256]{2,1,0:T(8,128)(2,1)S(1)}, bf16[2,128,256]{2,1,0:T(8,128)(2,1)S(1)}, bf16[512,896]{1,0:T(8,128)(2,1)S(1)}) custom-call(s32[20]{0:T(128)S(1)} %concatenate.13.refs_0_, bf16[128,896]{1,0:T(8,128)(2,1)S(1)} %bitcast.26, ...), custom_call_target="tpu_custom_call" | custom-call | flops 3758096384 | bytes 1835008 | tf_op jit(solution)/shard_map/attention/pallas_call | solution.py:156
  50.6 2.8 %attention.5 = (bf16[2,128,128]{2,1,0:T(8,128)(2,1)S(1)}, bf16[2,128,128]{2,1,0:T(8,128)(2,1)S(1)}, bf16[2,128,128]{2,1,0:T(8,128)(2,1)S(1)}, bf16[2,128,128]{2,...) custom-call(s32[20]{0:T(128)S(1)} %concatenate.13.refs_0_, bf16[128,896]{1,0:T(8,128)(2,1)S(1)} %bitcast.27, ...), custom_call_target="tpu_custom_call" | custom-call | flops 1879048192 | bytes 1835008 | tf_op jit(solution)/shard_map/attention/pallas_call | solution.py:156
  54.1 1.5 %collective-permute-start.15 = (bf16[2,128,256]{2,1,0:T(8,128)(2,1)S(1)}, bf16[2,128,256]{2,1,0:T(8,128)(2,1)S(1)}, u32[]{:S(2)}, u32[]{:S(2)}) collective-permute-start(bf16[2,128,256]{2,1,0:T(8,128)(2,1)S(1)} %get-tuple-element.46), channel_id=1, source_target_pairs={{0,2},{1,3},{2,0},{3,1},{4,6},{5,7},{6,4},{7,5},{8,10},{9,11},{10,... | collective-permute-start | bytes 393224 | tf_op jit(solution)/shard_map/ppermute | solution.py:26
  55.7 1.3 %collective-permute-start.23 = (bf16[128,896]{1,0:T(8,128)(2,1)S(1)}, bf16[128,896]{1,0:T(8,128)(2,1)S(1)}, u32[]{:S(2)}, u32[]{:S(2)}) collective-permute-start(bf16[128,896]{1,0:T(8,128)(2,1)S(1)} %slice.37), channel_id=1, source_target_pairs={{0,2},{1,3},{2,0},{3,1},{4,6},{5,7},{6,4},{7,5},{8,10},{9,11},{10,... | collective-permute-start | bytes 688136 | tf_op jit(solution)/shard_map/ppermute | solution.py:26
  57.0 0.8 %collective-permute-start.8 = (bf16[2,128,128]{2,1,0:T(8,128)(2,1)S(1)}, bf16[2,128,128]{2,1,0:T(8,128)(2,1)S(1)}, u32[]{:S(2)}, u32[]{:S(2)}) collective-permute-start(bf16[2,128,128]{2,1,0:T(8,128)(2,1)S(1)} %get-tuple-element.41), channel_id=1, source_target_pairs={{0,2},{1,3},{2,0},{3,1},{4,6},{5,7},{6,4},{7,5},{8,10},{9,11},{10,... | collective-permute-start | bytes 196616 | tf_op jit(solution)/shard_map/ppermute | solution.py:26
  58.2 8.5 %collective-permute-done.8.refs_2_ = bf16[2,128,128]{2,1,0:T(8,128)(2,1)S(1)} collective-permute-done((bf16[2,128,128]{2,1,0:T(8,128)(2,1)S(1)}, bf16[2,128,128]{2,1,0:T(8,128)(2,1)S(1)}, u32[]{:S(2)}, u32[]{:S(2)}) %collective-permute-start.8) | collective-permute-done | bytes 65568 | tf_op jit(solution)/shard_map/ppermute | solution.py:26
  67.2 1.1 %collective-permute-start.19 = (bf16[2,128,128]{2,1,0:T(8,128)(2,1)S(1)}, bf16[2,128,128]{2,1,0:T(8,128)(2,1)S(1)}, u32[]{:S(2)}, u32[]{:S(2)}) collective-permute-start(bf16[2,128,128]{2,1,0:T(8,128)(2,1)S(1)} %get-tuple-element.50), channel_id=1, source_target_pairs={{0,1},{1,0},{2,3},{3,2},{4,5},{5,4},{6,7},{7,6},{8,9},{9,8},{10,11... | collective-permute-start | bytes 196616 | tf_op jit(solution)/shard_map/ppermute | solution.py:26
  68.9 0.8 collective-permute-start.21
  69.8 2.6 %collective-permute-done.16.refs_7_ = bf16[2,128,256]{2,1,0:T(8,128)(2,1)S(1)} collective-permute-done((bf16[2,128,256]{2,1,0:T(8,128)(2,1)S(1)}, bf16[2,128,256]{2,1,0:T(8,128)(2,1)S(1)}, u32[]{:S(2)}, u32[]{:S(2)}) %collective-permute-start.16) | collective-permute-done | bytes 131104 | tf_op jit(solution)/shard_map/ppermute | solution.py:26
  72.4 1.5 %collective-permute-done.20.refs_10_ = bf16[2,128,128]{2,1,0:T(8,128)(2,1)S(1)} collective-permute-done((bf16[2,128,128]{2,1,0:T(8,128)(2,1)S(1)}, bf16[2,128,128]{2,1,0:T(8,128)(2,1)S(1)}, u32[]{:S(2)}, u32[]{:S(2)}) %collective-permute-start.20) | collective-permute-done | bytes 65568 | tf_op jit(solution)/shard_map/ppermute | solution.py:26
  73.9 1.3 %collective-permute-done.21.refs_11_ = bf16[2,128,128]{2,1,0:T(8,128)(2,1)S(1)} collective-permute-done((bf16[2,128,128]{2,1,0:T(8,128)(2,1)S(1)}, bf16[2,128,128]{2,1,0:T(8,128)(2,1)S(1)}, u32[]{:S(2)}, u32[]{:S(2)}) %collective-permute-start.21) | collective-permute-done | bytes 65568 | tf_op jit(solution)/shard_map/ppermute | solution.py:26
  75.2 1.8 %unpack.1 = (bf16[1,128,2048]{2,1,0:T(8,128)(2,1)}, bf16[1,128,2048]{2,1,0:T(8,128)(2,1)}) custom-call(s32[4]{0:T(128)S(1)} %pad_add_fusion.meta, bf16[2,128,128]{2,1,0:T(8,128)(2,1)S(1)} %get-tuple-element.39.refs_0_, bf16[2,128,128]{2,1,0:T(8,128)(2,1)S(1)} %collective-permute-done.7.refs_1_, bf16[2,128,128]{2,1,0:T(8,128)(2,1)S(1)} %collective-permute-done.8.refs_2_, ...), custom_call_target="tpu_custom_call" | custom-call | tf_op jit(solution)/shard_map/unpack/pallas_call | solution.py:193
  77.0 0.8 %slice_add_fusion = f32[128,896]{1,0:T(8,128)} fusion(f32[256,896]{1,0:T(8,128)S(1)} %convert_add_fusion, bf16[128,896]{1,0:T(8,128)(2,1)S(1)} %collective-permute-done.23), kind=kLoop, calls=%fused_computation.2 | loop fusion | flops 229376 | bytes 1146880 | tf_op jit(solution)/shard_map/add | solution.py:279
  (46 shorter events, 4.9 us)
Async XLA Ops:
  0.6 1.2 %copy-start = (bf16[896,512]{1,0:T(8,128)(2,1)S(1)}, bf16[896,512]{1,0:T(8,128)(2,1)}, u32[]{:S(2)}) copy-start(bf16[896,512]{1,0:T(8,128)(2,1)} %param.9) | copy-start | bytes 2752516
  1.8 0.7 copy-start.4
  1.9 0.7 copy-start.5
  2.9 1.1 %copy-start.1 = (bf16[1,128,2048]{2,1,0:T(8,128)(2,1)S(1)}, bf16[1,128,2048]{2,1,0:T(8,128)(2,1)}, u32[]{:S(2)}) copy-start(bf16[1,128,2048]{2,1,0:T(8,128)(2,1)} %queries) | copy-start | bytes 1572868
  4.0 1.0 %copy-start.2 = (bf16[1,128,2048]{2,1,0:T(8,128)(2,1)S(1)}, bf16[1,128,2048]{2,1,0:T(8,128)(2,1)}, u32[]{:S(2)}) copy-start(bf16[1,128,2048]{2,1,0:T(8,128)(2,1)} %grad_out) | copy-start | bytes 1572868
  5.0 3.9 %copy-start.3 = (bf16[1,2,64,896]{3,2,1,0:T(8,128)(2,1)S(1)}, bf16[1,2,64,896]{3,2,1,0:T(8,128)(2,1)}, u32[]{:S(2)}) copy-start(bf16[1,2,64,896]{3,2,1,0:T(8,128)(2,1)} %param.8) | copy-start | bytes 688132
  5.8 9.5 %collective-permute-start.2 = (bf16[272,512]{1,0:T(8,128)(2,1)S(1)}, bf16[272,512]{1,0:T(8,128)(2,1)S(1)}, u32[]{:S(2)}, u32[]{:S(2)}) collective-permute-start(bf16[272,512]{1,0:T(8,128)(2,1)S(1)} %get-tuple-element.35), channel_id=1, source_target_pairs={{0,3},{1,2},{2,1},{3,0},{4,7},{5,6},{6,5},{7,4},{8,11},{9,10},{10,... | collective-permute-start | bytes 835592 | tf_op jit(solution)/shard_map/ppermute | solution.py:26
  8.3 14.0 %collective-permute-start.1 = (bf16[272,512]{1,0:T(8,128)(2,1)S(1)}, bf16[272,512]{1,0:T(8,128)(2,1)S(1)}, u32[]{:S(2)}, u32[]{:S(2)}) collective-permute-start(bf16[272,512]{1,0:T(8,128)(2,1)S(1)} %get-tuple-element.34), channel_id=1, source_target_pairs={{0,2},{1,3},{2,0},{3,1},{4,6},{5,7},{6,4},{7,5},{8,10},{9,11},{10,... | collective-permute-start | bytes 835592 | tf_op jit(solution)/shard_map/ppermute | solution.py:26
  8.9 17.5 %collective-permute-start.3 = (bf16[128,896]{1,0:T(8,128)(2,1)S(1)}, bf16[128,896]{1,0:T(8,128)(2,1)S(1)}, u32[]{:S(2)}, u32[]{:S(2)}) collective-permute-start(bf16[128,896]{1,0:T(8,128)(2,1)S(1)} %bitcast.23), channel_id=1, source_target_pairs={{0,2},{1,3},{2,0},{3,1},{4,6},{5,7},{6,4},{7,5},{8,10},{9,11},{10,... | collective-permute-start | bytes 688136 | tf_op jit(solution)/shard_map/ppermute | solution.py:26
  10.3 20.1 %collective-permute-start.4 = (bf16[128,896]{1,0:T(8,128)(2,1)S(1)}, bf16[128,896]{1,0:T(8,128)(2,1)S(1)}, u32[]{:S(2)}, u32[]{:S(2)}) collective-permute-start(bf16[128,896]{1,0:T(8,128)(2,1)S(1)} %bitcast.24), channel_id=1, source_target_pairs={{0,1},{1,0},{2,3},{3,2},{4,5},{5,4},{6,7},{7,6},{8,9},{9,8},{10,11... | collective-permute-start | bytes 688136 | tf_op jit(solution)/shard_map/ppermute | solution.py:26
  10.5 19.3 %collective-permute-start = (bf16[272,512]{1,0:T(8,128)(2,1)S(1)}, bf16[272,512]{1,0:T(8,128)(2,1)S(1)}, u32[]{:S(2)}, u32[]{:S(2)}) collective-permute-start(bf16[272,512]{1,0:T(8,128)(2,1)S(1)} %get-tuple-element.33), channel_id=1, source_target_pairs={{0,1},{1,0},{2,3},{3,2},{4,5},{5,4},{6,7},{7,6},{8,9},{9,8},{10,11... | collective-permute-start | bytes 835592 | tf_op jit(solution)/shard_map/ppermute | solution.py:26
  15.3 14.4 %collective-permute-start.6 = (bf16[896,128]{1,0:T(8,128)(2,1)S(1)}, bf16[896,128]{1,0:T(8,128)(2,1)}, u32[]{:S(2)}, u32[]{:S(2)}) collective-permute-start(bf16[896,128]{1,0:T(8,128)(2,1)S(1)} %constant_dynamic-slice_fusion.refs_5_), channel_id=1, source_target_pairs={{0,16},{4,20},{8,24},{12,28},{16,0},{20,4},{24,8},{28,12},{1,17},{... | collective-permute-start | bytes 688136 | tf_op jit(solution)/shard_map/ppermute | solution.py:26
  22.3 9.8 %collective-permute-start.10 = (bf16[896,128]{1,0:T(8,128)(2,1)S(1)}, bf16[896,128]{1,0:T(8,128)(2,1)S(1)}, u32[]{:S(2)}, u32[]{:S(2)}) collective-permute-start(bf16[896,128]{1,0:T(8,128)(2,1)S(1)} %constant_dynamic-slice_fusion.refs_5_), channel_id=1, source_target_pairs={{0,4},{4,0},{8,12},{12,8},{16,20},{20,16},{24,28},{28,24},{1,5},{5... | collective-permute-start | bytes 688136 | tf_op jit(solution)/shard_map/ppermute | solution.py:26
  26.4 18.9 %collective-permute-start.12 = (bf16[896,128]{1,0:T(8,128)(2,1)S(1)}, bf16[896,128]{1,0:T(8,128)(2,1)}, u32[]{:S(2)}, u32[]{:S(2)}) collective-permute-start(bf16[896,128]{1,0:T(8,128)(2,1)S(1)} %constant_dynamic-slice_fusion.refs_5_), channel_id=1, source_target_pairs={{0,8},{4,12},{8,0},{12,4},{16,24},{20,28},{24,16},{28,20},{1,9},{5... | collective-permute-start | bytes 688136 | tf_op jit(solution)/shard_map/ppermute | solution.py:26
  29.7 12.4 %collective-permute-start.5 = (bf16[128,896]{1,0:T(8,128)(2,1)S(1)}, bf16[128,896]{1,0:T(8,128)(2,1)S(1)}, u32[]{:S(2)}, u32[]{:S(2)}) collective-permute-start(bf16[128,896]{1,0:T(8,128)(2,1)S(1)} %collective-permute-done.3.refs_2_), channel_id=1, source_target_pairs={{0,1},{1,0},{2,3},{3,2},{4,5},{5,4},{6,7},{7,6},{8,9},{9,8},{10,11... | collective-permute-start | bytes 688136 | tf_op jit(solution)/shard_map/ppermute | solution.py:26
  29.8 10.4 %collective-permute-start.13 = (bf16[896,128]{1,0:T(8,128)(2,1)}, bf16[896,128]{1,0:T(8,128)(2,1)}, u32[]{:S(2)}, u32[]{:S(2)}) collective-permute-start(bf16[896,128]{1,0:T(8,128)(2,1)} %collective-permute-done.6.refs_6_), channel_id=1, source_target_pairs={{0,8},{4,12},{8,0},{12,4},{16,24},{20,28},{24,16},{28,20},{1,9},{5... | collective-permute-start | bytes 688136 | tf_op jit(solution)/shard_map/ppermute | solution.py:26
  30.4 14.9 %collective-permute-start.11 = (bf16[896,128]{1,0:T(8,128)(2,1)}, bf16[896,128]{1,0:T(8,128)(2,1)}, u32[]{:S(2)}, u32[]{:S(2)}) collective-permute-start(bf16[896,128]{1,0:T(8,128)(2,1)} %collective-permute-done.6.refs_6_), channel_id=1, source_target_pairs={{0,4},{4,0},{8,12},{12,8},{16,20},{20,16},{24,28},{28,24},{1,5},{5... | collective-permute-start | bytes 688136 | tf_op jit(solution)/shard_map/ppermute | solution.py:26
  32.1 18.5 %collective-permute-start.17 = (bf16[896,128]{1,0:T(8,128)(2,1)S(1)}, bf16[896,128]{1,0:T(8,128)(2,1)S(1)}, u32[]{:S(2)}, u32[]{:S(2)}) collective-permute-start(bf16[896,128]{1,0:T(8,128)(2,1)S(1)} %collective-permute-done.10.refs_5_), channel_id=1, source_target_pairs={{0,8},{4,12},{8,0},{12,4},{16,24},{20,28},{24,16},{28,20},{1,9},{5... | collective-permute-start | bytes 688136 | tf_op jit(solution)/shard_map/ppermute | solution.py:26
  40.2 10.4 %collective-permute-start.18 = (bf16[896,128]{1,0:T(8,128)(2,1)}, bf16[896,128]{1,0:T(8,128)(2,1)S(1)}, u32[]{:S(2)}, u32[]{:S(2)}) collective-permute-start(bf16[896,128]{1,0:T(8,128)(2,1)} %collective-permute-done.13.refs_8_), channel_id=1, source_target_pairs={{0,4},{4,0},{8,12},{12,8},{16,20},{20,16},{24,28},{28,24},{1,5},{5... | collective-permute-start | bytes 688136 | tf_op jit(solution)/shard_map/ppermute | solution.py:26
  53.4 2.2 %collective-permute-start.22 = (bf16[256,896]{1,0:T(8,128)(2,1)S(1)}, bf16[256,896]{1,0:T(8,128)(2,1)S(1)}, u32[]{:S(2)}, u32[]{:S(2)}) collective-permute-start(bf16[256,896]{1,0:T(8,128)(2,1)S(1)} %get-tuple-element.56), channel_id=1, source_target_pairs={{0,1},{1,0},{2,3},{3,2},{4,5},{5,4},{6,7},{7,6},{8,9},{9,8},{10,11... | collective-permute-start | bytes 1376264 | tf_op jit(solution)/shard_map/ppermute | solution.py:26
  53.5 4.3 %collective-permute-start.7 = (bf16[2,128,128]{2,1,0:T(8,128)(2,1)S(1)}, bf16[2,128,128]{2,1,0:T(8,128)(2,1)S(1)}, u32[]{:S(2)}, u32[]{:S(2)}) collective-permute-start(bf16[2,128,128]{2,1,0:T(8,128)(2,1)S(1)} %get-tuple-element.40), channel_id=1, source_target_pairs={{0,1},{1,0},{2,3},{3,2},{4,5},{5,4},{6,7},{7,6},{8,9},{9,8},{10,11... | collective-permute-start | bytes 196616 | tf_op jit(solution)/shard_map/ppermute | solution.py:26
  54.0 14.3 %collective-permute-start.14 = (bf16[2,128,256]{2,1,0:T(8,128)(2,1)S(1)}, bf16[2,128,256]{2,1,0:T(8,128)(2,1)S(1)}, u32[]{:S(2)}, u32[]{:S(2)}) collective-permute-start(bf16[2,128,256]{2,1,0:T(8,128)(2,1)S(1)} %get-tuple-element.45), channel_id=1, source_target_pairs={{0,1},{1,0},{2,3},{3,2},{4,5},{5,4},{6,7},{7,6},{8,9},{9,8},{10,11... | collective-permute-start | bytes 393224 | tf_op jit(solution)/shard_map/ppermute | solution.py:26
  54.1 14.9 %collective-permute-start.15 = (bf16[2,128,256]{2,1,0:T(8,128)(2,1)S(1)}, bf16[2,128,256]{2,1,0:T(8,128)(2,1)S(1)}, u32[]{:S(2)}, u32[]{:S(2)}) collective-permute-start(bf16[2,128,256]{2,1,0:T(8,128)(2,1)S(1)} %get-tuple-element.46), channel_id=1, source_target_pairs={{0,2},{1,3},{2,0},{3,1},{4,6},{5,7},{6,4},{7,5},{8,10},{9,11},{10,... | collective-permute-start | bytes 393224 | tf_op jit(solution)/shard_map/ppermute | solution.py:26
  55.7 21.3 %collective-permute-start.23 = (bf16[128,896]{1,0:T(8,128)(2,1)S(1)}, bf16[128,896]{1,0:T(8,128)(2,1)S(1)}, u32[]{:S(2)}, u32[]{:S(2)}) collective-permute-start(bf16[128,896]{1,0:T(8,128)(2,1)S(1)} %slice.37), channel_id=1, source_target_pairs={{0,2},{1,3},{2,0},{3,1},{4,6},{5,7},{6,4},{7,5},{8,10},{9,11},{10,... | collective-permute-start | bytes 688136 | tf_op jit(solution)/shard_map/ppermute | solution.py:26
  57.0 9.7 %collective-permute-start.8 = (bf16[2,128,128]{2,1,0:T(8,128)(2,1)S(1)}, bf16[2,128,128]{2,1,0:T(8,128)(2,1)S(1)}, u32[]{:S(2)}, u32[]{:S(2)}) collective-permute-start(bf16[2,128,128]{2,1,0:T(8,128)(2,1)S(1)} %get-tuple-element.41), channel_id=1, source_target_pairs={{0,2},{1,3},{2,0},{3,1},{4,6},{5,7},{6,4},{7,5},{8,10},{9,11},{10,... | collective-permute-start | bytes 196616 | tf_op jit(solution)/shard_map/ppermute | solution.py:26
  57.8 9.4 %collective-permute-start.9 = (bf16[2,128,128]{2,1,0:T(8,128)(2,1)S(1)}, bf16[2,128,128]{2,1,0:T(8,128)(2,1)S(1)}, u32[]{:S(2)}, u32[]{:S(2)}) collective-permute-start(bf16[2,128,128]{2,1,0:T(8,128)(2,1)S(1)} %get-tuple-element.42), channel_id=1, source_target_pairs={{0,3},{1,2},{2,1},{3,0},{4,7},{5,6},{6,5},{7,4},{8,11},{9,10},{10,... | collective-permute-start | bytes 196616 | tf_op jit(solution)/shard_map/ppermute | solution.py:26
  66.7 5.7 %collective-permute-start.16 = (bf16[2,128,256]{2,1,0:T(8,128)(2,1)S(1)}, bf16[2,128,256]{2,1,0:T(8,128)(2,1)S(1)}, u32[]{:S(2)}, u32[]{:S(2)}) collective-permute-start(bf16[2,128,256]{2,1,0:T(8,128)(2,1)S(1)} %get-tuple-element.47), channel_id=1, source_target_pairs={{0,3},{1,2},{2,1},{3,0},{4,7},{5,6},{6,5},{7,4},{8,11},{9,10},{10,... | collective-permute-start | bytes 393224 | tf_op jit(solution)/shard_map/ppermute | solution.py:26
  67.2 5.3 %collective-permute-start.19 = (bf16[2,128,128]{2,1,0:T(8,128)(2,1)S(1)}, bf16[2,128,128]{2,1,0:T(8,128)(2,1)S(1)}, u32[]{:S(2)}, u32[]{:S(2)}) collective-permute-start(bf16[2,128,128]{2,1,0:T(8,128)(2,1)S(1)} %get-tuple-element.50), channel_id=1, source_target_pairs={{0,1},{1,0},{2,3},{3,2},{4,5},{5,4},{6,7},{7,6},{8,9},{9,8},{10,11... | collective-permute-start | bytes 196616 | tf_op jit(solution)/shard_map/ppermute | solution.py:26
  68.3 5.6 %collective-permute-start.20 = (bf16[2,128,128]{2,1,0:T(8,128)(2,1)S(1)}, bf16[2,128,128]{2,1,0:T(8,128)(2,1)S(1)}, u32[]{:S(2)}, u32[]{:S(2)}) collective-permute-start(bf16[2,128,128]{2,1,0:T(8,128)(2,1)S(1)} %get-tuple-element.51), channel_id=1, source_target_pairs={{0,2},{1,3},{2,0},{3,1},{4,6},{5,7},{6,4},{7,5},{8,10},{9,11},{10,... | collective-permute-start | bytes 196616 | tf_op jit(solution)/shard_map/ppermute | solution.py:26
  68.9 6.3 %collective-permute-start.21 = (bf16[2,128,128]{2,1,0:T(8,128)(2,1)S(1)}, bf16[2,128,128]{2,1,0:T(8,128)(2,1)S(1)}, u32[]{:S(2)}, u32[]{:S(2)}) collective-permute-start(bf16[2,128,128]{2,1,0:T(8,128)(2,1)S(1)} %get-tuple-element.52), channel_id=1, source_target_pairs={{0,3},{1,2},{2,1},{3,0},{4,7},{5,6},{6,5},{7,4},{8,11},{9,10},{10,... | collective-permute-start | bytes 196616 | tf_op jit(solution)/shard_map/ppermute | solution.py:26

commit v3 on v2

--- a/solution.py
+++ b/solution.py
@@ -33,44 +33,79 @@
     return result
 
 
-def pack_body(seq_size, reads, meta, queries, grad_out, *pieces):
+def bundles(seq_size, item, dtype):
+    sizes = [1] + [1 << b for b in range(seq_size.bit_length() - 1)]
+    return [jax.ShapeDtypeStruct((size, *item), dtype) for size in sizes]
+
+
+def item_of(refs, k):
+    return refs[k.bit_length()].at[k - ((1 << k.bit_length()) >> 1)]
+
+
+def exchange(arrays, seq_size):
+    waiting = {b: [(0, array)] for b, array in enumerate(arrays[1:])}
+    found = {0: arrays[0][0]}
+    for b in reversed(range(len(arrays) - 1)):
+        for origin, array in waiting[b]:
+            arrived = xor_send(array, "seq", seq_size, 1 << b)
+            origin = origin | (1 << b)
+            found[origin] = arrived[0]
+            for c in range(b):
+                waiting[c].append((origin, arrived[1 << c : 2 << c]))
+    return [found[j] for j in range(seq_size)]
+
+
+def pack_body(seq_size, reads, groups, meta, queries, grad_out, *refs):
     own, first = meta[0], meta[1]
     tokens = queries.shape[1]
-    lanes = lax.broadcasted_iota(jnp.int32, (EXTRA, pieces[0].shape[1]), 1)
+    each = len(refs) // len(groups)
+    for g, heads in enumerate(groups):
+        arrays = refs[g * each : (g + 1) * each]
+        for k in range(seq_size):
+            piece = item_of(arrays, k)
+            for i, r in enumerate(heads):
+                column = pl.multiple_of(((first ^ r) * seq_size + (own ^ k)) * HEAD_SIZE, HEAD_SIZE)
+                place = slice(i * HEAD_SIZE, (i + 1) * HEAD_SIZE)
+                piece[:tokens, place] = queries[0, :, pl.ds(column, HEAD_SIZE)]
+                piece[tokens : 2 * tokens, place] = grad_out[0, :, pl.ds(column, HEAD_SIZE)]
+    lanes = lax.broadcasted_iota(jnp.int32, (EXTRA, refs[0].shape[2]), 1)
     positions = jnp.zeros(lanes.shape, jnp.int32)
     for i in range(reads):
         positions = jnp.where(lanes == i, meta[4 + i], positions)
     positions = positions.astype(jnp.float32).astype(jnp.bfloat16)
     for k in range(seq_size):
-        for r in range(HEADS // seq_size):
-            column = pl.multiple_of(((first ^ r) * seq_size + (own ^ k)) * HEAD_SIZE, HEAD_SIZE)
-            place = slice(r * HEAD_SIZE, (r + 1) * HEAD_SIZE)
-            pieces[k][:tokens, place] = queries[0, :, pl.ds(column, HEAD_SIZE)]
-            pieces[k][tokens : 2 * tokens, place] = grad_out[0, :, pl.ds(column, HEAD_SIZE)]
-        pieces[k][2 * tokens :, :] = positions
-
-
-def pack(meta, queries, grad_out, seq_size):
+        item_of(refs[:each], k)[2 * tokens :, :] = positions
+
+
+def pack(meta, queries, grad_out, groups, seq_size):
     tokens = queries.shape[1]
-    shape = jax.ShapeDtypeStruct((2 * tokens + EXTRA, HEADS // seq_size * HEAD_SIZE), jnp.bfloat16)
-    return pl.pallas_call(
-        functools.partial(pack_body, seq_size, meta.shape[0] - 4),
-        out_shape=[shape] * seq_size,
-        in_specs=[pl.BlockSpec(memory_space=pltpu.SMEM)] + [pl.BlockSpec(memory_space=pltpu.VMEM)] * 2,
-        out_specs=[pl.BlockSpec(memory_space=pltpu.VMEM)] * seq_size,
+    vmem = pl.BlockSpec(memory_space=pltpu.VMEM)
+    out_shape = []
+    for g, heads in enumerate(groups):
+        rows = 2 * tokens + (EXTRA if g == 0 else 0)
+        out_shape += bundles(seq_size, (rows, len(heads) * HEAD_SIZE), jnp.bfloat16)
+    outs = pl.pallas_call(
+        functools.partial(pack_body, seq_size, meta.shape[0] - 4, groups),
+        out_shape=out_shape,
+        in_specs=[pl.BlockSpec(memory_space=pltpu.SMEM)] + [vmem] * 2,
+        out_specs=[vmem] * len(out_shape),
         compiler_params=pltpu.CompilerParams(vmem_limit_bytes=vmem_bytes(0)),
         name="pack",
     )(meta, queries, grad_out)
-
-
-def attention_body(seq_size, spans, heads, has_prior, last, *refs):
-    count = len(heads)
+    each = len(outs) // len(groups)
+    return [outs[g * each : (g + 1) * each] for g in range(len(groups))]
+
+
+def attention_body(seq_size, spans, takes, has_prior, last, *refs):
+    count = len(takes)
+    sources = max(source for source, _ in takes) + 1
     meta, refs = refs[0], refs[1:]
     stored, refs = refs[:seq_size], refs[seq_size:]
     weights, refs = refs[: 2 * count], refs[2 * count :]
-    pieces, refs = refs[:seq_size], refs[seq_size:]
+    pieces, refs = refs[: sources * seq_size], refs[sources * seq_size :]
     prior, refs = (refs[0], refs[1:]) if has_prior else (None, refs)
-    outs, refs = refs[:seq_size], refs[seq_size:]
+    levels = seq_size.bit_length()
+    outs, refs = refs[:levels], refs[levels:]
     grads, refs = (refs[:2], refs[2:]) if last else (refs[:1], refs[1:])
     enc, pair, kv, d_kv = refs
     block = stored[0].shape[0]
@@ -85,20 +120,21 @@
         for c in range(spans):
             at = 4 + (k * spans + c) * READS
             spots.append((k, c, [pl.multiple_of(meta[at + r] * NLEN, NLEN) for r in range(READS)]))
-    for i, head in enumerate(heads):
+    for i in range(count):
         first, second = weights[2 * i][...], weights[2 * i + 1][...]
         wide = slice(2 * i * HEAD_SIZE, 2 * (i + 1) * HEAD_SIZE)
         pair[:, 2 * i * HEAD_SIZE : (2 * i + 1) * HEAD_SIZE] = jnp.where(keys_first, first, second)
         pair[:, (2 * i + 1) * HEAD_SIZE : (2 * i + 2) * HEAD_SIZE] = jnp.where(keys_first, second, first)
         kv[...] = jnp.dot(enc[...], pair[:, wide], preferred_element_type=jnp.float32).astype(jnp.bfloat16)
         d_kv[:, wide] = jnp.zeros((rows, 2 * HEAD_SIZE), jnp.float32)
-        columns = slice(head * HEAD_SIZE, (head + 1) * HEAD_SIZE)
-        out_columns = slice(i * HEAD_SIZE, (i + 1) * HEAD_SIZE)
+        columns = slice(i * HEAD_SIZE, (i + 1) * HEAD_SIZE)
+        source, at = takes[i]
+        taken = slice(at * HEAD_SIZE, (at + 1) * HEAD_SIZE)
         reads, queries, grad_rows, scores, d_probs = [], [], [], [], []
         for k, c, starts in spots:
             read = jnp.concatenate([kv[pl.ds(start, NLEN), :] for start in starts], axis=0)
-            query = pieces[k][c * SPAN : (c + 1) * SPAN, columns]
-            grad = pieces[k][tokens + c * SPAN : tokens + (c + 1) * SPAN, columns]
+            query = pieces[source * seq_size + k][c * SPAN : (c + 1) * SPAN, taken]
+            grad = pieces[source * seq_size + k][tokens + c * SPAN : tokens + (c + 1) * SPAN, taken]
             reads.append((read[:, :HEAD_SIZE], read[:, HEAD_SIZE:]))
             queries.append(query)
             grad_rows.append(grad)
@@ -114,10 +150,10 @@
         for n, (k, c, starts) in enumerate(spots):
             keys, values = reads[n]
             span = slice(c * SPAN, (c + 1) * SPAN)
-            outs[k][0, span, out_columns] = jnp.dot(
+            item_of(outs, k)[0, span, columns] = jnp.dot(
                 probs_low[n], values, preferred_element_type=jnp.float32
             ).astype(jnp.bfloat16)
-            outs[k][1, span, out_columns] = jnp.dot(
+            item_of(outs, k)[1, span, columns] = jnp.dot(
                 d_scores[n], keys, preferred_element_type=jnp.float32
             ).astype(jnp.bfloat16)
             d_keys = lax.dot_general(d_scores[n], queries[n], TN, preferred_element_type=jnp.float32)
@@ -139,22 +175,29 @@
             grads[0][place, :] = term.astype(grads[0].dtype)
 
 
-def attention(meta, stored, weights, pieces, heads, spans, prior, last):
-    seq_size = len(pieces)
+def attention(meta, stored, weights, takes, spans, prior, last):
+    seq_size = len(stored)
+    sources = []
+    for source, _ in takes:
+        if not any(source is known for known in sources):
+            sources.append(source)
+    takes = [([source is known for known in sources].index(True), at) for source, at in takes]
+    pieces = [piece for source in sources for piece in source]
     block, width = stored[0].shape
     rows = seq_size * block
-    count = len(heads)
+    count = len(weights) // 2
     prior = [] if prior is None else [prior]
     vmem = pl.BlockSpec(memory_space=pltpu.VMEM)
     operands = [*stored, *weights, *pieces, *prior]
-    out_shape = [jax.ShapeDtypeStruct((2, spans * SPAN, count * HEAD_SIZE), jnp.bfloat16)] * seq_size
+    out_shape = bundles(seq_size, (2, spans * SPAN, count * HEAD_SIZE), jnp.bfloat16)
+    levels = len(out_shape)
     if last:
         out_shape.append(jax.ShapeDtypeStruct((rows // 2, width), jnp.float32))
         out_shape.append(jax.ShapeDtypeStruct((rows // 2, width), jnp.bfloat16))
     else:
         out_shape.append(jax.ShapeDtypeStruct((rows, width), jnp.bfloat16))
     outs = pl.pallas_call(
-        functools.partial(attention_body, seq_size, spans, heads, len(prior), last),
+        functools.partial(attention_body, seq_size, spans, takes, len(prior), last),
         out_shape=out_shape,
         in_specs=[pl.BlockSpec(memory_space=pltpu.SMEM)] + [vmem] * len(operands),
         out_specs=[vmem] * len(out_shape),
@@ -170,7 +213,7 @@
         ),
         name="attention",
     )(meta, *operands)
-    return outs[:seq_size], outs[seq_size:]
+    return outs[:levels], outs[levels:]
 
 
 def unpack_body(seq_size, groups, meta, *refs):
@@ -204,25 +247,17 @@
     return lax.dynamic_slice_in_dim(kv_weight, column, HEAD_SIZE, axis=1)
 
 
-def gather_split(mine, dp_size):
-    send = functools.partial(xor_send, axis="dp", size=dp_size)
-    far = send(mine, bit=4)
-    near = send(mine, bit=2)
-    side = send(mine, bit=1)
-    near_far = send(far, bit=2)
-    side_far = send(far, bit=1)
-    side_near = send(side, bit=2)
-    side_near_far = send(near_far, bit=1)
-    return [(mine, far), (side, side_far), (near, near_far), (side_near, side_near_far)]
-
-
-def gather_whole(kv_weight, own, seq_size):
+def whole_weights(kv_weight, own, seq_size):
     whole = lax.all_gather(kv_weight, "dp", axis=1, tiled=True)
     pairs = []
     for r in range(HEADS // seq_size):
         column = (r * seq_size + own) * HEAD_SIZE
         pairs.append((weight_slice(whole, column), weight_slice(whole, column + HEADS * HEAD_SIZE)))
     return pairs
+
+
+def tie(*values):
+    return lax.optimization_barrier(values)
 
 
 def per_device(dp_size, seq_size, queries, grad_out, encoded, kv_weight, neighbour_ids, slot_map):
@@ -237,43 +272,56 @@
     assert pool_size <= 256 and 1 << bits == seq_size
     split = dp_size == 8 and 2 * HEADS == dp_size * seq_size
     send = functools.partial(xor_send, axis="seq", size=seq_size)
+    move = functools.partial(xor_send, axis="dp", size=dp_size)
 
     if split:
-        mine = weight_slice(kv_weight, own * HEAD_SIZE)
-        mine, queries, grad_out, encoded, neighbour_ids = lax.optimization_barrier(
-            (mine, queries, grad_out, encoded, neighbour_ids)
-        )
-        pairs = gather_split(mine, dp_size)
         first = place % (HEADS // seq_size)
         keys_first = (place < dp_size // 2).astype(jnp.int32)
         groups = [(0,), (1, 2), (3,)]
+        packed = [(0, 1), (2, 3)]
     else:
-        pairs = gather_whole(kv_weight, own, seq_size)
         first, keys_first = place * 0, place * 0 + 1
-        groups = [tuple(range(HEADS // seq_size))]
+        groups = packed = [tuple(range(HEADS // seq_size))]
 
     matches = neighbour_ids[0][:, :, None] == jnp.arange(pool_size, dtype=jnp.int32)[None, None, :]
     positions = jnp.sum(jnp.where(matches, slot_map[0][None, None, :], 0), axis=2).reshape(-1)
     head_meta = jnp.stack([own, first, keys_first, place])
-    pieces = pack(jnp.concatenate([head_meta, positions]), queries, grad_out, seq_size)
-    pieces = [pieces[0]] + [send(pieces[k], bit=k) for k in range(1, seq_size)]
+    pieces = pack(jnp.concatenate([head_meta, positions]), queries, grad_out, packed, seq_size)
+    early = exchange(pieces[0], seq_size)
     stored = [encoded[0].reshape(per_owner * NLEN, width)]
     for level in range(bits - 1, -1, -1):
         stored = stored + [send(rows, bit=1 << level) for rows in stored]
     positions = jnp.concatenate(
         [positions]
-        + [piece[2 * tokens, : spans * READS].astype(jnp.int32) for piece in pieces[1:]]
+        + [piece[2 * tokens, : spans * READS].astype(jnp.int32) for piece in early[1:]]
     )
     relative = bit_reverse((positions // per_owner) ^ own, bits) * per_owner + positions % per_owner
     meta = jnp.concatenate([head_meta, relative])
 
-    parts, grads = [], [None]
-    for heads in groups:
-        weights = [block for head in heads for block in pairs[head]]
+    if split:
+        mine = weight_slice(kv_weight, own * HEAD_SIZE)
+        far, near, side = move(mine, bit=4), move(mine, bit=2), move(mine, bit=1)
+        far, near, side, meta, early, stored, late = tie(far, near, side, meta, early, stored, pieces[1])
+        near_far, side_far = move(far, bit=2), move(far, bit=1)
+        late = exchange(late, seq_size)
+        outs, (grads,) = attention(meta, stored, [mine, far], [(early, 0)], spans, None, False)
+        parts = exchange(outs, seq_size)
+        near_far, side_far, side, grads = tie(near_far, side_far, side, grads)
+        side_near, side_near_far = move(side, bit=2), move(near_far, bit=1)
+        late, parts, grads = tie(late, parts, grads)
+        outs, (grads,) = attention(
+            meta, stored, [side, side_far, near, near_far], [(early, 1), (late, 0)], spans, grads, False
+        )
+        parts = parts + exchange(outs, seq_size)
         outs, grads = attention(
-            meta, stored, weights, pieces, heads, spans, grads[0], heads == groups[-1]
+            meta, stored, [side_near, side_near_far], [(late, 1)], spans, grads, True
         )
-        parts = parts + [outs[0]] + [send(outs[k], bit=k) for k in range(1, seq_size)]
+        parts = parts + exchange(outs, seq_size)
+    else:
+        weights = [block for pair in whole_weights(kv_weight, own, seq_size) for block in pair]
+        takes = [(early, i) for i in range(HEADS // seq_size)]
+        outs, grads = attention(meta, stored, weights, takes, spans, None, True)
+        parts = exchange(outs, seq_size)
     total, leaving = grads
     for level in range(bits):
         total = total + send(leaving, bit=1 << level).astype(jnp.float32)

time: 78.2 us -> 62 us (0.79)
  waiting for transfers between devices: 32.3 us -> 18 us
  starting transfers between devices: 25.5 us -> 21.5 us
  local copies, waits for them, and re-layouts: 4.24 us -> 7.35 us
  Pallas kernels: 13.8 us -> 12.7 us
    ppermute x24 -> x27, waiting for transfers between devices: 32.3 us -> 18 us  [xor_send(): return lax.ppermute(value, axis, [(i, i ^ bit) for i in range(size)])]
    ppermute x24 -> x27, starting transfers between devices: 25.5 us -> 21.5 us  [xor_send(): return lax.ppermute(value, axis, [(i, i ^ bit) for i in range(size)])]
    unnamed x12 -> x28, local copies, waits for them, and re-layouts: 3.93 us -> 5.98 us
    pallas_call x4, Pallas kernels: 12 us -> 10.9 us  [the longest x3 10.1 us: attention(): pl.pallas_call(functools.partial(attention_body, seq_size, spans, takes,...]
    squeeze x0 -> x1, local copies, waits for them, and re-layouts: none -> 0.99 us  [exchange(): found[origin] = arrived[0]]
  transfers between devices with their start and end apart: 24 -> 27, of which waited for: 10 -> 11; matrix products, arithmetic and copies ran while one was open for 1% -> 2% of each run, Pallas kernels for 13% -> 19%
where the time goes in v3:
time: 62 us; the launch traced here: 61.7 us
  starting transfers between devices  21.5 us (35%)
  waiting for transfers between devices  18 us (29%)
  Pallas kernels  12.7 us (20%)
  local copies, waits for them, and re-layouts  7.35 us (12%)
  other arithmetic  1.29 us (2%)
  between operations  0.88 us (1%)
    ppermute x27, starting transfers between devices, xor_send(): return lax.ppermute(value, axis, [(i, i ^ bit) for i in range(size)])  21.5 us
    ppermute x27, waiting for transfers between devices, xor_send(): return lax.ppermute(value, axis, [(i, i ^ bit) for i in range(size)])  18 us
    pallas_call x3, Pallas kernels, attention(): pl.pallas_call(functools.partial(attention_body, seq_size, spans, takes,...  10.1 us
    unnamed x28, local copies, waits for them, and re-layouts  5.98 us
    pallas_call x1, Pallas kernels, unpack(): pl.pallas_call(functools.partial(unpack_body, seq_size, groups), out_shap...  1.79 us
  transfers between devices with their start and end apart: 27, of which 11 were waited for; matrix products, arithmetic and copies ran while one was open for 2% of the time, Pallas kernels for 19%

profile of v3, /device:TPU:0, one launch (start us, length us, event | category | flops | bytes accessed | tf_op | source)
XLA Modules:
  0.0 61.7 jit_solution(15080945497875976756)
XLA Ops:
  0.7 0.7 %copy-done.12 = s32[1,2,2]{2,1,0:T(2,128)S(1)} copy-done((s32[1,2,2]{2,1,0:T(2,128)S(1)}, s32[1,2,2]{2,1,0:T(2,128)}, u32[]{:S(2)}) %copy-start.12) | copy-done | bytes 40
  1.8 1.1 %copy-done.1 = bf16[1,128,2048]{2,1,0:T(8,128)(2,1)S(1)} copy-done((bf16[1,128,2048]{2,1,0:T(8,128)(2,1)S(1)}, bf16[1,128,2048]{2,1,0:T(8,128)(2,1)}, u32[]{:S(2)}) %copy-start.1) | copy-done | bytes 524312
  2.9 1.0 %copy-done.2 = bf16[1,128,2048]{2,1,0:T(8,128)(2,1)S(1)} copy-done((bf16[1,128,2048]{2,1,0:T(8,128)(2,1)S(1)}, bf16[1,128,2048]{2,1,0:T(8,128)(2,1)}, u32[]{:S(2)}) %copy-start.2) | copy-done | bytes 524312
  3.9 0.8 %pack.1 = (bf16[1,272,256]{2,1,0:T(8,128)(2,1)S(1)}, bf16[1,272,256]{2,1,0:T(8,128)(2,1)S(1)}, bf16[2,272,256]{2,1,0:T(8,128)(2,1)S(1)}, bf16[1,256,256]{2,1,0:T...) custom-call(s32[8]{0:T(128)S(1)} %concatenate.11.meta, ...), custom_call_target="tpu_custom_call" | custom-call | tf_op jit(solution)/shard_map/pack/pallas_call | solution.py:87
  4.7 0.6 %copy-done.10 = bf16[1,256,256]{2,1,0:T(8,128)(2,1)} copy-done((bf16[1,256,256]{2,1,0:T(8,128)(2,1)}, bf16[1,256,256]{2,1,0:T(8,128)(2,1)S(1)}, u32[]{:S(2)}) %copy-start.10) | copy-done | bytes 131096
  5.8 2.5 %collective-permute-start.4 = (bf16[2,272,256]{2,1,0:T(8,128)(2,1)S(1)}, bf16[2,272,256]{2,1,0:T(8,128)(2,1)}, u32[]{:S(2)}, u32[]{:S(2)}) collective-permute-start(bf16[2,272,256]{2,1,0:T(8,128)(2,1)S(1)} %get-tuple-element.53), channel_id=1, source_target_pairs={{0,2},{1,3},{2,0},{3,1},{4,6},{5,7},{6,4},{7,5},{8,10},{9,11},{10,... | collective-permute-start | bytes 835592 | tf_op jit(solution)/shard_map/ppermute | solution.py:26
  8.4 2.7 %collective-permute-start = (bf16[896,128]{1,0:T(8,128)(2,1)S(1)}, bf16[896,128]{1,0:T(8,128)(2,1)S(1)}, u32[]{:S(2)}, u32[]{:S(2)}) collective-permute-start(bf16[896,128]{1,0:T(8,128)(2,1)S(1)} %constant_dynamic-slice_fusion.refs_5_), channel_id=1, source_target_pairs={{0,16},{4,20},{8,24},{12,28},{16,0},{20,4},{24,8},{28,12},{1,17},{... | collective-permute-start | bytes 688136 | tf_op jit(solution)/shard_map/ppermute | solution.py:26
  11.0 1.6 %collective-permute-start.1 = (bf16[896,128]{1,0:T(8,128)(2,1)S(1)}, bf16[896,128]{1,0:T(8,128)(2,1)S(1)}, u32[]{:S(2)}, u32[]{:S(2)}) collective-permute-start(bf16[896,128]{1,0:T(8,128)(2,1)S(1)} %constant_dynamic-slice_fusion.refs_5_), channel_id=1, source_target_pairs={{0,8},{4,12},{8,0},{12,4},{16,24},{20,28},{24,16},{28,20},{1,9},{5... | collective-permute-start | bytes 688136 | tf_op jit(solution)/shard_map/ppermute | solution.py:26
  12.6 1.5 %collective-permute-start.2 = (bf16[896,128]{1,0:T(8,128)(2,1)S(1)}, bf16[896,128]{1,0:T(8,128)(2,1)S(1)}, u32[]{:S(2)}, u32[]{:S(2)}) collective-permute-start(bf16[896,128]{1,0:T(8,128)(2,1)S(1)} %constant_dynamic-slice_fusion.refs_5_), channel_id=1, source_target_pairs={{0,4},{4,0},{8,12},{12,8},{16,20},{20,16},{24,28},{28,24},{1,5},{5... | collective-permute-start | bytes 688136 | tf_op jit(solution)/shard_map/ppermute | solution.py:26
  14.7 1.0 %collective-permute-done.4 = bf16[2,272,256]{2,1,0:T(8,128)(2,1)} collective-permute-done((bf16[2,272,256]{2,1,0:T(8,128)(2,1)S(1)}, bf16[2,272,256]{2,1,0:T(8,128)(2,1)}, u32[]{:S(2)}, u32[]{:S(2)}) %collective-permute-start.4) | collective-permute-done | bytes 278560 | tf_op jit(solution)/shard_map/ppermute | solution.py:26
  15.8 1.0 %slice_bitcast_fusion = (bf16[272,256]{1,0:T(8,128)(2,1)S(1)}, bf16[1,272,256]{2,1,0:T(8,128)(2,1)S(1)}) fusion(bf16[2,272,256]{2,1,0:T(8,128)(2,1)} %collective-permute-done.4), kind=kLoop, calls=%fused_computation.3 | loop fusion | bytes 557056 | tf_op jit(solution)/shard_map/squeeze | solution.py:52
  16.8 4.2 %collective-permute-done.6.refs_2_ = bf16[128,896]{1,0:T(8,128)(2,1)S(1)} collective-permute-done((bf16[128,896]{1,0:T(8,128)(2,1)S(1)}, bf16[128,896]{1,0:T(8,128)(2,1)S(1)}, u32[]{:S(2)}, u32[]{:S(2)}) %collective-permute-start.6) | collective-permute-done | bytes 229408 | tf_op jit(solution)/shard_map/ppermute | solution.py:26
  21.6 0.7 %copy-done.7 = bf16[1,272,256]{2,1,0:T(8,128)(2,1)} copy-done((bf16[1,272,256]{2,1,0:T(8,128)(2,1)}, bf16[1,272,256]{2,1,0:T(8,128)(2,1)S(1)}, u32[]{:S(2)}) %copy-start.7) | copy-done | bytes 139288
  22.9 1.2 %collective-permute-start.10 = (bf16[2,256,256]{2,1,0:T(8,128)(2,1)S(1)}, bf16[2,256,256]{2,1,0:T(8,128)(2,1)S(1)}, u32[]{:S(2)}, u32[]{:S(2)}) collective-permute-start(bf16[2,256,256]{2,1,0:T(8,128)(2,1)S(1)} %get-tuple-element.60), channel_id=1, source_target_pairs={{0,2},{1,3},{2,0},{3,1},{4,6},{5,7},{6,4},{7,5},{8,10},{9,11},{10,... | collective-permute-start | bytes 786440 | tf_op jit(solution)/shard_map/ppermute | solution.py:26
  24.1 1.6 %collective-permute-start.15 = (bf16[896,128]{1,0:T(8,128)(2,1)S(1)}, bf16[896,128]{1,0:T(8,128)(2,1)S(1)}, u32[]{:S(2)}, u32[]{:S(2)}) collective-permute-start(bf16[896,128]{1,0:T(8,128)(2,1)S(1)} %collective-permute-done.refs_6_), channel_id=1, source_target_pairs={{0,8},{4,12},{8,0},{12,4},{16,24},{20,28},{24,16},{28,20},{1,9},{5... | collective-permute-start | bytes 688136 | tf_op jit(solution)/shard_map/ppermute | solution.py:26
  25.7 1.5 %collective-permute-start.16 = (bf16[896,128]{1,0:T(8,128)(2,1)S(1)}, bf16[896,128]{1,0:T(8,128)(2,1)S(1)}, u32[]{:S(2)}, u32[]{:S(2)}) collective-permute-start(bf16[896,128]{1,0:T(8,128)(2,1)S(1)} %collective-permute-done.refs_6_), channel_id=1, source_target_pairs={{0,4},{4,0},{8,12},{12,8},{16,20},{20,16},{24,28},{28,24},{1,5},{5... | collective-permute-start | bytes 688136 | tf_op jit(solution)/shard_map/ppermute | solution.py:26
  27.2 0.9 %copy-done.5 = bf16[1,272,256]{2,1,0:T(8,128)(2,1)S(1)} copy-done((bf16[1,272,256]{2,1,0:T(8,128)(2,1)S(1)}, bf16[1,272,256]{2,1,0:T(8,128)(2,1)}, u32[]{:S(2)}) %copy-start.5) | copy-done | bytes 139288
  28.1 0.9 %copy-done.8 = bf16[1,272,256]{2,1,0:T(8,128)(2,1)S(1)} copy-done((bf16[1,272,256]{2,1,0:T(8,128)(2,1)S(1)}, bf16[1,272,256]{2,1,0:T(8,128)(2,1)}, u32[]{:S(2)}) %copy-start.8) | copy-done | bytes 139288
  29.0 2.7 %attention.3 = (bf16[1,2,128,128]{3,2,1,0:T(8,128)(2,1)S(1)}, bf16[1,2,128,128]{3,2,1,0:T(8,128)(2,1)S(1)}, bf16[2,2,128,128]{3,2,1,0:T(8,128)(2,1)S(1)}, bf16[512,896]{1,0:T(8,128)(2,1)S(1)}) custom-call(s32[20]{0:T(128)S(1)} %concatenate.13.refs_0_, bf16[128,896]{1,0:T(8,128)(2,1)S(1)} %bitcast.59, bf16[128,896]{1,0:T(8,128)(2,1)S(1)} %collective-permute-done.6.refs_2_, ...), custom_call_target="tpu_custom_call" | custom-call | flops 1879048192 | bytes 1835008 | tf_op jit(solution)/shard_map/attention/pallas_call | solution.py:199
  32.9 4.9 %collective-permute-done.13 = bf16[2,2,128,128]{3,2,1,0:T(8,128)(2,1)S(1)} collective-permute-done((bf16[2,2,128,128]{3,2,1,0:T(8,128)(2,1)S(1)}, bf16[2,2,128,128]{3,2,1,0:T(8,128)(2,1)S(1)}, u32[]{:S(2)}, u32[]{:S(2)}) %collective-permute-start.13) | collective-permute-done | bytes 131104 | tf_op jit(solution)/shard_map/ppermute | solution.py:26
  38.9 0.8 %collective-permute-start.21 = (bf16[896,128]{1,0:T(8,128)(2,1)S(1)}, bf16[896,128]{1,0:T(8,128)(2,1)S(1)}, u32[]{:S(2)}, u32[]{:S(2)}) collective-permute-start(bf16[896,128]{1,0:T(8,128)(2,1)S(1)} %collective-permute-done.15.refs_8_), channel_id=1, source_target_pairs={{0,4},{4,0},{8,12},{12,8},{16,20},{20,16},{24,28},{28,24},{1,5},{5... | collective-permute-start | bytes 688136 | tf_op jit(solution)/shard_map/ppermute | solution.py:26
  39.7 4.6 %attention.4 = (bf16[1,2,128,256]{3,2,1,0:T(8,128)(2,1)S(1)}, bf16[1,2,128,256]{3,2,1,0:T(8,128)(2,1)S(1)}, bf16[2,2,128,256]{3,2,1,0:T(8,128)(2,1)S(1)}, bf16[512,896]{1,0:T(8,128)(2,1)S(1)}) custom-call(s32[20]{0:T(128)S(1)} %concatenate.13.refs_0_, bf16[128,896]{1,0:T(8,128)(2,1)S(1)} %bitcast.60, bf16[128,896]{1,0:T(8,128)(2,1)S(1)} %collective-permute-done.6.refs_2_, ...), custom_call_target="tpu_custom_call" | custom-call | flops 3758096384 | bytes 1835008 | tf_op jit(solution)/shard_map/attention/pallas_call | solution.py:199
  44.4 1.6 %collective-permute-start.18 = (bf16[2,2,128,256]{3,2,1,0:T(8,128)(2,1)S(1)}, bf16[2,2,128,256]{3,2,1,0:T(8,128)(2,1)S(1)}, u32[]{:S(2)}, u32[]{:S(2)}) collective-permute-start(bf16[2,2,128,256]{3,2,1,0:T(8,128)(2,1)S(1)} %get-tuple-element.92), channel_id=1, source_target_pairs={{0,2},{1,3},{2,0},{3,1},{4,6},{5,7},{6,4},{7,5},{8,10},{9,11},{10,... | collective-permute-start | bytes 786440 | tf_op jit(solution)/shard_map/ppermute | solution.py:26
  46.2 2.7 %attention.5 = (bf16[1,2,128,128]{3,2,1,0:T(8,128)(2,1)S(1)}, bf16[1,2,128,128]{3,2,1,0:T(8,128)(2,1)S(1)}, bf16[2,2,128,128]{3,2,1,0:T(8,128)(2,1)S(1)}, f32[256,896]{1,0:T(8,128)S(1)}, bf16[256,896]{1,0:T(8,128)(2,1)S(1)}) custom-call(s32[20]{0:T(128)S(1)} %concatenate.13.refs_0_, bf16[128,896]{1,0:T(8,128)(2,1)S(1)} %bitcast.61, ...), custom_call_target="tpu_custom_call" | custom-call | flops 1879048192 | bytes 1835008 | tf_op jit(solution)/shard_map/attention/pallas_call | solution.py:199
  49.6 0.8 %collective-permute-start.23 = (bf16[2,2,128,128]{3,2,1,0:T(8,128)(2,1)S(1)}, bf16[2,2,128,128]{3,2,1,0:T(8,128)(2,1)S(1)}, u32[]{:S(2)}, u32[]{:S(2)}) collective-permute-start(bf16[2,2,128,128]{3,2,1,0:T(8,128)(2,1)S(1)} %get-tuple-element.96), channel_id=1, source_target_pairs={{0,2},{1,3},{2,0},{3,1},{4,6},{5,7},{6,4},{7,5},{8,10},{9,11},{10,... | collective-permute-start | bytes 393224 | tf_op jit(solution)/shard_map/ppermute | solution.py:26
  50.4 2.2 %collective-permute-done.18 = bf16[2,2,128,256]{3,2,1,0:T(8,128)(2,1)S(1)} collective-permute-done((bf16[2,2,128,256]{3,2,1,0:T(8,128)(2,1)S(1)}, bf16[2,2,128,256]{3,2,1,0:T(8,128)(2,1)S(1)}, u32[]{:S(2)}, u32[]{:S(2)}) %collective-permute-start.18) | collective-permute-done | bytes 262176 | tf_op jit(solution)/shard_map/ppermute | solution.py:26
  52.9 1.3 %collective-permute-start.26 = (bf16[128,896]{1,0:T(8,128)(2,1)S(1)}, bf16[128,896]{1,0:T(8,128)(2,1)S(1)}, u32[]{:S(2)}, u32[]{:S(2)}) collective-permute-start(bf16[128,896]{1,0:T(8,128)(2,1)S(1)} %slice.92), channel_id=1, source_target_pairs={{0,2},{1,3},{2,0},{3,1},{4,6},{5,7},{6,4},{7,5},{8,10},{9,11},{10,... | collective-permute-start | bytes 688136 | tf_op jit(solution)/shard_map/ppermute | solution.py:26
  54.1 1.3 %collective-permute-done.23 = bf16[2,2,128,128]{3,2,1,0:T(8,128)(2,1)S(1)} collective-permute-done((bf16[2,2,128,128]{3,2,1,0:T(8,128)(2,1)S(1)}, bf16[2,2,128,128]{3,2,1,0:T(8,128)(2,1)S(1)}, u32[]{:S(2)}, u32[]{:S(2)}) %collective-permute-start.23) | collective-permute-done | bytes 131104 | tf_op jit(solution)/shard_map/ppermute | solution.py:26
  55.7 1.2 %collective-permute-done.24 = bf16[1,2,128,128]{3,2,1,0:T(8,128)(2,1)S(1)} collective-permute-done((bf16[1,2,128,128]{3,2,1,0:T(8,128)(2,1)S(1)}, bf16[1,2,128,128]{3,2,1,0:T(8,128)(2,1)S(1)}, u32[]{:S(2)}, u32[]{:S(2)}) %collective-permute-start.24) | collective-permute-done | bytes 65568 | tf_op jit(solution)/shard_map/ppermute | solution.py:26
  56.8 1.8 %unpack.1 = (bf16[1,128,2048]{2,1,0:T(8,128)(2,1)}, bf16[1,128,2048]{2,1,0:T(8,128)(2,1)}) custom-call(s32[4]{0:T(128)S(1)} %pad_add_fusion.meta, bf16[2,128,128]{2,1,0:T(8,128)(2,1)S(1)} %bitcast.51, bf16[2,128,128]{2,1,0:T(8,128)(2,1)S(1)} %bitcast.52, bf16[2,128,128]{2,1,0:T(8,128)(2,1)S(1)} %get-tuple-element.79.refs_2_, ...), custom_call_target="tpu_custom_call" | custom-call | tf_op jit(solution)/shard_map/unpack/pallas_call | solution.py:236
  58.6 2.3 %collective-permute-done.26 = bf16[128,896]{1,0:T(8,128)(2,1)S(1)} collective-permute-done((bf16[128,896]{1,0:T(8,128)(2,1)S(1)}, bf16[128,896]{1,0:T(8,128)(2,1)S(1)}, u32[]{:S(2)}, u32[]{:S(2)}) %collective-permute-start.26) | collective-permute-done | bytes 229408 | tf_op jit(solution)/shard_map/ppermute | solution.py:26
  60.9 0.8 %slice_add_fusion = f32[128,896]{1,0:T(8,128)} fusion(f32[256,896]{1,0:T(8,128)S(1)} %convert_add_fusion, bf16[128,896]{1,0:T(8,128)(2,1)S(1)} %collective-permute-done.26), kind=kLoop, calls=%fused_computation.2 | loop fusion | flops 229376 | bytes 1146880 | tf_op jit(solution)/shard_map/add | solution.py:327
  (73 shorter events, 6.2 us)
Async XLA Ops:
  0.6 7.7 %copy-start = (bf16[896,512]{1,0:T(8,128)(2,1)S(1)}, bf16[896,512]{1,0:T(8,128)(2,1)}, u32[]{:S(2)}) copy-start(bf16[896,512]{1,0:T(8,128)(2,1)} %param.9) | copy-start | bytes 2752516
  5.4 8.7 %collective-permute-start.3 = (bf16[1,272,256]{2,1,0:T(8,128)(2,1)S(1)}, bf16[1,272,256]{2,1,0:T(8,128)(2,1)S(1)}, u32[]{:S(2)}, u32[]{:S(2)}) collective-permute-start(bf16[1,272,256]{2,1,0:T(8,128)(2,1)S(1)} %get-tuple-element.52), channel_id=1, source_target_pairs={{0,1},{1,0},{2,3},{3,2},{4,5},{5,4},{6,7},{7,6},{8,9},{9,8},{10,11... | collective-permute-start | bytes 417800 | tf_op jit(solution)/shard_map/ppermute | solution.py:26
  5.8 9.9 %collective-permute-start.4 = (bf16[2,272,256]{2,1,0:T(8,128)(2,1)S(1)}, bf16[2,272,256]{2,1,0:T(8,128)(2,1)}, u32[]{:S(2)}, u32[]{:S(2)}) collective-permute-start(bf16[2,272,256]{2,1,0:T(8,128)(2,1)S(1)} %get-tuple-element.53), channel_id=1, source_target_pairs={{0,2},{1,3},{2,0},{3,1},{4,6},{5,7},{6,4},{7,5},{8,10},{9,11},{10,... | collective-permute-start | bytes 835592 | tf_op jit(solution)/shard_map/ppermute | solution.py:26
  8.3 5.8 %copy-start.3 = (bf16[1,2,64,896]{3,2,1,0:T(8,128)(2,1)S(1)}, bf16[1,2,64,896]{3,2,1,0:T(8,128)(2,1)}, u32[]{:S(2)}) copy-start(bf16[1,2,64,896]{3,2,1,0:T(8,128)(2,1)} %param.8) | copy-start | bytes 688132
  8.4 14.1 %collective-permute-start = (bf16[896,128]{1,0:T(8,128)(2,1)S(1)}, bf16[896,128]{1,0:T(8,128)(2,1)S(1)}, u32[]{:S(2)}, u32[]{:S(2)}) collective-permute-start(bf16[896,128]{1,0:T(8,128)(2,1)S(1)} %constant_dynamic-slice_fusion.refs_5_), channel_id=1, source_target_pairs={{0,16},{4,20},{8,24},{12,28},{16,0},{20,4},{24,8},{28,12},{1,17},{... | collective-permute-start | bytes 688136 | tf_op jit(solution)/shard_map/ppermute | solution.py:26
  11.0 11.4 %collective-permute-start.1 = (bf16[896,128]{1,0:T(8,128)(2,1)S(1)}, bf16[896,128]{1,0:T(8,128)(2,1)S(1)}, u32[]{:S(2)}, u32[]{:S(2)}) collective-permute-start(bf16[896,128]{1,0:T(8,128)(2,1)S(1)} %constant_dynamic-slice_fusion.refs_5_), channel_id=1, source_target_pairs={{0,8},{4,12},{8,0},{12,4},{16,24},{20,28},{24,16},{28,20},{1,9},{5... | collective-permute-start | bytes 688136 | tf_op jit(solution)/shard_map/ppermute | solution.py:26
  12.6 9.8 %collective-permute-start.2 = (bf16[896,128]{1,0:T(8,128)(2,1)S(1)}, bf16[896,128]{1,0:T(8,128)(2,1)S(1)}, u32[]{:S(2)}, u32[]{:S(2)}) collective-permute-start(bf16[896,128]{1,0:T(8,128)(2,1)S(1)} %constant_dynamic-slice_fusion.refs_5_), channel_id=1, source_target_pairs={{0,4},{4,0},{8,12},{12,8},{16,20},{20,16},{24,28},{28,24},{1,5},{5... | collective-permute-start | bytes 688136 | tf_op jit(solution)/shard_map/ppermute | solution.py:26
  14.1 2.6 %copy-start.4 = (bf16[1,272,256]{2,1,0:T(8,128)(2,1)}, bf16[1,272,256]{2,1,0:T(8,128)(2,1)S(1)}, u32[]{:S(2)}) copy-start(bf16[1,272,256]{2,1,0:T(8,128)(2,1)S(1)} %collective-permute-done.3) | copy-start | bytes 417796
  14.1 7.0 %collective-permute-start.6 = (bf16[128,896]{1,0:T(8,128)(2,1)S(1)}, bf16[128,896]{1,0:T(8,128)(2,1)S(1)}, u32[]{:S(2)}, u32[]{:S(2)}) collective-permute-start(bf16[128,896]{1,0:T(8,128)(2,1)S(1)} %bitcast.57), channel_id=1, source_target_pairs={{0,2},{1,3},{2,0},{3,1},{4,6},{5,7},{6,4},{7,5},{8,10},{9,11},{10,... | collective-permute-start | bytes 688136 | tf_op jit(solution)/shard_map/ppermute | solution.py:26
  16.8 4.3 %collective-permute-start.5 = (bf16[1,272,256]{2,1,0:T(8,128)(2,1)S(1)}, bf16[1,272,256]{2,1,0:T(8,128)(2,1)S(1)}, u32[]{:S(2)}, u32[]{:S(2)}) collective-permute-start(bf16[1,272,256]{2,1,0:T(8,128)(2,1)S(1)} %get-tuple-element.102), channel_id=1, source_target_pairs={{0,1},{1,0},{2,3},{3,2},{4,5},{5,4},{6,7},{7,6},{8,9},{9,8},{10,11... | collective-permute-start | bytes 417800 | tf_op jit(solution)/shard_map/ppermute | solution.py:26
  21.1 1.5 %collective-permute-start.7 = (bf16[128,896]{1,0:T(8,128)(2,1)S(1)}, bf16[128,896]{1,0:T(8,128)(2,1)S(1)}, u32[]{:S(2)}, u32[]{:S(2)}) collective-permute-start(bf16[128,896]{1,0:T(8,128)(2,1)S(1)} %bitcast.58), channel_id=1, source_target_pairs={{0,1},{1,0},{2,3},{3,2},{4,5},{5,4},{6,7},{7,6},{8,9},{9,8},{10,11... | collective-permute-start | bytes 688136 | tf_op jit(solution)/shard_map/ppermute | solution.py:26
  21.1 1.8 %collective-permute-start.8 = (bf16[128,896]{1,0:T(8,128)(2,1)S(1)}, bf16[128,896]{1,0:T(8,128)(2,1)S(1)}, u32[]{:S(2)}, u32[]{:S(2)}) collective-permute-start(bf16[128,896]{1,0:T(8,128)(2,1)S(1)} %collective-permute-done.6.refs_2_), channel_id=1, source_target_pairs={{0,1},{1,0},{2,3},{3,2},{4,5},{5,4},{6,7},{7,6},{8,9},{9,8},{10,11... | collective-permute-start | bytes 688136 | tf_op jit(solution)/shard_map/ppermute | solution.py:26
  22.9 9.5 %collective-permute-start.10 = (bf16[2,256,256]{2,1,0:T(8,128)(2,1)S(1)}, bf16[2,256,256]{2,1,0:T(8,128)(2,1)S(1)}, u32[]{:S(2)}, u32[]{:S(2)}) collective-permute-start(bf16[2,256,256]{2,1,0:T(8,128)(2,1)S(1)} %get-tuple-element.60), channel_id=1, source_target_pairs={{0,2},{1,3},{2,0},{3,1},{4,6},{5,7},{6,4},{7,5},{8,10},{9,11},{10,... | collective-permute-start | bytes 786440 | tf_op jit(solution)/shard_map/ppermute | solution.py:26
  24.1 13.7 %collective-permute-start.15 = (bf16[896,128]{1,0:T(8,128)(2,1)S(1)}, bf16[896,128]{1,0:T(8,128)(2,1)S(1)}, u32[]{:S(2)}, u32[]{:S(2)}) collective-permute-start(bf16[896,128]{1,0:T(8,128)(2,1)S(1)} %collective-permute-done.refs_6_), channel_id=1, source_target_pairs={{0,8},{4,12},{8,0},{12,4},{16,24},{20,28},{24,16},{28,20},{1,9},{5... | collective-permute-start | bytes 688136 | tf_op jit(solution)/shard_map/ppermute | solution.py:26
  25.7 12.8 %collective-permute-start.16 = (bf16[896,128]{1,0:T(8,128)(2,1)S(1)}, bf16[896,128]{1,0:T(8,128)(2,1)S(1)}, u32[]{:S(2)}, u32[]{:S(2)}) collective-permute-start(bf16[896,128]{1,0:T(8,128)(2,1)S(1)} %collective-permute-done.refs_6_), channel_id=1, source_target_pairs={{0,4},{4,0},{8,12},{12,8},{16,20},{20,16},{24,28},{28,24},{1,5},{5... | collective-permute-start | bytes 688136 | tf_op jit(solution)/shard_map/ppermute | solution.py:26
  27.2 12.5 %collective-permute-start.9 = (bf16[1,256,256]{2,1,0:T(8,128)(2,1)S(1)}, bf16[1,256,256]{2,1,0:T(8,128)(2,1)S(1)}, u32[]{:S(2)}, u32[]{:S(2)}) collective-permute-start(bf16[1,256,256]{2,1,0:T(8,128)(2,1)S(1)} %get-tuple-element.59), channel_id=1, source_target_pairs={{0,1},{1,0},{2,3},{3,2},{4,5},{5,4},{6,7},{7,6},{8,9},{9,8},{10,11... | collective-permute-start | bytes 393224 | tf_op jit(solution)/shard_map/ppermute | solution.py:26
  31.8 7.1 %collective-permute-start.12 = (bf16[1,2,128,128]{3,2,1,0:T(8,128)(2,1)S(1)}, bf16[1,2,128,128]{3,2,1,0:T(8,128)(2,1)S(1)}, u32[]{:S(2)}, u32[]{:S(2)}) collective-permute-start(bf16[1,2,128,128]{3,2,1,0:T(8,128)(2,1)S(1)} %get-tuple-element.72), channel_id=1, source_target_pairs={{0,1},{1,0},{2,3},{3,2},{4,5},{5,4},{6,7},{7,6},{8,9},{9,8},{10,11... | collective-permute-start | bytes 196616 | tf_op jit(solution)/shard_map/ppermute | solution.py:26
  32.4 5.5 %collective-permute-start.13 = (bf16[2,2,128,128]{3,2,1,0:T(8,128)(2,1)S(1)}, bf16[2,2,128,128]{3,2,1,0:T(8,128)(2,1)S(1)}, u32[]{:S(2)}, u32[]{:S(2)}) collective-permute-start(bf16[2,2,128,128]{3,2,1,0:T(8,128)(2,1)S(1)} %get-tuple-element.73), channel_id=1, source_target_pairs={{0,2},{1,3},{2,0},{3,1},{4,6},{5,7},{6,4},{7,5},{8,10},{9,11},{10,... | collective-permute-start | bytes 393224 | tf_op jit(solution)/shard_map/ppermute | solution.py:26
  32.9 6.8 %copy-start.11 = (bf16[1,256,256]{2,1,0:T(8,128)(2,1)S(1)}, bf16[1,256,256]{2,1,0:T(8,128)(2,1)}, u32[]{:S(2)}) copy-start(bf16[1,256,256]{2,1,0:T(8,128)(2,1)} %copy-done.10) | copy-start | bytes 393220
  37.8 1.9 %copy-start.9 = (bf16[1,272,256]{2,1,0:T(8,128)(2,1)S(1)}, bf16[1,272,256]{2,1,0:T(8,128)(2,1)}, u32[]{:S(2)}) copy-start(bf16[1,272,256]{2,1,0:T(8,128)(2,1)} %copy-done.7) | copy-start | bytes 417796
  37.9 1.9 %collective-permute-start.11 = (bf16[1,256,256]{2,1,0:T(8,128)(2,1)S(1)}, bf16[1,256,256]{2,1,0:T(8,128)(2,1)S(1)}, u32[]{:S(2)}, u32[]{:S(2)}) collective-permute-start(bf16[1,256,256]{2,1,0:T(8,128)(2,1)S(1)} %get-tuple-element.105), channel_id=1, source_target_pairs={{0,1},{1,0},{2,3},{3,2},{4,5},{5,4},{6,7},{7,6},{8,9},{9,8},{10,11... | collective-permute-start | bytes 393224 | tf_op jit(solution)/shard_map/ppermute | solution.py:26
  37.9 1.8 %collective-permute-start.14 = (bf16[1,2,128,128]{3,2,1,0:T(8,128)(2,1)S(1)}, bf16[1,2,128,128]{3,2,1,0:T(8,128)(2,1)S(1)}, u32[]{:S(2)}, u32[]{:S(2)}) collective-permute-start(bf16[1,2,128,128]{3,2,1,0:T(8,128)(2,1)S(1)} %get-tuple-element.109), channel_id=1, source_target_pairs={{0,1},{1,0},{2,3},{3,2},{4,5},{5,4},{6,7},{7,6},{8,9},{9,8},{10,11... | collective-permute-start | bytes 196616 | tf_op jit(solution)/shard_map/ppermute | solution.py:26
  38.5 7.6 %collective-permute-start.20 = (bf16[896,128]{1,0:T(8,128)(2,1)S(1)}, bf16[896,128]{1,0:T(8,128)(2,1)S(1)}, u32[]{:S(2)}, u32[]{:S(2)}) collective-permute-start(bf16[896,128]{1,0:T(8,128)(2,1)S(1)} %collective-permute-done.2.refs_5_), channel_id=1, source_target_pairs={{0,8},{4,12},{8,0},{12,4},{16,24},{20,28},{24,16},{28,20},{1,9},{5... | collective-permute-start | bytes 688136 | tf_op jit(solution)/shard_map/ppermute | solution.py:26
  38.9 7.3 %collective-permute-start.21 = (bf16[896,128]{1,0:T(8,128)(2,1)S(1)}, bf16[896,128]{1,0:T(8,128)(2,1)S(1)}, u32[]{:S(2)}, u32[]{:S(2)}) collective-permute-start(bf16[896,128]{1,0:T(8,128)(2,1)S(1)} %collective-permute-done.15.refs_8_), channel_id=1, source_target_pairs={{0,4},{4,0},{8,12},{12,8},{16,20},{20,16},{24,28},{28,24},{1,5},{5... | collective-permute-start | bytes 688136 | tf_op jit(solution)/shard_map/ppermute | solution.py:26
  44.4 8.3 %collective-permute-start.18 = (bf16[2,2,128,256]{3,2,1,0:T(8,128)(2,1)S(1)}, bf16[2,2,128,256]{3,2,1,0:T(8,128)(2,1)S(1)}, u32[]{:S(2)}, u32[]{:S(2)}) collective-permute-start(bf16[2,2,128,256]{3,2,1,0:T(8,128)(2,1)S(1)} %get-tuple-element.92), channel_id=1, source_target_pairs={{0,2},{1,3},{2,0},{3,1},{4,6},{5,7},{6,4},{7,5},{8,10},{9,11},{10,... | collective-permute-start | bytes 786440 | tf_op jit(solution)/shard_map/ppermute | solution.py:26
  49.0 3.8 %collective-permute-start.25 = (bf16[256,896]{1,0:T(8,128)(2,1)S(1)}, bf16[256,896]{1,0:T(8,128)(2,1)S(1)}, u32[]{:S(2)}, u32[]{:S(2)}) collective-permute-start(bf16[256,896]{1,0:T(8,128)(2,1)S(1)} %get-tuple-element.100), channel_id=1, source_target_pairs={{0,1},{1,0},{2,3},{3,2},{4,5},{5,4},{6,7},{7,6},{8,9},{9,8},{10,11... | collective-permute-start | bytes 1376264 | tf_op jit(solution)/shard_map/ppermute | solution.py:26
  49.0 6.6 %collective-permute-start.17 = (bf16[1,2,128,256]{3,2,1,0:T(8,128)(2,1)S(1)}, bf16[1,2,128,256]{3,2,1,0:T(8,128)(2,1)S(1)}, u32[]{:S(2)}, u32[]{:S(2)}) collective-permute-start(bf16[1,2,128,256]{3,2,1,0:T(8,128)(2,1)S(1)} %get-tuple-element.91), channel_id=1, source_target_pairs={{0,1},{1,0},{2,3},{3,2},{4,5},{5,4},{6,7},{7,6},{8,9},{9,8},{10,11... | collective-permute-start | bytes 393224 | tf_op jit(solution)/shard_map/ppermute | solution.py:26
  49.5 6.1 %collective-permute-start.22 = (bf16[1,2,128,128]{3,2,1,0:T(8,128)(2,1)S(1)}, bf16[1,2,128,128]{3,2,1,0:T(8,128)(2,1)S(1)}, u32[]{:S(2)}, u32[]{:S(2)}) collective-permute-start(bf16[1,2,128,128]{3,2,1,0:T(8,128)(2,1)S(1)} %get-tuple-element.95), channel_id=1, source_target_pairs={{0,1},{1,0},{2,3},{3,2},{4,5},{5,4},{6,7},{7,6},{8,9},{9,8},{10,11... | collective-permute-start | bytes 196616 | tf_op jit(solution)/shard_map/ppermute | solution.py:26
  49.6 5.8 %collective-permute-start.23 = (bf16[2,2,128,128]{3,2,1,0:T(8,128)(2,1)S(1)}, bf16[2,2,128,128]{3,2,1,0:T(8,128)(2,1)S(1)}, u32[]{:S(2)}, u32[]{:S(2)}) collective-permute-start(bf16[2,2,128,128]{3,2,1,0:T(8,128)(2,1)S(1)} %get-tuple-element.96), channel_id=1, source_target_pairs={{0,2},{1,3},{2,0},{3,1},{4,6},{5,7},{6,4},{7,5},{8,10},{9,11},{10,... | collective-permute-start | bytes 393224 | tf_op jit(solution)/shard_map/ppermute | solution.py:26
  52.7 4.2 %collective-permute-start.19 = (bf16[1,2,128,256]{3,2,1,0:T(8,128)(2,1)S(1)}, bf16[1,2,128,256]{3,2,1,0:T(8,128)(2,1)S(1)}, u32[]{:S(2)}, u32[]{:S(2)}) collective-permute-start(bf16[1,2,128,256]{3,2,1,0:T(8,128)(2,1)S(1)} %get-tuple-element.103), channel_id=1, source_target_pairs={{0,1},{1,0},{2,3},{3,2},{4,5},{5,4},{6,7},{7,6},{8,9},{9,8},{10,11... | collective-permute-start | bytes 393224 | tf_op jit(solution)/shard_map/ppermute | solution.py:26
  52.9 8.1 %collective-permute-start.26 = (bf16[128,896]{1,0:T(8,128)(2,1)S(1)}, bf16[128,896]{1,0:T(8,128)(2,1)S(1)}, u32[]{:S(2)}, u32[]{:S(2)}) collective-permute-start(bf16[128,896]{1,0:T(8,128)(2,1)S(1)} %slice.92), channel_id=1, source_target_pairs={{0,2},{1,3},{2,0},{3,1},{4,6},{5,7},{6,4},{7,5},{8,10},{9,11},{10,... | collective-permute-start | bytes 688136 | tf_op jit(solution)/shard_map/ppermute | solution.py:26
  55.5 1.3 %collective-permute-start.24 = (bf16[1,2,128,128]{3,2,1,0:T(8,128)(2,1)S(1)}, bf16[1,2,128,128]{3,2,1,0:T(8,128)(2,1)S(1)}, u32[]{:S(2)}, u32[]{:S(2)}) collective-permute-start(bf16[1,2,128,128]{3,2,1,0:T(8,128)(2,1)S(1)} %get-tuple-element.107), channel_id=1, source_target_pairs={{0,1},{1,0},{2,3},{3,2},{4,5},{5,4},{6,7},{7,6},{8,9},{9,8},{10,11... | collective-permute-start | bytes 196616 | tf_op jit(solution)/shard_map/ppermute | solution.py:26
  (9 other events, 8.6 us)

commit v4 on v3

v4 whole, which is shorter than its diff:
```python
import functools

import jax
import jax.numpy as jnp
from jax import lax
from jax.experimental import pallas as pl
from jax.experimental.pallas import tpu as pltpu
from jax.sharding import PartitionSpec as P

HEAD_SIZE = 128
HEADS = 16
SPAN = 64
NLEN = 64
READS = 2

NT = (((1,), (1,)), ((), ()))
TN = (((0,), (0,)), ((), ()))
EXTRA = 16
SMALL_BYTES = 4 << 20


def vmem_bytes(rows):
    return (3 << 20) + rows * (13 << 10)


def xor_send(value, axis, size, bit):
    return lax.ppermute(value, axis, [(i, i ^ bit) for i in range(size)])


def bit_reverse(index, bits):
    result = index * 0
    for i in range(bits):
        result = result + (((index >> i) & 1) << (bits - 1 - i))
    return result


def bundles(seq_size, item, dtype):
    sizes = [1] + [1 << b for b in range(seq_size.bit_length() - 1)]
    return [jax.ShapeDtypeStruct((size, *item), dtype) for size in sizes]


def item_of(refs, k):
    return refs[k.bit_length()].at[k - ((1 << k.bit_length()) >> 1)]


def cross(arrays, seq_size, top):
    return [*arrays[:top], xor_send(arrays[top], "seq", seq_size, 1 << (top - 1)), *arrays[top + 1 :]]


def forward(arrays, seq_size):
    top = len(arrays) - 1
    waiting = {b: [(0, array)] for b, array in enumerate(arrays[1:])}
    found = {0: (arrays[0], 0)}
    for b in reversed(range(top)):
        for origin, array in waiting[b]:
            arrived = array if b == top - 1 else xor_send(array, "seq", seq_size, 1 << b)
            origin = origin | (1 << b)
            found[origin] = (arrived, 0)
            for c in range(b):
                waiting[c].append((origin, arrived[1 << c : 2 << c]))
    return [found[j] for j in range(seq_size)]


def exchange(arrays, seq_size):
    return forward(cross(arrays, seq_size, len(arrays) - 1), seq_size)


def operands_of(items):
    arrays = []
    places = []
    for array, index in items:
        at = [array is known for known in arrays]
        if True not in at:
            at.append(True)
            arrays.append(array)
        places.append((at.index(True), index))
    return arrays, places


def pack_body(seq_size, groups, meta, ids, slots, queries, grad_out, *refs):
    held, sems = refs[-2], refs[-1]
    refs = refs[:-2]
    own, first = meta[0], meta[1]
    tokens = queries.shape[1]
    half = tokens // 2
    copies = []
    for part in range(2):
        for which, source in enumerate((queries, grad_out)):
            rows = pl.ds(part * half, half)
            copy = pltpu.make_async_copy(
                source.at[0, rows], held.at[which, rows], sems.at[2 * part + which]
            )
            copy.start()
            copies.append(copy)
    each = len(refs) // len(groups)
    spans = ids.shape[1]
    lanes = lax.broadcasted_iota(jnp.int32, (EXTRA, refs[0].shape[2]), 1)
    positions = jnp.zeros(lanes.shape, jnp.int32)
    for i in range(spans * READS):
        positions = jnp.where(lanes == i, slots[0, ids[0, i // READS, i % READS]], positions)
    positions = positions.astype(jnp.float32).astype(jnp.bfloat16)
    for k in range(seq_size):
        item_of(refs[:each], k)[2 * tokens :, :] = positions
    for part in range(2):
        for which in range(2):
            copies[2 * part + which].wait()
        rows = slice(part * half, (part + 1) * half)
        for g, heads in enumerate(groups):
            arrays = refs[g * each : (g + 1) * each]
            for k in range(seq_size):
                piece = item_of(arrays, k)
                for i, r in enumerate(heads):
                    column = pl.multiple_of(((first ^ r) * seq_size + (own ^ k)) * HEAD_SIZE, HEAD_SIZE)
                    place = slice(i * HEAD_SIZE, (i + 1) * HEAD_SIZE)
                    for which in range(2):
                        target = slice(which * tokens + rows.start, which * tokens + rows.stop)
                        piece[target, place] = held[which, rows, pl.ds(column, HEAD_SIZE)]


def pack(meta, neighbour_ids, slot_map, queries, grad_out, groups, seq_size):
    tokens, columns = queries.shape[1:]
    smem = pl.BlockSpec(memory_space=pltpu.SMEM)
    hbm = pl.BlockSpec(memory_space=pltpu.HBM)
    out_shape = []
    for g, heads in enumerate(groups):
        rows = 2 * tokens + (EXTRA if g == 0 else 0)
        out_shape += bundles(seq_size, (rows, len(heads) * HEAD_SIZE), jnp.bfloat16)
    outs = pl.pallas_call(
        functools.partial(pack_body, seq_size, groups),
        out_shape=out_shape,
        in_specs=[smem] * 3 + [hbm] * 2,
        out_specs=[pl.BlockSpec(memory_space=pltpu.VMEM)] * len(out_shape),
        scratch_shapes=[
            pltpu.VMEM((2, tokens, columns), jnp.bfloat16),
            pltpu.SemaphoreType.DMA((4,)),
        ],
        compiler_params=pltpu.CompilerParams(vmem_limit_bytes=SMALL_BYTES),
        cost_estimate=pl.CostEstimate(flops=0, bytes_accessed=0, transcendentals=0),
        name="pack",
    )(meta, neighbour_ids, slot_map, queries, grad_out)
    each = len(outs) // len(groups)
    return [outs[g * each : (g + 1) * each] for g in range(len(groups))]


def relative_positions(pieces, own, per_owner, tokens):
    bits = len(pieces).bit_length() - 1
    shift = per_owner.bit_length() - 1
    rows = [piece[2 * tokens : 2 * tokens + 8, :HEAD_SIZE] for piece in pieces]
    out = []
    for row in rows:
        position = row.astype(jnp.float32).astype(jnp.int32)
        owner = bit_reverse((position >> shift) ^ own, bits)
        out.append((owner << shift) + (position & (per_owner - 1)))
    return out


def attention_body(seq_size, spans, takes, places, arrays, per_owner, finds, has_prior, last, *refs):
    count = len(takes)
    meta, refs = refs[0], refs[1:]
    table, refs = (None, refs) if finds else (refs[0], refs[1:])
    stored, refs = refs[:seq_size], refs[seq_size:]
    weights, refs = refs[: 2 * count], refs[2 * count :]
    pieces, refs = refs[:arrays], refs[arrays:]
    pieces = [pieces[at].at[index] for at, index in places]
    prior, refs = (refs[0], refs[1:]) if has_prior else (None, refs)
    levels = seq_size.bit_length()
    outs, refs = refs[:levels], refs[levels:]
    grads, refs = (refs[:2], refs[2:]) if last else (refs[:1], refs[1:])
    if finds:
        found, refs = refs[0], refs[1:]
    enc, pair, kv, d_kv = refs[:4]
    block = stored[0].shape[0]
    rows = enc.shape[0]
    tokens = spans * SPAN
    scale = HEAD_SIZE ** (-0.5)
    keys_first = meta[2] == 1
    for i in range(seq_size):
        enc[i * block : (i + 1) * block] = stored[i][...]
    if finds:
        for k, rows_of in enumerate(relative_positions(pieces[:seq_size], meta[0], per_owner, tokens)):
            found[8 * k : 8 * k + 8, :] = rows_of
        table, sem = refs[4:]
        copy = pltpu.make_async_copy(found, table, sem)
        copy.start()
        copy.wait()
    spots = []
    for k in range(seq_size):
        for c in range(spans):
            starts = [table[8 * k, c * READS + r] * NLEN for r in range(READS)]
            spots.append((k, c, [pl.multiple_of(start, NLEN) for start in starts]))
    for i in range(count):
        first, second = weights[2 * i][...], weights[2 * i + 1][...]
        wide = slice(2 * i * HEAD_SIZE, 2 * (i + 1) * HEAD_SIZE)
        pair[:, 2 * i * HEAD_SIZE : (2 * i + 1) * HEAD_SIZE] = jnp.where(keys_first, first, second)
        pair[:, (2 * i + 1) * HEAD_SIZE : (2 * i + 2) * HEAD_SIZE] = jnp.where(keys_first, second, first)
        kv[...] = jnp.dot(enc[...], pair[:, wide], preferred_element_type=jnp.float32).astype(jnp.bfloat16)
        d_kv[:, wide] = jnp.zeros((rows, 2 * HEAD_SIZE), jnp.float32)
        columns = slice(i * HEAD_SIZE, (i + 1) * HEAD_SIZE)
        source, at = takes[i]
        taken = slice(at * HEAD_SIZE, (at + 1) * HEAD_SIZE)
        reads, queries, grad_rows, scores, d_probs = [], [], [], [], []
        for k, c, starts in spots:
            read = jnp.concatenate([kv[pl.ds(start, NLEN), :] for start in starts], axis=0)
            query = pieces[source * seq_size + k][c * SPAN : (c + 1) * SPAN, taken]
            grad = pieces[source * seq_size + k][tokens + c * SPAN : tokens + (c + 1) * SPAN, taken]
            reads.append((read[:, :HEAD_SIZE], read[:, HEAD_SIZE:]))
            queries.append(query)
            grad_rows.append(grad)
            scores.append(lax.dot_general(query, reads[-1][0], NT, preferred_element_type=jnp.float32))
            d_probs.append(lax.dot_general(grad, reads[-1][1], NT, preferred_element_type=jnp.float32))
        probs_low, d_scores = [], []
        for score, d_prob in zip(scores, d_probs):
            expos = jnp.exp(score * scale)
            probs = expos / jnp.sum(expos, axis=-1, keepdims=True)
            delta = jnp.sum(probs * d_prob, axis=-1, keepdims=True)
            probs_low.append(probs.astype(jnp.bfloat16))
            d_scores.append((probs * (d_prob - delta) * scale).astype(jnp.bfloat16))
        for n, (k, c, starts) in enumerate(spots):
            keys, values = reads[n]
            span = slice(c * SPAN, (c + 1) * SPAN)
            item_of(outs, k)[0, span, columns] = jnp.dot(
                probs_low[n], values, preferred_element_type=jnp.float32
            ).astype(jnp.bfloat16)
            item_of(outs, k)[1, span, columns] = jnp.dot(
                d_scores[n], keys, preferred_element_type=jnp.float32
            ).astype(jnp.bfloat16)
            d_keys = lax.dot_general(d_scores[n], queries[n], TN, preferred_element_type=jnp.float32)
            d_values = lax.dot_general(probs_low[n], grad_rows[n], TN, preferred_element_type=jnp.float32)
            both = jnp.concatenate([d_keys, d_values], axis=1)
            for r, start in enumerate(starts):
                d_kv[pl.ds(start, NLEN), wide] += both[r * NLEN : (r + 1) * NLEN]
    half = rows // 2
    for part in range(2):
        place = slice(part * half, (part + 1) * half)
        term = lax.dot_general(
            d_kv[place, :].astype(jnp.bfloat16), pair[...], NT, preferred_element_type=jnp.float32
        )
        if has_prior:
            term = term + prior[place, :].astype(jnp.float32)
        if last:
            grads[part][...] = term.astype(grads[part].dtype)
        else:
            grads[0][place, :] = term.astype(grads[0].dtype)


def attention(meta, table, stored, weights, takes, spans, per_owner, prior, last):
    seq_size = len(stored)
    sources = []
    for source, _ in takes:
        if not any(source is known for known in sources):
            sources.append(source)
    takes = [([source is known for known in sources].index(True), at) for source, at in takes]
    arrays, places = operands_of([item for source in sources for item in source])
    block, width = stored[0].shape
    rows = seq_size * block
    count = len(weights) // 2
    prior = [] if prior is None else [prior]
    vmem = pl.BlockSpec(memory_space=pltpu.VMEM)
    operands = [*stored, *weights, *arrays, *prior]
    finds = table is None
    scalars = [meta] if finds else [meta, table]
    table_shape = (8 * seq_size, HEAD_SIZE)
    out_shape = bundles(seq_size, (2, spans * SPAN, count * HEAD_SIZE), jnp.bfloat16)
    levels = len(out_shape)
    if last:
        out_shape.append(jax.ShapeDtypeStruct((rows // 2, width), jnp.float32))
        out_shape.append(jax.ShapeDtypeStruct((rows // 2, width), jnp.bfloat16))
    else:
        out_shape.append(jax.ShapeDtypeStruct((rows, width), jnp.bfloat16))
    grads = len(out_shape) - levels
    scratch = [
        pltpu.VMEM((rows, width), jnp.bfloat16),
        pltpu.VMEM((width, 2 * count * HEAD_SIZE), jnp.bfloat16),
        pltpu.VMEM((rows, 2 * HEAD_SIZE), jnp.bfloat16),
        pltpu.VMEM((rows, 2 * count * HEAD_SIZE), jnp.float32),
    ]
    if finds:
        out_shape.append(jax.ShapeDtypeStruct(table_shape, jnp.int32))
        scratch += [pltpu.SMEM(table_shape, jnp.int32), pltpu.SemaphoreType.DMA]
    outs = pl.pallas_call(
        functools.partial(
            attention_body, seq_size, spans, takes, places, len(arrays), per_owner, finds, len(prior), last
        ),
        out_shape=out_shape,
        in_specs=[pl.BlockSpec(memory_space=pltpu.SMEM)] * len(scalars) + [vmem] * len(operands),
        out_specs=[vmem] * len(out_shape),
        scratch_shapes=scratch,
        compiler_params=pltpu.CompilerParams(vmem_limit_bytes=vmem_bytes(rows)),
        cost_estimate=pl.CostEstimate(
            flops=0, bytes_accessed=0, transcendentals=0
        ),
        name="attention",
    )(*scalars, *operands)
    return outs[:levels], outs[levels : levels + grads], outs[-1] if finds else table


def unpack_body(seq_size, groups, places, meta, *refs):
    attended, grad_queries = refs[-2:]
    own, first = meta[0], meta[1]
    for g, heads in enumerate(groups):
        for k in range(seq_size):
            at, index = places[g * seq_size + k]
            for i, r in enumerate(heads):
                column = pl.multiple_of(((first ^ r) * seq_size + (own ^ k)) * HEAD_SIZE, HEAD_SIZE)
                place = slice(i * HEAD_SIZE, (i + 1) * HEAD_SIZE)
                attended[0, :, pl.ds(column, HEAD_SIZE)] = refs[at][index, 0, :, place]
                grad_queries[0, :, pl.ds(column, HEAD_SIZE)] = refs[at][index, 1, :, place]


def unpack(meta, items, groups, seq_size):
    arrays, places = operands_of(items)
    tokens = arrays[0].shape[2]
    shape = jax.ShapeDtypeStruct((1, tokens, HEADS * HEAD_SIZE), jnp.bfloat16)
    vmem = pl.BlockSpec(memory_space=pltpu.VMEM)
    return pl.pallas_call(
        functools.partial(unpack_body, seq_size, groups, places),
        out_shape=[shape, shape],
        in_specs=[pl.BlockSpec(memory_space=pltpu.SMEM)] + [vmem] * len(arrays),
        out_specs=[vmem, vmem],
        compiler_params=pltpu.CompilerParams(vmem_limit_bytes=SMALL_BYTES),
        cost_estimate=pl.CostEstimate(flops=0, bytes_accessed=0, transcendentals=0),
        name="unpack",
    )(meta, *arrays)


def weight_slice(kv_weight, column):
    return lax.dynamic_slice_in_dim(kv_weight, column, HEAD_SIZE, axis=1)


def whole_weights(kv_weight, own, seq_size):
    whole = lax.all_gather(kv_weight, "dp", axis=1, tiled=True)
    pairs = []
    for r in range(HEADS // seq_size):
        column = (r * seq_size + own) * HEAD_SIZE
        pairs.append((weight_slice(whole, column), weight_slice(whole, column + HEADS * HEAD_SIZE)))
    return pairs


def tie(*values):
    return lax.optimization_barrier(values)


def per_device(dp_size, seq_size, queries, grad_out, encoded, kv_weight, neighbour_ids, slot_map):
    own = lax.axis_index("seq")
    place = lax.axis_index("dp")
    bits = seq_size.bit_length() - 1
    per_owner = encoded.shape[1]
    spans = neighbour_ids.shape[1]
    tokens = queries.shape[1]
    width = encoded.shape[3]
    pool_size = slot_map.shape[1]
    assert pool_size <= 256 and 1 << bits == seq_size and per_owner & (per_owner - 1) == 0
    split = dp_size == 8 and 2 * HEADS == dp_size * seq_size
    send = functools.partial(xor_send, axis="seq", size=seq_size)
    move = functools.partial(xor_send, axis="dp", size=dp_size)

    if split:
        first = place % (HEADS // seq_size)
        keys_first = (place < dp_size // 2).astype(jnp.int32)
        groups = [(0,), (1, 2), (3,)]
        packed = [(0,), (1, 2, 3)]
    else:
        first, keys_first = place * 0, place * 0 + 1
        groups = packed = [tuple(range(HEADS // seq_size))]

    head_meta = jnp.stack([own, first, keys_first, place])
    pieces = pack(head_meta, neighbour_ids, slot_map, queries, grad_out, packed, seq_size)
    stored = [encoded[0].reshape(per_owner * NLEN, width)]
    if not split:
        for level in range(bits - 1, -1, -1):
            stored = stored + [send(rows, bit=1 << level) for rows in stored]
    if split:
        mine = weight_slice(kv_weight, own * HEAD_SIZE)
        stored = stored + [send(stored[0], bit=2)]
        stored = stored + [send(rows, bit=1) for rows in stored]
        early = cross(pieces[0], seq_size, bits)
        far, near, side, stored, early = tie(
            move(mine, bit=4), move(mine, bit=2), move(mine, bit=1), stored, early
        )
        near_far, side_far = move(far, bit=2), move(far, bit=1)
        early = forward(early, seq_size)
        late = cross(pieces[1], seq_size, bits)
        attend = functools.partial(attention, head_meta, spans=spans, per_owner=per_owner)
        outs, (grads,), table = attend(
            None, stored, [mine, far], [(early, 0)], prior=None, last=False
        )
        parts_a = cross(outs, seq_size, bits)
        near_far, side_far, side, near, late, grads = tie(near_far, side_far, side, near, late, grads)
        side_near_far, side_near = move(near_far, bit=1), move(side, bit=2)
        late = forward(late, seq_size)
        outs, (grads,), _ = attend(
            table, stored, [side, side_far, near, near_far], [(late, 0), (late, 1)], prior=grads, last=False
        )
        parts_b = cross(outs, seq_size, bits)
        grads, parts_a = tie(grads, parts_a)
        outs, grads, _ = attend(
            table, stored, [side_near, side_near_far], [(late, 2)], prior=grads, last=True
        )
        parts_b, parts_c = tie(parts_b, cross(outs, seq_size, bits))
        items = [item for parts in (parts_a, parts_b, parts_c) for item in forward(parts, seq_size)]
    else:
        weights = [block for pair in whole_weights(kv_weight, own, seq_size) for block in pair]
        early = exchange(pieces[0], seq_size)
        takes = [(early, i) for i in range(HEADS // seq_size)]
        outs, grads, _ = attention(head_meta, None, stored, weights, takes, spans, per_owner, None, True)
        items = exchange(outs, seq_size)
    total, leaving = grads
    for level in range(bits):
        total = total + send(leaving, bit=1 << level).astype(jnp.float32)
        half = total.shape[0] // 2
        if level < bits - 1:
            total, leaving = total[:half], total[half:].astype(jnp.bfloat16)
    attended, grad_queries = unpack(head_meta, items, groups, seq_size)
    return attended, grad_queries, total.reshape(1, per_owner, NLEN, width)


def solution(mesh):
    in_specs = (
        P("dp", "seq", None),
        P("dp", "seq", None),
        P("dp", "seq", None, None),
        P(None, "dp"),
        P("dp", "seq", None),
        P("dp", None),
    )
    out_specs = (P("dp", "seq", None), P("dp", "seq", None), P("dp", "seq", None, None))
    return jax.shard_map(
        functools.partial(per_device, mesh.shape["dp"], mesh.shape["seq"]),
        mesh=mesh,
        in_specs=in_specs,
        out_specs=out_specs,
        check_vma=False,
    )
```

time: 62 us -> 58.8 us (0.948)
  local copies, waits for them, and re-layouts: 7.35 us -> 3.97 us
  Pallas kernels: 12.7 us -> 14.2 us
  waiting for transfers between devices: 18 us -> 17.2 us
    unnamed x28 -> x12, local copies, waits for them, and re-layouts: 5.98 us -> 3.86 us
    pallas_call x3, Pallas kernels: 10.1 us -> 11.5 us  [attention(): pl.pallas_call(functools.partial(attention_body, seq_size, spans, takes,...]
    squeeze x1 -> x0, local copies, waits for them, and re-layouts: 0.99 us -> none  [exchange(): found[origin] = arrived[0]]
    ppermute x27, waiting for transfers between devices: 18 us -> 17.2 us  [xor_send(): return lax.ppermute(value, axis, [(i, i ^ bit) for i in range(size)])]
  transfers between devices with their start and end apart: 27 -> 27, of which waited for: 11 -> 10; matrix products, arithmetic and copies ran while one was open for 2% -> 0% of each run, Pallas kernels for 19% -> 19%
where the time goes in v4:
time: 58.8 us; the launch traced here: 58.5 us
  starting transfers between devices  21.4 us (36%)
  waiting for transfers between devices  17.2 us (29%)
  Pallas kernels  14.2 us (24%)
  local copies, waits for them, and re-layouts  3.97 us (7%)
  other arithmetic  0.97 us (2%)
  between operations  0.8 us (1%)
    ppermute x27, starting transfers between devices, xor_send(): return lax.ppermute(value, axis, [(i, i ^ bit) for i in range(size)])  21.4 us
    ppermute x27, waiting for transfers between devices, xor_send(): return lax.ppermute(value, axis, [(i, i ^ bit) for i in range(size)])  17.2 us
    pallas_call x3, Pallas kernels, attention(): pl.pallas_call(functools.partial(attention_body, seq_size, spans, takes,...  11.5 us
    unnamed x12, local copies, waits for them, and re-layouts  3.86 us
    pallas_call x1, Pallas kernels, unpack(): pl.pallas_call(functools.partial(unpack_body, seq_size, groups, places),...  1.8 us
  transfers between devices with their start and end apart: 27, of which 10 were waited for; matrix products, arithmetic and copies ran while one was open for 0% of the time, Pallas kernels for 19%

profile of v4, /device:TPU:0, one launch (start us, length us, event | category | flops | bytes accessed | tf_op | source)
XLA Modules:
  0.0 58.5 jit_solution(1423354010579799459)
XLA Ops:
  0.7 1.2 %copy-done = bf16[896,512]{1,0:T(8,128)(2,1)S(1)} copy-done((bf16[896,512]{1,0:T(8,128)(2,1)S(1)}, bf16[896,512]{1,0:T(8,128)(2,1)}, u32[]{:S(2)}) %copy-start) | copy-done | bytes 917528
  1.9 4.1 %collective-permute-start = (bf16[896,128]{1,0:T(8,128)(2,1)S(1)}, bf16[896,128]{1,0:T(8,128)(2,1)S(1)}, u32[]{:S(2)}, u32[]{:S(2)}) collective-permute-start(bf16[896,128]{1,0:T(8,128)(2,1)S(1)} %constant_dynamic-slice_fusion.refs_5_), channel_id=1, source_target_pairs={{0,16},{4,20},{8,24},{12,28},{16,0},{20,4},{24,8},{28,12},{1,17},{... | collective-permute-start | bytes 688136 | tf_op jit(solution)/shard_map/ppermute | solution.py:27
  6.0 1.5 %collective-permute-start.3 = (bf16[128,896]{1,0:T(8,128)(2,1)S(1)}, bf16[128,896]{1,0:T(8,128)(2,1)S(1)}, u32[]{:S(2)}, u32[]{:S(2)}) collective-permute-start(bf16[128,896]{1,0:T(8,128)(2,1)S(1)} %bitcast.6), channel_id=1, source_target_pairs={{0,2},{1,3},{2,0},{3,1},{4,6},{5,7},{6,4},{7,5},{8,10},{9,11},{10,... | collective-permute-start | bytes 688136 | tf_op jit(solution)/shard_map/ppermute | solution.py:27
  7.5 0.6 %copy-done.4 = s32[1,2,2]{2,1,0:T(2,128)S(1)} copy-done((s32[1,2,2]{2,1,0:T(2,128)S(1)}, s32[1,2,2]{2,1,0:T(2,128)}, u32[]{:S(2)}) %copy-start.4) | copy-done | bytes 40
  8.1 1.0 %copy-done.2 = bf16[1,128,2048]{2,1,0:T(8,128)(2,1)S(1)} copy-done((bf16[1,128,2048]{2,1,0:T(8,128)(2,1)S(1)}, bf16[1,128,2048]{2,1,0:T(8,128)(2,1)}, u32[]{:S(2)}) %copy-start.2) | copy-done | bytes 524312
  9.2 1.0 %copy-done.3 = bf16[1,128,2048]{2,1,0:T(8,128)(2,1)S(1)} copy-done((bf16[1,128,2048]{2,1,0:T(8,128)(2,1)S(1)}, bf16[1,128,2048]{2,1,0:T(8,128)(2,1)}, u32[]{:S(2)}) %copy-start.3) | copy-done | bytes 524312
  10.2 1.0 %pack.1 = (bf16[1,272,128]{2,1,0:T(8,128)(2,1)S(1)}, bf16[1,272,128]{2,1,0:T(8,128)(2,1)S(1)}, bf16[2,272,128]{2,1,0:T(8,128)(2,1)S(1)}, bf16[1,256,384]{2,1,0:T...) custom-call(s32[4]{0:T(128)S(1)} %pad_add_fusion.meta.refs_0_, ...), custom_call_target="tpu_custom_call" | custom-call | tf_op jit(solution)/shard_map/pack/pallas_call | solution.py:128
  11.2 0.6 %collective-permute-start.6 = (bf16[2,272,128]{2,1,0:T(8,128)(2,1)S(1)}, bf16[2,272,128]{2,1,0:T(8,128)(2,1)S(1)}, u32[]{:S(2)}, u32[]{:S(2)}) collective-permute-start(bf16[2,272,128]{2,1,0:T(8,128)(2,1)S(1)} %get-tuple-element.55), channel_id=1, source_target_pairs={{0,2},{1,3},{2,0},{3,1},{4,6},{5,7},{6,4},{7,5},{8,10},{9,11},{10,... | collective-permute-start | bytes 417800 | tf_op jit(solution)/shard_map/ppermute | solution.py:27
  11.8 1.6 %collective-permute-start.1 = (bf16[896,128]{1,0:T(8,128)(2,1)S(1)}, bf16[896,128]{1,0:T(8,128)(2,1)S(1)}, u32[]{:S(2)}, u32[]{:S(2)}) collective-permute-start(bf16[896,128]{1,0:T(8,128)(2,1)S(1)} %constant_dynamic-slice_fusion.refs_5_), channel_id=1, source_target_pairs={{0,8},{4,12},{8,0},{12,4},{16,24},{20,28},{24,16},{28,20},{1,9},{5... | collective-permute-start | bytes 688136 | tf_op jit(solution)/shard_map/ppermute | solution.py:27
  13.4 1.5 %collective-permute-start.2 = (bf16[896,128]{1,0:T(8,128)(2,1)S(1)}, bf16[896,128]{1,0:T(8,128)(2,1)S(1)}, u32[]{:S(2)}, u32[]{:S(2)}) collective-permute-start(bf16[896,128]{1,0:T(8,128)(2,1)S(1)} %constant_dynamic-slice_fusion.refs_5_), channel_id=1, source_target_pairs={{0,4},{4,0},{8,12},{12,8},{16,20},{20,16},{24,28},{28,24},{1,5},{5... | collective-permute-start | bytes 688136 | tf_op jit(solution)/shard_map/ppermute | solution.py:27
  14.9 1.4 %collective-permute-done.6.refs_9_ = bf16[2,272,128]{2,1,0:T(8,128)(2,1)S(1)} collective-permute-done((bf16[2,272,128]{2,1,0:T(8,128)(2,1)S(1)}, bf16[2,272,128]{2,1,0:T(8,128)(2,1)S(1)}, u32[]{:S(2)}, u32[]{:S(2)}) %collective-permute-start.6) | collective-permute-done | bytes 139296 | tf_op jit(solution)/shard_map/ppermute | solution.py:27
  16.3 0.5 collective-permute-start.5
  16.8 1.3 %collective-permute-start.11 = (bf16[2,256,384]{2,1,0:T(8,128)(2,1)S(1)}, bf16[2,256,384]{2,1,0:T(8,128)(2,1)S(1)}, u32[]{:S(2)}, u32[]{:S(2)}) collective-permute-start(bf16[2,256,384]{2,1,0:T(8,128)(2,1)S(1)} %get-tuple-element.69), channel_id=1, source_target_pairs={{0,2},{1,3},{2,0},{3,1},{4,6},{5,7},{6,4},{7,5},{8,10},{9,11},{10,... | collective-permute-start | bytes 1179656 | tf_op jit(solution)/shard_map/ppermute | solution.py:27
  18.1 3.3 %collective-permute-done.1.refs_8_ = bf16[896,128]{1,0:T(8,128)(2,1)S(1)} collective-permute-done((bf16[896,128]{1,0:T(8,128)(2,1)S(1)}, bf16[896,128]{1,0:T(8,128)(2,1)S(1)}, u32[]{:S(2)}, u32[]{:S(2)}) %collective-permute-start.1) | collective-permute-done | bytes 229408 | tf_op jit(solution)/shard_map/ppermute | solution.py:27
  21.4 1.6 %collective-permute-start.10 = (bf16[896,128]{1,0:T(8,128)(2,1)S(1)}, bf16[896,128]{1,0:T(8,128)(2,1)S(1)}, u32[]{:S(2)}, u32[]{:S(2)}) collective-permute-start(bf16[896,128]{1,0:T(8,128)(2,1)S(1)} %collective-permute-done.refs_6_), channel_id=1, source_target_pairs={{0,4},{4,0},{8,12},{12,8},{16,20},{20,16},{24,28},{28,24},{1,5},{5... | collective-permute-start | bytes 688136 | tf_op jit(solution)/shard_map/ppermute | solution.py:27
  23.1 0.5 collective-permute-start.7
  23.6 0.7 %collective-permute-done.8.refs_10_ = bf16[1,272,128]{2,1,0:T(8,128)(2,1)S(1)} collective-permute-done((bf16[1,272,128]{2,1,0:T(8,128)(2,1)S(1)}, bf16[1,272,128]{2,1,0:T(8,128)(2,1)S(1)}, u32[]{:S(2)}, u32[]{:S(2)}) %collective-permute-start.8) | collective-permute-done | bytes 69664 | tf_op jit(solution)/shard_map/ppermute | solution.py:27
  24.5 3.5 %attention.3 = (bf16[1,2,128,128]{3,2,1,0:T(8,128)(2,1)S(1)}, bf16[1,2,128,128]{3,2,1,0:T(8,128)(2,1)S(1)}, bf16[2,2,128,128]{3,2,1,0:T(8,128)(2,1)S(1)}, bf16[512,896]{1,0:T(8,128)(2,1)S(1)}, s32[32,128]{1,0:T(8,128)S(1)}) custom-call(s32[4]{0:T(128)S(1)} %pad_add_fusion.meta.refs_0_, bf16[128,896]{1,0:T(8,128)(2,1)S(1)} %bitcast.8, ...), custom_call_target="tpu_custom_call" | custom-call | tf_op jit(solution)/shard_map/attention/pallas_call | solution.py:280
  28.1 0.9 %collective-permute-done.10.refs_7_ = bf16[896,128]{1,0:T(8,128)(2,1)S(1)} collective-permute-done((bf16[896,128]{1,0:T(8,128)(2,1)S(1)}, bf16[896,128]{1,0:T(8,128)(2,1)S(1)}, u32[]{:S(2)}, u32[]{:S(2)}) %collective-permute-start.10) | collective-permute-done | bytes 229408 | tf_op jit(solution)/shard_map/ppermute | solution.py:27
  29.0 1.3 %collective-permute-done.9.refs_9_ = bf16[896,128]{1,0:T(8,128)(2,1)S(1)} collective-permute-done((bf16[896,128]{1,0:T(8,128)(2,1)S(1)}, bf16[896,128]{1,0:T(8,128)(2,1)S(1)}, u32[]{:S(2)}, u32[]{:S(2)}) %collective-permute-start.9) | collective-permute-done | bytes 229408 | tf_op jit(solution)/shard_map/ppermute | solution.py:27
  31.6 1.5 %collective-permute-start.14 = (bf16[2,2,128,128]{3,2,1,0:T(8,128)(2,1)S(1)}, bf16[2,2,128,128]{3,2,1,0:T(8,128)(2,1)S(1)}, u32[]{:S(2)}, u32[]{:S(2)}) collective-permute-start(bf16[2,2,128,128]{3,2,1,0:T(8,128)(2,1)S(1)} %get-tuple-element.82), channel_id=1, source_target_pairs={{0,2},{1,3},{2,0},{3,1},{4,6},{5,7},{6,4},{7,5},{8,10},{9,11},{10,... | collective-permute-start | bytes 393224 | tf_op jit(solution)/shard_map/ppermute | solution.py:27
  33.2 4.9 %attention.4 = (bf16[1,2,128,256]{3,2,1,0:T(8,128)(2,1)S(1)}, bf16[1,2,128,256]{3,2,1,0:T(8,128)(2,1)S(1)}, bf16[2,2,128,256]{3,2,1,0:T(8,128)(2,1)S(1)}, bf16[512,896]{1,0:T(8,128)(2,1)S(1)}) custom-call(s32[4]{0:T(128)S(1)} %pad_add_fusion.meta.refs_0_, s32[32,128]{1,0:T(8,128)S(1)} %get-tuple-element.64.refs_1_, bf16[128,896]{1,0:T(8,128)(2,1)S(1)} %bitcast.9, ...), custom_call_target="tpu_custom_call" | custom-call | tf_op jit(solution)/shard_map/attention/pallas_call | solution.py:280
  38.1 3.0 %attention.5 = (bf16[1,2,128,128]{3,2,1,0:T(8,128)(2,1)S(1)}, bf16[1,2,128,128]{3,2,1,0:T(8,128)(2,1)S(1)}, bf16[2,2,128,128]{3,2,1,0:T(8,128)(2,1)S(1)}, f32[256,896]{1,0:T(8,128)S(1)}, bf16[256,896]{1,0:T(8,128)(2,1)S(1)}) custom-call(s32[4]{0:T(128)S(1)} %pad_add_fusion.meta.refs_0_, s32[32,128]{1,0:T(8,128)S(1)} %get-tuple-element.64.refs_1_, ...), custom_call_target="tpu_custom_call" | custom-call | tf_op jit(solution)/shard_map/attention/pallas_call | solution.py:280
  41.2 1.4 %collective-permute-start.17 = (bf16[2,2,128,256]{3,2,1,0:T(8,128)(2,1)S(1)}, bf16[2,2,128,256]{3,2,1,0:T(8,128)(2,1)S(1)}, u32[]{:S(2)}, u32[]{:S(2)}) collective-permute-start(bf16[2,2,128,256]{3,2,1,0:T(8,128)(2,1)S(1)} %get-tuple-element.88), channel_id=1, source_target_pairs={{0,2},{1,3},{2,0},{3,1},{4,6},{5,7},{6,4},{7,5},{8,10},{9,11},{10,... | collective-permute-start | bytes 786440 | tf_op jit(solution)/shard_map/ppermute | solution.py:27
  42.6 0.7 %collective-permute-start.20 = (bf16[2,2,128,128]{3,2,1,0:T(8,128)(2,1)S(1)}, bf16[2,2,128,128]{3,2,1,0:T(8,128)(2,1)S(1)}, u32[]{:S(2)}, u32[]{:S(2)}) collective-permute-start(bf16[2,2,128,128]{3,2,1,0:T(8,128)(2,1)S(1)} %get-tuple-element.92), channel_id=1, source_target_pairs={{0,2},{1,3},{2,0},{3,1},{4,6},{5,7},{6,4},{7,5},{8,10},{9,11},{10,... | collective-permute-start | bytes 393224 | tf_op jit(solution)/shard_map/ppermute | solution.py:27
  43.5 1.4 %collective-permute-start.26 = (bf16[128,896]{1,0:T(8,128)(2,1)S(1)}, bf16[128,896]{1,0:T(8,128)(2,1)S(1)}, u32[]{:S(2)}, u32[]{:S(2)}) collective-permute-start(bf16[128,896]{1,0:T(8,128)(2,1)S(1)} %slice.33), channel_id=1, source_target_pairs={{0,2},{1,3},{2,0},{3,1},{4,6},{5,7},{6,4},{7,5},{8,10},{9,11},{10,... | collective-permute-start | bytes 688136 | tf_op jit(solution)/shard_map/ppermute | solution.py:27
  44.9 0.5 collective-permute-start.15
  45.4 7.9 %collective-permute-done.20.refs_10_ = bf16[2,2,128,128]{3,2,1,0:T(8,128)(2,1)S(1)} collective-permute-done((bf16[2,2,128,128]{3,2,1,0:T(8,128)(2,1)S(1)}, bf16[2,2,128,128]{3,2,1,0:T(8,128)(2,1)S(1)}, u32[]{:S(2)}, u32[]{:S(2)}) %collective-permute-start.20) | collective-permute-done | bytes 131104 | tf_op jit(solution)/shard_map/ppermute | solution.py:27
  54.4 0.7 %collective-permute-done.24.refs_11_ = bf16[1,2,128,128]{3,2,1,0:T(8,128)(2,1)S(1)} collective-permute-done((bf16[1,2,128,128]{3,2,1,0:T(8,128)(2,1)S(1)}, bf16[1,2,128,128]{3,2,1,0:T(8,128)(2,1)S(1)}, u32[]{:S(2)}, u32[]{:S(2)}) %collective-permute-start.24) | collective-permute-done | bytes 65568 | tf_op jit(solution)/shard_map/ppermute | solution.py:27
  55.3 1.8 %unpack.1 = (bf16[1,128,2048]{2,1,0:T(8,128)(2,1)}, bf16[1,128,2048]{2,1,0:T(8,128)(2,1)}) custom-call(s32[4]{0:T(128)S(1)} %pad_add_fusion.meta.refs_0_, bf16[1,2,128,128]{3,2,1,0:T(8,128)(2,1)S(1)} %get-tuple-element.83.refs_0_, bf16[1,2,128,128]{3,2,1,0:T(8,128)(2,1)S(1)} %collective-permute-done.15.refs_1_, ...), custom_call_target="tpu_custom_call" | custom-call | tf_op jit(solution)/shard_map/unpack/pallas_call | solution.py:315
  57.1 0.6 collective-permute-done.26
  57.7 0.8 %slice_add_fusion = f32[128,896]{1,0:T(8,128)} fusion(f32[256,896]{1,0:T(8,128)S(1)} %convert_add_fusion, bf16[128,896]{1,0:T(8,128)(2,1)S(1)} %collective-permute-done.26), kind=kLoop, calls=%fused_computation.2 | loop fusion | flops 229376 | bytes 1146880 | tf_op jit(solution)/shard_map/add | solution.py:409
  (49 shorter events, 3.2 us)
Async XLA Ops:
  0.6 1.2 %copy-start = (bf16[896,512]{1,0:T(8,128)(2,1)S(1)}, bf16[896,512]{1,0:T(8,128)(2,1)}, u32[]{:S(2)}) copy-start(bf16[896,512]{1,0:T(8,128)(2,1)} %param.9) | copy-start | bytes 2752516
  1.8 4.1 %copy-start.1 = (bf16[1,2,64,896]{3,2,1,0:T(8,128)(2,1)S(1)}, bf16[1,2,64,896]{3,2,1,0:T(8,128)(2,1)}, u32[]{:S(2)}) copy-start(bf16[1,2,64,896]{3,2,1,0:T(8,128)(2,1)} %param.8) | copy-start | bytes 688132
  1.9 15.0 %collective-permute-start = (bf16[896,128]{1,0:T(8,128)(2,1)S(1)}, bf16[896,128]{1,0:T(8,128)(2,1)S(1)}, u32[]{:S(2)}, u32[]{:S(2)}) collective-permute-start(bf16[896,128]{1,0:T(8,128)(2,1)S(1)} %constant_dynamic-slice_fusion.refs_5_), channel_id=1, source_target_pairs={{0,16},{4,20},{8,24},{12,28},{16,0},{20,4},{24,8},{28,12},{1,17},{... | collective-permute-start | bytes 688136 | tf_op jit(solution)/shard_map/ppermute | solution.py:27
  6.0 10.4 %collective-permute-start.3 = (bf16[128,896]{1,0:T(8,128)(2,1)S(1)}, bf16[128,896]{1,0:T(8,128)(2,1)S(1)}, u32[]{:S(2)}, u32[]{:S(2)}) collective-permute-start(bf16[128,896]{1,0:T(8,128)(2,1)S(1)} %bitcast.6), channel_id=1, source_target_pairs={{0,2},{1,3},{2,0},{3,1},{4,6},{5,7},{6,4},{7,5},{8,10},{9,11},{10,... | collective-permute-start | bytes 688136 | tf_op jit(solution)/shard_map/ppermute | solution.py:27
  7.5 0.7 %copy-start.5 = (s32[1,8]{1,0:T(1,128)S(1)}, s32[1,8]{1,0:T(1,128)}, u32[]{:S(2)}) copy-start(s32[1,8]{1,0:T(1,128)} %slots.1) | copy-start | bytes 100
  8.1 1.0 %copy-start.2 = (bf16[1,128,2048]{2,1,0:T(8,128)(2,1)S(1)}, bf16[1,128,2048]{2,1,0:T(8,128)(2,1)}, u32[]{:S(2)}) copy-start(bf16[1,128,2048]{2,1,0:T(8,128)(2,1)} %queries.1) | copy-start | bytes 1572868
  9.2 1.0 %copy-start.3 = (bf16[1,128,2048]{2,1,0:T(8,128)(2,1)S(1)}, bf16[1,128,2048]{2,1,0:T(8,128)(2,1)}, u32[]{:S(2)}) copy-start(bf16[1,128,2048]{2,1,0:T(8,128)(2,1)} %grad_out.1) | copy-start | bytes 1572868
  11.2 5.1 %collective-permute-start.6 = (bf16[2,272,128]{2,1,0:T(8,128)(2,1)S(1)}, bf16[2,272,128]{2,1,0:T(8,128)(2,1)S(1)}, u32[]{:S(2)}, u32[]{:S(2)}) collective-permute-start(bf16[2,272,128]{2,1,0:T(8,128)(2,1)S(1)} %get-tuple-element.55), channel_id=1, source_target_pairs={{0,2},{1,3},{2,0},{3,1},{4,6},{5,7},{6,4},{7,5},{8,10},{9,11},{10,... | collective-permute-start | bytes 417800 | tf_op jit(solution)/shard_map/ppermute | solution.py:27
  11.8 9.6 %collective-permute-start.1 = (bf16[896,128]{1,0:T(8,128)(2,1)S(1)}, bf16[896,128]{1,0:T(8,128)(2,1)S(1)}, u32[]{:S(2)}, u32[]{:S(2)}) collective-permute-start(bf16[896,128]{1,0:T(8,128)(2,1)S(1)} %constant_dynamic-slice_fusion.refs_5_), channel_id=1, source_target_pairs={{0,8},{4,12},{8,0},{12,4},{16,24},{20,28},{24,16},{28,20},{1,9},{5... | collective-permute-start | bytes 688136 | tf_op jit(solution)/shard_map/ppermute | solution.py:27
  13.4 8.0 %collective-permute-start.2 = (bf16[896,128]{1,0:T(8,128)(2,1)S(1)}, bf16[896,128]{1,0:T(8,128)(2,1)S(1)}, u32[]{:S(2)}, u32[]{:S(2)}) collective-permute-start(bf16[896,128]{1,0:T(8,128)(2,1)S(1)} %constant_dynamic-slice_fusion.refs_5_), channel_id=1, source_target_pairs={{0,4},{4,0},{8,12},{12,8},{16,20},{20,16},{24,28},{28,24},{1,5},{5... | collective-permute-start | bytes 688136 | tf_op jit(solution)/shard_map/ppermute | solution.py:27
  16.3 5.1 %collective-permute-start.4 = (bf16[128,896]{1,0:T(8,128)(2,1)S(1)}, bf16[128,896]{1,0:T(8,128)(2,1)S(1)}, u32[]{:S(2)}, u32[]{:S(2)}) collective-permute-start(bf16[128,896]{1,0:T(8,128)(2,1)S(1)} %bitcast.7), channel_id=1, source_target_pairs={{0,1},{1,0},{2,3},{3,2},{4,5},{5,4},{6,7},{7,6},{8,9},{9,8},{10,11... | collective-permute-start | bytes 688136 | tf_op jit(solution)/shard_map/ppermute | solution.py:27
  16.3 5.1 %collective-permute-start.5 = (bf16[128,896]{1,0:T(8,128)(2,1)S(1)}, bf16[128,896]{1,0:T(8,128)(2,1)S(1)}, u32[]{:S(2)}, u32[]{:S(2)}) collective-permute-start(bf16[128,896]{1,0:T(8,128)(2,1)S(1)} %collective-permute-done.3.refs_2_.refs_3_), channel_id=1, source_target_pairs={{0,1},{1,0},{2,3},{3,2},{4,5},{5,4},{6,7},{7,6},{8,9},{9,8},{10,11... | collective-permute-start | bytes 688136 | tf_op jit(solution)/shard_map/ppermute | solution.py:27
  16.8 11.3 %collective-permute-start.11 = (bf16[2,256,384]{2,1,0:T(8,128)(2,1)S(1)}, bf16[2,256,384]{2,1,0:T(8,128)(2,1)S(1)}, u32[]{:S(2)}, u32[]{:S(2)}) collective-permute-start(bf16[2,256,384]{2,1,0:T(8,128)(2,1)S(1)} %get-tuple-element.69), channel_id=1, source_target_pairs={{0,2},{1,3},{2,0},{3,1},{4,6},{5,7},{6,4},{7,5},{8,10},{9,11},{10,... | collective-permute-start | bytes 1179656 | tf_op jit(solution)/shard_map/ppermute | solution.py:27
  21.4 7.6 %collective-permute-start.10 = (bf16[896,128]{1,0:T(8,128)(2,1)S(1)}, bf16[896,128]{1,0:T(8,128)(2,1)S(1)}, u32[]{:S(2)}, u32[]{:S(2)}) collective-permute-start(bf16[896,128]{1,0:T(8,128)(2,1)S(1)} %collective-permute-done.refs_6_), channel_id=1, source_target_pairs={{0,4},{4,0},{8,12},{12,8},{16,20},{20,16},{24,28},{28,24},{1,5},{5... | collective-permute-start | bytes 688136 | tf_op jit(solution)/shard_map/ppermute | solution.py:27
  23.0 7.2 %collective-permute-start.9 = (bf16[896,128]{1,0:T(8,128)(2,1)S(1)}, bf16[896,128]{1,0:T(8,128)(2,1)S(1)}, u32[]{:S(2)}, u32[]{:S(2)}) collective-permute-start(bf16[896,128]{1,0:T(8,128)(2,1)S(1)} %collective-permute-done.refs_6_), channel_id=1, source_target_pairs={{0,8},{4,12},{8,0},{12,4},{16,24},{20,28},{24,16},{28,20},{1,9},{5... | collective-permute-start | bytes 688136 | tf_op jit(solution)/shard_map/ppermute | solution.py:27
  23.0 1.3 %collective-permute-start.8 = (bf16[1,272,128]{2,1,0:T(8,128)(2,1)S(1)}, bf16[1,272,128]{2,1,0:T(8,128)(2,1)S(1)}, u32[]{:S(2)}, u32[]{:S(2)}) collective-permute-start(bf16[1,272,128]{2,1,0:T(8,128)(2,1)S(1)} %slice.22), channel_id=1, source_target_pairs={{0,1},{1,0},{2,3},{3,2},{4,5},{5,4},{6,7},{7,6},{8,9},{9,8},{10,11... | collective-permute-start | bytes 208904 | tf_op jit(solution)/shard_map/ppermute | solution.py:27
  23.1 1.4 %collective-permute-start.7 = (bf16[1,272,128]{2,1,0:T(8,128)(2,1)S(1)}, bf16[1,272,128]{2,1,0:T(8,128)(2,1)S(1)}, u32[]{:S(2)}, u32[]{:S(2)}) collective-permute-start(bf16[1,272,128]{2,1,0:T(8,128)(2,1)S(1)} %get-tuple-element.62), channel_id=1, source_target_pairs={{0,1},{1,0},{2,3},{3,2},{4,5},{5,4},{6,7},{7,6},{8,9},{9,8},{10,11... | collective-permute-start | bytes 208904 | tf_op jit(solution)/shard_map/ppermute | solution.py:27
  30.3 7.8 %collective-permute-start.18 = (bf16[896,128]{1,0:T(8,128)(2,1)S(1)}, bf16[896,128]{1,0:T(8,128)(2,1)S(1)}, u32[]{:S(2)}, u32[]{:S(2)}) collective-permute-start(bf16[896,128]{1,0:T(8,128)(2,1)S(1)} %collective-permute-done.2.refs_6_), channel_id=1, source_target_pairs={{0,8},{4,12},{8,0},{12,4},{16,24},{20,28},{24,16},{28,20},{1,9},{5... | collective-permute-start | bytes 688136 | tf_op jit(solution)/shard_map/ppermute | solution.py:27
  30.6 7.5 %collective-permute-start.19 = (bf16[896,128]{1,0:T(8,128)(2,1)S(1)}, bf16[896,128]{1,0:T(8,128)(2,1)S(1)}, u32[]{:S(2)}, u32[]{:S(2)}) collective-permute-start(bf16[896,128]{1,0:T(8,128)(2,1)S(1)} %collective-permute-done.9.refs_9_), channel_id=1, source_target_pairs={{0,4},{4,0},{8,12},{12,8},{16,20},{20,16},{24,28},{28,24},{1,5},{5... | collective-permute-start | bytes 688136 | tf_op jit(solution)/shard_map/ppermute | solution.py:27
  31.0 2.1 %collective-permute-start.13 = (bf16[1,256,384]{2,1,0:T(8,128)(2,1)S(1)}, bf16[1,256,384]{2,1,0:T(8,128)(2,1)S(1)}, u32[]{:S(2)}, u32[]{:S(2)}) collective-permute-start(bf16[1,256,384]{2,1,0:T(8,128)(2,1)S(1)} %slice.23), channel_id=1, source_target_pairs={{0,1},{1,0},{2,3},{3,2},{4,5},{5,4},{6,7},{7,6},{8,9},{9,8},{10,11... | collective-permute-start | bytes 589832 | tf_op jit(solution)/shard_map/ppermute | solution.py:27
  31.1 2.0 %collective-permute-start.12 = (bf16[1,256,384]{2,1,0:T(8,128)(2,1)S(1)}, bf16[1,256,384]{2,1,0:T(8,128)(2,1)S(1)}, u32[]{:S(2)}, u32[]{:S(2)}) collective-permute-start(bf16[1,256,384]{2,1,0:T(8,128)(2,1)S(1)} %get-tuple-element.76), channel_id=1, source_target_pairs={{0,1},{1,0},{2,3},{3,2},{4,5},{5,4},{6,7},{7,6},{8,9},{9,8},{10,11... | collective-permute-start | bytes 589832 | tf_op jit(solution)/shard_map/ppermute | solution.py:27
  31.6 6.5 %collective-permute-start.14 = (bf16[2,2,128,128]{3,2,1,0:T(8,128)(2,1)S(1)}, bf16[2,2,128,128]{3,2,1,0:T(8,128)(2,1)S(1)}, u32[]{:S(2)}, u32[]{:S(2)}) collective-permute-start(bf16[2,2,128,128]{3,2,1,0:T(8,128)(2,1)S(1)} %get-tuple-element.82), channel_id=1, source_target_pairs={{0,2},{1,3},{2,0},{3,1},{4,6},{5,7},{6,4},{7,5},{8,10},{9,11},{10,... | collective-permute-start | bytes 393224 | tf_op jit(solution)/shard_map/ppermute | solution.py:27
  41.2 2.2 %collective-permute-start.25 = (bf16[256,896]{1,0:T(8,128)(2,1)S(1)}, bf16[256,896]{1,0:T(8,128)(2,1)S(1)}, u32[]{:S(2)}, u32[]{:S(2)}) collective-permute-start(bf16[256,896]{1,0:T(8,128)(2,1)S(1)} %get-tuple-element.102), channel_id=1, source_target_pairs={{0,1},{1,0},{2,3},{3,2},{4,5},{5,4},{6,7},{7,6},{8,9},{9,8},{10,11... | collective-permute-start | bytes 1376264 | tf_op jit(solution)/shard_map/ppermute | solution.py:27
  41.2 12.0 %collective-permute-start.17 = (bf16[2,2,128,256]{3,2,1,0:T(8,128)(2,1)S(1)}, bf16[2,2,128,256]{3,2,1,0:T(8,128)(2,1)S(1)}, u32[]{:S(2)}, u32[]{:S(2)}) collective-permute-start(bf16[2,2,128,256]{3,2,1,0:T(8,128)(2,1)S(1)} %get-tuple-element.88), channel_id=1, source_target_pairs={{0,2},{1,3},{2,0},{3,1},{4,6},{5,7},{6,4},{7,5},{8,10},{9,11},{10,... | collective-permute-start | bytes 786440 | tf_op jit(solution)/shard_map/ppermute | solution.py:27
  42.6 10.6 %collective-permute-start.20 = (bf16[2,2,128,128]{3,2,1,0:T(8,128)(2,1)S(1)}, bf16[2,2,128,128]{3,2,1,0:T(8,128)(2,1)S(1)}, u32[]{:S(2)}, u32[]{:S(2)}) collective-permute-start(bf16[2,2,128,128]{3,2,1,0:T(8,128)(2,1)S(1)} %get-tuple-element.92), channel_id=1, source_target_pairs={{0,2},{1,3},{2,0},{3,1},{4,6},{5,7},{6,4},{7,5},{8,10},{9,11},{10,... | collective-permute-start | bytes 393224 | tf_op jit(solution)/shard_map/ppermute | solution.py:27
  43.5 14.2 %collective-permute-start.26 = (bf16[128,896]{1,0:T(8,128)(2,1)S(1)}, bf16[128,896]{1,0:T(8,128)(2,1)S(1)}, u32[]{:S(2)}, u32[]{:S(2)}) collective-permute-start(bf16[128,896]{1,0:T(8,128)(2,1)S(1)} %slice.33), channel_id=1, source_target_pairs={{0,2},{1,3},{2,0},{3,1},{4,6},{5,7},{6,4},{7,5},{8,10},{9,11},{10,... | collective-permute-start | bytes 688136 | tf_op jit(solution)/shard_map/ppermute | solution.py:27
  44.9 9.0 %collective-permute-start.16 = (bf16[1,2,128,128]{3,2,1,0:T(8,128)(2,1)S(1)}, bf16[1,2,128,128]{3,2,1,0:T(8,128)(2,1)S(1)}, u32[]{:S(2)}, u32[]{:S(2)}) collective-permute-start(bf16[1,2,128,128]{3,2,1,0:T(8,128)(2,1)S(1)} %slice.24), channel_id=1, source_target_pairs={{0,1},{1,0},{2,3},{3,2},{4,5},{5,4},{6,7},{7,6},{8,9},{9,8},{10,11... | collective-permute-start | bytes 196616 | tf_op jit(solution)/shard_map/ppermute | solution.py:27
  44.9 9.1 %collective-permute-start.15 = (bf16[1,2,128,128]{3,2,1,0:T(8,128)(2,1)S(1)}, bf16[1,2,128,128]{3,2,1,0:T(8,128)(2,1)S(1)}, u32[]{:S(2)}, u32[]{:S(2)}) collective-permute-start(bf16[1,2,128,128]{3,2,1,0:T(8,128)(2,1)S(1)} %get-tuple-element.84), channel_id=1, source_target_pairs={{0,1},{1,0},{2,3},{3,2},{4,5},{5,4},{6,7},{7,6},{8,9},{9,8},{10,11... | collective-permute-start | bytes 196616 | tf_op jit(solution)/shard_map/ppermute | solution.py:27
  53.2 2.1 %collective-permute-start.22 = (bf16[1,2,128,256]{3,2,1,0:T(8,128)(2,1)S(1)}, bf16[1,2,128,256]{3,2,1,0:T(8,128)(2,1)S(1)}, u32[]{:S(2)}, u32[]{:S(2)}) collective-permute-start(bf16[1,2,128,256]{3,2,1,0:T(8,128)(2,1)S(1)} %slice.25), channel_id=1, source_target_pairs={{0,1},{1,0},{2,3},{3,2},{4,5},{5,4},{6,7},{7,6},{8,9},{9,8},{10,11... | collective-permute-start | bytes 393224 | tf_op jit(solution)/shard_map/ppermute | solution.py:27
  53.3 2.0 %collective-permute-start.21 = (bf16[1,2,128,256]{3,2,1,0:T(8,128)(2,1)S(1)}, bf16[1,2,128,256]{3,2,1,0:T(8,128)(2,1)S(1)}, u32[]{:S(2)}, u32[]{:S(2)}) collective-permute-start(bf16[1,2,128,256]{3,2,1,0:T(8,128)(2,1)S(1)} %get-tuple-element.94), channel_id=1, source_target_pairs={{0,1},{1,0},{2,3},{3,2},{4,5},{5,4},{6,7},{7,6},{8,9},{9,8},{10,11... | collective-permute-start | bytes 393224 | tf_op jit(solution)/shard_map/ppermute | solution.py:27
  53.8 1.3 %collective-permute-start.24 = (bf16[1,2,128,128]{3,2,1,0:T(8,128)(2,1)S(1)}, bf16[1,2,128,128]{3,2,1,0:T(8,128)(2,1)S(1)}, u32[]{:S(2)}, u32[]{:S(2)}) collective-permute-start(bf16[1,2,128,128]{3,2,1,0:T(8,128)(2,1)S(1)} %slice.26), channel_id=1, source_target_pairs={{0,1},{1,0},{2,3},{3,2},{4,5},{5,4},{6,7},{7,6},{8,9},{9,8},{10,11... | collective-permute-start | bytes 196616 | tf_op jit(solution)/shard_map/ppermute | solution.py:27
  54.0 1.3 %collective-permute-start.23 = (bf16[1,2,128,128]{3,2,1,0:T(8,128)(2,1)S(1)}, bf16[1,2,128,128]{3,2,1,0:T(8,128)(2,1)S(1)}, u32[]{:S(2)}, u32[]{:S(2)}) collective-permute-start(bf16[1,2,128,128]{3,2,1,0:T(8,128)(2,1)S(1)} %get-tuple-element.97), channel_id=1, source_target_pairs={{0,1},{1,0},{2,3},{3,2},{4,5},{5,4},{6,7},{7,6},{8,9},{9,8},{10,11... | collective-permute-start | bytes 196616 | tf_op jit(solution)/shard_map/ppermute | solution.py:27
  (1 other events, 0.7 us)

commit v5 on v4

--- a/solution.py
+++ b/solution.py
@@ -287,7 +287,7 @@
         scratch_shapes=scratch,
         compiler_params=pltpu.CompilerParams(vmem_limit_bytes=vmem_bytes(rows)),
         cost_estimate=pl.CostEstimate(
-            flops=0, bytes_accessed=0, transcendentals=0
+            flops=int(2.4e9) if last and len(prior) else 0, bytes_accessed=0, transcendentals=0
         ),
         name="attention",
     )(*scalars, *operands)
@@ -340,6 +340,17 @@
     return lax.optimization_barrier(values)
 
 
+def fold(total, arrived):
+    total = total + arrived.astype(jnp.float32)
+    half = total.shape[0] // 2
+    return total[:half], total[half:].astype(jnp.bfloat16)
+
+
+def tie_items(value, items):
+    tied = lax.optimization_barrier((value, [array for array, _ in items]))
+    return tied[0], [(array, index) for array, (_, index) in zip(tied[1], items)]
+
+
 def per_device(dp_size, seq_size, queries, grad_out, encoded, kv_weight, neighbour_ids, slot_map):
     own = lax.axis_index("seq")
     place = lax.axis_index("dp")
@@ -374,16 +385,16 @@
         stored = stored + [send(stored[0], bit=2)]
         stored = stored + [send(rows, bit=1) for rows in stored]
         early = cross(pieces[0], seq_size, bits)
-        far, near, side, stored, early = tie(
-            move(mine, bit=4), move(mine, bit=2), move(mine, bit=1), stored, early
-        )
-        near_far, side_far = move(far, bit=2), move(far, bit=1)
+        far, near, side, late = tie(move(mine, bit=4), move(mine, bit=2), move(mine, bit=1), pieces[1])
+        near_far = move(far, bit=2)
+        side_far = move(far, bit=1)
         early = forward(early, seq_size)
-        late = cross(pieces[1], seq_size, bits)
+        late = cross(late, seq_size, bits)
         attend = functools.partial(attention, head_meta, spans=spans, per_owner=per_owner)
         outs, (grads,), table = attend(
             None, stored, [mine, far], [(early, 0)], prior=None, last=False
         )
+        near_far, outs = tie(near_far, outs)
         parts_a = cross(outs, seq_size, bits)
         near_far, side_far, side, near, late, grads = tie(near_far, side_far, side, near, late, grads)
         side_near_far, side_near = move(near_far, bit=1), move(side, bit=2)
@@ -396,7 +407,9 @@
         outs, grads, _ = attend(
             table, stored, [side_near, side_near_far], [(late, 2)], prior=grads, last=True
         )
-        parts_b, parts_c = tie(parts_b, cross(outs, seq_size, bits))
+        parts_c = cross(outs, seq_size, bits)
+        grads, parts_b = tie(grads, parts_b)
+        total, leaving = fold(grads[0], send(grads[1], bit=1))
         items = [item for parts in (parts_a, parts_b, parts_c) for item in forward(parts, seq_size)]
     else:
         weights = [block for pair in whole_weights(kv_weight, own, seq_size) for block in pair]
@@ -404,12 +417,11 @@
         takes = [(early, i) for i in range(HEADS // seq_size)]
         outs, grads, _ = attention(head_meta, None, stored, weights, takes, spans, per_owner, None, True)
         items = exchange(outs, seq_size)
-    total, leaving = grads
-    for level in range(bits):
-        total = total + send(leaving, bit=1 << level).astype(jnp.float32)
-        half = total.shape[0] // 2
-        if level < bits - 1:
-            total, leaving = total[:half], total[half:].astype(jnp.bfloat16)
+    if not split:
+        total, leaving = grads
+        for level in range(bits - 1):
+            total, leaving = fold(total, send(leaving, bit=1 << level))
+    total = total + send(leaving, bit=1 << (bits - 1)).astype(jnp.float32)
     attended, grad_queries = unpack(head_meta, items, groups, seq_size)
     return attended, grad_queries, total.reshape(1, per_owner, NLEN, width)
 

time: 58.8 us -> 56.5 us (0.961)
  waiting for transfers between devices: 17.2 us -> 15.5 us
  starting transfers between devices: 21.4 us -> 20.8 us
    ppermute x27, waiting for transfers between devices: 17.2 us -> 15.5 us  [xor_send(): return lax.ppermute(value, axis, [(i, i ^ bit) for i in range(size)])]
  transfers between devices with their start and end apart: 27 -> 27, of which waited for: 10 -> 12; matrix products, arithmetic and copies ran while one was open for 0% -> 0% of each run, Pallas kernels for 19% -> 25%
where the time goes in v5:
time: 56.5 us; the launch traced here: 56.3 us
  starting transfers between devices  20.8 us (37%)
  waiting for transfers between devices  15.5 us (27%)
  Pallas kernels  14.2 us (25%)
  local copies, waits for them, and re-layouts  3.97 us (7%)
  other arithmetic  0.99 us (2%)
  between operations  0.76 us (1%)
    ppermute x27, starting transfers between devices, xor_send(): return lax.ppermute(value, axis, [(i, i ^ bit) for i in range(size)])  20.8 us
    ppermute x27, waiting for transfers between devices, xor_send(): return lax.ppermute(value, axis, [(i, i ^ bit) for i in range(size)])  15.5 us
    pallas_call x3, Pallas kernels, attention(): pl.pallas_call(functools.partial(attention_body, seq_size, spans, takes,...  11.5 us
    unnamed x12, local copies, waits for them, and re-layouts  3.86 us
    pallas_call x1, Pallas kernels, unpack(): pl.pallas_call(functools.partial(unpack_body, seq_size, groups, places),...  1.8 us
  transfers between devices with their start and end apart: 27, of which 12 were waited for; matrix products, arithmetic and copies ran while one was open for 0% of the time, Pallas kernels for 25%

profile of v5, /device:TPU:0, one launch (start us, length us, event | category | flops | bytes accessed | tf_op | source)
XLA Modules:
  0.0 56.3 jit_solution(11988878558553752601)
XLA Ops:
  0.7 1.2 %copy-done = bf16[896,512]{1,0:T(8,128)(2,1)S(1)} copy-done((bf16[896,512]{1,0:T(8,128)(2,1)S(1)}, bf16[896,512]{1,0:T(8,128)(2,1)}, u32[]{:S(2)}) %copy-start) | copy-done | bytes 917528
  1.9 4.1 %collective-permute-start.3 = (bf16[896,128]{1,0:T(8,128)(2,1)S(1)}, bf16[896,128]{1,0:T(8,128)(2,1)S(1)}, u32[]{:S(2)}, u32[]{:S(2)}) collective-permute-start(bf16[896,128]{1,0:T(8,128)(2,1)S(1)} %constant_dynamic-slice_fusion.refs_5_), channel_id=1, source_target_pairs={{0,16},{4,20},{8,24},{12,28},{16,0},{20,4},{24,8},{28,12},{1,17},{... | collective-permute-start | bytes 688136 | tf_op jit(solution)/shard_map/ppermute | solution.py:27
  6.0 1.6 %collective-permute-start.4 = (bf16[896,128]{1,0:T(8,128)(2,1)S(1)}, bf16[896,128]{1,0:T(8,128)(2,1)S(1)}, u32[]{:S(2)}, u32[]{:S(2)}) collective-permute-start(bf16[896,128]{1,0:T(8,128)(2,1)S(1)} %constant_dynamic-slice_fusion.refs_5_), channel_id=1, source_target_pairs={{0,8},{4,12},{8,0},{12,4},{16,24},{20,28},{24,16},{28,20},{1,9},{5... | collective-permute-start | bytes 688136 | tf_op jit(solution)/shard_map/ppermute | solution.py:27
  7.5 1.5 %collective-permute-start.5 = (bf16[896,128]{1,0:T(8,128)(2,1)S(1)}, bf16[896,128]{1,0:T(8,128)(2,1)S(1)}, u32[]{:S(2)}, u32[]{:S(2)}) collective-permute-start(bf16[896,128]{1,0:T(8,128)(2,1)S(1)} %constant_dynamic-slice_fusion.refs_5_), channel_id=1, source_target_pairs={{0,4},{4,0},{8,12},{12,8},{16,20},{20,16},{24,28},{28,24},{1,5},{5... | collective-permute-start | bytes 688136 | tf_op jit(solution)/shard_map/ppermute | solution.py:27
  9.1 1.5 %collective-permute-start = (bf16[128,896]{1,0:T(8,128)(2,1)S(1)}, bf16[128,896]{1,0:T(8,128)(2,1)S(1)}, u32[]{:S(2)}, u32[]{:S(2)}) collective-permute-start(bf16[128,896]{1,0:T(8,128)(2,1)S(1)} %bitcast.6), channel_id=1, source_target_pairs={{0,2},{1,3},{2,0},{3,1},{4,6},{5,7},{6,4},{7,5},{8,10},{9,11},{10,... | collective-permute-start | bytes 688136 | tf_op jit(solution)/shard_map/ppermute | solution.py:27
  10.6 0.6 %copy-done.4 = s32[1,2,2]{2,1,0:T(2,128)S(1)} copy-done((s32[1,2,2]{2,1,0:T(2,128)S(1)}, s32[1,2,2]{2,1,0:T(2,128)}, u32[]{:S(2)}) %copy-start.4) | copy-done | bytes 40
  11.2 1.0 %copy-done.2 = bf16[1,128,2048]{2,1,0:T(8,128)(2,1)S(1)} copy-done((bf16[1,128,2048]{2,1,0:T(8,128)(2,1)S(1)}, bf16[1,128,2048]{2,1,0:T(8,128)(2,1)}, u32[]{:S(2)}) %copy-start.2) | copy-done | bytes 524312
  12.3 1.0 %copy-done.3 = bf16[1,128,2048]{2,1,0:T(8,128)(2,1)S(1)} copy-done((bf16[1,128,2048]{2,1,0:T(8,128)(2,1)S(1)}, bf16[1,128,2048]{2,1,0:T(8,128)(2,1)}, u32[]{:S(2)}) %copy-start.3) | copy-done | bytes 524312
  13.3 1.0 %pack.1 = (bf16[1,272,128]{2,1,0:T(8,128)(2,1)S(1)}, bf16[1,272,128]{2,1,0:T(8,128)(2,1)S(1)}, bf16[2,272,128]{2,1,0:T(8,128)(2,1)S(1)}, bf16[1,256,384]{2,1,0:T...) custom-call(s32[4]{0:T(128)S(1)} %pad_add_fusion.meta.refs_0_, ...), custom_call_target="tpu_custom_call" | custom-call | tf_op jit(solution)/shard_map/pack/pallas_call | solution.py:128
  14.3 0.6 %collective-permute-start.7 = (bf16[2,272,128]{2,1,0:T(8,128)(2,1)S(1)}, bf16[2,272,128]{2,1,0:T(8,128)(2,1)S(1)}, u32[]{:S(2)}, u32[]{:S(2)}) collective-permute-start(bf16[2,272,128]{2,1,0:T(8,128)(2,1)S(1)} %get-tuple-element.58), channel_id=1, source_target_pairs={{0,2},{1,3},{2,0},{3,1},{4,6},{5,7},{6,4},{7,5},{8,10},{9,11},{10,... | collective-permute-start | bytes 417800 | tf_op jit(solution)/shard_map/ppermute | solution.py:27
  14.9 1.7 %collective-permute-done.3.refs_6_ = bf16[896,128]{1,0:T(8,128)(2,1)S(1)} collective-permute-done((bf16[896,128]{1,0:T(8,128)(2,1)S(1)}, bf16[896,128]{1,0:T(8,128)(2,1)S(1)}, u32[]{:S(2)}, u32[]{:S(2)}) %collective-permute-start.3) | collective-permute-done | bytes 229408 | tf_op jit(solution)/shard_map/ppermute | solution.py:27
  16.8 1.5 %collective-permute-start.11 = (bf16[2,256,384]{2,1,0:T(8,128)(2,1)S(1)}, bf16[2,256,384]{2,1,0:T(8,128)(2,1)S(1)}, u32[]{:S(2)}, u32[]{:S(2)}) collective-permute-start(bf16[2,256,384]{2,1,0:T(8,128)(2,1)S(1)} %get-tuple-element.68), channel_id=1, source_target_pairs={{0,2},{1,3},{2,0},{3,1},{4,6},{5,7},{6,4},{7,5},{8,10},{9,11},{10,... | collective-permute-start | bytes 1179656 | tf_op jit(solution)/shard_map/ppermute | solution.py:27
  18.3 2.1 %collective-permute-done.7.refs_9_ = bf16[2,272,128]{2,1,0:T(8,128)(2,1)S(1)} collective-permute-done((bf16[2,272,128]{2,1,0:T(8,128)(2,1)S(1)}, bf16[2,272,128]{2,1,0:T(8,128)(2,1)S(1)}, u32[]{:S(2)}, u32[]{:S(2)}) %collective-permute-start.7) | collective-permute-done | bytes 139296 | tf_op jit(solution)/shard_map/ppermute | solution.py:27
  20.5 0.5 collective-permute-start.1
  21.1 0.7 %collective-permute-done.8.refs_10_ = bf16[1,272,128]{2,1,0:T(8,128)(2,1)S(1)} collective-permute-done((bf16[1,272,128]{2,1,0:T(8,128)(2,1)S(1)}, bf16[1,272,128]{2,1,0:T(8,128)(2,1)S(1)}, u32[]{:S(2)}, u32[]{:S(2)}) %collective-permute-start.8) | collective-permute-done | bytes 69664 | tf_op jit(solution)/shard_map/ppermute | solution.py:27
  21.7 0.8 %collective-permute-start.10 = (bf16[896,128]{1,0:T(8,128)(2,1)S(1)}, bf16[896,128]{1,0:T(8,128)(2,1)S(1)}, u32[]{:S(2)}, u32[]{:S(2)}) collective-permute-start(bf16[896,128]{1,0:T(8,128)(2,1)S(1)} %collective-permute-done.3.refs_6_), channel_id=1, source_target_pairs={{0,4},{4,0},{8,12},{12,8},{16,20},{20,16},{24,28},{28,24},{1,5},{5... | collective-permute-start | bytes 688136 | tf_op jit(solution)/shard_map/ppermute | solution.py:27
  22.5 3.6 %attention.3 = (bf16[1,2,128,128]{3,2,1,0:T(8,128)(2,1)S(1)}, bf16[1,2,128,128]{3,2,1,0:T(8,128)(2,1)S(1)}, bf16[2,2,128,128]{3,2,1,0:T(8,128)(2,1)S(1)}, bf16[512,896]{1,0:T(8,128)(2,1)S(1)}, s32[32,128]{1,0:T(8,128)S(1)}) custom-call(s32[4]{0:T(128)S(1)} %pad_add_fusion.meta.refs_0_, bf16[128,896]{1,0:T(8,128)(2,1)S(1)} %bitcast.8, ...), custom_call_target="tpu_custom_call" | custom-call | tf_op jit(solution)/shard_map/attention/pallas_call | solution.py:280
  26.1 2.9 %collective-permute-done.9.refs_9_ = bf16[896,128]{1,0:T(8,128)(2,1)S(1)} collective-permute-done((bf16[896,128]{1,0:T(8,128)(2,1)S(1)}, bf16[896,128]{1,0:T(8,128)(2,1)S(1)}, u32[]{:S(2)}, u32[]{:S(2)}) %collective-permute-start.9) | collective-permute-done | bytes 229408 | tf_op jit(solution)/shard_map/ppermute | solution.py:27
  30.0 1.4 %collective-permute-start.17 = (bf16[896,128]{1,0:T(8,128)(2,1)S(1)}, bf16[896,128]{1,0:T(8,128)(2,1)S(1)}, u32[]{:S(2)}, u32[]{:S(2)}) collective-permute-start(bf16[896,128]{1,0:T(8,128)(2,1)S(1)} %collective-permute-done.5.refs_6_), channel_id=1, source_target_pairs={{0,8},{4,12},{8,0},{12,4},{16,24},{20,28},{24,16},{28,20},{1,9},{5... | collective-permute-start | bytes 688136 | tf_op jit(solution)/shard_map/ppermute | solution.py:27
  31.9 4.9 %attention.4 = (bf16[1,2,128,256]{3,2,1,0:T(8,128)(2,1)S(1)}, bf16[1,2,128,256]{3,2,1,0:T(8,128)(2,1)S(1)}, bf16[2,2,128,256]{3,2,1,0:T(8,128)(2,1)S(1)}, bf16[512,896]{1,0:T(8,128)(2,1)S(1)}) custom-call(s32[4]{0:T(128)S(1)} %pad_add_fusion.meta.refs_0_, s32[32,128]{1,0:T(8,128)S(1)} %get-tuple-element.59.refs_1_, bf16[128,896]{1,0:T(8,128)(2,1)S(1)} %bitcast.9, ...), custom_call_target="tpu_custom_call" | custom-call | tf_op jit(solution)/shard_map/attention/pallas_call | solution.py:280
  36.8 1.9 %collective-permute-start.19 = (bf16[2,2,128,256]{3,2,1,0:T(8,128)(2,1)S(1)}, bf16[2,2,128,256]{3,2,1,0:T(8,128)(2,1)S(1)}, u32[]{:S(2)}, u32[]{:S(2)}) collective-permute-start(bf16[2,2,128,256]{3,2,1,0:T(8,128)(2,1)S(1)} %get-tuple-element.90), channel_id=1, source_target_pairs={{0,2},{1,3},{2,0},{3,1},{4,6},{5,7},{6,4},{7,5},{8,10},{9,11},{10,... | collective-permute-start | bytes 786440 | tf_op jit(solution)/shard_map/ppermute | solution.py:27
  38.7 3.0 %attention.5 = (bf16[1,2,128,128]{3,2,1,0:T(8,128)(2,1)S(1)}, bf16[1,2,128,128]{3,2,1,0:T(8,128)(2,1)S(1)}, bf16[2,2,128,128]{3,2,1,0:T(8,128)(2,1)S(1)}, f32[256,896]{1,0:T(8,128)S(1)}, bf16[256,896]{1,0:T(8,128)(2,1)S(1)}) custom-call(s32[4]{0:T(128)S(1)} %pad_add_fusion.meta.refs_0_, s32[32,128]{1,0:T(8,128)S(1)} %get-tuple-element.59.refs_1_, ...), custom_call_target="tpu_custom_call" | custom-call | flops 2400000000 | tf_op jit(solution)/shard_map/attention/pallas_call | solution.py:280
  41.7 2.9 %collective-permute-done.19.refs_6_ = bf16[2,2,128,256]{3,2,1,0:T(8,128)(2,1)S(1)} collective-permute-done((bf16[2,2,128,256]{3,2,1,0:T(8,128)(2,1)S(1)}, bf16[2,2,128,256]{3,2,1,0:T(8,128)(2,1)S(1)}, u32[]{:S(2)}, u32[]{:S(2)}) %collective-permute-start.19) | collective-permute-done | bytes 262176 | tf_op jit(solution)/shard_map/ppermute | solution.py:27
  44.6 1.5 %collective-permute-start.23 = (bf16[2,2,128,128]{3,2,1,0:T(8,128)(2,1)S(1)}, bf16[2,2,128,128]{3,2,1,0:T(8,128)(2,1)S(1)}, u32[]{:S(2)}, u32[]{:S(2)}) collective-permute-start(bf16[2,2,128,128]{3,2,1,0:T(8,128)(2,1)S(1)} %get-tuple-element.96), channel_id=1, source_target_pairs={{0,2},{1,3},{2,0},{3,1},{4,6},{5,7},{6,4},{7,5},{8,10},{9,11},{10,... | collective-permute-start | bytes 393224 | tf_op jit(solution)/shard_map/ppermute | solution.py:27
  46.6 1.5 %collective-permute-start.26 = (bf16[128,896]{1,0:T(8,128)(2,1)S(1)}, bf16[128,896]{1,0:T(8,128)(2,1)S(1)}, u32[]{:S(2)}, u32[]{:S(2)}) collective-permute-start(bf16[128,896]{1,0:T(8,128)(2,1)S(1)} %slice.35), channel_id=1, source_target_pairs={{0,2},{1,3},{2,0},{3,1},{4,6},{5,7},{6,4},{7,5},{8,10},{9,11},{10,... | collective-permute-start | bytes 688136 | tf_op jit(solution)/shard_map/ppermute | solution.py:27
  48.1 0.5 collective-permute-start.15
  48.8 2.1 %collective-permute-done.23.refs_10_ = bf16[2,2,128,128]{3,2,1,0:T(8,128)(2,1)S(1)} collective-permute-done((bf16[2,2,128,128]{3,2,1,0:T(8,128)(2,1)S(1)}, bf16[2,2,128,128]{3,2,1,0:T(8,128)(2,1)S(1)}, u32[]{:S(2)}, u32[]{:S(2)}) %collective-permute-start.23) | collective-permute-done | bytes 131104 | tf_op jit(solution)/shard_map/ppermute | solution.py:27
  50.9 0.6 %collective-permute-start.22 = (bf16[1,2,128,128]{3,2,1,0:T(8,128)(2,1)S(1)}, bf16[1,2,128,128]{3,2,1,0:T(8,128)(2,1)S(1)}, u32[]{:S(2)}, u32[]{:S(2)}) collective-permute-start(bf16[1,2,128,128]{3,2,1,0:T(8,128)(2,1)S(1)} %get-tuple-element.95), channel_id=1, source_target_pairs={{0,1},{1,0},{2,3},{3,2},{4,5},{5,4},{6,7},{7,6},{8,9},{9,8},{10,11... | collective-permute-start | bytes 196616 | tf_op jit(solution)/shard_map/ppermute | solution.py:27
  51.6 0.8 %collective-permute-done.22.refs_9_ = bf16[1,2,128,128]{3,2,1,0:T(8,128)(2,1)S(1)} collective-permute-done((bf16[1,2,128,128]{3,2,1,0:T(8,128)(2,1)S(1)}, bf16[1,2,128,128]{3,2,1,0:T(8,128)(2,1)S(1)}, u32[]{:S(2)}, u32[]{:S(2)}) %collective-permute-start.22) | collective-permute-done | bytes 65568 | tf_op jit(solution)/shard_map/ppermute | solution.py:27
  52.8 1.8 %unpack.1 = (bf16[1,128,2048]{2,1,0:T(8,128)(2,1)}, bf16[1,128,2048]{2,1,0:T(8,128)(2,1)}) custom-call(s32[4]{0:T(128)S(1)} %pad_add_fusion.meta.refs_0_, bf16[1,2,128,128]{3,2,1,0:T(8,128)(2,1)S(1)} %get-tuple-element.82.refs_0_, bf16[1,2,128,128]{3,2,1,0:T(8,128)(2,1)S(1)} %collective-permute-done.15.refs_1_, ...), custom_call_target="tpu_custom_call" | custom-call | tf_op jit(solution)/shard_map/unpack/pallas_call | solution.py:315
  54.6 0.9 %collective-permute-done.26 = bf16[128,896]{1,0:T(8,128)(2,1)S(1)} collective-permute-done((bf16[128,896]{1,0:T(8,128)(2,1)S(1)}, bf16[128,896]{1,0:T(8,128)(2,1)S(1)}, u32[]{:S(2)}, u32[]{:S(2)}) %collective-permute-start.26) | collective-permute-done | bytes 229408 | tf_op jit(solution)/shard_map/ppermute | solution.py:27
  55.5 0.8 %slice_add_fusion = f32[128,896]{1,0:T(8,128)} fusion(f32[256,896]{1,0:T(8,128)S(1)} %convert_add_fusion, bf16[128,896]{1,0:T(8,128)(2,1)S(1)} %collective-permute-done.26), kind=kLoop, calls=%fused_computation.2 | loop fusion | flops 229376 | bytes 1146880 | tf_op jit(solution)/shard_map/add | solution.py:424
  (49 shorter events, 3.0 us)
Async XLA Ops:
  0.6 1.2 %copy-start = (bf16[896,512]{1,0:T(8,128)(2,1)S(1)}, bf16[896,512]{1,0:T(8,128)(2,1)}, u32[]{:S(2)}) copy-start(bf16[896,512]{1,0:T(8,128)(2,1)} %param.9) | copy-start | bytes 2752516
  1.8 7.2 %copy-start.1 = (bf16[1,2,64,896]{3,2,1,0:T(8,128)(2,1)S(1)}, bf16[1,2,64,896]{3,2,1,0:T(8,128)(2,1)}, u32[]{:S(2)}) copy-start(bf16[1,2,64,896]{3,2,1,0:T(8,128)(2,1)} %param.8) | copy-start | bytes 688132
  1.9 14.7 %collective-permute-start.3 = (bf16[896,128]{1,0:T(8,128)(2,1)S(1)}, bf16[896,128]{1,0:T(8,128)(2,1)S(1)}, u32[]{:S(2)}, u32[]{:S(2)}) collective-permute-start(bf16[896,128]{1,0:T(8,128)(2,1)S(1)} %constant_dynamic-slice_fusion.refs_5_), channel_id=1, source_target_pairs={{0,16},{4,20},{8,24},{12,28},{16,0},{20,4},{24,8},{28,12},{1,17},{... | collective-permute-start | bytes 688136 | tf_op jit(solution)/shard_map/ppermute | solution.py:27
  6.0 10.8 %collective-permute-start.4 = (bf16[896,128]{1,0:T(8,128)(2,1)S(1)}, bf16[896,128]{1,0:T(8,128)(2,1)S(1)}, u32[]{:S(2)}, u32[]{:S(2)}) collective-permute-start(bf16[896,128]{1,0:T(8,128)(2,1)S(1)} %constant_dynamic-slice_fusion.refs_5_), channel_id=1, source_target_pairs={{0,8},{4,12},{8,0},{12,4},{16,24},{20,28},{24,16},{28,20},{1,9},{5... | collective-permute-start | bytes 688136 | tf_op jit(solution)/shard_map/ppermute | solution.py:27
  7.5 9.2 %collective-permute-start.5 = (bf16[896,128]{1,0:T(8,128)(2,1)S(1)}, bf16[896,128]{1,0:T(8,128)(2,1)S(1)}, u32[]{:S(2)}, u32[]{:S(2)}) collective-permute-start(bf16[896,128]{1,0:T(8,128)(2,1)S(1)} %constant_dynamic-slice_fusion.refs_5_), channel_id=1, source_target_pairs={{0,4},{4,0},{8,12},{12,8},{16,20},{20,16},{24,28},{28,24},{1,5},{5... | collective-permute-start | bytes 688136 | tf_op jit(solution)/shard_map/ppermute | solution.py:27
  9.1 11.9 %collective-permute-start = (bf16[128,896]{1,0:T(8,128)(2,1)S(1)}, bf16[128,896]{1,0:T(8,128)(2,1)S(1)}, u32[]{:S(2)}, u32[]{:S(2)}) collective-permute-start(bf16[128,896]{1,0:T(8,128)(2,1)S(1)} %bitcast.6), channel_id=1, source_target_pairs={{0,2},{1,3},{2,0},{3,1},{4,6},{5,7},{6,4},{7,5},{8,10},{9,11},{10,... | collective-permute-start | bytes 688136 | tf_op jit(solution)/shard_map/ppermute | solution.py:27
  10.5 0.7 %copy-start.5 = (s32[1,8]{1,0:T(1,128)S(1)}, s32[1,8]{1,0:T(1,128)}, u32[]{:S(2)}) copy-start(s32[1,8]{1,0:T(1,128)} %slots.1) | copy-start | bytes 100
  11.2 1.0 %copy-start.2 = (bf16[1,128,2048]{2,1,0:T(8,128)(2,1)S(1)}, bf16[1,128,2048]{2,1,0:T(8,128)(2,1)}, u32[]{:S(2)}) copy-start(bf16[1,128,2048]{2,1,0:T(8,128)(2,1)} %queries.1) | copy-start | bytes 1572868
  12.3 1.0 %copy-start.3 = (bf16[1,128,2048]{2,1,0:T(8,128)(2,1)S(1)}, bf16[1,128,2048]{2,1,0:T(8,128)(2,1)}, u32[]{:S(2)}) copy-start(bf16[1,128,2048]{2,1,0:T(8,128)(2,1)} %grad_out.1) | copy-start | bytes 1572868
  14.3 6.2 %collective-permute-start.7 = (bf16[2,272,128]{2,1,0:T(8,128)(2,1)S(1)}, bf16[2,272,128]{2,1,0:T(8,128)(2,1)S(1)}, u32[]{:S(2)}, u32[]{:S(2)}) collective-permute-start(bf16[2,272,128]{2,1,0:T(8,128)(2,1)S(1)} %get-tuple-element.58), channel_id=1, source_target_pairs={{0,2},{1,3},{2,0},{3,1},{4,6},{5,7},{6,4},{7,5},{8,10},{9,11},{10,... | collective-permute-start | bytes 417800 | tf_op jit(solution)/shard_map/ppermute | solution.py:27
  16.8 12.6 %collective-permute-start.11 = (bf16[2,256,384]{2,1,0:T(8,128)(2,1)S(1)}, bf16[2,256,384]{2,1,0:T(8,128)(2,1)S(1)}, u32[]{:S(2)}, u32[]{:S(2)}) collective-permute-start(bf16[2,256,384]{2,1,0:T(8,128)(2,1)S(1)} %get-tuple-element.68), channel_id=1, source_target_pairs={{0,2},{1,3},{2,0},{3,1},{4,6},{5,7},{6,4},{7,5},{8,10},{9,11},{10,... | collective-permute-start | bytes 1179656 | tf_op jit(solution)/shard_map/ppermute | solution.py:27
  18.3 2.7 %collective-permute-start.6 = (bf16[1,272,128]{2,1,0:T(8,128)(2,1)S(1)}, bf16[1,272,128]{2,1,0:T(8,128)(2,1)S(1)}, u32[]{:S(2)}, u32[]{:S(2)}) collective-permute-start(bf16[1,272,128]{2,1,0:T(8,128)(2,1)S(1)} %get-tuple-element.57), channel_id=1, source_target_pairs={{0,1},{1,0},{2,3},{3,2},{4,5},{5,4},{6,7},{7,6},{8,9},{9,8},{10,11... | collective-permute-start | bytes 208904 | tf_op jit(solution)/shard_map/ppermute | solution.py:27
  20.5 1.3 %collective-permute-start.8 = (bf16[1,272,128]{2,1,0:T(8,128)(2,1)S(1)}, bf16[1,272,128]{2,1,0:T(8,128)(2,1)S(1)}, u32[]{:S(2)}, u32[]{:S(2)}) collective-permute-start(bf16[1,272,128]{2,1,0:T(8,128)(2,1)S(1)} %slice.29), channel_id=1, source_target_pairs={{0,1},{1,0},{2,3},{3,2},{4,5},{5,4},{6,7},{7,6},{8,9},{9,8},{10,11... | collective-permute-start | bytes 208904 | tf_op jit(solution)/shard_map/ppermute | solution.py:27
  20.5 2.1 %collective-permute-start.1 = (bf16[128,896]{1,0:T(8,128)(2,1)S(1)}, bf16[128,896]{1,0:T(8,128)(2,1)S(1)}, u32[]{:S(2)}, u32[]{:S(2)}) collective-permute-start(bf16[128,896]{1,0:T(8,128)(2,1)S(1)} %bitcast.7), channel_id=1, source_target_pairs={{0,1},{1,0},{2,3},{3,2},{4,5},{5,4},{6,7},{7,6},{8,9},{9,8},{10,11... | collective-permute-start | bytes 688136 | tf_op jit(solution)/shard_map/ppermute | solution.py:27
  21.0 1.6 %collective-permute-start.2 = (bf16[128,896]{1,0:T(8,128)(2,1)S(1)}, bf16[128,896]{1,0:T(8,128)(2,1)S(1)}, u32[]{:S(2)}, u32[]{:S(2)}) collective-permute-start(bf16[128,896]{1,0:T(8,128)(2,1)S(1)} %collective-permute-done.refs_2_.refs_3_), channel_id=1, source_target_pairs={{0,1},{1,0},{2,3},{3,2},{4,5},{5,4},{6,7},{7,6},{8,9},{9,8},{10,11... | collective-permute-start | bytes 688136 | tf_op jit(solution)/shard_map/ppermute | solution.py:27
  21.1 7.9 %collective-permute-start.9 = (bf16[896,128]{1,0:T(8,128)(2,1)S(1)}, bf16[896,128]{1,0:T(8,128)(2,1)S(1)}, u32[]{:S(2)}, u32[]{:S(2)}) collective-permute-start(bf16[896,128]{1,0:T(8,128)(2,1)S(1)} %collective-permute-done.3.refs_6_), channel_id=1, source_target_pairs={{0,8},{4,12},{8,0},{12,4},{16,24},{20,28},{24,16},{28,20},{1,9},{5... | collective-permute-start | bytes 688136 | tf_op jit(solution)/shard_map/ppermute | solution.py:27
  21.7 7.7 %collective-permute-start.10 = (bf16[896,128]{1,0:T(8,128)(2,1)S(1)}, bf16[896,128]{1,0:T(8,128)(2,1)S(1)}, u32[]{:S(2)}, u32[]{:S(2)}) collective-permute-start(bf16[896,128]{1,0:T(8,128)(2,1)S(1)} %collective-permute-done.3.refs_6_), channel_id=1, source_target_pairs={{0,4},{4,0},{8,12},{12,8},{16,20},{20,16},{24,28},{28,24},{1,5},{5... | collective-permute-start | bytes 688136 | tf_op jit(solution)/shard_map/ppermute | solution.py:27
  29.4 2.4 %collective-permute-start.13 = (bf16[1,256,384]{2,1,0:T(8,128)(2,1)S(1)}, bf16[1,256,384]{2,1,0:T(8,128)(2,1)S(1)}, u32[]{:S(2)}, u32[]{:S(2)}) collective-permute-start(bf16[1,256,384]{2,1,0:T(8,128)(2,1)S(1)} %slice.23), channel_id=1, source_target_pairs={{0,1},{1,0},{2,3},{3,2},{4,5},{5,4},{6,7},{7,6},{8,9},{9,8},{10,11... | collective-permute-start | bytes 589832 | tf_op jit(solution)/shard_map/ppermute | solution.py:27
  29.5 2.4 %collective-permute-start.12 = (bf16[1,256,384]{2,1,0:T(8,128)(2,1)S(1)}, bf16[1,256,384]{2,1,0:T(8,128)(2,1)S(1)}, u32[]{:S(2)}, u32[]{:S(2)}) collective-permute-start(bf16[1,256,384]{2,1,0:T(8,128)(2,1)S(1)} %get-tuple-element.75), channel_id=1, source_target_pairs={{0,1},{1,0},{2,3},{3,2},{4,5},{5,4},{6,7},{7,6},{8,9},{9,8},{10,11... | collective-permute-start | bytes 589832 | tf_op jit(solution)/shard_map/ppermute | solution.py:27
  30.0 8.6 %collective-permute-start.17 = (bf16[896,128]{1,0:T(8,128)(2,1)S(1)}, bf16[896,128]{1,0:T(8,128)(2,1)S(1)}, u32[]{:S(2)}, u32[]{:S(2)}) collective-permute-start(bf16[896,128]{1,0:T(8,128)(2,1)S(1)} %collective-permute-done.5.refs_6_), channel_id=1, source_target_pairs={{0,8},{4,12},{8,0},{12,4},{16,24},{20,28},{24,16},{28,20},{1,9},{5... | collective-permute-start | bytes 688136 | tf_op jit(solution)/shard_map/ppermute | solution.py:27
  31.4 7.3 %collective-permute-start.18 = (bf16[896,128]{1,0:T(8,128)(2,1)S(1)}, bf16[896,128]{1,0:T(8,128)(2,1)S(1)}, u32[]{:S(2)}, u32[]{:S(2)}) collective-permute-start(bf16[896,128]{1,0:T(8,128)(2,1)S(1)} %collective-permute-done.9.refs_9_), channel_id=1, source_target_pairs={{0,4},{4,0},{8,12},{12,8},{16,20},{20,16},{24,28},{28,24},{1,5},{5... | collective-permute-start | bytes 688136 | tf_op jit(solution)/shard_map/ppermute | solution.py:27
  31.6 7.0 %collective-permute-start.14 = (bf16[2,2,128,128]{3,2,1,0:T(8,128)(2,1)S(1)}, bf16[2,2,128,128]{3,2,1,0:T(8,128)(2,1)S(1)}, u32[]{:S(2)}, u32[]{:S(2)}) collective-permute-start(bf16[2,2,128,128]{3,2,1,0:T(8,128)(2,1)S(1)} %get-tuple-element.81), channel_id=1, source_target_pairs={{0,2},{1,3},{2,0},{3,1},{4,6},{5,7},{6,4},{7,5},{8,10},{9,11},{10,... | collective-permute-start | bytes 393224 | tf_op jit(solution)/shard_map/ppermute | solution.py:27
  36.8 7.9 %collective-permute-start.19 = (bf16[2,2,128,256]{3,2,1,0:T(8,128)(2,1)S(1)}, bf16[2,2,128,256]{3,2,1,0:T(8,128)(2,1)S(1)}, u32[]{:S(2)}, u32[]{:S(2)}) collective-permute-start(bf16[2,2,128,256]{3,2,1,0:T(8,128)(2,1)S(1)} %get-tuple-element.90), channel_id=1, source_target_pairs={{0,2},{1,3},{2,0},{3,1},{4,6},{5,7},{6,4},{7,5},{8,10},{9,11},{10,... | collective-permute-start | bytes 786440 | tf_op jit(solution)/shard_map/ppermute | solution.py:27
  44.6 1.8 %collective-permute-start.25 = (bf16[256,896]{1,0:T(8,128)(2,1)S(1)}, bf16[256,896]{1,0:T(8,128)(2,1)S(1)}, u32[]{:S(2)}, u32[]{:S(2)}) collective-permute-start(bf16[256,896]{1,0:T(8,128)(2,1)S(1)} %get-tuple-element.100), channel_id=1, source_target_pairs={{0,1},{1,0},{2,3},{3,2},{4,5},{5,4},{6,7},{7,6},{8,9},{9,8},{10,11... | collective-permute-start | bytes 1376264 | tf_op jit(solution)/shard_map/ppermute | solution.py:27
  44.6 6.3 %collective-permute-start.23 = (bf16[2,2,128,128]{3,2,1,0:T(8,128)(2,1)S(1)}, bf16[2,2,128,128]{3,2,1,0:T(8,128)(2,1)S(1)}, u32[]{:S(2)}, u32[]{:S(2)}) collective-permute-start(bf16[2,2,128,128]{3,2,1,0:T(8,128)(2,1)S(1)} %get-tuple-element.96), channel_id=1, source_target_pairs={{0,2},{1,3},{2,0},{3,1},{4,6},{5,7},{6,4},{7,5},{8,10},{9,11},{10,... | collective-permute-start | bytes 393224 | tf_op jit(solution)/shard_map/ppermute | solution.py:27
  46.6 8.9 %collective-permute-start.26 = (bf16[128,896]{1,0:T(8,128)(2,1)S(1)}, bf16[128,896]{1,0:T(8,128)(2,1)S(1)}, u32[]{:S(2)}, u32[]{:S(2)}) collective-permute-start(bf16[128,896]{1,0:T(8,128)(2,1)S(1)} %slice.35), channel_id=1, source_target_pairs={{0,2},{1,3},{2,0},{3,1},{4,6},{5,7},{6,4},{7,5},{8,10},{9,11},{10,... | collective-permute-start | bytes 688136 | tf_op jit(solution)/shard_map/ppermute | solution.py:27
  48.1 2.8 %collective-permute-start.16 = (bf16[1,2,128,128]{3,2,1,0:T(8,128)(2,1)S(1)}, bf16[1,2,128,128]{3,2,1,0:T(8,128)(2,1)S(1)}, u32[]{:S(2)}, u32[]{:S(2)}) collective-permute-start(bf16[1,2,128,128]{3,2,1,0:T(8,128)(2,1)S(1)} %slice.24), channel_id=1, source_target_pairs={{0,1},{1,0},{2,3},{3,2},{4,5},{5,4},{6,7},{7,6},{8,9},{9,8},{10,11... | collective-permute-start | bytes 196616 | tf_op jit(solution)/shard_map/ppermute | solution.py:27
  48.1 3.4 %collective-permute-start.15 = (bf16[1,2,128,128]{3,2,1,0:T(8,128)(2,1)S(1)}, bf16[1,2,128,128]{3,2,1,0:T(8,128)(2,1)S(1)}, u32[]{:S(2)}, u32[]{:S(2)}) collective-permute-start(bf16[1,2,128,128]{3,2,1,0:T(8,128)(2,1)S(1)} %get-tuple-element.83), channel_id=1, source_target_pairs={{0,1},{1,0},{2,3},{3,2},{4,5},{5,4},{6,7},{7,6},{8,9},{9,8},{10,11... | collective-permute-start | bytes 196616 | tf_op jit(solution)/shard_map/ppermute | solution.py:27
  48.6 4.1 %collective-permute-start.21 = (bf16[1,2,128,256]{3,2,1,0:T(8,128)(2,1)S(1)}, bf16[1,2,128,256]{3,2,1,0:T(8,128)(2,1)S(1)}, u32[]{:S(2)}, u32[]{:S(2)}) collective-permute-start(bf16[1,2,128,256]{3,2,1,0:T(8,128)(2,1)S(1)} %slice.25), channel_id=1, source_target_pairs={{0,1},{1,0},{2,3},{3,2},{4,5},{5,4},{6,7},{7,6},{8,9},{9,8},{10,11... | collective-permute-start | bytes 393224 | tf_op jit(solution)/shard_map/ppermute | solution.py:27
  50.9 1.9 %collective-permute-start.20 = (bf16[1,2,128,256]{3,2,1,0:T(8,128)(2,1)S(1)}, bf16[1,2,128,256]{3,2,1,0:T(8,128)(2,1)S(1)}, u32[]{:S(2)}, u32[]{:S(2)}) collective-permute-start(bf16[1,2,128,256]{3,2,1,0:T(8,128)(2,1)S(1)} %get-tuple-element.92), channel_id=1, source_target_pairs={{0,1},{1,0},{2,3},{3,2},{4,5},{5,4},{6,7},{7,6},{8,9},{9,8},{10,11... | collective-permute-start | bytes 393224 | tf_op jit(solution)/shard_map/ppermute | solution.py:27
  50.9 1.5 %collective-permute-start.22 = (bf16[1,2,128,128]{3,2,1,0:T(8,128)(2,1)S(1)}, bf16[1,2,128,128]{3,2,1,0:T(8,128)(2,1)S(1)}, u32[]{:S(2)}, u32[]{:S(2)}) collective-permute-start(bf16[1,2,128,128]{3,2,1,0:T(8,128)(2,1)S(1)} %get-tuple-element.95), channel_id=1, source_target_pairs={{0,1},{1,0},{2,3},{3,2},{4,5},{5,4},{6,7},{7,6},{8,9},{9,8},{10,11... | collective-permute-start | bytes 196616 | tf_op jit(solution)/shard_map/ppermute | solution.py:27
  51.5 1.3 %collective-permute-start.24 = (bf16[1,2,128,128]{3,2,1,0:T(8,128)(2,1)S(1)}, bf16[1,2,128,128]{3,2,1,0:T(8,128)(2,1)S(1)}, u32[]{:S(2)}, u32[]{:S(2)}) collective-permute-start(bf16[1,2,128,128]{3,2,1,0:T(8,128)(2,1)S(1)} %slice.30), channel_id=1, source_target_pairs={{0,1},{1,0},{2,3},{3,2},{4,5},{5,4},{6,7},{7,6},{8,9},{9,8},{10,11... | collective-permute-start | bytes 196616 | tf_op jit(solution)/shard_map/ppermute | solution.py:27
  (1 other events, 0.7 us)

commit v6 on v5

--- a/solution.py
+++ b/solution.py
@@ -154,21 +154,30 @@
     return out
 
 
+def spots_of(table, seq_size, spans):
+    spots = []
+    for k in range(seq_size):
+        for c in range(spans):
+            starts = [table[8 * k, c * READS + r] * NLEN for r in range(READS)]
+            spots.append((k, c, [pl.multiple_of(start, NLEN) for start in starts]))
+    return spots
+
+
 def attention_body(seq_size, spans, takes, places, arrays, per_owner, finds, has_prior, last, *refs):
     count = len(takes)
     meta, refs = refs[0], refs[1:]
-    table, refs = (None, refs) if finds else (refs[0], refs[1:])
     stored, refs = refs[:seq_size], refs[seq_size:]
     weights, refs = refs[: 2 * count], refs[2 * count :]
     pieces, refs = refs[:arrays], refs[arrays:]
     pieces = [pieces[at].at[index] for at, index in places]
     prior, refs = (refs[0], refs[1:]) if has_prior else (None, refs)
+    table, refs = (None, refs) if finds else (refs[0], refs[1:])
     levels = seq_size.bit_length()
     outs, refs = refs[:levels], refs[levels:]
     grads, refs = (refs[:2], refs[2:]) if last else (refs[:1], refs[1:])
     if finds:
-        found, refs = refs[0], refs[1:]
-    enc, pair, kv, d_kv = refs[:4]
+        table, refs = refs[0], refs[1:]
+    enc, pair, kv, d_kv, found, sem = refs
     block = stored[0].shape[0]
     rows = enc.shape[0]
     tokens = spans * SPAN
@@ -178,57 +187,60 @@
         enc[i * block : (i + 1) * block] = stored[i][...]
     if finds:
         for k, rows_of in enumerate(relative_positions(pieces[:seq_size], meta[0], per_owner, tokens)):
-            found[8 * k : 8 * k + 8, :] = rows_of
-        table, sem = refs[4:]
-        copy = pltpu.make_async_copy(found, table, sem)
-        copy.start()
-        copy.wait()
-    spots = []
-    for k in range(seq_size):
-        for c in range(spans):
-            starts = [table[8 * k, c * READS + r] * NLEN for r in range(READS)]
-            spots.append((k, c, [pl.multiple_of(start, NLEN) for start in starts]))
+            table[8 * k : 8 * k + 8, :] = rows_of
+    copy = pltpu.make_async_copy(table, found, sem)
+    copy.start()
     for i in range(count):
         first, second = weights[2 * i][...], weights[2 * i + 1][...]
-        wide = slice(2 * i * HEAD_SIZE, 2 * (i + 1) * HEAD_SIZE)
         pair[:, 2 * i * HEAD_SIZE : (2 * i + 1) * HEAD_SIZE] = jnp.where(keys_first, first, second)
         pair[:, (2 * i + 1) * HEAD_SIZE : (2 * i + 2) * HEAD_SIZE] = jnp.where(keys_first, second, first)
-        kv[...] = jnp.dot(enc[...], pair[:, wide], preferred_element_type=jnp.float32).astype(jnp.bfloat16)
-        d_kv[:, wide] = jnp.zeros((rows, 2 * HEAD_SIZE), jnp.float32)
-        columns = slice(i * HEAD_SIZE, (i + 1) * HEAD_SIZE)
+        wide = slice(2 * i * HEAD_SIZE, 2 * (i + 1) * HEAD_SIZE)
+        kv[:, wide] = jnp.dot(enc[...], pair[:, wide], preferred_element_type=jnp.float32).astype(jnp.bfloat16)
+    d_kv[...] = jnp.zeros_like(d_kv)
+    copy.wait()
+    units = [(i, *spot) for i in range(count) for spot in spots_of(found, seq_size, spans)]
+    reads, queries, grad_rows, scores, d_probs = [], [], [], [], []
+    for i, k, c, starts in units:
+        wide = slice(2 * i * HEAD_SIZE, 2 * (i + 1) * HEAD_SIZE)
         source, at = takes[i]
         taken = slice(at * HEAD_SIZE, (at + 1) * HEAD_SIZE)
-        reads, queries, grad_rows, scores, d_probs = [], [], [], [], []
-        for k, c, starts in spots:
-            read = jnp.concatenate([kv[pl.ds(start, NLEN), :] for start in starts], axis=0)
-            query = pieces[source * seq_size + k][c * SPAN : (c + 1) * SPAN, taken]
-            grad = pieces[source * seq_size + k][tokens + c * SPAN : tokens + (c + 1) * SPAN, taken]
-            reads.append((read[:, :HEAD_SIZE], read[:, HEAD_SIZE:]))
-            queries.append(query)
-            grad_rows.append(grad)
-            scores.append(lax.dot_general(query, reads[-1][0], NT, preferred_element_type=jnp.float32))
-            d_probs.append(lax.dot_general(grad, reads[-1][1], NT, preferred_element_type=jnp.float32))
-        probs_low, d_scores = [], []
-        for score, d_prob in zip(scores, d_probs):
-            expos = jnp.exp(score * scale)
-            probs = expos / jnp.sum(expos, axis=-1, keepdims=True)
-            delta = jnp.sum(probs * d_prob, axis=-1, keepdims=True)
-            probs_low.append(probs.astype(jnp.bfloat16))
-            d_scores.append((probs * (d_prob - delta) * scale).astype(jnp.bfloat16))
-        for n, (k, c, starts) in enumerate(spots):
-            keys, values = reads[n]
-            span = slice(c * SPAN, (c + 1) * SPAN)
-            item_of(outs, k)[0, span, columns] = jnp.dot(
-                probs_low[n], values, preferred_element_type=jnp.float32
-            ).astype(jnp.bfloat16)
-            item_of(outs, k)[1, span, columns] = jnp.dot(
-                d_scores[n], keys, preferred_element_type=jnp.float32
-            ).astype(jnp.bfloat16)
-            d_keys = lax.dot_general(d_scores[n], queries[n], TN, preferred_element_type=jnp.float32)
-            d_values = lax.dot_general(probs_low[n], grad_rows[n], TN, preferred_element_type=jnp.float32)
-            both = jnp.concatenate([d_keys, d_values], axis=1)
-            for r, start in enumerate(starts):
-                d_kv[pl.ds(start, NLEN), wide] += both[r * NLEN : (r + 1) * NLEN]
+        read = jnp.concatenate([kv[pl.ds(start, NLEN), wide] for start in starts], axis=0)
+        query = pieces[source * seq_size + k][c * SPAN : (c + 1) * SPAN, taken]
+        grad = pieces[source * seq_size + k][tokens + c * SPAN : tokens + (c + 1) * SPAN, taken]
+        reads.append((read[:, :HEAD_SIZE], read[:, HEAD_SIZE:]))
+        queries.append(query)
+        grad_rows.append(grad)
+        scores.append(lax.dot_general(query, reads[-1][0], NT, preferred_element_type=jnp.float32))
+        d_probs.append(lax.dot_general(grad, reads[-1][1], NT, preferred_element_type=jnp.float32))
+    probs_low, d_scores = [], []
+    for score, d_prob in zip(scores, d_probs):
+        expos = jnp.exp(score * scale)
+        probs = expos * (1.0 / jnp.sum(expos, axis=-1, keepdims=True))
+        delta = jnp.sum(probs * d_prob, axis=-1, keepdims=True)
+        probs_low.append(probs.astype(jnp.bfloat16))
+        d_scores.append((probs * (d_prob - delta) * scale).astype(jnp.bfloat16))
+    for n, (i, k, c, _) in enumerate(units):
+        keys, values = reads[n]
+        span = slice(c * SPAN, (c + 1) * SPAN)
+        columns = slice(i * HEAD_SIZE, (i + 1) * HEAD_SIZE)
+        item_of(outs, k)[0, span, columns] = jnp.dot(
+            probs_low[n], values, preferred_element_type=jnp.float32
+        ).astype(jnp.bfloat16)
+        item_of(outs, k)[1, span, columns] = jnp.dot(
+            d_scores[n], keys, preferred_element_type=jnp.float32
+        ).astype(jnp.bfloat16)
+    both = [
+        (
+            lax.dot_general(d_scores[n], queries[n], TN, preferred_element_type=jnp.float32),
+            lax.dot_general(probs_low[n], grad_rows[n], TN, preferred_element_type=jnp.float32),
+        )
+        for n in range(len(units))
+    ]
+    for n, (i, _, _, starts) in enumerate(units):
+        for r, start in enumerate(starts):
+            for part in range(2):
+                wide = slice((2 * i + part) * HEAD_SIZE, (2 * i + part + 1) * HEAD_SIZE)
+                d_kv[pl.ds(start, NLEN), wide] += both[n][part][r * NLEN : (r + 1) * NLEN]
     half = rows // 2
     for part in range(2):
         place = slice(part * half, (part + 1) * half)
@@ -256,9 +268,8 @@
     count = len(weights) // 2
     prior = [] if prior is None else [prior]
     vmem = pl.BlockSpec(memory_space=pltpu.VMEM)
-    operands = [*stored, *weights, *arrays, *prior]
     finds = table is None
-    scalars = [meta] if finds else [meta, table]
+    operands = [*stored, *weights, *arrays, *prior] + ([] if finds else [table])
     table_shape = (8 * seq_size, HEAD_SIZE)
     out_shape = bundles(seq_size, (2, spans * SPAN, count * HEAD_SIZE), jnp.bfloat16)
     levels = len(out_shape)
@@ -271,18 +282,19 @@
     scratch = [
         pltpu.VMEM((rows, width), jnp.bfloat16),
         pltpu.VMEM((width, 2 * count * HEAD_SIZE), jnp.bfloat16),
-        pltpu.VMEM((rows, 2 * HEAD_SIZE), jnp.bfloat16),
+        pltpu.VMEM((rows, 2 * count * HEAD_SIZE), jnp.bfloat16),
         pltpu.VMEM((rows, 2 * count * HEAD_SIZE), jnp.float32),
+        pltpu.SMEM(table_shape, jnp.int32),
+        pltpu.SemaphoreType.DMA,
     ]
     if finds:
         out_shape.append(jax.ShapeDtypeStruct(table_shape, jnp.int32))
-        scratch += [pltpu.SMEM(table_shape, jnp.int32), pltpu.SemaphoreType.DMA]
     outs = pl.pallas_call(
         functools.partial(
             attention_body, seq_size, spans, takes, places, len(arrays), per_owner, finds, len(prior), last
         ),
         out_shape=out_shape,
-        in_specs=[pl.BlockSpec(memory_space=pltpu.SMEM)] * len(scalars) + [vmem] * len(operands),
+        in_specs=[pl.BlockSpec(memory_space=pltpu.SMEM)] + [vmem] * len(operands),
         out_specs=[vmem] * len(out_shape),
         scratch_shapes=scratch,
         compiler_params=pltpu.CompilerParams(vmem_limit_bytes=vmem_bytes(rows)),
@@ -290,7 +302,7 @@
             flops=int(2.4e9) if last and len(prior) else 0, bytes_accessed=0, transcendentals=0
         ),
         name="attention",
-    )(*scalars, *operands)
+    )(meta, *operands)
     return outs[:levels], outs[levels : levels + grads], outs[-1] if finds else table
 
 

time: 56.5 us -> 55.3 us (0.979)
  Pallas kernels: 14.2 us -> 13.2 us
    pallas_call x3, Pallas kernels: 11.5 us -> 10.5 us  [attention(): pl.pallas_call(functools.partial(attention_body, seq_size, spans, takes,...]
  transfers between devices with their start and end apart: 27 -> 27, of which waited for: 12 -> 14; matrix products, arithmetic and copies ran while one was open for 0% -> 0% of each run, Pallas kernels for 25% -> 24%
where the time goes in v6:
time: 55.3 us; the launch traced here: 55 us
  starting transfers between devices  20.8 us (38%)
  waiting for transfers between devices  15.2 us (27%)
  Pallas kernels  13.2 us (24%)
  local copies, waits for them, and re-layouts  3.97 us (7%)
  other arithmetic  0.99 us (2%)
  between operations  0.76 us (1%)
    ppermute x27, starting transfers between devices, xor_send(): return lax.ppermute(value, axis, [(i, i ^ bit) for i in range(size)])  20.8 us
    ppermute x27, waiting for transfers between devices, xor_send(): return lax.ppermute(value, axis, [(i, i ^ bit) for i in range(size)])  15.2 us
    pallas_call x3, Pallas kernels, attention(): pl.pallas_call(functools.partial(attention_body, seq_size, spans, takes,...  10.5 us
    unnamed x12, local copies, waits for them, and re-layouts  3.86 us
    pallas_call x1, Pallas kernels, unpack(): pl.pallas_call(functools.partial(unpack_body, seq_size, groups, places),...  1.8 us
  transfers between devices with their start and end apart: 27, of which 14 were waited for; matrix products, arithmetic and copies ran while one was open for 0% of the time, Pallas kernels for 24%

profile of v6, /device:TPU:0, one launch (start us, length us, event | category | flops | bytes accessed | tf_op | source)
XLA Modules:
  0.0 55.0 jit_solution(16724272419053026910)
XLA Ops:
  0.7 1.2 %copy-done = bf16[896,512]{1,0:T(8,128)(2,1)S(1)} copy-done((bf16[896,512]{1,0:T(8,128)(2,1)S(1)}, bf16[896,512]{1,0:T(8,128)(2,1)}, u32[]{:S(2)}) %copy-start) | copy-done | bytes 917528
  1.9 4.1 %collective-permute-start.3 = (bf16[896,128]{1,0:T(8,128)(2,1)S(1)}, bf16[896,128]{1,0:T(8,128)(2,1)S(1)}, u32[]{:S(2)}, u32[]{:S(2)}) collective-permute-start(bf16[896,128]{1,0:T(8,128)(2,1)S(1)} %constant_dynamic-slice_fusion.refs_5_), channel_id=1, source_target_pairs={{0,16},{4,20},{8,24},{12,28},{16,0},{20,4},{24,8},{28,12},{1,17},{... | collective-permute-start | bytes 688136 | tf_op jit(solution)/shard_map/ppermute | solution.py:27
  6.0 1.6 %collective-permute-start.4 = (bf16[896,128]{1,0:T(8,128)(2,1)S(1)}, bf16[896,128]{1,0:T(8,128)(2,1)S(1)}, u32[]{:S(2)}, u32[]{:S(2)}) collective-permute-start(bf16[896,128]{1,0:T(8,128)(2,1)S(1)} %constant_dynamic-slice_fusion.refs_5_), channel_id=1, source_target_pairs={{0,8},{4,12},{8,0},{12,4},{16,24},{20,28},{24,16},{28,20},{1,9},{5... | collective-permute-start | bytes 688136 | tf_op jit(solution)/shard_map/ppermute | solution.py:27
  7.5 1.5 %collective-permute-start.5 = (bf16[896,128]{1,0:T(8,128)(2,1)S(1)}, bf16[896,128]{1,0:T(8,128)(2,1)S(1)}, u32[]{:S(2)}, u32[]{:S(2)}) collective-permute-start(bf16[896,128]{1,0:T(8,128)(2,1)S(1)} %constant_dynamic-slice_fusion.refs_5_), channel_id=1, source_target_pairs={{0,4},{4,0},{8,12},{12,8},{16,20},{20,16},{24,28},{28,24},{1,5},{5... | collective-permute-start | bytes 688136 | tf_op jit(solution)/shard_map/ppermute | solution.py:27
  9.1 1.5 %collective-permute-start = (bf16[128,896]{1,0:T(8,128)(2,1)S(1)}, bf16[128,896]{1,0:T(8,128)(2,1)S(1)}, u32[]{:S(2)}, u32[]{:S(2)}) collective-permute-start(bf16[128,896]{1,0:T(8,128)(2,1)S(1)} %bitcast.6), channel_id=1, source_target_pairs={{0,2},{1,3},{2,0},{3,1},{4,6},{5,7},{6,4},{7,5},{8,10},{9,11},{10,... | collective-permute-start | bytes 688136 | tf_op jit(solution)/shard_map/ppermute | solution.py:27
  10.6 0.6 %copy-done.4 = s32[1,2,2]{2,1,0:T(2,128)S(1)} copy-done((s32[1,2,2]{2,1,0:T(2,128)S(1)}, s32[1,2,2]{2,1,0:T(2,128)}, u32[]{:S(2)}) %copy-start.4) | copy-done | bytes 40
  11.2 1.0 %copy-done.2 = bf16[1,128,2048]{2,1,0:T(8,128)(2,1)S(1)} copy-done((bf16[1,128,2048]{2,1,0:T(8,128)(2,1)S(1)}, bf16[1,128,2048]{2,1,0:T(8,128)(2,1)}, u32[]{:S(2)}) %copy-start.2) | copy-done | bytes 524312
  12.3 1.0 %copy-done.3 = bf16[1,128,2048]{2,1,0:T(8,128)(2,1)S(1)} copy-done((bf16[1,128,2048]{2,1,0:T(8,128)(2,1)S(1)}, bf16[1,128,2048]{2,1,0:T(8,128)(2,1)}, u32[]{:S(2)}) %copy-start.3) | copy-done | bytes 524312
  13.3 1.0 %pack.1 = (bf16[1,272,128]{2,1,0:T(8,128)(2,1)S(1)}, bf16[1,272,128]{2,1,0:T(8,128)(2,1)S(1)}, bf16[2,272,128]{2,1,0:T(8,128)(2,1)S(1)}, bf16[1,256,384]{2,1,0:T...) custom-call(s32[4]{0:T(128)S(1)} %pad_add_fusion.meta.refs_0_, ...), custom_call_target="tpu_custom_call" | custom-call | tf_op jit(solution)/shard_map/pack/pallas_call | solution.py:128
  14.3 0.6 %collective-permute-start.8 = (bf16[2,272,128]{2,1,0:T(8,128)(2,1)S(1)}, bf16[2,272,128]{2,1,0:T(8,128)(2,1)S(1)}, u32[]{:S(2)}, u32[]{:S(2)}) collective-permute-start(bf16[2,272,128]{2,1,0:T(8,128)(2,1)S(1)} %get-tuple-element.58), channel_id=1, source_target_pairs={{0,2},{1,3},{2,0},{3,1},{4,6},{5,7},{6,4},{7,5},{8,10},{9,11},{10,... | collective-permute-start | bytes 417800 | tf_op jit(solution)/shard_map/ppermute | solution.py:27
  14.9 1.7 %collective-permute-done.3.refs_6_ = bf16[896,128]{1,0:T(8,128)(2,1)S(1)} collective-permute-done((bf16[896,128]{1,0:T(8,128)(2,1)S(1)}, bf16[896,128]{1,0:T(8,128)(2,1)S(1)}, u32[]{:S(2)}, u32[]{:S(2)}) %collective-permute-start.3) | collective-permute-done | bytes 229408 | tf_op jit(solution)/shard_map/ppermute | solution.py:27
  16.8 1.5 %collective-permute-start.11 = (bf16[2,256,384]{2,1,0:T(8,128)(2,1)S(1)}, bf16[2,256,384]{2,1,0:T(8,128)(2,1)S(1)}, u32[]{:S(2)}, u32[]{:S(2)}) collective-permute-start(bf16[2,256,384]{2,1,0:T(8,128)(2,1)S(1)} %get-tuple-element.67), channel_id=1, source_target_pairs={{0,2},{1,3},{2,0},{3,1},{4,6},{5,7},{6,4},{7,5},{8,10},{9,11},{10,... | collective-permute-start | bytes 1179656 | tf_op jit(solution)/shard_map/ppermute | solution.py:27
  18.3 2.1 %collective-permute-done.8.refs_9_ = bf16[2,272,128]{2,1,0:T(8,128)(2,1)S(1)} collective-permute-done((bf16[2,272,128]{2,1,0:T(8,128)(2,1)S(1)}, bf16[2,272,128]{2,1,0:T(8,128)(2,1)S(1)}, u32[]{:S(2)}, u32[]{:S(2)}) %collective-permute-start.8) | collective-permute-done | bytes 139296 | tf_op jit(solution)/shard_map/ppermute | solution.py:27
  21.1 0.7 %collective-permute-done.9.refs_10_ = bf16[1,272,128]{2,1,0:T(8,128)(2,1)S(1)} collective-permute-done((bf16[1,272,128]{2,1,0:T(8,128)(2,1)S(1)}, bf16[1,272,128]{2,1,0:T(8,128)(2,1)S(1)}, u32[]{:S(2)}, u32[]{:S(2)}) %collective-permute-start.9) | collective-permute-done | bytes 69664 | tf_op jit(solution)/shard_map/ppermute | solution.py:27
  21.7 0.8 %collective-permute-start.10 = (bf16[896,128]{1,0:T(8,128)(2,1)S(1)}, bf16[896,128]{1,0:T(8,128)(2,1)S(1)}, u32[]{:S(2)}, u32[]{:S(2)}) collective-permute-start(bf16[896,128]{1,0:T(8,128)(2,1)S(1)} %collective-permute-done.3.refs_6_), channel_id=1, source_target_pairs={{0,4},{4,0},{8,12},{12,8},{16,20},{20,16},{24,28},{28,24},{1,5},{5... | collective-permute-start | bytes 688136 | tf_op jit(solution)/shard_map/ppermute | solution.py:27
  22.5 3.5 %attention.3 = (bf16[1,2,128,128]{3,2,1,0:T(8,128)(2,1)S(1)}, bf16[1,2,128,128]{3,2,1,0:T(8,128)(2,1)S(1)}, bf16[2,2,128,128]{3,2,1,0:T(8,128)(2,1)S(1)}, bf16[512,896]{1,0:T(8,128)(2,1)S(1)}, s32[32,128]{1,0:T(8,128)S(1)}) custom-call(s32[4]{0:T(128)S(1)} %pad_add_fusion.meta.refs_0_, bf16[128,896]{1,0:T(8,128)(2,1)S(1)} %bitcast.8, ...), custom_call_target="tpu_custom_call" | custom-call | tf_op jit(solution)/shard_map/attention/pallas_call | solution.py:292
  26.1 2.9 %collective-permute-done.6.refs_8_ = bf16[896,128]{1,0:T(8,128)(2,1)S(1)} collective-permute-done((bf16[896,128]{1,0:T(8,128)(2,1)S(1)}, bf16[896,128]{1,0:T(8,128)(2,1)S(1)}, u32[]{:S(2)}, u32[]{:S(2)}) %collective-permute-start.6) | collective-permute-done | bytes 229408 | tf_op jit(solution)/shard_map/ppermute | solution.py:27
  30.0 1.4 %collective-permute-start.17 = (bf16[896,128]{1,0:T(8,128)(2,1)S(1)}, bf16[896,128]{1,0:T(8,128)(2,1)S(1)}, u32[]{:S(2)}, u32[]{:S(2)}) collective-permute-start(bf16[896,128]{1,0:T(8,128)(2,1)S(1)} %collective-permute-done.5.refs_5_), channel_id=1, source_target_pairs={{0,8},{4,12},{8,0},{12,4},{16,24},{20,28},{24,16},{28,20},{1,9},{5... | collective-permute-start | bytes 688136 | tf_op jit(solution)/shard_map/ppermute | solution.py:27
  31.9 3.6 %attention.4 = (bf16[1,2,128,256]{3,2,1,0:T(8,128)(2,1)S(1)}, bf16[1,2,128,256]{3,2,1,0:T(8,128)(2,1)S(1)}, bf16[2,2,128,256]{3,2,1,0:T(8,128)(2,1)S(1)}, bf16[512,896]{1,0:T(8,128)(2,1)S(1)}) custom-call(s32[4]{0:T(128)S(1)} %pad_add_fusion.meta.refs_0_, bf16[128,896]{1,0:T(8,128)(2,1)S(1)} %bitcast.9, bf16[128,896]{1,0:T(8,128)(2,1)S(1)} %collective-permute-done.refs_2_, ...), custom_call_target="tpu_custom_call" | custom-call | tf_op jit(solution)/shard_map/attention/pallas_call | solution.py:292
  35.5 1.9 %collective-permute-start.19 = (bf16[2,2,128,256]{3,2,1,0:T(8,128)(2,1)S(1)}, bf16[2,2,128,256]{3,2,1,0:T(8,128)(2,1)S(1)}, u32[]{:S(2)}, u32[]{:S(2)}) collective-permute-start(bf16[2,2,128,256]{3,2,1,0:T(8,128)(2,1)S(1)} %get-tuple-element.90), channel_id=1, source_target_pairs={{0,2},{1,3},{2,0},{3,1},{4,6},{5,7},{6,4},{7,5},{8,10},{9,11},{10,... | collective-permute-start | bytes 786440 | tf_op jit(solution)/shard_map/ppermute | solution.py:27
  37.6 1.1 %collective-permute-done.18.refs_6_ = bf16[896,128]{1,0:T(8,128)(2,1)S(1)} collective-permute-done((bf16[896,128]{1,0:T(8,128)(2,1)S(1)}, bf16[896,128]{1,0:T(8,128)(2,1)S(1)}, u32[]{:S(2)}, u32[]{:S(2)}) %collective-permute-start.18) | collective-permute-done | bytes 229408 | tf_op jit(solution)/shard_map/ppermute | solution.py:27
  38.7 3.3 %attention.5 = (bf16[1,2,128,128]{3,2,1,0:T(8,128)(2,1)S(1)}, bf16[1,2,128,128]{3,2,1,0:T(8,128)(2,1)S(1)}, bf16[2,2,128,128]{3,2,1,0:T(8,128)(2,1)S(1)}, f32[256,896]{1,0:T(8,128)S(1)}, bf16[256,896]{1,0:T(8,128)(2,1)S(1)}) custom-call(s32[4]{0:T(128)S(1)} %pad_add_fusion.meta.refs_0_, bf16[128,896]{1,0:T(8,128)(2,1)S(1)} %bitcast.10, ...), custom_call_target="tpu_custom_call" | custom-call | flops 2400000000 | tf_op jit(solution)/shard_map/attention/pallas_call | solution.py:292
  42.0 1.4 %collective-permute-done.19.refs_6_ = bf16[2,2,128,256]{3,2,1,0:T(8,128)(2,1)S(1)} collective-permute-done((bf16[2,2,128,256]{3,2,1,0:T(8,128)(2,1)S(1)}, bf16[2,2,128,256]{3,2,1,0:T(8,128)(2,1)S(1)}, u32[]{:S(2)}, u32[]{:S(2)}) %collective-permute-start.19) | collective-permute-done | bytes 262176 | tf_op jit(solution)/shard_map/ppermute | solution.py:27
  43.4 1.5 %collective-permute-start.23 = (bf16[2,2,128,128]{3,2,1,0:T(8,128)(2,1)S(1)}, bf16[2,2,128,128]{3,2,1,0:T(8,128)(2,1)S(1)}, u32[]{:S(2)}, u32[]{:S(2)}) collective-permute-start(bf16[2,2,128,128]{3,2,1,0:T(8,128)(2,1)S(1)} %get-tuple-element.96), channel_id=1, source_target_pairs={{0,2},{1,3},{2,0},{3,1},{4,6},{5,7},{6,4},{7,5},{8,10},{9,11},{10,... | collective-permute-start | bytes 393224 | tf_op jit(solution)/shard_map/ppermute | solution.py:27
  45.3 1.5 %collective-permute-start.26 = (bf16[128,896]{1,0:T(8,128)(2,1)S(1)}, bf16[128,896]{1,0:T(8,128)(2,1)S(1)}, u32[]{:S(2)}, u32[]{:S(2)}) collective-permute-start(bf16[128,896]{1,0:T(8,128)(2,1)S(1)} %slice.35), channel_id=1, source_target_pairs={{0,2},{1,3},{2,0},{3,1},{4,6},{5,7},{6,4},{7,5},{8,10},{9,11},{10,... | collective-permute-start | bytes 688136 | tf_op jit(solution)/shard_map/ppermute | solution.py:27
  46.9 0.5 collective-permute-start.15
  47.5 2.1 %collective-permute-done.23.refs_10_ = bf16[2,2,128,128]{3,2,1,0:T(8,128)(2,1)S(1)} collective-permute-done((bf16[2,2,128,128]{3,2,1,0:T(8,128)(2,1)S(1)}, bf16[2,2,128,128]{3,2,1,0:T(8,128)(2,1)S(1)}, u32[]{:S(2)}, u32[]{:S(2)}) %collective-permute-start.23) | collective-permute-done | bytes 131104 | tf_op jit(solution)/shard_map/ppermute | solution.py:27
  49.7 0.6 %collective-permute-start.22 = (bf16[1,2,128,128]{3,2,1,0:T(8,128)(2,1)S(1)}, bf16[1,2,128,128]{3,2,1,0:T(8,128)(2,1)S(1)}, u32[]{:S(2)}, u32[]{:S(2)}) collective-permute-start(bf16[1,2,128,128]{3,2,1,0:T(8,128)(2,1)S(1)} %get-tuple-element.95), channel_id=1, source_target_pairs={{0,1},{1,0},{2,3},{3,2},{4,5},{5,4},{6,7},{7,6},{8,9},{9,8},{10,11... | collective-permute-start | bytes 196616 | tf_op jit(solution)/shard_map/ppermute | solution.py:27
  50.3 0.8 %collective-permute-done.22.refs_9_ = bf16[1,2,128,128]{3,2,1,0:T(8,128)(2,1)S(1)} collective-permute-done((bf16[1,2,128,128]{3,2,1,0:T(8,128)(2,1)S(1)}, bf16[1,2,128,128]{3,2,1,0:T(8,128)(2,1)S(1)}, u32[]{:S(2)}, u32[]{:S(2)}) %collective-permute-start.22) | collective-permute-done | bytes 65568 | tf_op jit(solution)/shard_map/ppermute | solution.py:27
  51.5 1.8 %unpack.1 = (bf16[1,128,2048]{2,1,0:T(8,128)(2,1)}, bf16[1,128,2048]{2,1,0:T(8,128)(2,1)}) custom-call(s32[4]{0:T(128)S(1)} %pad_add_fusion.meta.refs_0_, bf16[1,2,128,128]{3,2,1,0:T(8,128)(2,1)S(1)} %get-tuple-element.82.refs_0_, bf16[1,2,128,128]{3,2,1,0:T(8,128)(2,1)S(1)} %collective-permute-done.15.refs_1_, ...), custom_call_target="tpu_custom_call" | custom-call | tf_op jit(solution)/shard_map/unpack/pallas_call | solution.py:327
  53.3 0.9 %collective-permute-done.26 = bf16[128,896]{1,0:T(8,128)(2,1)S(1)} collective-permute-done((bf16[128,896]{1,0:T(8,128)(2,1)S(1)}, bf16[128,896]{1,0:T(8,128)(2,1)S(1)}, u32[]{:S(2)}, u32[]{:S(2)}) %collective-permute-start.26) | collective-permute-done | bytes 229408 | tf_op jit(solution)/shard_map/ppermute | solution.py:27
  54.2 0.8 %slice_add_fusion = f32[128,896]{1,0:T(8,128)} fusion(f32[256,896]{1,0:T(8,128)S(1)} %convert_add_fusion, bf16[128,896]{1,0:T(8,128)(2,1)S(1)} %collective-permute-done.26), kind=kLoop, calls=%fused_computation.2 | loop fusion | flops 229376 | bytes 1146880 | tf_op jit(solution)/shard_map/add | solution.py:436
  (49 shorter events, 3.7 us)
Async XLA Ops:
  0.6 1.2 %copy-start = (bf16[896,512]{1,0:T(8,128)(2,1)S(1)}, bf16[896,512]{1,0:T(8,128)(2,1)}, u32[]{:S(2)}) copy-start(bf16[896,512]{1,0:T(8,128)(2,1)} %param.9) | copy-start | bytes 2752516
  1.8 7.2 %copy-start.1 = (bf16[1,2,64,896]{3,2,1,0:T(8,128)(2,1)S(1)}, bf16[1,2,64,896]{3,2,1,0:T(8,128)(2,1)}, u32[]{:S(2)}) copy-start(bf16[1,2,64,896]{3,2,1,0:T(8,128)(2,1)} %param.8) | copy-start | bytes 688132
  1.9 14.7 %collective-permute-start.3 = (bf16[896,128]{1,0:T(8,128)(2,1)S(1)}, bf16[896,128]{1,0:T(8,128)(2,1)S(1)}, u32[]{:S(2)}, u32[]{:S(2)}) collective-permute-start(bf16[896,128]{1,0:T(8,128)(2,1)S(1)} %constant_dynamic-slice_fusion.refs_5_), channel_id=1, source_target_pairs={{0,16},{4,20},{8,24},{12,28},{16,0},{20,4},{24,8},{28,12},{1,17},{... | collective-permute-start | bytes 688136 | tf_op jit(solution)/shard_map/ppermute | solution.py:27
  6.0 10.8 %collective-permute-start.4 = (bf16[896,128]{1,0:T(8,128)(2,1)S(1)}, bf16[896,128]{1,0:T(8,128)(2,1)S(1)}, u32[]{:S(2)}, u32[]{:S(2)}) collective-permute-start(bf16[896,128]{1,0:T(8,128)(2,1)S(1)} %constant_dynamic-slice_fusion.refs_5_), channel_id=1, source_target_pairs={{0,8},{4,12},{8,0},{12,4},{16,24},{20,28},{24,16},{28,20},{1,9},{5... | collective-permute-start | bytes 688136 | tf_op jit(solution)/shard_map/ppermute | solution.py:27
  7.5 9.2 %collective-permute-start.5 = (bf16[896,128]{1,0:T(8,128)(2,1)S(1)}, bf16[896,128]{1,0:T(8,128)(2,1)S(1)}, u32[]{:S(2)}, u32[]{:S(2)}) collective-permute-start(bf16[896,128]{1,0:T(8,128)(2,1)S(1)} %constant_dynamic-slice_fusion.refs_5_), channel_id=1, source_target_pairs={{0,4},{4,0},{8,12},{12,8},{16,20},{20,16},{24,28},{28,24},{1,5},{5... | collective-permute-start | bytes 688136 | tf_op jit(solution)/shard_map/ppermute | solution.py:27
  9.1 11.9 %collective-permute-start = (bf16[128,896]{1,0:T(8,128)(2,1)S(1)}, bf16[128,896]{1,0:T(8,128)(2,1)S(1)}, u32[]{:S(2)}, u32[]{:S(2)}) collective-permute-start(bf16[128,896]{1,0:T(8,128)(2,1)S(1)} %bitcast.6), channel_id=1, source_target_pairs={{0,2},{1,3},{2,0},{3,1},{4,6},{5,7},{6,4},{7,5},{8,10},{9,11},{10,... | collective-permute-start | bytes 688136 | tf_op jit(solution)/shard_map/ppermute | solution.py:27
  10.5 0.7 %copy-start.5 = (s32[1,8]{1,0:T(1,128)S(1)}, s32[1,8]{1,0:T(1,128)}, u32[]{:S(2)}) copy-start(s32[1,8]{1,0:T(1,128)} %slots.1) | copy-start | bytes 100
  11.2 1.0 %copy-start.2 = (bf16[1,128,2048]{2,1,0:T(8,128)(2,1)S(1)}, bf16[1,128,2048]{2,1,0:T(8,128)(2,1)}, u32[]{:S(2)}) copy-start(bf16[1,128,2048]{2,1,0:T(8,128)(2,1)} %queries.1) | copy-start | bytes 1572868
  12.3 1.0 %copy-start.3 = (bf16[1,128,2048]{2,1,0:T(8,128)(2,1)S(1)}, bf16[1,128,2048]{2,1,0:T(8,128)(2,1)}, u32[]{:S(2)}) copy-start(bf16[1,128,2048]{2,1,0:T(8,128)(2,1)} %grad_out.1) | copy-start | bytes 1572868
  14.3 6.2 %collective-permute-start.8 = (bf16[2,272,128]{2,1,0:T(8,128)(2,1)S(1)}, bf16[2,272,128]{2,1,0:T(8,128)(2,1)S(1)}, u32[]{:S(2)}, u32[]{:S(2)}) collective-permute-start(bf16[2,272,128]{2,1,0:T(8,128)(2,1)S(1)} %get-tuple-element.58), channel_id=1, source_target_pairs={{0,2},{1,3},{2,0},{3,1},{4,6},{5,7},{6,4},{7,5},{8,10},{9,11},{10,... | collective-permute-start | bytes 417800 | tf_op jit(solution)/shard_map/ppermute | solution.py:27
  16.8 12.6 %collective-permute-start.11 = (bf16[2,256,384]{2,1,0:T(8,128)(2,1)S(1)}, bf16[2,256,384]{2,1,0:T(8,128)(2,1)S(1)}, u32[]{:S(2)}, u32[]{:S(2)}) collective-permute-start(bf16[2,256,384]{2,1,0:T(8,128)(2,1)S(1)} %get-tuple-element.67), channel_id=1, source_target_pairs={{0,2},{1,3},{2,0},{3,1},{4,6},{5,7},{6,4},{7,5},{8,10},{9,11},{10,... | collective-permute-start | bytes 1179656 | tf_op jit(solution)/shard_map/ppermute | solution.py:27
  18.3 2.7 %collective-permute-start.7 = (bf16[1,272,128]{2,1,0:T(8,128)(2,1)S(1)}, bf16[1,272,128]{2,1,0:T(8,128)(2,1)S(1)}, u32[]{:S(2)}, u32[]{:S(2)}) collective-permute-start(bf16[1,272,128]{2,1,0:T(8,128)(2,1)S(1)} %get-tuple-element.57), channel_id=1, source_target_pairs={{0,1},{1,0},{2,3},{3,2},{4,5},{5,4},{6,7},{7,6},{8,9},{9,8},{10,11... | collective-permute-start | bytes 208904 | tf_op jit(solution)/shard_map/ppermute | solution.py:27
  20.5 1.3 %collective-permute-start.9 = (bf16[1,272,128]{2,1,0:T(8,128)(2,1)S(1)}, bf16[1,272,128]{2,1,0:T(8,128)(2,1)S(1)}, u32[]{:S(2)}, u32[]{:S(2)}) collective-permute-start(bf16[1,272,128]{2,1,0:T(8,128)(2,1)S(1)} %slice.29), channel_id=1, source_target_pairs={{0,1},{1,0},{2,3},{3,2},{4,5},{5,4},{6,7},{7,6},{8,9},{9,8},{10,11... | collective-permute-start | bytes 208904 | tf_op jit(solution)/shard_map/ppermute | solution.py:27
  20.5 2.1 %collective-permute-start.1 = (bf16[128,896]{1,0:T(8,128)(2,1)S(1)}, bf16[128,896]{1,0:T(8,128)(2,1)S(1)}, u32[]{:S(2)}, u32[]{:S(2)}) collective-permute-start(bf16[128,896]{1,0:T(8,128)(2,1)S(1)} %bitcast.7), channel_id=1, source_target_pairs={{0,1},{1,0},{2,3},{3,2},{4,5},{5,4},{6,7},{7,6},{8,9},{9,8},{10,11... | collective-permute-start | bytes 688136 | tf_op jit(solution)/shard_map/ppermute | solution.py:27
  21.0 1.6 %collective-permute-start.2 = (bf16[128,896]{1,0:T(8,128)(2,1)S(1)}, bf16[128,896]{1,0:T(8,128)(2,1)S(1)}, u32[]{:S(2)}, u32[]{:S(2)}) collective-permute-start(bf16[128,896]{1,0:T(8,128)(2,1)S(1)} %collective-permute-done.refs_2_), channel_id=1, source_target_pairs={{0,1},{1,0},{2,3},{3,2},{4,5},{5,4},{6,7},{7,6},{8,9},{9,8},{10,11... | collective-permute-start | bytes 688136 | tf_op jit(solution)/shard_map/ppermute | solution.py:27
  21.1 7.9 %collective-permute-start.6 = (bf16[896,128]{1,0:T(8,128)(2,1)S(1)}, bf16[896,128]{1,0:T(8,128)(2,1)S(1)}, u32[]{:S(2)}, u32[]{:S(2)}) collective-permute-start(bf16[896,128]{1,0:T(8,128)(2,1)S(1)} %collective-permute-done.3.refs_6_), channel_id=1, source_target_pairs={{0,8},{4,12},{8,0},{12,4},{16,24},{20,28},{24,16},{28,20},{1,9},{5... | collective-permute-start | bytes 688136 | tf_op jit(solution)/shard_map/ppermute | solution.py:27
  21.7 7.7 %collective-permute-start.10 = (bf16[896,128]{1,0:T(8,128)(2,1)S(1)}, bf16[896,128]{1,0:T(8,128)(2,1)S(1)}, u32[]{:S(2)}, u32[]{:S(2)}) collective-permute-start(bf16[896,128]{1,0:T(8,128)(2,1)S(1)} %collective-permute-done.3.refs_6_), channel_id=1, source_target_pairs={{0,4},{4,0},{8,12},{12,8},{16,20},{20,16},{24,28},{28,24},{1,5},{5... | collective-permute-start | bytes 688136 | tf_op jit(solution)/shard_map/ppermute | solution.py:27
  29.4 2.4 %collective-permute-start.13 = (bf16[1,256,384]{2,1,0:T(8,128)(2,1)S(1)}, bf16[1,256,384]{2,1,0:T(8,128)(2,1)S(1)}, u32[]{:S(2)}, u32[]{:S(2)}) collective-permute-start(bf16[1,256,384]{2,1,0:T(8,128)(2,1)S(1)} %slice.23), channel_id=1, source_target_pairs={{0,1},{1,0},{2,3},{3,2},{4,5},{5,4},{6,7},{7,6},{8,9},{9,8},{10,11... | collective-permute-start | bytes 589832 | tf_op jit(solution)/shard_map/ppermute | solution.py:27
  29.5 2.4 %collective-permute-start.12 = (bf16[1,256,384]{2,1,0:T(8,128)(2,1)S(1)}, bf16[1,256,384]{2,1,0:T(8,128)(2,1)S(1)}, u32[]{:S(2)}, u32[]{:S(2)}) collective-permute-start(bf16[1,256,384]{2,1,0:T(8,128)(2,1)S(1)} %get-tuple-element.74), channel_id=1, source_target_pairs={{0,1},{1,0},{2,3},{3,2},{4,5},{5,4},{6,7},{7,6},{8,9},{9,8},{10,11... | collective-permute-start | bytes 589832 | tf_op jit(solution)/shard_map/ppermute | solution.py:27
  30.0 7.6 %collective-permute-start.17 = (bf16[896,128]{1,0:T(8,128)(2,1)S(1)}, bf16[896,128]{1,0:T(8,128)(2,1)S(1)}, u32[]{:S(2)}, u32[]{:S(2)}) collective-permute-start(bf16[896,128]{1,0:T(8,128)(2,1)S(1)} %collective-permute-done.5.refs_5_), channel_id=1, source_target_pairs={{0,8},{4,12},{8,0},{12,4},{16,24},{20,28},{24,16},{28,20},{1,9},{5... | collective-permute-start | bytes 688136 | tf_op jit(solution)/shard_map/ppermute | solution.py:27
  31.4 7.3 %collective-permute-start.18 = (bf16[896,128]{1,0:T(8,128)(2,1)S(1)}, bf16[896,128]{1,0:T(8,128)(2,1)S(1)}, u32[]{:S(2)}, u32[]{:S(2)}) collective-permute-start(bf16[896,128]{1,0:T(8,128)(2,1)S(1)} %collective-permute-done.6.refs_8_), channel_id=1, source_target_pairs={{0,4},{4,0},{8,12},{12,8},{16,20},{20,16},{24,28},{28,24},{1,5},{5... | collective-permute-start | bytes 688136 | tf_op jit(solution)/shard_map/ppermute | solution.py:27
  31.6 5.7 %collective-permute-start.14 = (bf16[2,2,128,128]{3,2,1,0:T(8,128)(2,1)S(1)}, bf16[2,2,128,128]{3,2,1,0:T(8,128)(2,1)S(1)}, u32[]{:S(2)}, u32[]{:S(2)}) collective-permute-start(bf16[2,2,128,128]{3,2,1,0:T(8,128)(2,1)S(1)} %get-tuple-element.81), channel_id=1, source_target_pairs={{0,2},{1,3},{2,0},{3,1},{4,6},{5,7},{6,4},{7,5},{8,10},{9,11},{10,... | collective-permute-start | bytes 393224 | tf_op jit(solution)/shard_map/ppermute | solution.py:27
  35.5 7.9 %collective-permute-start.19 = (bf16[2,2,128,256]{3,2,1,0:T(8,128)(2,1)S(1)}, bf16[2,2,128,256]{3,2,1,0:T(8,128)(2,1)S(1)}, u32[]{:S(2)}, u32[]{:S(2)}) collective-permute-start(bf16[2,2,128,256]{3,2,1,0:T(8,128)(2,1)S(1)} %get-tuple-element.90), channel_id=1, source_target_pairs={{0,2},{1,3},{2,0},{3,1},{4,6},{5,7},{6,4},{7,5},{8,10},{9,11},{10,... | collective-permute-start | bytes 786440 | tf_op jit(solution)/shard_map/ppermute | solution.py:27
  43.4 1.8 %collective-permute-start.25 = (bf16[256,896]{1,0:T(8,128)(2,1)S(1)}, bf16[256,896]{1,0:T(8,128)(2,1)S(1)}, u32[]{:S(2)}, u32[]{:S(2)}) collective-permute-start(bf16[256,896]{1,0:T(8,128)(2,1)S(1)} %get-tuple-element.100), channel_id=1, source_target_pairs={{0,1},{1,0},{2,3},{3,2},{4,5},{5,4},{6,7},{7,6},{8,9},{9,8},{10,11... | collective-permute-start | bytes 1376264 | tf_op jit(solution)/shard_map/ppermute | solution.py:27
  43.4 6.3 %collective-permute-start.23 = (bf16[2,2,128,128]{3,2,1,0:T(8,128)(2,1)S(1)}, bf16[2,2,128,128]{3,2,1,0:T(8,128)(2,1)S(1)}, u32[]{:S(2)}, u32[]{:S(2)}) collective-permute-start(bf16[2,2,128,128]{3,2,1,0:T(8,128)(2,1)S(1)} %get-tuple-element.96), channel_id=1, source_target_pairs={{0,2},{1,3},{2,0},{3,1},{4,6},{5,7},{6,4},{7,5},{8,10},{9,11},{10,... | collective-permute-start | bytes 393224 | tf_op jit(solution)/shard_map/ppermute | solution.py:27
  45.3 8.9 %collective-permute-start.26 = (bf16[128,896]{1,0:T(8,128)(2,1)S(1)}, bf16[128,896]{1,0:T(8,128)(2,1)S(1)}, u32[]{:S(2)}, u32[]{:S(2)}) collective-permute-start(bf16[128,896]{1,0:T(8,128)(2,1)S(1)} %slice.35), channel_id=1, source_target_pairs={{0,2},{1,3},{2,0},{3,1},{4,6},{5,7},{6,4},{7,5},{8,10},{9,11},{10,... | collective-permute-start | bytes 688136 | tf_op jit(solution)/shard_map/ppermute | solution.py:27
  46.9 2.8 %collective-permute-start.16 = (bf16[1,2,128,128]{3,2,1,0:T(8,128)(2,1)S(1)}, bf16[1,2,128,128]{3,2,1,0:T(8,128)(2,1)S(1)}, u32[]{:S(2)}, u32[]{:S(2)}) collective-permute-start(bf16[1,2,128,128]{3,2,1,0:T(8,128)(2,1)S(1)} %slice.24), channel_id=1, source_target_pairs={{0,1},{1,0},{2,3},{3,2},{4,5},{5,4},{6,7},{7,6},{8,9},{9,8},{10,11... | collective-permute-start | bytes 196616 | tf_op jit(solution)/shard_map/ppermute | solution.py:27
  46.9 3.4 %collective-permute-start.15 = (bf16[1,2,128,128]{3,2,1,0:T(8,128)(2,1)S(1)}, bf16[1,2,128,128]{3,2,1,0:T(8,128)(2,1)S(1)}, u32[]{:S(2)}, u32[]{:S(2)}) collective-permute-start(bf16[1,2,128,128]{3,2,1,0:T(8,128)(2,1)S(1)} %get-tuple-element.83), channel_id=1, source_target_pairs={{0,1},{1,0},{2,3},{3,2},{4,5},{5,4},{6,7},{7,6},{8,9},{9,8},{10,11... | collective-permute-start | bytes 196616 | tf_op jit(solution)/shard_map/ppermute | solution.py:27
  47.4 4.1 %collective-permute-start.21 = (bf16[1,2,128,256]{3,2,1,0:T(8,128)(2,1)S(1)}, bf16[1,2,128,256]{3,2,1,0:T(8,128)(2,1)S(1)}, u32[]{:S(2)}, u32[]{:S(2)}) collective-permute-start(bf16[1,2,128,256]{3,2,1,0:T(8,128)(2,1)S(1)} %slice.25), channel_id=1, source_target_pairs={{0,1},{1,0},{2,3},{3,2},{4,5},{5,4},{6,7},{7,6},{8,9},{9,8},{10,11... | collective-permute-start | bytes 393224 | tf_op jit(solution)/shard_map/ppermute | solution.py:27
  49.7 1.9 %collective-permute-start.20 = (bf16[1,2,128,256]{3,2,1,0:T(8,128)(2,1)S(1)}, bf16[1,2,128,256]{3,2,1,0:T(8,128)(2,1)S(1)}, u32[]{:S(2)}, u32[]{:S(2)}) collective-permute-start(bf16[1,2,128,256]{3,2,1,0:T(8,128)(2,1)S(1)} %get-tuple-element.92), channel_id=1, source_target_pairs={{0,1},{1,0},{2,3},{3,2},{4,5},{5,4},{6,7},{7,6},{8,9},{9,8},{10,11... | collective-permute-start | bytes 393224 | tf_op jit(solution)/shard_map/ppermute | solution.py:27
  49.7 1.5 %collective-permute-start.22 = (bf16[1,2,128,128]{3,2,1,0:T(8,128)(2,1)S(1)}, bf16[1,2,128,128]{3,2,1,0:T(8,128)(2,1)S(1)}, u32[]{:S(2)}, u32[]{:S(2)}) collective-permute-start(bf16[1,2,128,128]{3,2,1,0:T(8,128)(2,1)S(1)} %get-tuple-element.95), channel_id=1, source_target_pairs={{0,1},{1,0},{2,3},{3,2},{4,5},{5,4},{6,7},{7,6},{8,9},{9,8},{10,11... | collective-permute-start | bytes 196616 | tf_op jit(solution)/shard_map/ppermute | solution.py:27
  50.3 1.3 %collective-permute-start.24 = (bf16[1,2,128,128]{3,2,1,0:T(8,128)(2,1)S(1)}, bf16[1,2,128,128]{3,2,1,0:T(8,128)(2,1)S(1)}, u32[]{:S(2)}, u32[]{:S(2)}) collective-permute-start(bf16[1,2,128,128]{3,2,1,0:T(8,128)(2,1)S(1)} %slice.30), channel_id=1, source_target_pairs={{0,1},{1,0},{2,3},{3,2},{4,5},{5,4},{6,7},{7,6},{8,9},{9,8},{10,11... | collective-permute-start | bytes 196616 | tf_op jit(solution)/shard_map/ppermute | solution.py:27
  (1 other events, 0.7 us)

commit v7 on v6

--- a/solution.py
+++ b/solution.py
@@ -177,14 +177,12 @@
     grads, refs = (refs[:2], refs[2:]) if last else (refs[:1], refs[1:])
     if finds:
         table, refs = refs[0], refs[1:]
-    enc, pair, kv, d_kv, found, sem = refs
+    pair, kv, d_kv, found, sem = refs
     block = stored[0].shape[0]
-    rows = enc.shape[0]
+    rows = d_kv.shape[0]
     tokens = spans * SPAN
     scale = HEAD_SIZE ** (-0.5)
     keys_first = meta[2] == 1
-    for i in range(seq_size):
-        enc[i * block : (i + 1) * block] = stored[i][...]
     if finds:
         for k, rows_of in enumerate(relative_positions(pieces[:seq_size], meta[0], per_owner, tokens)):
             table[8 * k : 8 * k + 8, :] = rows_of
@@ -195,7 +193,10 @@
         pair[:, 2 * i * HEAD_SIZE : (2 * i + 1) * HEAD_SIZE] = jnp.where(keys_first, first, second)
         pair[:, (2 * i + 1) * HEAD_SIZE : (2 * i + 2) * HEAD_SIZE] = jnp.where(keys_first, second, first)
         wide = slice(2 * i * HEAD_SIZE, 2 * (i + 1) * HEAD_SIZE)
-        kv[:, wide] = jnp.dot(enc[...], pair[:, wide], preferred_element_type=jnp.float32).astype(jnp.bfloat16)
+        for n in range(seq_size):
+            kv[n * block : (n + 1) * block, wide] = jnp.dot(
+                stored[n][...], pair[:, wide], preferred_element_type=jnp.float32
+            ).astype(jnp.bfloat16)
     d_kv[...] = jnp.zeros_like(d_kv)
     copy.wait()
     units = [(i, *spot) for i in range(count) for spot in spots_of(found, seq_size, spans)]
@@ -280,7 +281,6 @@
         out_shape.append(jax.ShapeDtypeStruct((rows, width), jnp.bfloat16))
     grads = len(out_shape) - levels
     scratch = [
-        pltpu.VMEM((rows, width), jnp.bfloat16),
         pltpu.VMEM((width, 2 * count * HEAD_SIZE), jnp.bfloat16),
         pltpu.VMEM((rows, 2 * count * HEAD_SIZE), jnp.bfloat16),
         pltpu.VMEM((rows, 2 * count * HEAD_SIZE), jnp.float32),

time: 55.3 us -> 55.3 us (level)
  waiting for transfers between devices: 15.2 us -> 16.2 us
  Pallas kernels: 13.2 us -> 12.3 us
    ppermute x27, waiting for transfers between devices: 15.2 us -> 16.2 us  [xor_send(): return lax.ppermute(value, axis, [(i, i ^ bit) for i in range(size)])]
    pallas_call x3, Pallas kernels: 10.5 us -> 9.57 us  [attention(): pl.pallas_call(functools.partial(attention_body, seq_size, spans, takes,...]
  transfers between devices with their start and end apart: 27 -> 27, of which waited for: 14 -> 14; matrix products, arithmetic and copies ran while one was open for 0% -> 0% of each run, Pallas kernels for 24% -> 22%
where the time goes in v7:
time: 55.3 us; the launch traced here: 55 us
  starting transfers between devices  20.8 us (38%)
  waiting for transfers between devices  16.2 us (29%)
  Pallas kernels  12.3 us (22%)
  local copies, waits for them, and re-layouts  3.97 us (7%)
  other arithmetic  0.99 us (2%)
  between operations  0.76 us (1%)
    ppermute x27, starting transfers between devices, xor_send(): return lax.ppermute(value, axis, [(i, i ^ bit) for i in range(size)])  20.8 us
    ppermute x27, waiting for transfers between devices, xor_send(): return lax.ppermute(value, axis, [(i, i ^ bit) for i in range(size)])  16.2 us
    pallas_call x3, Pallas kernels, attention(): pl.pallas_call(functools.partial(attention_body, seq_size, spans, takes,...  9.57 us
    unnamed x12, local copies, waits for them, and re-layouts  3.86 us
    pallas_call x1, Pallas kernels, unpack(): pl.pallas_call(functools.partial(unpack_body, seq_size, groups, places),...  1.8 us
  transfers between devices with their start and end apart: 27, of which 14 were waited for; matrix products, arithmetic and copies ran while one was open for 0% of the time, Pallas kernels for 22%

profile of v7, /device:TPU:0, one launch (start us, length us, event | category | flops | bytes accessed | tf_op | source)
XLA Modules:
  0.0 55.0 jit_solution(2783420055526931952)
XLA Ops:
  0.7 1.2 %copy-done = bf16[896,512]{1,0:T(8,128)(2,1)S(1)} copy-done((bf16[896,512]{1,0:T(8,128)(2,1)S(1)}, bf16[896,512]{1,0:T(8,128)(2,1)}, u32[]{:S(2)}) %copy-start) | copy-done | bytes 917528
  1.9 4.1 %collective-permute-start.3 = (bf16[896,128]{1,0:T(8,128)(2,1)S(1)}, bf16[896,128]{1,0:T(8,128)(2,1)S(1)}, u32[]{:S(2)}, u32[]{:S(2)}) collective-permute-start(bf16[896,128]{1,0:T(8,128)(2,1)S(1)} %constant_dynamic-slice_fusion.refs_5_), channel_id=1, source_target_pairs={{0,16},{4,20},{8,24},{12,28},{16,0},{20,4},{24,8},{28,12},{1,17},{... | collective-permute-start | bytes 688136 | tf_op jit(solution)/shard_map/ppermute | solution.py:27
  6.0 1.6 %collective-permute-start.4 = (bf16[896,128]{1,0:T(8,128)(2,1)S(1)}, bf16[896,128]{1,0:T(8,128)(2,1)S(1)}, u32[]{:S(2)}, u32[]{:S(2)}) collective-permute-start(bf16[896,128]{1,0:T(8,128)(2,1)S(1)} %constant_dynamic-slice_fusion.refs_5_), channel_id=1, source_target_pairs={{0,8},{4,12},{8,0},{12,4},{16,24},{20,28},{24,16},{28,20},{1,9},{5... | collective-permute-start | bytes 688136 | tf_op jit(solution)/shard_map/ppermute | solution.py:27
  7.5 1.5 %collective-permute-start.5 = (bf16[896,128]{1,0:T(8,128)(2,1)S(1)}, bf16[896,128]{1,0:T(8,128)(2,1)S(1)}, u32[]{:S(2)}, u32[]{:S(2)}) collective-permute-start(bf16[896,128]{1,0:T(8,128)(2,1)S(1)} %constant_dynamic-slice_fusion.refs_5_), channel_id=1, source_target_pairs={{0,4},{4,0},{8,12},{12,8},{16,20},{20,16},{24,28},{28,24},{1,5},{5... | collective-permute-start | bytes 688136 | tf_op jit(solution)/shard_map/ppermute | solution.py:27
  9.1 1.5 %collective-permute-start = (bf16[128,896]{1,0:T(8,128)(2,1)S(1)}, bf16[128,896]{1,0:T(8,128)(2,1)S(1)}, u32[]{:S(2)}, u32[]{:S(2)}) collective-permute-start(bf16[128,896]{1,0:T(8,128)(2,1)S(1)} %bitcast.6), channel_id=1, source_target_pairs={{0,2},{1,3},{2,0},{3,1},{4,6},{5,7},{6,4},{7,5},{8,10},{9,11},{10,... | collective-permute-start | bytes 688136 | tf_op jit(solution)/shard_map/ppermute | solution.py:27
  10.6 0.6 %copy-done.4 = s32[1,2,2]{2,1,0:T(2,128)S(1)} copy-done((s32[1,2,2]{2,1,0:T(2,128)S(1)}, s32[1,2,2]{2,1,0:T(2,128)}, u32[]{:S(2)}) %copy-start.4) | copy-done | bytes 40
  11.2 1.0 %copy-done.2 = bf16[1,128,2048]{2,1,0:T(8,128)(2,1)S(1)} copy-done((bf16[1,128,2048]{2,1,0:T(8,128)(2,1)S(1)}, bf16[1,128,2048]{2,1,0:T(8,128)(2,1)}, u32[]{:S(2)}) %copy-start.2) | copy-done | bytes 524312
  12.3 1.0 %copy-done.3 = bf16[1,128,2048]{2,1,0:T(8,128)(2,1)S(1)} copy-done((bf16[1,128,2048]{2,1,0:T(8,128)(2,1)S(1)}, bf16[1,128,2048]{2,1,0:T(8,128)(2,1)}, u32[]{:S(2)}) %copy-start.3) | copy-done | bytes 524312
  13.3 1.0 %pack.1 = (bf16[1,272,128]{2,1,0:T(8,128)(2,1)S(1)}, bf16[1,272,128]{2,1,0:T(8,128)(2,1)S(1)}, bf16[2,272,128]{2,1,0:T(8,128)(2,1)S(1)}, bf16[1,256,384]{2,1,0:T...) custom-call(s32[4]{0:T(128)S(1)} %pad_add_fusion.meta.refs_0_, ...), custom_call_target="tpu_custom_call" | custom-call | tf_op jit(solution)/shard_map/pack/pallas_call | solution.py:128
  14.3 0.6 %collective-permute-start.8 = (bf16[2,272,128]{2,1,0:T(8,128)(2,1)S(1)}, bf16[2,272,128]{2,1,0:T(8,128)(2,1)S(1)}, u32[]{:S(2)}, u32[]{:S(2)}) collective-permute-start(bf16[2,272,128]{2,1,0:T(8,128)(2,1)S(1)} %get-tuple-element.58), channel_id=1, source_target_pairs={{0,2},{1,3},{2,0},{3,1},{4,6},{5,7},{6,4},{7,5},{8,10},{9,11},{10,... | collective-permute-start | bytes 417800 | tf_op jit(solution)/shard_map/ppermute | solution.py:27
  14.9 1.7 %collective-permute-done.3.refs_6_ = bf16[896,128]{1,0:T(8,128)(2,1)S(1)} collective-permute-done((bf16[896,128]{1,0:T(8,128)(2,1)S(1)}, bf16[896,128]{1,0:T(8,128)(2,1)S(1)}, u32[]{:S(2)}, u32[]{:S(2)}) %collective-permute-start.3) | collective-permute-done | bytes 229408 | tf_op jit(solution)/shard_map/ppermute | solution.py:27
  16.8 1.5 %collective-permute-start.11 = (bf16[2,256,384]{2,1,0:T(8,128)(2,1)S(1)}, bf16[2,256,384]{2,1,0:T(8,128)(2,1)S(1)}, u32[]{:S(2)}, u32[]{:S(2)}) collective-permute-start(bf16[2,256,384]{2,1,0:T(8,128)(2,1)S(1)} %get-tuple-element.67), channel_id=1, source_target_pairs={{0,2},{1,3},{2,0},{3,1},{4,6},{5,7},{6,4},{7,5},{8,10},{9,11},{10,... | collective-permute-start | bytes 1179656 | tf_op jit(solution)/shard_map/ppermute | solution.py:27
  18.3 2.1 %collective-permute-done.8.refs_9_ = bf16[2,272,128]{2,1,0:T(8,128)(2,1)S(1)} collective-permute-done((bf16[2,272,128]{2,1,0:T(8,128)(2,1)S(1)}, bf16[2,272,128]{2,1,0:T(8,128)(2,1)S(1)}, u32[]{:S(2)}, u32[]{:S(2)}) %collective-permute-start.8) | collective-permute-done | bytes 139296 | tf_op jit(solution)/shard_map/ppermute | solution.py:27
  21.1 0.7 %collective-permute-done.9.refs_10_ = bf16[1,272,128]{2,1,0:T(8,128)(2,1)S(1)} collective-permute-done((bf16[1,272,128]{2,1,0:T(8,128)(2,1)S(1)}, bf16[1,272,128]{2,1,0:T(8,128)(2,1)S(1)}, u32[]{:S(2)}, u32[]{:S(2)}) %collective-permute-start.9) | collective-permute-done | bytes 69664 | tf_op jit(solution)/shard_map/ppermute | solution.py:27
  21.7 0.8 %collective-permute-start.10 = (bf16[896,128]{1,0:T(8,128)(2,1)S(1)}, bf16[896,128]{1,0:T(8,128)(2,1)S(1)}, u32[]{:S(2)}, u32[]{:S(2)}) collective-permute-start(bf16[896,128]{1,0:T(8,128)(2,1)S(1)} %collective-permute-done.3.refs_6_), channel_id=1, source_target_pairs={{0,4},{4,0},{8,12},{12,8},{16,20},{20,16},{24,28},{28,24},{1,5},{5... | collective-permute-start | bytes 688136 | tf_op jit(solution)/shard_map/ppermute | solution.py:27
  22.5 3.0 %attention.3 = (bf16[1,2,128,128]{3,2,1,0:T(8,128)(2,1)S(1)}, bf16[1,2,128,128]{3,2,1,0:T(8,128)(2,1)S(1)}, bf16[2,2,128,128]{3,2,1,0:T(8,128)(2,1)S(1)}, bf16[512,896]{1,0:T(8,128)(2,1)S(1)}, s32[32,128]{1,0:T(8,128)S(1)}) custom-call(s32[4]{0:T(128)S(1)} %pad_add_fusion.meta.refs_0_, bf16[128,896]{1,0:T(8,128)(2,1)S(1)} %bitcast.8, ...), custom_call_target="tpu_custom_call" | custom-call | tf_op jit(solution)/shard_map/attention/pallas_call | solution.py:292
  25.6 3.4 %collective-permute-done.6.refs_8_ = bf16[896,128]{1,0:T(8,128)(2,1)S(1)} collective-permute-done((bf16[896,128]{1,0:T(8,128)(2,1)S(1)}, bf16[896,128]{1,0:T(8,128)(2,1)S(1)}, u32[]{:S(2)}, u32[]{:S(2)}) %collective-permute-start.6) | collective-permute-done | bytes 229408 | tf_op jit(solution)/shard_map/ppermute | solution.py:27
  30.0 1.4 %collective-permute-start.17 = (bf16[896,128]{1,0:T(8,128)(2,1)S(1)}, bf16[896,128]{1,0:T(8,128)(2,1)S(1)}, u32[]{:S(2)}, u32[]{:S(2)}) collective-permute-start(bf16[896,128]{1,0:T(8,128)(2,1)S(1)} %collective-permute-done.5.refs_5_), channel_id=1, source_target_pairs={{0,8},{4,12},{8,0},{12,4},{16,24},{20,28},{24,16},{28,20},{1,9},{5... | collective-permute-start | bytes 688136 | tf_op jit(solution)/shard_map/ppermute | solution.py:27
  31.9 3.7 %attention.4 = (bf16[1,2,128,256]{3,2,1,0:T(8,128)(2,1)S(1)}, bf16[1,2,128,256]{3,2,1,0:T(8,128)(2,1)S(1)}, bf16[2,2,128,256]{3,2,1,0:T(8,128)(2,1)S(1)}, bf16[512,896]{1,0:T(8,128)(2,1)S(1)}) custom-call(s32[4]{0:T(128)S(1)} %pad_add_fusion.meta.refs_0_, bf16[128,896]{1,0:T(8,128)(2,1)S(1)} %bitcast.9, bf16[128,896]{1,0:T(8,128)(2,1)S(1)} %collective-permute-done.refs_2_, ...), custom_call_target="tpu_custom_call" | custom-call | tf_op jit(solution)/shard_map/attention/pallas_call | solution.py:292
  35.5 1.9 %collective-permute-start.19 = (bf16[2,2,128,256]{3,2,1,0:T(8,128)(2,1)S(1)}, bf16[2,2,128,256]{3,2,1,0:T(8,128)(2,1)S(1)}, u32[]{:S(2)}, u32[]{:S(2)}) collective-permute-start(bf16[2,2,128,256]{3,2,1,0:T(8,128)(2,1)S(1)} %get-tuple-element.90), channel_id=1, source_target_pairs={{0,2},{1,3},{2,0},{3,1},{4,6},{5,7},{6,4},{7,5},{8,10},{9,11},{10,... | collective-permute-start | bytes 786440 | tf_op jit(solution)/shard_map/ppermute | solution.py:27
  37.6 1.1 %collective-permute-done.18.refs_6_ = bf16[896,128]{1,0:T(8,128)(2,1)S(1)} collective-permute-done((bf16[896,128]{1,0:T(8,128)(2,1)S(1)}, bf16[896,128]{1,0:T(8,128)(2,1)S(1)}, u32[]{:S(2)}, u32[]{:S(2)}) %collective-permute-start.18) | collective-permute-done | bytes 229408 | tf_op jit(solution)/shard_map/ppermute | solution.py:27
  38.7 2.9 %attention.5 = (bf16[1,2,128,128]{3,2,1,0:T(8,128)(2,1)S(1)}, bf16[1,2,128,128]{3,2,1,0:T(8,128)(2,1)S(1)}, bf16[2,2,128,128]{3,2,1,0:T(8,128)(2,1)S(1)}, f32[256,896]{1,0:T(8,128)S(1)}, bf16[256,896]{1,0:T(8,128)(2,1)S(1)}) custom-call(s32[4]{0:T(128)S(1)} %pad_add_fusion.meta.refs_0_, bf16[128,896]{1,0:T(8,128)(2,1)S(1)} %bitcast.10, ...), custom_call_target="tpu_custom_call" | custom-call | flops 2400000000 | tf_op jit(solution)/shard_map/attention/pallas_call | solution.py:292
  41.5 1.9 %collective-permute-done.19.refs_6_ = bf16[2,2,128,256]{3,2,1,0:T(8,128)(2,1)S(1)} collective-permute-done((bf16[2,2,128,256]{3,2,1,0:T(8,128)(2,1)S(1)}, bf16[2,2,128,256]{3,2,1,0:T(8,128)(2,1)S(1)}, u32[]{:S(2)}, u32[]{:S(2)}) %collective-permute-start.19) | collective-permute-done | bytes 262176 | tf_op jit(solution)/shard_map/ppermute | solution.py:27
  43.4 1.5 %collective-permute-start.23 = (bf16[2,2,128,128]{3,2,1,0:T(8,128)(2,1)S(1)}, bf16[2,2,128,128]{3,2,1,0:T(8,128)(2,1)S(1)}, u32[]{:S(2)}, u32[]{:S(2)}) collective-permute-start(bf16[2,2,128,128]{3,2,1,0:T(8,128)(2,1)S(1)} %get-tuple-element.96), channel_id=1, source_target_pairs={{0,2},{1,3},{2,0},{3,1},{4,6},{5,7},{6,4},{7,5},{8,10},{9,11},{10,... | collective-permute-start | bytes 393224 | tf_op jit(solution)/shard_map/ppermute | solution.py:27
  45.4 1.5 %collective-permute-start.26 = (bf16[128,896]{1,0:T(8,128)(2,1)S(1)}, bf16[128,896]{1,0:T(8,128)(2,1)S(1)}, u32[]{:S(2)}, u32[]{:S(2)}) collective-permute-start(bf16[128,896]{1,0:T(8,128)(2,1)S(1)} %slice.35), channel_id=1, source_target_pairs={{0,2},{1,3},{2,0},{3,1},{4,6},{5,7},{6,4},{7,5},{8,10},{9,11},{10,... | collective-permute-start | bytes 688136 | tf_op jit(solution)/shard_map/ppermute | solution.py:27
  46.9 0.5 collective-permute-start.15
  47.6 2.1 %collective-permute-done.23.refs_10_ = bf16[2,2,128,128]{3,2,1,0:T(8,128)(2,1)S(1)} collective-permute-done((bf16[2,2,128,128]{3,2,1,0:T(8,128)(2,1)S(1)}, bf16[2,2,128,128]{3,2,1,0:T(8,128)(2,1)S(1)}, u32[]{:S(2)}, u32[]{:S(2)}) %collective-permute-start.23) | collective-permute-done | bytes 131104 | tf_op jit(solution)/shard_map/ppermute | solution.py:27
  49.7 0.6 %collective-permute-start.22 = (bf16[1,2,128,128]{3,2,1,0:T(8,128)(2,1)S(1)}, bf16[1,2,128,128]{3,2,1,0:T(8,128)(2,1)S(1)}, u32[]{:S(2)}, u32[]{:S(2)}) collective-permute-start(bf16[1,2,128,128]{3,2,1,0:T(8,128)(2,1)S(1)} %get-tuple-element.95), channel_id=1, source_target_pairs={{0,1},{1,0},{2,3},{3,2},{4,5},{5,4},{6,7},{7,6},{8,9},{9,8},{10,11... | collective-permute-start | bytes 196616 | tf_op jit(solution)/shard_map/ppermute | solution.py:27
  50.4 0.8 %collective-permute-done.22.refs_9_ = bf16[1,2,128,128]{3,2,1,0:T(8,128)(2,1)S(1)} collective-permute-done((bf16[1,2,128,128]{3,2,1,0:T(8,128)(2,1)S(1)}, bf16[1,2,128,128]{3,2,1,0:T(8,128)(2,1)S(1)}, u32[]{:S(2)}, u32[]{:S(2)}) %collective-permute-start.22) | collective-permute-done | bytes 65568 | tf_op jit(solution)/shard_map/ppermute | solution.py:27
  51.6 1.8 %unpack.1 = (bf16[1,128,2048]{2,1,0:T(8,128)(2,1)}, bf16[1,128,2048]{2,1,0:T(8,128)(2,1)}) custom-call(s32[4]{0:T(128)S(1)} %pad_add_fusion.meta.refs_0_, bf16[1,2,128,128]{3,2,1,0:T(8,128)(2,1)S(1)} %get-tuple-element.82.refs_0_, bf16[1,2,128,128]{3,2,1,0:T(8,128)(2,1)S(1)} %collective-permute-done.15.refs_1_, ...), custom_call_target="tpu_custom_call" | custom-call | tf_op jit(solution)/shard_map/unpack/pallas_call | solution.py:327
  53.3 0.9 %collective-permute-done.26 = bf16[128,896]{1,0:T(8,128)(2,1)S(1)} collective-permute-done((bf16[128,896]{1,0:T(8,128)(2,1)S(1)}, bf16[128,896]{1,0:T(8,128)(2,1)S(1)}, u32[]{:S(2)}, u32[]{:S(2)}) %collective-permute-start.26) | collective-permute-done | bytes 229408 | tf_op jit(solution)/shard_map/ppermute | solution.py:27
  54.2 0.8 %slice_add_fusion = f32[128,896]{1,0:T(8,128)} fusion(f32[256,896]{1,0:T(8,128)S(1)} %convert_add_fusion, bf16[128,896]{1,0:T(8,128)(2,1)S(1)} %collective-permute-done.26), kind=kLoop, calls=%fused_computation.2 | loop fusion | flops 229376 | bytes 1146880 | tf_op jit(solution)/shard_map/add | solution.py:436
  (49 shorter events, 3.7 us)
Async XLA Ops:
  0.6 1.2 %copy-start = (bf16[896,512]{1,0:T(8,128)(2,1)S(1)}, bf16[896,512]{1,0:T(8,128)(2,1)}, u32[]{:S(2)}) copy-start(bf16[896,512]{1,0:T(8,128)(2,1)} %param.9) | copy-start | bytes 2752516
  1.8 7.2 %copy-start.1 = (bf16[1,2,64,896]{3,2,1,0:T(8,128)(2,1)S(1)}, bf16[1,2,64,896]{3,2,1,0:T(8,128)(2,1)}, u32[]{:S(2)}) copy-start(bf16[1,2,64,896]{3,2,1,0:T(8,128)(2,1)} %param.8) | copy-start | bytes 688132
  1.9 14.7 %collective-permute-start.3 = (bf16[896,128]{1,0:T(8,128)(2,1)S(1)}, bf16[896,128]{1,0:T(8,128)(2,1)S(1)}, u32[]{:S(2)}, u32[]{:S(2)}) collective-permute-start(bf16[896,128]{1,0:T(8,128)(2,1)S(1)} %constant_dynamic-slice_fusion.refs_5_), channel_id=1, source_target_pairs={{0,16},{4,20},{8,24},{12,28},{16,0},{20,4},{24,8},{28,12},{1,17},{... | collective-permute-start | bytes 688136 | tf_op jit(solution)/shard_map/ppermute | solution.py:27
  6.0 10.8 %collective-permute-start.4 = (bf16[896,128]{1,0:T(8,128)(2,1)S(1)}, bf16[896,128]{1,0:T(8,128)(2,1)S(1)}, u32[]{:S(2)}, u32[]{:S(2)}) collective-permute-start(bf16[896,128]{1,0:T(8,128)(2,1)S(1)} %constant_dynamic-slice_fusion.refs_5_), channel_id=1, source_target_pairs={{0,8},{4,12},{8,0},{12,4},{16,24},{20,28},{24,16},{28,20},{1,9},{5... | collective-permute-start | bytes 688136 | tf_op jit(solution)/shard_map/ppermute | solution.py:27
  7.5 9.2 %collective-permute-start.5 = (bf16[896,128]{1,0:T(8,128)(2,1)S(1)}, bf16[896,128]{1,0:T(8,128)(2,1)S(1)}, u32[]{:S(2)}, u32[]{:S(2)}) collective-permute-start(bf16[896,128]{1,0:T(8,128)(2,1)S(1)} %constant_dynamic-slice_fusion.refs_5_), channel_id=1, source_target_pairs={{0,4},{4,0},{8,12},{12,8},{16,20},{20,16},{24,28},{28,24},{1,5},{5... | collective-permute-start | bytes 688136 | tf_op jit(solution)/shard_map/ppermute | solution.py:27
  9.1 11.9 %collective-permute-start = (bf16[128,896]{1,0:T(8,128)(2,1)S(1)}, bf16[128,896]{1,0:T(8,128)(2,1)S(1)}, u32[]{:S(2)}, u32[]{:S(2)}) collective-permute-start(bf16[128,896]{1,0:T(8,128)(2,1)S(1)} %bitcast.6), channel_id=1, source_target_pairs={{0,2},{1,3},{2,0},{3,1},{4,6},{5,7},{6,4},{7,5},{8,10},{9,11},{10,... | collective-permute-start | bytes 688136 | tf_op jit(solution)/shard_map/ppermute | solution.py:27
  10.5 0.7 %copy-start.5 = (s32[1,8]{1,0:T(1,128)S(1)}, s32[1,8]{1,0:T(1,128)}, u32[]{:S(2)}) copy-start(s32[1,8]{1,0:T(1,128)} %slots.1) | copy-start | bytes 100
  11.2 1.0 %copy-start.2 = (bf16[1,128,2048]{2,1,0:T(8,128)(2,1)S(1)}, bf16[1,128,2048]{2,1,0:T(8,128)(2,1)}, u32[]{:S(2)}) copy-start(bf16[1,128,2048]{2,1,0:T(8,128)(2,1)} %queries.1) | copy-start | bytes 1572868
  12.3 1.0 %copy-start.3 = (bf16[1,128,2048]{2,1,0:T(8,128)(2,1)S(1)}, bf16[1,128,2048]{2,1,0:T(8,128)(2,1)}, u32[]{:S(2)}) copy-start(bf16[1,128,2048]{2,1,0:T(8,128)(2,1)} %grad_out.1) | copy-start | bytes 1572868
  14.3 6.2 %collective-permute-start.8 = (bf16[2,272,128]{2,1,0:T(8,128)(2,1)S(1)}, bf16[2,272,128]{2,1,0:T(8,128)(2,1)S(1)}, u32[]{:S(2)}, u32[]{:S(2)}) collective-permute-start(bf16[2,272,128]{2,1,0:T(8,128)(2,1)S(1)} %get-tuple-element.58), channel_id=1, source_target_pairs={{0,2},{1,3},{2,0},{3,1},{4,6},{5,7},{6,4},{7,5},{8,10},{9,11},{10,... | collective-permute-start | bytes 417800 | tf_op jit(solution)/shard_map/ppermute | solution.py:27
  16.8 12.6 %collective-permute-start.11 = (bf16[2,256,384]{2,1,0:T(8,128)(2,1)S(1)}, bf16[2,256,384]{2,1,0:T(8,128)(2,1)S(1)}, u32[]{:S(2)}, u32[]{:S(2)}) collective-permute-start(bf16[2,256,384]{2,1,0:T(8,128)(2,1)S(1)} %get-tuple-element.67), channel_id=1, source_target_pairs={{0,2},{1,3},{2,0},{3,1},{4,6},{5,7},{6,4},{7,5},{8,10},{9,11},{10,... | collective-permute-start | bytes 1179656 | tf_op jit(solution)/shard_map/ppermute | solution.py:27
  18.3 2.7 %collective-permute-start.7 = (bf16[1,272,128]{2,1,0:T(8,128)(2,1)S(1)}, bf16[1,272,128]{2,1,0:T(8,128)(2,1)S(1)}, u32[]{:S(2)}, u32[]{:S(2)}) collective-permute-start(bf16[1,272,128]{2,1,0:T(8,128)(2,1)S(1)} %get-tuple-element.57), channel_id=1, source_target_pairs={{0,1},{1,0},{2,3},{3,2},{4,5},{5,4},{6,7},{7,6},{8,9},{9,8},{10,11... | collective-permute-start | bytes 208904 | tf_op jit(solution)/shard_map/ppermute | solution.py:27
  20.5 1.3 %collective-permute-start.9 = (bf16[1,272,128]{2,1,0:T(8,128)(2,1)S(1)}, bf16[1,272,128]{2,1,0:T(8,128)(2,1)S(1)}, u32[]{:S(2)}, u32[]{:S(2)}) collective-permute-start(bf16[1,272,128]{2,1,0:T(8,128)(2,1)S(1)} %slice.29), channel_id=1, source_target_pairs={{0,1},{1,0},{2,3},{3,2},{4,5},{5,4},{6,7},{7,6},{8,9},{9,8},{10,11... | collective-permute-start | bytes 208904 | tf_op jit(solution)/shard_map/ppermute | solution.py:27
  20.5 2.1 %collective-permute-start.1 = (bf16[128,896]{1,0:T(8,128)(2,1)S(1)}, bf16[128,896]{1,0:T(8,128)(2,1)S(1)}, u32[]{:S(2)}, u32[]{:S(2)}) collective-permute-start(bf16[128,896]{1,0:T(8,128)(2,1)S(1)} %bitcast.7), channel_id=1, source_target_pairs={{0,1},{1,0},{2,3},{3,2},{4,5},{5,4},{6,7},{7,6},{8,9},{9,8},{10,11... | collective-permute-start | bytes 688136 | tf_op jit(solution)/shard_map/ppermute | solution.py:27
  21.0 1.6 %collective-permute-start.2 = (bf16[128,896]{1,0:T(8,128)(2,1)S(1)}, bf16[128,896]{1,0:T(8,128)(2,1)S(1)}, u32[]{:S(2)}, u32[]{:S(2)}) collective-permute-start(bf16[128,896]{1,0:T(8,128)(2,1)S(1)} %collective-permute-done.refs_2_), channel_id=1, source_target_pairs={{0,1},{1,0},{2,3},{3,2},{4,5},{5,4},{6,7},{7,6},{8,9},{9,8},{10,11... | collective-permute-start | bytes 688136 | tf_op jit(solution)/shard_map/ppermute | solution.py:27
  21.1 7.9 %collective-permute-start.6 = (bf16[896,128]{1,0:T(8,128)(2,1)S(1)}, bf16[896,128]{1,0:T(8,128)(2,1)S(1)}, u32[]{:S(2)}, u32[]{:S(2)}) collective-permute-start(bf16[896,128]{1,0:T(8,128)(2,1)S(1)} %collective-permute-done.3.refs_6_), channel_id=1, source_target_pairs={{0,8},{4,12},{8,0},{12,4},{16,24},{20,28},{24,16},{28,20},{1,9},{5... | collective-permute-start | bytes 688136 | tf_op jit(solution)/shard_map/ppermute | solution.py:27
  21.7 7.7 %collective-permute-start.10 = (bf16[896,128]{1,0:T(8,128)(2,1)S(1)}, bf16[896,128]{1,0:T(8,128)(2,1)S(1)}, u32[]{:S(2)}, u32[]{:S(2)}) collective-permute-start(bf16[896,128]{1,0:T(8,128)(2,1)S(1)} %collective-permute-done.3.refs_6_), channel_id=1, source_target_pairs={{0,4},{4,0},{8,12},{12,8},{16,20},{20,16},{24,28},{28,24},{1,5},{5... | collective-permute-start | bytes 688136 | tf_op jit(solution)/shard_map/ppermute | solution.py:27
  29.4 2.4 %collective-permute-start.13 = (bf16[1,256,384]{2,1,0:T(8,128)(2,1)S(1)}, bf16[1,256,384]{2,1,0:T(8,128)(2,1)S(1)}, u32[]{:S(2)}, u32[]{:S(2)}) collective-permute-start(bf16[1,256,384]{2,1,0:T(8,128)(2,1)S(1)} %slice.23), channel_id=1, source_target_pairs={{0,1},{1,0},{2,3},{3,2},{4,5},{5,4},{6,7},{7,6},{8,9},{9,8},{10,11... | collective-permute-start | bytes 589832 | tf_op jit(solution)/shard_map/ppermute | solution.py:27
  29.5 2.4 %collective-permute-start.12 = (bf16[1,256,384]{2,1,0:T(8,128)(2,1)S(1)}, bf16[1,256,384]{2,1,0:T(8,128)(2,1)S(1)}, u32[]{:S(2)}, u32[]{:S(2)}) collective-permute-start(bf16[1,256,384]{2,1,0:T(8,128)(2,1)S(1)} %get-tuple-element.74), channel_id=1, source_target_pairs={{0,1},{1,0},{2,3},{3,2},{4,5},{5,4},{6,7},{7,6},{8,9},{9,8},{10,11... | collective-permute-start | bytes 589832 | tf_op jit(solution)/shard_map/ppermute | solution.py:27
  30.0 7.6 %collective-permute-start.17 = (bf16[896,128]{1,0:T(8,128)(2,1)S(1)}, bf16[896,128]{1,0:T(8,128)(2,1)S(1)}, u32[]{:S(2)}, u32[]{:S(2)}) collective-permute-start(bf16[896,128]{1,0:T(8,128)(2,1)S(1)} %collective-permute-done.5.refs_5_), channel_id=1, source_target_pairs={{0,8},{4,12},{8,0},{12,4},{16,24},{20,28},{24,16},{28,20},{1,9},{5... | collective-permute-start | bytes 688136 | tf_op jit(solution)/shard_map/ppermute | solution.py:27
  31.4 7.3 %collective-permute-start.18 = (bf16[896,128]{1,0:T(8,128)(2,1)S(1)}, bf16[896,128]{1,0:T(8,128)(2,1)S(1)}, u32[]{:S(2)}, u32[]{:S(2)}) collective-permute-start(bf16[896,128]{1,0:T(8,128)(2,1)S(1)} %collective-permute-done.6.refs_8_), channel_id=1, source_target_pairs={{0,4},{4,0},{8,12},{12,8},{16,20},{20,16},{24,28},{28,24},{1,5},{5... | collective-permute-start | bytes 688136 | tf_op jit(solution)/shard_map/ppermute | solution.py:27
  31.6 5.8 %collective-permute-start.14 = (bf16[2,2,128,128]{3,2,1,0:T(8,128)(2,1)S(1)}, bf16[2,2,128,128]{3,2,1,0:T(8,128)(2,1)S(1)}, u32[]{:S(2)}, u32[]{:S(2)}) collective-permute-start(bf16[2,2,128,128]{3,2,1,0:T(8,128)(2,1)S(1)} %get-tuple-element.81), channel_id=1, source_target_pairs={{0,2},{1,3},{2,0},{3,1},{4,6},{5,7},{6,4},{7,5},{8,10},{9,11},{10,... | collective-permute-start | bytes 393224 | tf_op jit(solution)/shard_map/ppermute | solution.py:27
  35.5 7.9 %collective-permute-start.19 = (bf16[2,2,128,256]{3,2,1,0:T(8,128)(2,1)S(1)}, bf16[2,2,128,256]{3,2,1,0:T(8,128)(2,1)S(1)}, u32[]{:S(2)}, u32[]{:S(2)}) collective-permute-start(bf16[2,2,128,256]{3,2,1,0:T(8,128)(2,1)S(1)} %get-tuple-element.90), channel_id=1, source_target_pairs={{0,2},{1,3},{2,0},{3,1},{4,6},{5,7},{6,4},{7,5},{8,10},{9,11},{10,... | collective-permute-start | bytes 786440 | tf_op jit(solution)/shard_map/ppermute | solution.py:27
  43.4 1.8 %collective-permute-start.25 = (bf16[256,896]{1,0:T(8,128)(2,1)S(1)}, bf16[256,896]{1,0:T(8,128)(2,1)S(1)}, u32[]{:S(2)}, u32[]{:S(2)}) collective-permute-start(bf16[256,896]{1,0:T(8,128)(2,1)S(1)} %get-tuple-element.100), channel_id=1, source_target_pairs={{0,1},{1,0},{2,3},{3,2},{4,5},{5,4},{6,7},{7,6},{8,9},{9,8},{10,11... | collective-permute-start | bytes 1376264 | tf_op jit(solution)/shard_map/ppermute | solution.py:27
  43.4 6.3 %collective-permute-start.23 = (bf16[2,2,128,128]{3,2,1,0:T(8,128)(2,1)S(1)}, bf16[2,2,128,128]{3,2,1,0:T(8,128)(2,1)S(1)}, u32[]{:S(2)}, u32[]{:S(2)}) collective-permute-start(bf16[2,2,128,128]{3,2,1,0:T(8,128)(2,1)S(1)} %get-tuple-element.96), channel_id=1, source_target_pairs={{0,2},{1,3},{2,0},{3,1},{4,6},{5,7},{6,4},{7,5},{8,10},{9,11},{10,... | collective-permute-start | bytes 393224 | tf_op jit(solution)/shard_map/ppermute | solution.py:27
  45.4 8.9 %collective-permute-start.26 = (bf16[128,896]{1,0:T(8,128)(2,1)S(1)}, bf16[128,896]{1,0:T(8,128)(2,1)S(1)}, u32[]{:S(2)}, u32[]{:S(2)}) collective-permute-start(bf16[128,896]{1,0:T(8,128)(2,1)S(1)} %slice.35), channel_id=1, source_target_pairs={{0,2},{1,3},{2,0},{3,1},{4,6},{5,7},{6,4},{7,5},{8,10},{9,11},{10,... | collective-permute-start | bytes 688136 | tf_op jit(solution)/shard_map/ppermute | solution.py:27
  46.9 2.8 %collective-permute-start.16 = (bf16[1,2,128,128]{3,2,1,0:T(8,128)(2,1)S(1)}, bf16[1,2,128,128]{3,2,1,0:T(8,128)(2,1)S(1)}, u32[]{:S(2)}, u32[]{:S(2)}) collective-permute-start(bf16[1,2,128,128]{3,2,1,0:T(8,128)(2,1)S(1)} %slice.24), channel_id=1, source_target_pairs={{0,1},{1,0},{2,3},{3,2},{4,5},{5,4},{6,7},{7,6},{8,9},{9,8},{10,11... | collective-permute-start | bytes 196616 | tf_op jit(solution)/shard_map/ppermute | solution.py:27
  46.9 3.4 %collective-permute-start.15 = (bf16[1,2,128,128]{3,2,1,0:T(8,128)(2,1)S(1)}, bf16[1,2,128,128]{3,2,1,0:T(8,128)(2,1)S(1)}, u32[]{:S(2)}, u32[]{:S(2)}) collective-permute-start(bf16[1,2,128,128]{3,2,1,0:T(8,128)(2,1)S(1)} %get-tuple-element.83), channel_id=1, source_target_pairs={{0,1},{1,0},{2,3},{3,2},{4,5},{5,4},{6,7},{7,6},{8,9},{9,8},{10,11... | collective-permute-start | bytes 196616 | tf_op jit(solution)/shard_map/ppermute | solution.py:27
  47.4 4.1 %collective-permute-start.21 = (bf16[1,2,128,256]{3,2,1,0:T(8,128)(2,1)S(1)}, bf16[1,2,128,256]{3,2,1,0:T(8,128)(2,1)S(1)}, u32[]{:S(2)}, u32[]{:S(2)}) collective-permute-start(bf16[1,2,128,256]{3,2,1,0:T(8,128)(2,1)S(1)} %slice.25), channel_id=1, source_target_pairs={{0,1},{1,0},{2,3},{3,2},{4,5},{5,4},{6,7},{7,6},{8,9},{9,8},{10,11... | collective-permute-start | bytes 393224 | tf_op jit(solution)/shard_map/ppermute | solution.py:27
  49.7 1.9 %collective-permute-start.20 = (bf16[1,2,128,256]{3,2,1,0:T(8,128)(2,1)S(1)}, bf16[1,2,128,256]{3,2,1,0:T(8,128)(2,1)S(1)}, u32[]{:S(2)}, u32[]{:S(2)}) collective-permute-start(bf16[1,2,128,256]{3,2,1,0:T(8,128)(2,1)S(1)} %get-tuple-element.92), channel_id=1, source_target_pairs={{0,1},{1,0},{2,3},{3,2},{4,5},{5,4},{6,7},{7,6},{8,9},{9,8},{10,11... | collective-permute-start | bytes 393224 | tf_op jit(solution)/shard_map/ppermute | solution.py:27
  49.7 1.5 %collective-permute-start.22 = (bf16[1,2,128,128]{3,2,1,0:T(8,128)(2,1)S(1)}, bf16[1,2,128,128]{3,2,1,0:T(8,128)(2,1)S(1)}, u32[]{:S(2)}, u32[]{:S(2)}) collective-permute-start(bf16[1,2,128,128]{3,2,1,0:T(8,128)(2,1)S(1)} %get-tuple-element.95), channel_id=1, source_target_pairs={{0,1},{1,0},{2,3},{3,2},{4,5},{5,4},{6,7},{7,6},{8,9},{9,8},{10,11... | collective-permute-start | bytes 196616 | tf_op jit(solution)/shard_map/ppermute | solution.py:27
  50.3 1.3 %collective-permute-start.24 = (bf16[1,2,128,128]{3,2,1,0:T(8,128)(2,1)S(1)}, bf16[1,2,128,128]{3,2,1,0:T(8,128)(2,1)S(1)}, u32[]{:S(2)}, u32[]{:S(2)}) collective-permute-start(bf16[1,2,128,128]{3,2,1,0:T(8,128)(2,1)S(1)} %slice.30), channel_id=1, source_target_pairs={{0,1},{1,0},{2,3},{3,2},{4,5},{5,4},{6,7},{7,6},{8,9},{9,8},{10,11... | collective-permute-start | bytes 196616 | tf_op jit(solution)/shard_map/ppermute | solution.py:27
  (1 other events, 0.7 us)

commit v8 on v7

--- a/solution.py
+++ b/solution.py
@@ -145,10 +145,10 @@
 def relative_positions(pieces, own, per_owner, tokens):
     bits = len(pieces).bit_length() - 1
     shift = per_owner.bit_length() - 1
-    rows = [piece[2 * tokens : 2 * tokens + 8, :HEAD_SIZE] for piece in pieces]
+    rows = [piece[2 * tokens : 2 * tokens + EXTRA, :HEAD_SIZE] for piece in pieces]
     out = []
     for row in rows:
-        position = row.astype(jnp.float32).astype(jnp.int32)
+        position = row.astype(jnp.float32).astype(jnp.int32)[:8]
         owner = bit_reverse((position >> shift) ^ own, bits)
         out.append((owner << shift) + (position & (per_owner - 1)))
     return out

time: 55.3 us -> 55.3 us (level)
  no operation moved by 1% of the time
where the time goes in v8:
time: 55.3 us; the launch traced here: 55 us
  starting transfers between devices  20.8 us (38%)
  waiting for transfers between devices  16.2 us (29%)
  Pallas kernels  12.3 us (22%)
  local copies, waits for them, and re-layouts  3.97 us (7%)
  other arithmetic  0.99 us (2%)
  between operations  0.76 us (1%)
    ppermute x27, starting transfers between devices, xor_send(): return lax.ppermute(value, axis, [(i, i ^ bit) for i in range(size)])  20.8 us
    ppermute x27, waiting for transfers between devices, xor_send(): return lax.ppermute(value, axis, [(i, i ^ bit) for i in range(size)])  16.2 us
    pallas_call x3, Pallas kernels, attention(): pl.pallas_call(functools.partial(attention_body, seq_size, spans, takes,...  9.58 us
    unnamed x12, local copies, waits for them, and re-layouts  3.86 us
    pallas_call x1, Pallas kernels, unpack(): pl.pallas_call(functools.partial(unpack_body, seq_size, groups, places),...  1.8 us
  transfers between devices with their start and end apart: 27, of which 14 were waited for; matrix products, arithmetic and copies ran while one was open for 0% of the time, Pallas kernels for 22%

profile of v8, /device:TPU:0, one launch (start us, length us, event | category | flops | bytes accessed | tf_op | source)
XLA Modules:
  0.0 55.0 jit_solution(2783420055526931952)
XLA Ops:
  0.7 1.2 %copy-done = bf16[896,512]{1,0:T(8,128)(2,1)S(1)} copy-done((bf16[896,512]{1,0:T(8,128)(2,1)S(1)}, bf16[896,512]{1,0:T(8,128)(2,1)}, u32[]{:S(2)}) %copy-start) | copy-done | bytes 917528
  1.9 4.1 %collective-permute-start.3 = (bf16[896,128]{1,0:T(8,128)(2,1)S(1)}, bf16[896,128]{1,0:T(8,128)(2,1)S(1)}, u32[]{:S(2)}, u32[]{:S(2)}) collective-permute-start(bf16[896,128]{1,0:T(8,128)(2,1)S(1)} %constant_dynamic-slice_fusion.refs_5_), channel_id=1, source_target_pairs={{0,16},{4,20},{8,24},{12,28},{16,0},{20,4},{24,8},{28,12},{1,17},{... | collective-permute-start | bytes 688136 | tf_op jit(solution)/shard_map/ppermute | solution.py:27
  6.0 1.6 %collective-permute-start.4 = (bf16[896,128]{1,0:T(8,128)(2,1)S(1)}, bf16[896,128]{1,0:T(8,128)(2,1)S(1)}, u32[]{:S(2)}, u32[]{:S(2)}) collective-permute-start(bf16[896,128]{1,0:T(8,128)(2,1)S(1)} %constant_dynamic-slice_fusion.refs_5_), channel_id=1, source_target_pairs={{0,8},{4,12},{8,0},{12,4},{16,24},{20,28},{24,16},{28,20},{1,9},{5... | collective-permute-start | bytes 688136 | tf_op jit(solution)/shard_map/ppermute | solution.py:27
  7.5 1.5 %collective-permute-start.5 = (bf16[896,128]{1,0:T(8,128)(2,1)S(1)}, bf16[896,128]{1,0:T(8,128)(2,1)S(1)}, u32[]{:S(2)}, u32[]{:S(2)}) collective-permute-start(bf16[896,128]{1,0:T(8,128)(2,1)S(1)} %constant_dynamic-slice_fusion.refs_5_), channel_id=1, source_target_pairs={{0,4},{4,0},{8,12},{12,8},{16,20},{20,16},{24,28},{28,24},{1,5},{5... | collective-permute-start | bytes 688136 | tf_op jit(solution)/shard_map/ppermute | solution.py:27
  9.1 1.5 %collective-permute-start = (bf16[128,896]{1,0:T(8,128)(2,1)S(1)}, bf16[128,896]{1,0:T(8,128)(2,1)S(1)}, u32[]{:S(2)}, u32[]{:S(2)}) collective-permute-start(bf16[128,896]{1,0:T(8,128)(2,1)S(1)} %bitcast.6), channel_id=1, source_target_pairs={{0,2},{1,3},{2,0},{3,1},{4,6},{5,7},{6,4},{7,5},{8,10},{9,11},{10,... | collective-permute-start | bytes 688136 | tf_op jit(solution)/shard_map/ppermute | solution.py:27
  10.6 0.6 %copy-done.4 = s32[1,2,2]{2,1,0:T(2,128)S(1)} copy-done((s32[1,2,2]{2,1,0:T(2,128)S(1)}, s32[1,2,2]{2,1,0:T(2,128)}, u32[]{:S(2)}) %copy-start.4) | copy-done | bytes 40
  11.2 1.0 %copy-done.2 = bf16[1,128,2048]{2,1,0:T(8,128)(2,1)S(1)} copy-done((bf16[1,128,2048]{2,1,0:T(8,128)(2,1)S(1)}, bf16[1,128,2048]{2,1,0:T(8,128)(2,1)}, u32[]{:S(2)}) %copy-start.2) | copy-done | bytes 524312
  12.3 1.0 %copy-done.3 = bf16[1,128,2048]{2,1,0:T(8,128)(2,1)S(1)} copy-done((bf16[1,128,2048]{2,1,0:T(8,128)(2,1)S(1)}, bf16[1,128,2048]{2,1,0:T(8,128)(2,1)}, u32[]{:S(2)}) %copy-start.3) | copy-done | bytes 524312
  13.3 1.0 %pack.1 = (bf16[1,272,128]{2,1,0:T(8,128)(2,1)S(1)}, bf16[1,272,128]{2,1,0:T(8,128)(2,1)S(1)}, bf16[2,272,128]{2,1,0:T(8,128)(2,1)S(1)}, bf16[1,256,384]{2,1,0:T...) custom-call(s32[4]{0:T(128)S(1)} %pad_add_fusion.meta.refs_0_, ...), custom_call_target="tpu_custom_call" | custom-call | tf_op jit(solution)/shard_map/pack/pallas_call | solution.py:128
  14.3 0.6 %collective-permute-start.8 = (bf16[2,272,128]{2,1,0:T(8,128)(2,1)S(1)}, bf16[2,272,128]{2,1,0:T(8,128)(2,1)S(1)}, u32[]{:S(2)}, u32[]{:S(2)}) collective-permute-start(bf16[2,272,128]{2,1,0:T(8,128)(2,1)S(1)} %get-tuple-element.58), channel_id=1, source_target_pairs={{0,2},{1,3},{2,0},{3,1},{4,6},{5,7},{6,4},{7,5},{8,10},{9,11},{10,... | collective-permute-start | bytes 417800 | tf_op jit(solution)/shard_map/ppermute | solution.py:27
  14.9 1.7 %collective-permute-done.3.refs_6_ = bf16[896,128]{1,0:T(8,128)(2,1)S(1)} collective-permute-done((bf16[896,128]{1,0:T(8,128)(2,1)S(1)}, bf16[896,128]{1,0:T(8,128)(2,1)S(1)}, u32[]{:S(2)}, u32[]{:S(2)}) %collective-permute-start.3) | collective-permute-done | bytes 229408 | tf_op jit(solution)/shard_map/ppermute | solution.py:27
  16.8 1.5 %collective-permute-start.11 = (bf16[2,256,384]{2,1,0:T(8,128)(2,1)S(1)}, bf16[2,256,384]{2,1,0:T(8,128)(2,1)S(1)}, u32[]{:S(2)}, u32[]{:S(2)}) collective-permute-start(bf16[2,256,384]{2,1,0:T(8,128)(2,1)S(1)} %get-tuple-element.67), channel_id=1, source_target_pairs={{0,2},{1,3},{2,0},{3,1},{4,6},{5,7},{6,4},{7,5},{8,10},{9,11},{10,... | collective-permute-start | bytes 1179656 | tf_op jit(solution)/shard_map/ppermute | solution.py:27
  18.3 2.1 %collective-permute-done.8.refs_9_ = bf16[2,272,128]{2,1,0:T(8,128)(2,1)S(1)} collective-permute-done((bf16[2,272,128]{2,1,0:T(8,128)(2,1)S(1)}, bf16[2,272,128]{2,1,0:T(8,128)(2,1)S(1)}, u32[]{:S(2)}, u32[]{:S(2)}) %collective-permute-start.8) | collective-permute-done | bytes 139296 | tf_op jit(solution)/shard_map/ppermute | solution.py:27
  21.1 0.7 %collective-permute-done.9.refs_10_ = bf16[1,272,128]{2,1,0:T(8,128)(2,1)S(1)} collective-permute-done((bf16[1,272,128]{2,1,0:T(8,128)(2,1)S(1)}, bf16[1,272,128]{2,1,0:T(8,128)(2,1)S(1)}, u32[]{:S(2)}, u32[]{:S(2)}) %collective-permute-start.9) | collective-permute-done | bytes 69664 | tf_op jit(solution)/shard_map/ppermute | solution.py:27
  21.7 0.8 %collective-permute-start.10 = (bf16[896,128]{1,0:T(8,128)(2,1)S(1)}, bf16[896,128]{1,0:T(8,128)(2,1)S(1)}, u32[]{:S(2)}, u32[]{:S(2)}) collective-permute-start(bf16[896,128]{1,0:T(8,128)(2,1)S(1)} %collective-permute-done.3.refs_6_), channel_id=1, source_target_pairs={{0,4},{4,0},{8,12},{12,8},{16,20},{20,16},{24,28},{28,24},{1,5},{5... | collective-permute-start | bytes 688136 | tf_op jit(solution)/shard_map/ppermute | solution.py:27
  22.5 3.0 %attention.3 = (bf16[1,2,128,128]{3,2,1,0:T(8,128)(2,1)S(1)}, bf16[1,2,128,128]{3,2,1,0:T(8,128)(2,1)S(1)}, bf16[2,2,128,128]{3,2,1,0:T(8,128)(2,1)S(1)}, bf16[512,896]{1,0:T(8,128)(2,1)S(1)}, s32[32,128]{1,0:T(8,128)S(1)}) custom-call(s32[4]{0:T(128)S(1)} %pad_add_fusion.meta.refs_0_, bf16[128,896]{1,0:T(8,128)(2,1)S(1)} %bitcast.8, ...), custom_call_target="tpu_custom_call" | custom-call | tf_op jit(solution)/shard_map/attention/pallas_call | solution.py:292
  25.6 3.4 %collective-permute-done.6.refs_8_ = bf16[896,128]{1,0:T(8,128)(2,1)S(1)} collective-permute-done((bf16[896,128]{1,0:T(8,128)(2,1)S(1)}, bf16[896,128]{1,0:T(8,128)(2,1)S(1)}, u32[]{:S(2)}, u32[]{:S(2)}) %collective-permute-start.6) | collective-permute-done | bytes 229408 | tf_op jit(solution)/shard_map/ppermute | solution.py:27
  30.0 1.4 %collective-permute-start.17 = (bf16[896,128]{1,0:T(8,128)(2,1)S(1)}, bf16[896,128]{1,0:T(8,128)(2,1)S(1)}, u32[]{:S(2)}, u32[]{:S(2)}) collective-permute-start(bf16[896,128]{1,0:T(8,128)(2,1)S(1)} %collective-permute-done.5.refs_5_), channel_id=1, source_target_pairs={{0,8},{4,12},{8,0},{12,4},{16,24},{20,28},{24,16},{28,20},{1,9},{5... | collective-permute-start | bytes 688136 | tf_op jit(solution)/shard_map/ppermute | solution.py:27
  31.9 3.7 %attention.4 = (bf16[1,2,128,256]{3,2,1,0:T(8,128)(2,1)S(1)}, bf16[1,2,128,256]{3,2,1,0:T(8,128)(2,1)S(1)}, bf16[2,2,128,256]{3,2,1,0:T(8,128)(2,1)S(1)}, bf16[512,896]{1,0:T(8,128)(2,1)S(1)}) custom-call(s32[4]{0:T(128)S(1)} %pad_add_fusion.meta.refs_0_, bf16[128,896]{1,0:T(8,128)(2,1)S(1)} %bitcast.9, bf16[128,896]{1,0:T(8,128)(2,1)S(1)} %collective-permute-done.refs_2_, ...), custom_call_target="tpu_custom_call" | custom-call | tf_op jit(solution)/shard_map/attention/pallas_call | solution.py:292
  35.5 1.9 %collective-permute-start.19 = (bf16[2,2,128,256]{3,2,1,0:T(8,128)(2,1)S(1)}, bf16[2,2,128,256]{3,2,1,0:T(8,128)(2,1)S(1)}, u32[]{:S(2)}, u32[]{:S(2)}) collective-permute-start(bf16[2,2,128,256]{3,2,1,0:T(8,128)(2,1)S(1)} %get-tuple-element.90), channel_id=1, source_target_pairs={{0,2},{1,3},{2,0},{3,1},{4,6},{5,7},{6,4},{7,5},{8,10},{9,11},{10,... | collective-permute-start | bytes 786440 | tf_op jit(solution)/shard_map/ppermute | solution.py:27
  37.6 1.1 %collective-permute-done.18.refs_6_ = bf16[896,128]{1,0:T(8,128)(2,1)S(1)} collective-permute-done((bf16[896,128]{1,0:T(8,128)(2,1)S(1)}, bf16[896,128]{1,0:T(8,128)(2,1)S(1)}, u32[]{:S(2)}, u32[]{:S(2)}) %collective-permute-start.18) | collective-permute-done | bytes 229408 | tf_op jit(solution)/shard_map/ppermute | solution.py:27
  38.7 2.9 %attention.5 = (bf16[1,2,128,128]{3,2,1,0:T(8,128)(2,1)S(1)}, bf16[1,2,128,128]{3,2,1,0:T(8,128)(2,1)S(1)}, bf16[2,2,128,128]{3,2,1,0:T(8,128)(2,1)S(1)}, f32[256,896]{1,0:T(8,128)S(1)}, bf16[256,896]{1,0:T(8,128)(2,1)S(1)}) custom-call(s32[4]{0:T(128)S(1)} %pad_add_fusion.meta.refs_0_, bf16[128,896]{1,0:T(8,128)(2,1)S(1)} %bitcast.10, ...), custom_call_target="tpu_custom_call" | custom-call | flops 2400000000 | tf_op jit(solution)/shard_map/attention/pallas_call | solution.py:292
  41.5 1.9 %collective-permute-done.19.refs_6_ = bf16[2,2,128,256]{3,2,1,0:T(8,128)(2,1)S(1)} collective-permute-done((bf16[2,2,128,256]{3,2,1,0:T(8,128)(2,1)S(1)}, bf16[2,2,128,256]{3,2,1,0:T(8,128)(2,1)S(1)}, u32[]{:S(2)}, u32[]{:S(2)}) %collective-permute-start.19) | collective-permute-done | bytes 262176 | tf_op jit(solution)/shard_map/ppermute | solution.py:27
  43.4 1.5 %collective-permute-start.23 = (bf16[2,2,128,128]{3,2,1,0:T(8,128)(2,1)S(1)}, bf16[2,2,128,128]{3,2,1,0:T(8,128)(2,1)S(1)}, u32[]{:S(2)}, u32[]{:S(2)}) collective-permute-start(bf16[2,2,128,128]{3,2,1,0:T(8,128)(2,1)S(1)} %get-tuple-element.96), channel_id=1, source_target_pairs={{0,2},{1,3},{2,0},{3,1},{4,6},{5,7},{6,4},{7,5},{8,10},{9,11},{10,... | collective-permute-start | bytes 393224 | tf_op jit(solution)/shard_map/ppermute | solution.py:27
  45.4 1.5 %collective-permute-start.26 = (bf16[128,896]{1,0:T(8,128)(2,1)S(1)}, bf16[128,896]{1,0:T(8,128)(2,1)S(1)}, u32[]{:S(2)}, u32[]{:S(2)}) collective-permute-start(bf16[128,896]{1,0:T(8,128)(2,1)S(1)} %slice.35), channel_id=1, source_target_pairs={{0,2},{1,3},{2,0},{3,1},{4,6},{5,7},{6,4},{7,5},{8,10},{9,11},{10,... | collective-permute-start | bytes 688136 | tf_op jit(solution)/shard_map/ppermute | solution.py:27
  46.9 0.5 collective-permute-start.15
  47.6 2.1 %collective-permute-done.23.refs_10_ = bf16[2,2,128,128]{3,2,1,0:T(8,128)(2,1)S(1)} collective-permute-done((bf16[2,2,128,128]{3,2,1,0:T(8,128)(2,1)S(1)}, bf16[2,2,128,128]{3,2,1,0:T(8,128)(2,1)S(1)}, u32[]{:S(2)}, u32[]{:S(2)}) %collective-permute-start.23) | collective-permute-done | bytes 131104 | tf_op jit(solution)/shard_map/ppermute | solution.py:27
  49.7 0.6 %collective-permute-start.22 = (bf16[1,2,128,128]{3,2,1,0:T(8,128)(2,1)S(1)}, bf16[1,2,128,128]{3,2,1,0:T(8,128)(2,1)S(1)}, u32[]{:S(2)}, u32[]{:S(2)}) collective-permute-start(bf16[1,2,128,128]{3,2,1,0:T(8,128)(2,1)S(1)} %get-tuple-element.95), channel_id=1, source_target_pairs={{0,1},{1,0},{2,3},{3,2},{4,5},{5,4},{6,7},{7,6},{8,9},{9,8},{10,11... | collective-permute-start | bytes 196616 | tf_op jit(solution)/shard_map/ppermute | solution.py:27
  50.4 0.8 %collective-permute-done.22.refs_9_ = bf16[1,2,128,128]{3,2,1,0:T(8,128)(2,1)S(1)} collective-permute-done((bf16[1,2,128,128]{3,2,1,0:T(8,128)(2,1)S(1)}, bf16[1,2,128,128]{3,2,1,0:T(8,128)(2,1)S(1)}, u32[]{:S(2)}, u32[]{:S(2)}) %collective-permute-start.22) | collective-permute-done | bytes 65568 | tf_op jit(solution)/shard_map/ppermute | solution.py:27
  51.6 1.8 %unpack.1 = (bf16[1,128,2048]{2,1,0:T(8,128)(2,1)}, bf16[1,128,2048]{2,1,0:T(8,128)(2,1)}) custom-call(s32[4]{0:T(128)S(1)} %pad_add_fusion.meta.refs_0_, bf16[1,2,128,128]{3,2,1,0:T(8,128)(2,1)S(1)} %get-tuple-element.82.refs_0_, bf16[1,2,128,128]{3,2,1,0:T(8,128)(2,1)S(1)} %collective-permute-done.15.refs_1_, ...), custom_call_target="tpu_custom_call" | custom-call | tf_op jit(solution)/shard_map/unpack/pallas_call | solution.py:327
  53.3 0.9 %collective-permute-done.26 = bf16[128,896]{1,0:T(8,128)(2,1)S(1)} collective-permute-done((bf16[128,896]{1,0:T(8,128)(2,1)S(1)}, bf16[128,896]{1,0:T(8,128)(2,1)S(1)}, u32[]{:S(2)}, u32[]{:S(2)}) %collective-permute-start.26) | collective-permute-done | bytes 229408 | tf_op jit(solution)/shard_map/ppermute | solution.py:27
  54.2 0.8 %slice_add_fusion = f32[128,896]{1,0:T(8,128)} fusion(f32[256,896]{1,0:T(8,128)S(1)} %convert_add_fusion, bf16[128,896]{1,0:T(8,128)(2,1)S(1)} %collective-permute-done.26), kind=kLoop, calls=%fused_computation.2 | loop fusion | flops 229376 | bytes 1146880 | tf_op jit(solution)/shard_map/add | solution.py:436
  (49 shorter events, 3.7 us)
Async XLA Ops:
  0.6 1.2 %copy-start = (bf16[896,512]{1,0:T(8,128)(2,1)S(1)}, bf16[896,512]{1,0:T(8,128)(2,1)}, u32[]{:S(2)}) copy-start(bf16[896,512]{1,0:T(8,128)(2,1)} %param.9) | copy-start | bytes 2752516
  1.8 7.2 %copy-start.1 = (bf16[1,2,64,896]{3,2,1,0:T(8,128)(2,1)S(1)}, bf16[1,2,64,896]{3,2,1,0:T(8,128)(2,1)}, u32[]{:S(2)}) copy-start(bf16[1,2,64,896]{3,2,1,0:T(8,128)(2,1)} %param.8) | copy-start | bytes 688132
  1.9 14.7 %collective-permute-start.3 = (bf16[896,128]{1,0:T(8,128)(2,1)S(1)}, bf16[896,128]{1,0:T(8,128)(2,1)S(1)}, u32[]{:S(2)}, u32[]{:S(2)}) collective-permute-start(bf16[896,128]{1,0:T(8,128)(2,1)S(1)} %constant_dynamic-slice_fusion.refs_5_), channel_id=1, source_target_pairs={{0,16},{4,20},{8,24},{12,28},{16,0},{20,4},{24,8},{28,12},{1,17},{... | collective-permute-start | bytes 688136 | tf_op jit(solution)/shard_map/ppermute | solution.py:27
  6.0 10.8 %collective-permute-start.4 = (bf16[896,128]{1,0:T(8,128)(2,1)S(1)}, bf16[896,128]{1,0:T(8,128)(2,1)S(1)}, u32[]{:S(2)}, u32[]{:S(2)}) collective-permute-start(bf16[896,128]{1,0:T(8,128)(2,1)S(1)} %constant_dynamic-slice_fusion.refs_5_), channel_id=1, source_target_pairs={{0,8},{4,12},{8,0},{12,4},{16,24},{20,28},{24,16},{28,20},{1,9},{5... | collective-permute-start | bytes 688136 | tf_op jit(solution)/shard_map/ppermute | solution.py:27
  7.5 9.2 %collective-permute-start.5 = (bf16[896,128]{1,0:T(8,128)(2,1)S(1)}, bf16[896,128]{1,0:T(8,128)(2,1)S(1)}, u32[]{:S(2)}, u32[]{:S(2)}) collective-permute-start(bf16[896,128]{1,0:T(8,128)(2,1)S(1)} %constant_dynamic-slice_fusion.refs_5_), channel_id=1, source_target_pairs={{0,4},{4,0},{8,12},{12,8},{16,20},{20,16},{24,28},{28,24},{1,5},{5... | collective-permute-start | bytes 688136 | tf_op jit(solution)/shard_map/ppermute | solution.py:27
  9.1 11.9 %collective-permute-start = (bf16[128,896]{1,0:T(8,128)(2,1)S(1)}, bf16[128,896]{1,0:T(8,128)(2,1)S(1)}, u32[]{:S(2)}, u32[]{:S(2)}) collective-permute-start(bf16[128,896]{1,0:T(8,128)(2,1)S(1)} %bitcast.6), channel_id=1, source_target_pairs={{0,2},{1,3},{2,0},{3,1},{4,6},{5,7},{6,4},{7,5},{8,10},{9,11},{10,... | collective-permute-start | bytes 688136 | tf_op jit(solution)/shard_map/ppermute | solution.py:27
  10.5 0.7 %copy-start.5 = (s32[1,8]{1,0:T(1,128)S(1)}, s32[1,8]{1,0:T(1,128)}, u32[]{:S(2)}) copy-start(s32[1,8]{1,0:T(1,128)} %slots.1) | copy-start | bytes 100
  11.2 1.0 %copy-start.2 = (bf16[1,128,2048]{2,1,0:T(8,128)(2,1)S(1)}, bf16[1,128,2048]{2,1,0:T(8,128)(2,1)}, u32[]{:S(2)}) copy-start(bf16[1,128,2048]{2,1,0:T(8,128)(2,1)} %queries.1) | copy-start | bytes 1572868
  12.3 1.0 %copy-start.3 = (bf16[1,128,2048]{2,1,0:T(8,128)(2,1)S(1)}, bf16[1,128,2048]{2,1,0:T(8,128)(2,1)}, u32[]{:S(2)}) copy-start(bf16[1,128,2048]{2,1,0:T(8,128)(2,1)} %grad_out.1) | copy-start | bytes 1572868
  14.3 6.2 %collective-permute-start.8 = (bf16[2,272,128]{2,1,0:T(8,128)(2,1)S(1)}, bf16[2,272,128]{2,1,0:T(8,128)(2,1)S(1)}, u32[]{:S(2)}, u32[]{:S(2)}) collective-permute-start(bf16[2,272,128]{2,1,0:T(8,128)(2,1)S(1)} %get-tuple-element.58), channel_id=1, source_target_pairs={{0,2},{1,3},{2,0},{3,1},{4,6},{5,7},{6,4},{7,5},{8,10},{9,11},{10,... | collective-permute-start | bytes 417800 | tf_op jit(solution)/shard_map/ppermute | solution.py:27
  16.8 12.6 %collective-permute-start.11 = (bf16[2,256,384]{2,1,0:T(8,128)(2,1)S(1)}, bf16[2,256,384]{2,1,0:T(8,128)(2,1)S(1)}, u32[]{:S(2)}, u32[]{:S(2)}) collective-permute-start(bf16[2,256,384]{2,1,0:T(8,128)(2,1)S(1)} %get-tuple-element.67), channel_id=1, source_target_pairs={{0,2},{1,3},{2,0},{3,1},{4,6},{5,7},{6,4},{7,5},{8,10},{9,11},{10,... | collective-permute-start | bytes 1179656 | tf_op jit(solution)/shard_map/ppermute | solution.py:27
  18.3 2.7 %collective-permute-start.7 = (bf16[1,272,128]{2,1,0:T(8,128)(2,1)S(1)}, bf16[1,272,128]{2,1,0:T(8,128)(2,1)S(1)}, u32[]{:S(2)}, u32[]{:S(2)}) collective-permute-start(bf16[1,272,128]{2,1,0:T(8,128)(2,1)S(1)} %get-tuple-element.57), channel_id=1, source_target_pairs={{0,1},{1,0},{2,3},{3,2},{4,5},{5,4},{6,7},{7,6},{8,9},{9,8},{10,11... | collective-permute-start | bytes 208904 | tf_op jit(solution)/shard_map/ppermute | solution.py:27
  20.5 1.3 %collective-permute-start.9 = (bf16[1,272,128]{2,1,0:T(8,128)(2,1)S(1)}, bf16[1,272,128]{2,1,0:T(8,128)(2,1)S(1)}, u32[]{:S(2)}, u32[]{:S(2)}) collective-permute-start(bf16[1,272,128]{2,1,0:T(8,128)(2,1)S(1)} %slice.29), channel_id=1, source_target_pairs={{0,1},{1,0},{2,3},{3,2},{4,5},{5,4},{6,7},{7,6},{8,9},{9,8},{10,11... | collective-permute-start | bytes 208904 | tf_op jit(solution)/shard_map/ppermute | solution.py:27
  20.5 2.1 %collective-permute-start.1 = (bf16[128,896]{1,0:T(8,128)(2,1)S(1)}, bf16[128,896]{1,0:T(8,128)(2,1)S(1)}, u32[]{:S(2)}, u32[]{:S(2)}) collective-permute-start(bf16[128,896]{1,0:T(8,128)(2,1)S(1)} %bitcast.7), channel_id=1, source_target_pairs={{0,1},{1,0},{2,3},{3,2},{4,5},{5,4},{6,7},{7,6},{8,9},{9,8},{10,11... | collective-permute-start | bytes 688136 | tf_op jit(solution)/shard_map/ppermute | solution.py:27
  21.0 1.6 %collective-permute-start.2 = (bf16[128,896]{1,0:T(8,128)(2,1)S(1)}, bf16[128,896]{1,0:T(8,128)(2,1)S(1)}, u32[]{:S(2)}, u32[]{:S(2)}) collective-permute-start(bf16[128,896]{1,0:T(8,128)(2,1)S(1)} %collective-permute-done.refs_2_), channel_id=1, source_target_pairs={{0,1},{1,0},{2,3},{3,2},{4,5},{5,4},{6,7},{7,6},{8,9},{9,8},{10,11... | collective-permute-start | bytes 688136 | tf_op jit(solution)/shard_map/ppermute | solution.py:27
  21.1 7.9 %collective-permute-start.6 = (bf16[896,128]{1,0:T(8,128)(2,1)S(1)}, bf16[896,128]{1,0:T(8,128)(2,1)S(1)}, u32[]{:S(2)}, u32[]{:S(2)}) collective-permute-start(bf16[896,128]{1,0:T(8,128)(2,1)S(1)} %collective-permute-done.3.refs_6_), channel_id=1, source_target_pairs={{0,8},{4,12},{8,0},{12,4},{16,24},{20,28},{24,16},{28,20},{1,9},{5... | collective-permute-start | bytes 688136 | tf_op jit(solution)/shard_map/ppermute | solution.py:27
  21.7 7.7 %collective-permute-start.10 = (bf16[896,128]{1,0:T(8,128)(2,1)S(1)}, bf16[896,128]{1,0:T(8,128)(2,1)S(1)}, u32[]{:S(2)}, u32[]{:S(2)}) collective-permute-start(bf16[896,128]{1,0:T(8,128)(2,1)S(1)} %collective-permute-done.3.refs_6_), channel_id=1, source_target_pairs={{0,4},{4,0},{8,12},{12,8},{16,20},{20,16},{24,28},{28,24},{1,5},{5... | collective-permute-start | bytes 688136 | tf_op jit(solution)/shard_map/ppermute | solution.py:27
  29.4 2.4 %collective-permute-start.13 = (bf16[1,256,384]{2,1,0:T(8,128)(2,1)S(1)}, bf16[1,256,384]{2,1,0:T(8,128)(2,1)S(1)}, u32[]{:S(2)}, u32[]{:S(2)}) collective-permute-start(bf16[1,256,384]{2,1,0:T(8,128)(2,1)S(1)} %slice.23), channel_id=1, source_target_pairs={{0,1},{1,0},{2,3},{3,2},{4,5},{5,4},{6,7},{7,6},{8,9},{9,8},{10,11... | collective-permute-start | bytes 589832 | tf_op jit(solution)/shard_map/ppermute | solution.py:27
  29.5 2.4 %collective-permute-start.12 = (bf16[1,256,384]{2,1,0:T(8,128)(2,1)S(1)}, bf16[1,256,384]{2,1,0:T(8,128)(2,1)S(1)}, u32[]{:S(2)}, u32[]{:S(2)}) collective-permute-start(bf16[1,256,384]{2,1,0:T(8,128)(2,1)S(1)} %get-tuple-element.74), channel_id=1, source_target_pairs={{0,1},{1,0},{2,3},{3,2},{4,5},{5,4},{6,7},{7,6},{8,9},{9,8},{10,11... | collective-permute-start | bytes 589832 | tf_op jit(solution)/shard_map/ppermute | solution.py:27
  30.0 7.6 %collective-permute-start.17 = (bf16[896,128]{1,0:T(8,128)(2,1)S(1)}, bf16[896,128]{1,0:T(8,128)(2,1)S(1)}, u32[]{:S(2)}, u32[]{:S(2)}) collective-permute-start(bf16[896,128]{1,0:T(8,128)(2,1)S(1)} %collective-permute-done.5.refs_5_), channel_id=1, source_target_pairs={{0,8},{4,12},{8,0},{12,4},{16,24},{20,28},{24,16},{28,20},{1,9},{5... | collective-permute-start | bytes 688136 | tf_op jit(solution)/shard_map/ppermute | solution.py:27
  31.4 7.3 %collective-permute-start.18 = (bf16[896,128]{1,0:T(8,128)(2,1)S(1)}, bf16[896,128]{1,0:T(8,128)(2,1)S(1)}, u32[]{:S(2)}, u32[]{:S(2)}) collective-permute-start(bf16[896,128]{1,0:T(8,128)(2,1)S(1)} %collective-permute-done.6.refs_8_), channel_id=1, source_target_pairs={{0,4},{4,0},{8,12},{12,8},{16,20},{20,16},{24,28},{28,24},{1,5},{5... | collective-permute-start | bytes 688136 | tf_op jit(solution)/shard_map/ppermute | solution.py:27
  31.6 5.8 %collective-permute-start.14 = (bf16[2,2,128,128]{3,2,1,0:T(8,128)(2,1)S(1)}, bf16[2,2,128,128]{3,2,1,0:T(8,128)(2,1)S(1)}, u32[]{:S(2)}, u32[]{:S(2)}) collective-permute-start(bf16[2,2,128,128]{3,2,1,0:T(8,128)(2,1)S(1)} %get-tuple-element.81), channel_id=1, source_target_pairs={{0,2},{1,3},{2,0},{3,1},{4,6},{5,7},{6,4},{7,5},{8,10},{9,11},{10,... | collective-permute-start | bytes 393224 | tf_op jit(solution)/shard_map/ppermute | solution.py:27
  35.5 7.9 %collective-permute-start.19 = (bf16[2,2,128,256]{3,2,1,0:T(8,128)(2,1)S(1)}, bf16[2,2,128,256]{3,2,1,0:T(8,128)(2,1)S(1)}, u32[]{:S(2)}, u32[]{:S(2)}) collective-permute-start(bf16[2,2,128,256]{3,2,1,0:T(8,128)(2,1)S(1)} %get-tuple-element.90), channel_id=1, source_target_pairs={{0,2},{1,3},{2,0},{3,1},{4,6},{5,7},{6,4},{7,5},{8,10},{9,11},{10,... | collective-permute-start | bytes 786440 | tf_op jit(solution)/shard_map/ppermute | solution.py:27
  43.4 1.8 %collective-permute-start.25 = (bf16[256,896]{1,0:T(8,128)(2,1)S(1)}, bf16[256,896]{1,0:T(8,128)(2,1)S(1)}, u32[]{:S(2)}, u32[]{:S(2)}) collective-permute-start(bf16[256,896]{1,0:T(8,128)(2,1)S(1)} %get-tuple-element.100), channel_id=1, source_target_pairs={{0,1},{1,0},{2,3},{3,2},{4,5},{5,4},{6,7},{7,6},{8,9},{9,8},{10,11... | collective-permute-start | bytes 1376264 | tf_op jit(solution)/shard_map/ppermute | solution.py:27
  43.4 6.3 %collective-permute-start.23 = (bf16[2,2,128,128]{3,2,1,0:T(8,128)(2,1)S(1)}, bf16[2,2,128,128]{3,2,1,0:T(8,128)(2,1)S(1)}, u32[]{:S(2)}, u32[]{:S(2)}) collective-permute-start(bf16[2,2,128,128]{3,2,1,0:T(8,128)(2,1)S(1)} %get-tuple-element.96), channel_id=1, source_target_pairs={{0,2},{1,3},{2,0},{3,1},{4,6},{5,7},{6,4},{7,5},{8,10},{9,11},{10,... | collective-permute-start | bytes 393224 | tf_op jit(solution)/shard_map/ppermute | solution.py:27
  45.4 8.9 %collective-permute-start.26 = (bf16[128,896]{1,0:T(8,128)(2,1)S(1)}, bf16[128,896]{1,0:T(8,128)(2,1)S(1)}, u32[]{:S(2)}, u32[]{:S(2)}) collective-permute-start(bf16[128,896]{1,0:T(8,128)(2,1)S(1)} %slice.35), channel_id=1, source_target_pairs={{0,2},{1,3},{2,0},{3,1},{4,6},{5,7},{6,4},{7,5},{8,10},{9,11},{10,... | collective-permute-start | bytes 688136 | tf_op jit(solution)/shard_map/ppermute | solution.py:27
  46.9 2.8 %collective-permute-start.16 = (bf16[1,2,128,128]{3,2,1,0:T(8,128)(2,1)S(1)}, bf16[1,2,128,128]{3,2,1,0:T(8,128)(2,1)S(1)}, u32[]{:S(2)}, u32[]{:S(2)}) collective-permute-start(bf16[1,2,128,128]{3,2,1,0:T(8,128)(2,1)S(1)} %slice.24), channel_id=1, source_target_pairs={{0,1},{1,0},{2,3},{3,2},{4,5},{5,4},{6,7},{7,6},{8,9},{9,8},{10,11... | collective-permute-start | bytes 196616 | tf_op jit(solution)/shard_map/ppermute | solution.py:27
  46.9 3.4 %collective-permute-start.15 = (bf16[1,2,128,128]{3,2,1,0:T(8,128)(2,1)S(1)}, bf16[1,2,128,128]{3,2,1,0:T(8,128)(2,1)S(1)}, u32[]{:S(2)}, u32[]{:S(2)}) collective-permute-start(bf16[1,2,128,128]{3,2,1,0:T(8,128)(2,1)S(1)} %get-tuple-element.83), channel_id=1, source_target_pairs={{0,1},{1,0},{2,3},{3,2},{4,5},{5,4},{6,7},{7,6},{8,9},{9,8},{10,11... | collective-permute-start | bytes 196616 | tf_op jit(solution)/shard_map/ppermute | solution.py:27
  47.4 4.1 %collective-permute-start.21 = (bf16[1,2,128,256]{3,2,1,0:T(8,128)(2,1)S(1)}, bf16[1,2,128,256]{3,2,1,0:T(8,128)(2,1)S(1)}, u32[]{:S(2)}, u32[]{:S(2)}) collective-permute-start(bf16[1,2,128,256]{3,2,1,0:T(8,128)(2,1)S(1)} %slice.25), channel_id=1, source_target_pairs={{0,1},{1,0},{2,3},{3,2},{4,5},{5,4},{6,7},{7,6},{8,9},{9,8},{10,11... | collective-permute-start | bytes 393224 | tf_op jit(solution)/shard_map/ppermute | solution.py:27
  49.7 1.9 %collective-permute-start.20 = (bf16[1,2,128,256]{3,2,1,0:T(8,128)(2,1)S(1)}, bf16[1,2,128,256]{3,2,1,0:T(8,128)(2,1)S(1)}, u32[]{:S(2)}, u32[]{:S(2)}) collective-permute-start(bf16[1,2,128,256]{3,2,1,0:T(8,128)(2,1)S(1)} %get-tuple-element.92), channel_id=1, source_target_pairs={{0,1},{1,0},{2,3},{3,2},{4,5},{5,4},{6,7},{7,6},{8,9},{9,8},{10,11... | collective-permute-start | bytes 393224 | tf_op jit(solution)/shard_map/ppermute | solution.py:27
  49.7 1.5 %collective-permute-start.22 = (bf16[1,2,128,128]{3,2,1,0:T(8,128)(2,1)S(1)}, bf16[1,2,128,128]{3,2,1,0:T(8,128)(2,1)S(1)}, u32[]{:S(2)}, u32[]{:S(2)}) collective-permute-start(bf16[1,2,128,128]{3,2,1,0:T(8,128)(2,1)S(1)} %get-tuple-element.95), channel_id=1, source_target_pairs={{0,1},{1,0},{2,3},{3,2},{4,5},{5,4},{6,7},{7,6},{8,9},{9,8},{10,11... | collective-permute-start | bytes 196616 | tf_op jit(solution)/shard_map/ppermute | solution.py:27
  50.3 1.3 %collective-permute-start.24 = (bf16[1,2,128,128]{3,2,1,0:T(8,128)(2,1)S(1)}, bf16[1,2,128,128]{3,2,1,0:T(8,128)(2,1)S(1)}, u32[]{:S(2)}, u32[]{:S(2)}) collective-permute-start(bf16[1,2,128,128]{3,2,1,0:T(8,128)(2,1)S(1)} %slice.30), channel_id=1, source_target_pairs={{0,1},{1,0},{2,3},{3,2},{4,5},{5,4},{6,7},{7,6},{8,9},{9,8},{10,11... | collective-permute-start | bytes 196616 | tf_op jit(solution)/shard_map/ppermute | solution.py:27
  (1 other events, 0.7 us)
